TPU v7x, 32 devices: a whole 2x2x4 slice. The times are simulated.
32 devices in a mesh: group: 2 (over x), expert: 16 (over z, y, core).
Axes of the slice: x: 2, y: 2, z: 4, core: 2. Of those that a mesh axis runs over, the one named last changes fastest.
Arguments:
- tokens: bfloat16 [4096, 1536], P(('group', 'expert')), parts along dimension 0, may hold values from -6 to 6
- expert_ids: int32 [4096, 4], P(('group', 'expert')), parts along dimension 0, may hold values from 0 to 15, all different within a row; in each aligned block of 128 rows (0 to 127, 128 to 255, ...) at most 64 rows name the same one
- gate_levels: int32 [4096, 4], P(('group', 'expert')), parts along dimension 0, may hold values from 1 to 1023
- failed_device: int32 [1], replicated, may hold values from 0 to 15
- replica_holders: int32 [16, 4], replicated, may hold values from 0 to 15, as said below
- w_gate: bfloat16 [16, 1536, 1536], P('expert'), may hold values from -0.15625 to 0.15625
- w_down: bfloat16 [16, 1536, 1536], P('expert'), may hold values from -0.15625 to 0.15625
- spare_gate: bfloat16 [16, 1536, 384], P('expert'), may hold values from -0.15625 to 0.15625
- spare_down: bfloat16 [16, 384, 1536], P('expert'), may hold values from -0.15625 to 0.15625
Outputs:
- layer_out: bfloat16 [4096, 1536], P(('group', 'expert')), parts along dimension 0
There are 2 independent parts, one for each index of `group`. A program takes and returns all parts, laid end to end along the dimension named above; an argument that names none is the same for every part. Nothing has to cross between parts.
Inputs may be any that keep to these rules, and one draw needn't show every extreme that they name: `expert_ids`: within the rows of one device, no expert is named more than 64 times, and in some device's rows one expert is named exactly 64 times. `replica_holders`: each row e lists 4 distinct devices, none equal to e; every device appears in exactly 4 rows.
All inputs are finite; a program needn't handle non-finite values.
Results may differ from a plain program's by a relative error of at most 0.0059.
Values may be sent and summed in bfloat16 or wider, within the bound.
No kernel may reach another device: no remote copies, remote signals or barrier semaphores. Data moves between devices by JAX's collectives and lax.ppermute only.
A program may use at most 128 MiB of HBM per device.

v0:
```python
import jax
import jax.numpy as jnp
from jax import lax
from jax.sharding import PartitionSpec as P


def gated_unit(values):
    return values * jax.nn.sigmoid(1.702 * values)


def spare_term(rows_in, gate_part, down_part):
    hidden = gated_unit(jnp.dot(rows_in, gate_part, preferred_element_type=jnp.float32)).astype(
        jnp.bfloat16
    )
    return jnp.dot(hidden, down_part, preferred_element_type=jnp.float32)


def shards(
    tokens,
    expert_ids,
    gate_levels,
    failed_device,
    replica_holders,
    w_gate,
    w_down,
    spare_gate,
    spare_down,
):
    owners = lax.axis_size("expert")
    tok_count, top_count = expert_ids.shape
    capacity = 2 * tok_count * top_count // owners
    width = tokens.shape[1]
    pair_ids = expert_ids.reshape(-1)
    owner_iota = jnp.arange(owners, dtype=jnp.int32)
    onehot_pairs = (pair_ids[:, None] == owner_iota[None, :]).astype(jnp.int32)
    earlier = jnp.cumsum(onehot_pairs, axis=0) - onehot_pairs
    slot_index = jnp.sum(earlier * onehot_pairs, axis=1)
    flat_slot = (pair_ids * capacity + slot_index).reshape(tok_count, top_count)
    slot_iota = jnp.arange(owners * capacity, dtype=jnp.int32)
    picker = jnp.any(slot_iota[:, None, None] == flat_slot[None, :, :], axis=2).astype(jnp.bfloat16)
    outgoing = jnp.dot(picker, tokens, preferred_element_type=jnp.float32).astype(jnp.bfloat16)
    outgoing = outgoing.reshape(owners, capacity, width)
    gate_local = w_gate[0]
    down_local = w_down[0]
    hidden = gated_unit(
        jnp.einsum(
            "scd,df->scf",
            lax.all_to_all(outgoing, "expert", split_axis=0, concat_axis=0, tiled=True),
            gate_local,
            preferred_element_type=jnp.float32,
        )
    ).astype(jnp.bfloat16)
    result = jnp.einsum(
        "scf,fd->scd", hidden, down_local, preferred_element_type=jnp.float32
    ).astype(jnp.bfloat16)
    returned = lax.all_to_all(result, "expert", split_axis=0, concat_axis=0, tiled=True)
    failed_id = failed_device[0]
    holder_row = lax.dynamic_index_in_dim(replica_holders, failed_id, 0, keepdims=False)
    standby_in = lax.dynamic_index_in_dim(outgoing, failed_id, 0, keepdims=False)
    spare_in = spare_gate[0]
    spare_out = spare_down[0]
    my_index = lax.axis_index("expert")
    holder_flag = jnp.any(holder_row == my_index).astype(jnp.float32)
    gathered = lax.all_gather(standby_in, "expert", axis=0, tiled=True)
    summed = lax.psum_scatter(
        spare_term(gathered, spare_in, spare_out) * holder_flag,
        "expert",
        scatter_dimension=0,
        tiled=True,
    )
    standby_out = summed.astype(jnp.bfloat16)
    zero_index = jnp.zeros((), jnp.int32)
    merged = lax.dynamic_update_slice(
        returned, standby_out[None], (failed_id, zero_index, zero_index)
    )
    flat_rows = merged.reshape(owners * capacity, width)
    picked = flat_rows[flat_slot]
    level_weights = gate_levels.astype(jnp.float32) / 1024.0
    combined = jnp.sum(picked.astype(jnp.float32) * level_weights[:, :, None], axis=1)
    return combined.astype(jnp.bfloat16)


def solution(mesh):
    in_specs = (
        P(("group", "expert"), None),
        P(("group", "expert"), None),
        P(("group", "expert"), None),
        P(),
        P(),
        P("expert", None, None),
        P("expert", None, None),
        P("expert", None, None),
        P("expert", None, None),
    )
    out_specs = P(("group", "expert"), None)
    return jax.shard_map(shards, mesh=mesh, in_specs=in_specs, out_specs=out_specs, check_vma=False)
```

profile of v0, /device:TPU:0, one launch (start us, length us, event | category | flops | bytes accessed | tf_op | source)
XLA Modules:
  0.0 265.8 jit_solution(3297279403789674114)
XLA Ops:
  6.5 0.0 copy-start
  6.5 0.0 all-gather.3.cloned.1.call-start
  6.5 0.9 copy.25
  7.4 0.1 eq.50
  7.5 0.1 eq.46
  8.3 1.2 reduce-window.6
  9.5 0.2 slice_reduce_fusion
  9.7 0.1 fusion.26
  9.8 0.1 reduce_sum.21
  9.9 0.1 copy.28
  10.0 0.7 compare_select_fusion
  10.7 0.4 fusion.11
  11.1 3.7 %convolution_convert_fusion = bf16[1024,1536]{1,0:T(8,128)(2,1)} fusion(pred[1024,128]{1,0:T(8,128)(4,1)S(1)} %fusion.11, bf16[128,1536]{1,0:T(8,128)(2,1)} %param.9), kind=kOutput, calls=%fused_computation.8 | convolution fusion | flops 404226048 | bytes 3670016 | tf_op jit(solution)/shard_map/dot_general | solution.py:41
  14.7 1.6 constant_dynamic-slice_fusion
  16.3 0.0 all-gather.3.cloned.1.call-update
  16.4 0.0 copy-start.1
  16.4 0.0 copy-start.3
  16.4 7.6 %all-to-all-start = ((bf16[16,64,1536]{2,1,0:T(8,128)(2,1)}), bf16[16,64,1536]{2,1,0:T(8,128)(2,1)}, u32[]{:S(2)}, u32[]{:S(2)}) async-start(bf16[16,64,1536]{2,1,0:T(8,128)(2,1)} %bitcast.61), calls=%async_computation | async-start | bytes 6291456 | tf_op jit(solution)/shard_map/all_to_all | solution.py:48
  24.0 0.0 reduce-scatter.2.cloned.1.call-start
  24.0 0.0 copy-done.1
  24.0 0.8 fusion.28
  25.5 71.2 %all-gather.3.cloned.1.call-done = bf16[1,1024,1536]{2,1,0:T(8,128)(2,1)} async-done(((bf16[1,64,1536]{2,1,0:T(8,128)(2,1)}), bf16[1,1024,1536]{2,1,0:T(8,128)(2,1)}) %all-gather.3.cloned.1.call-update) | async-done | bytes 3145744 | tf_op jit(solution)/shard_map/all_gather | solution.py:64
  96.8 0.0 copy-done
  96.8 0.0 copy-done.3
  96.8 8.0 %convolution_multiply_fusion = f32[1024,1536]{1,0:T(8,128)} fusion(f32[]{:T(128)S(6)} %convert_element_type.41, bf16[1,384,1536]{2,1,0:T(8,128)(2,1)S(1)} %copy-done, bf16[1,1536,384]{2,1,0:T(8,128)(2,1)S(1)} %copy-done.3, bf16[1,1024,1536]{2,1,0:T(8,128)(2,1)} %all-gather.3.cloned.1.call-done), kind=kOutput, calls=%fused_computation.6 | convolution fusion | flops 2419851264 | bytes 11796484 | tf_op jit(solution)/shard_map/dot_general | solution.py:15
  104.7 0.0 reduce-scatter.2.cloned.1.call-update
  104.8 0.0 all-to-all-done
  104.8 8.8 %multiply_convert_fusion = bf16[16,64,1536]{2,1,0:T(8,128)(2,1)S(1)} fusion(bf16[16,64,1536]{2,1,0:T(8,128)(2,1)} %all-to-all-done, bf16[1,1536,1536]{2,1,0:T(8,128)(2,1)} %param.14), kind=kOutput, calls=%fused_computation.1 | convolution fusion | flops 4841275392 | bytes 11010048 | tf_op jit(solution)/shard_map/scd,df->scf/dot_general | solution.py:46
  113.5 8.8 %fusion.6 = bf16[16,64,1536]{2,1,0:T(8,128)(2,1)} fusion(bf16[16,64,1536]{2,1,0:T(8,128)(2,1)S(1)} %multiply_convert_fusion, bf16[1,1536,1536]{2,1,0:T(8,128)(2,1)} %param.15), kind=kOutput, calls=%fused_computation.7 | convolution fusion | flops 4833411072 | bytes 11010048 | tf_op jit(solution)/shard_map/scf,fd->scd/dot_general | solution.py:53
  122.3 0.0 copy-start.2
  122.3 13.4 %all-to-all-start.1 = ((bf16[16,64,1536]{2,1,0:T(8,128)(2,1)}), bf16[16,64,1536]{2,1,0:T(8,128)(2,1)}, u32[]{:S(2)}, u32[]{:S(2)}) async-start(bf16[16,64,1536]{2,1,0:T(8,128)(2,1)} %fusion.6), calls=%async_computation.1 | async-start | bytes 6291456 | tf_op jit(solution)/shard_map/all_to_all | solution.py:56
  135.8 0.1 copy.29
  135.9 0.1 reshape.40
  136.0 0.0 copy-done.2
  136.0 0.1 copy.30
  136.1 84.3 %all-to-all-done.1 = bf16[16,64,1536]{2,1,0:T(8,128)(2,1)} async-done(((bf16[16,64,1536]{2,1,0:T(8,128)(2,1)}), bf16[16,64,1536]{2,1,0:T(8,128)(2,1)}, u32[]{:S(2)}, u32[]{:S(2)}) %all-to-all-start.1) | async-done | bytes 3145760 | tf_op jit(solution)/shard_map/all_to_all | solution.py:56
  220.4 23.8 %reduce-scatter.2.cloned.1.call-done = f32[64,1536]{1,0:T(8,128)} async-done(((f32[1024,1536]{1,0:T(8,128)}), f32[64,1536]{1,0:T(8,128)}) %reduce-scatter.2.cloned.1.call-update) | async-done | bytes 393232 | tf_op jit(solution)/shard_map/reduce_scatter | solution.py:65
  244.3 1.7 bitcast_dynamic-update-slice_fusion
  246.0 5.9 %gather_fusion = bf16[512,1536]{1,0:T(8,128)(2,1)S(1)} fusion(bf16[1024,1536]{1,0:T(8,128)(2,1)} %bitcast.11, s32[1024]{0:T(1024)S(1)} %pad_clamp_fusion), kind=kCustom, calls=%fused_computation | custom fusion | bytes 3147776 | tf_op jit(solution)/shard_map/gather | solution.py:77
  251.9 2.2 reshape.49
  254.0 4.9 %multiply_reduce_fusion = bf16[128,1536]{1,0:T(8,128)(2,1)} fusion(f32[128,4,1536]{2,1,0:T(4,128)} %reshape.49, f32[128,4]{1,0:T(8,128)S(1)} %copy.30), kind=kLoop, calls=%fused_computation.11 | loop fusion | flops 1376256 | bytes 3540992 | tf_op jit(solution)/shard_map/reduce_sum | solution.py:79
  (5 shorter events, 0.1 us)
Async XLA Ops:
  6.5 90.2 %copy-start = (bf16[1,384,1536]{2,1,0:T(8,128)(2,1)S(1)}, bf16[1,384,1536]{2,1,0:T(8,128)(2,1)}, u32[]{:S(2)}) copy-start(bf16[1,384,1536]{2,1,0:T(8,128)(2,1)} %param.17) | copy-start | bytes 3538948
  6.5 90.2 %all-gather.3.cloned.1.call-start = ((), (), s32[]{:S(2)}) async-start(), calls=%async_computation.4 | async-start | bytes 3342336 | tf_op jit(solution)/shard_map/all_gather | solution.py:64
  16.4 7.7 %copy-start.1 = (s32[16,4]{0,1:T(4,128)S(1)}, s32[16,4]{0,1:T(4,128)}, u32[]{:S(2)}) copy-start(s32[16,4]{0,1:T(4,128)} %param.13) | copy-start | bytes 772
  16.4 80.4 %copy-start.3 = (bf16[1,1536,384]{2,1,0:T(8,128)(2,1)S(1)}, bf16[1,1536,384]{2,1,0:T(8,128)(2,1)}, u32[]{:S(2)}) copy-start(bf16[1,1536,384]{2,1,0:T(8,128)(2,1)} %param.16) | copy-start | bytes 3538948
  16.4 88.4 %all-to-all-start = ((bf16[16,64,1536]{2,1,0:T(8,128)(2,1)}), bf16[16,64,1536]{2,1,0:T(8,128)(2,1)}, u32[]{:S(2)}, u32[]{:S(2)}) async-start(bf16[16,64,1536]{2,1,0:T(8,128)(2,1)} %bitcast.61), calls=%async_computation | async-start | bytes 6291456 | tf_op jit(solution)/shard_map/all_to_all | solution.py:48
  24.0 220.3 %reduce-scatter.2.cloned.1.call-start = ((), (), s32[]{:S(2)}) async-start(), calls=%async_computation.3 | async-start | bytes 6684672 | tf_op jit(solution)/shard_map/reduce_scatter | solution.py:65
  122.3 13.7 %copy-start.2 = (s32[128,4]{0,1:T(4,128)S(1)}, s32[128,4]{0,1:T(4,128)}, u32[]{:S(2)}) copy-start(s32[128,4]{0,1:T(4,128)} %param.11) | copy-start | bytes 6148
  122.3 98.1 %all-to-all-start.1 = ((bf16[16,64,1536]{2,1,0:T(8,128)(2,1)}), bf16[16,64,1536]{2,1,0:T(8,128)(2,1)}, u32[]{:S(2)}, u32[]{:S(2)}) async-start(bf16[16,64,1536]{2,1,0:T(8,128)(2,1)} %fusion.6), calls=%async_computation.1 | async-start | bytes 6291456 | tf_op jit(solution)/shard_map/all_to_all | solution.py:56
Sparse Core Ops, SparseCore 0:
  16.5 80.2 all-gather.2
  104.9 139.3 reduce-scatter.1
where the time goes:
time: 266 us
  waiting for transfers between devices  179 us (67%)
  matrix products  29.2 us (11%)
  starting transfers between devices  21.1 us (8%)
  between operations  14.9 us (6%)
  local copies, waits for them, and re-layouts  11.5 us (4%)
  other arithmetic  9.75 us (4%)
    all_to_all x1, waiting for transfers between devices, shards(): lax.all_to_all(result, 'expert', split_axis=0, concat_axis=0, tiled=True)  84.3 us
    all_gather x1, waiting for transfers between devices, shards(): gathered = lax.all_gather(standby_in, 'expert', axis=0, tiled=True)  71.2 us
    reduce_scatter x1, waiting for transfers between devices, shards(): lax.psum_scatter(spare_term(gathered, spare_in, spare_out) * holder_flag,...  23.8 us
    all_to_all x1, starting transfers between devices, shards(): lax.all_to_all(result, 'expert', split_axis=0, concat_axis=0, tiled=True)  13.4 us
    dot_general x1, matrix products, shards(): jnp.einsum('scf,fd->scd', hidden, down_local, preferred_element_type=jnp....  8.79 us
    dot_general x1, matrix products, shards(): jnp.einsum('scd,df->scf', lax.all_to_all(outgoing, 'expert', split_axis=0...  8.75 us
    dot_general x1, matrix products, spare_term(): return jnp.dot(hidden, down_part, preferred_element_type=jnp.float32)  7.98 us
    all_to_all x1, starting transfers between devices, shards(): lax.all_to_all(outgoing, 'expert', split_axis=0, concat_axis=0, tiled=True)  7.57 us
  transfers between devices with their start and end apart: 4, of which 3 were waited for; matrix products, arithmetic and copies ran while one was open for 10% of the time, Pallas kernels for 0%

commit v1 on v0

v1 whole, which is shorter than its diff:
```python
import functools
import jax
import jax.numpy as jnp
from jax import lax
from jax.experimental import pallas as pl
from jax.experimental.pallas import tpu as pltpu
from jax.sharding import PartitionSpec as P

LEVELS = 1024


def gated_unit(values):
    return values * jax.nn.sigmoid(1.702 * values)


def expert_kernel(
    scalars,
    codes,
    tokens,
    w_gate,
    w_down,
    spare_gate,
    spare_down,
    out,
    rows_in,
    spare_in,
    hidden,
    spare_hidden,
    rows_out,
    *,
    subs,
    sources,
    capacity,
):
    tok = codes.shape[2]
    part = sources * tok
    rows = sources * capacity
    width = tokens.shape[1]
    tile = 512
    my_id, failed_id, holds = scalars[0], scalars[1], scalars[2]
    serves = my_id != failed_id

    before = (
        lax.broadcasted_iota(jnp.int32, (tok, tok), 0)
        < lax.broadcasted_iota(jnp.int32, (tok, tok), 1)
    ).astype(jnp.bfloat16)
    row_iota = lax.broadcasted_iota(jnp.int32, (rows, tok), 0)

    def picker(code, wanted, live):
        named = ((code // LEVELS) == wanted) & live
        mask = jnp.sum(named.astype(jnp.float32), axis=1)
        level = jnp.sum(jnp.where(named, (code % LEVELS), 0).astype(jnp.float32), axis=1) / LEVELS
        rank = jnp.dot(mask.astype(jnp.bfloat16), before, preferred_element_type=jnp.float32)
        picks, weights = [], None
        for s in range(sources):
            place = jnp.where(mask[s : s + 1] > 0, rank[s : s + 1].astype(jnp.int32) + s * capacity, -1)
            hit = row_iota == place
            scaled = jnp.sum(jnp.where(hit, level[s : s + 1], 0.0), axis=1, keepdims=True)
            weights = scaled if weights is None else weights + scaled
            picks.append(hit.astype(jnp.float32).astype(jnp.bfloat16))
        return jnp.concatenate(picks, axis=1), weights

    picks, weights, spare_weights = [], [], []
    for j in range(subs):
        code = codes[j * sources : (j + 1) * sources]
        pick, weight = picker(code, my_id, serves)
        spare_pick, spare_weight = picker(code, failed_id, holds > 0)
        both = jnp.concatenate([pick, spare_pick], axis=0)
        picks.append(both)
        weights.append(weight)
        spare_weights.append(spare_weight)
        for n in range(0, width, tile):
            got = jnp.dot(
                both, tokens[j * part : (j + 1) * part, n : n + tile], preferred_element_type=jnp.float32
            ).astype(jnp.bfloat16)
            rows_in[j * rows : (j + 1) * rows, n : n + tile] = got[:rows]
            spare_in[j * rows : (j + 1) * rows, n : n + tile] = got[rows:]

    for n in range(0, hidden.shape[1], tile):
        hidden[:, n : n + tile] = gated_unit(
            jnp.dot(rows_in[...], w_gate[0, :, n : n + tile], preferred_element_type=jnp.float32)
        ).astype(jnp.bfloat16)
    for n in range(0, width, tile):
        result = jnp.dot(hidden[...], w_down[0, :, n : n + tile], preferred_element_type=jnp.float32)
        result = result.astype(jnp.bfloat16).astype(jnp.float32)
        for j in range(subs):
            rows_out[j, :rows, n : n + tile] = (result[j * rows : (j + 1) * rows] * weights[j]).astype(
                jnp.bfloat16
            )

    @pl.when(holds > 0)
    def _():
        spare_hidden[...] = gated_unit(
            jnp.dot(spare_in[...], spare_gate[0], preferred_element_type=jnp.float32)
        ).astype(jnp.bfloat16)
        for n in range(0, width, tile):
            result = jnp.dot(
                spare_hidden[...], spare_down[0, :, n : n + tile], preferred_element_type=jnp.float32
            )
            for j in range(subs):
                rows_out[j, rows:, n : n + tile] = (
                    result[j * rows : (j + 1) * rows] * spare_weights[j]
                ).astype(jnp.bfloat16)

    @pl.when(holds <= 0)
    def _():
        rows_out[:, rows:, :] = jnp.zeros((subs, rows, width), jnp.bfloat16)

    for j in range(subs):
        for n in range(0, width, tile):
            out[j * part : (j + 1) * part, n : n + tile] = lax.dot_general(
                picks[j],
                rows_out[j, :, n : n + tile],
                (((0,), (0,)), ((), ())),
                preferred_element_type=jnp.float32,
            ).astype(jnp.bfloat16)


def run_experts(scalars, codes, tokens, w_gate, w_down, spare_gate, spare_down, capacity):
    owners, top, tok = codes.shape
    width, inner, spare = w_gate.shape[1], w_gate.shape[2], spare_gate.shape[2]
    sources = max(1, 128 // capacity)
    subs = 2 if sources * tok <= 512 else 1
    step = subs * sources
    rows = sources * capacity
    whole = lambda a: pl.BlockSpec(a.shape, lambda i: (0, 0, 0), pipeline_mode=pl.Buffered(1))
    return pl.pallas_call(
        functools.partial(expert_kernel, subs=subs, sources=sources, capacity=capacity),
        grid=(owners // step,),
        out_shape=jax.ShapeDtypeStruct((owners * tok, width), jnp.bfloat16),
        in_specs=[
            pl.BlockSpec(memory_space=pltpu.SMEM),
            pl.BlockSpec((step, top, tok), lambda i: (i, 0, 0)),
            pl.BlockSpec((step * tok, width), lambda i: (i, 0)),
            whole(w_gate),
            whole(w_down),
            whole(spare_gate),
            whole(spare_down),
        ],
        out_specs=pl.BlockSpec((step * tok, width), lambda i: (i, 0)),
        scratch_shapes=[
            pltpu.VMEM((subs * rows, width), jnp.bfloat16),
            pltpu.VMEM((subs * rows, width), jnp.bfloat16),
            pltpu.VMEM((subs * rows, inner), jnp.bfloat16),
            pltpu.VMEM((subs * rows, spare), jnp.bfloat16),
            pltpu.VMEM((subs, 2 * rows, width), jnp.bfloat16),
        ],
        compiler_params=pltpu.CompilerParams(vmem_limit_bytes=56 * 1024 * 1024),
        cost_estimate=pl.CostEstimate(
            flops=owners * capacity * 4 * width * (inner + spare),
            bytes_accessed=4 * width * (inner + spare) + 4 * owners * tok * width,
            transcendentals=owners * capacity * inner,
        ),
        name="experts",
    )(scalars, codes, tokens, w_gate, w_down, spare_gate, spare_down)


def shards(
    tokens,
    expert_ids,
    gate_levels,
    failed_device,
    replica_holders,
    w_gate,
    w_down,
    spare_gate,
    spare_down,
):
    owners = lax.axis_size("expert")
    tok_count, top_count = expert_ids.shape
    capacity = 2 * tok_count * top_count // owners
    my_index = lax.axis_index("expert").astype(jnp.int32)
    failed_id = failed_device[0]
    holder_row = lax.dynamic_index_in_dim(replica_holders, failed_id, 0, keepdims=False)
    holds = jnp.any(holder_row == my_index).astype(jnp.int32)
    scalars = jnp.stack([my_index, failed_id, holds])
    codes = (expert_ids * LEVELS + gate_levels).T
    all_codes = lax.all_gather(codes, "expert", axis=0)
    all_tokens = lax.all_gather(tokens, "expert", axis=0, tiled=True)
    dense = run_experts(
        scalars, all_codes, all_tokens, w_gate, w_down, spare_gate, spare_down, capacity
    )
    return lax.psum_scatter(dense, "expert", scatter_dimension=0, tiled=True)


def solution(mesh):
    in_specs = (
        P(("group", "expert"), None),
        P(("group", "expert"), None),
        P(("group", "expert"), None),
        P(),
        P(),
        P("expert", None, None),
        P("expert", None, None),
        P("expert", None, None),
        P("expert", None, None),
    )
    out_specs = P(("group", "expert"), None)
    return jax.shard_map(shards, mesh=mesh, in_specs=in_specs, out_specs=out_specs, check_vma=False)
```

time: 266 us -> 192 us (0.72)
  waiting for transfers between devices: 179 us -> 123 us
  matrix products: 29.2 us -> 0 us
  Pallas kernels: 0 us -> 26.2 us
  blocking collectives: 0 us -> 24.8 us
  starting transfers between devices: 21.1 us -> 0.04 us
  local copies, waits for them, and re-layouts: 11.5 us -> 0 us
  other arithmetic: 9.75 us -> 2.79 us
    all_to_all x2 -> x0, waiting for transfers between devices: 84.3 us -> none  [the longest x1 84.3 us: shards(): lax.all_to_all(result, 'expert', split_axis=0, concat_axis=0, tiled=True)]
    reduce_scatter x1, waiting for transfers between devices: 23.8 us -> 83.8 us  [shards(): return lax.psum_scatter(dense, 'expert', scatter_dimension=0, tiled=True)]
    all_gather x1, waiting for transfers between devices: 71.2 us -> 38.2 us  [shards(): all_tokens = lax.all_gather(tokens, 'expert', axis=0, tiled=True)]
    dot_general x4 -> x0, matrix products: 29.2 us -> none  [the longest x1 8.79 us: shards(): jnp.einsum('scf,fd->scd', hidden, down_local, preferred_element_type=jnp....]
    pallas_call x0 -> x1, Pallas kernels: none -> 26.2 us  [run_experts(): pl.pallas_call(functools.partial(expert_kernel, subs=subs, sources=source...]
    all_gather x0 -> x1, blocking collectives: none -> 24.8 us  [shards(): all_codes = lax.all_gather(codes, 'expert', axis=0)]
    all_to_all x2 -> x0, starting transfers between devices: 21 us -> none  [the longest x1 13.4 us: shards(): lax.all_to_all(result, 'expert', split_axis=0, concat_axis=0, tiled=True)]
    gather x1 -> x0, local copies, waits for them, and re-layouts: 5.89 us -> none  [shards(): picked = flat_rows[flat_slot]]
  transfers between devices with their start and end apart: 4 -> 2, of which waited for: 3 -> 2; matrix products, arithmetic and copies ran while one was open for 10% -> 1% of each run, Pallas kernels for 0% -> 0%
where the time goes in v1:
time: 192 us; the launch traced here: 191 us
  waiting for transfers between devices  123 us (64%)
  Pallas kernels  26.2 us (14%)
  blocking collectives  24.8 us (13%)
  between operations  14.7 us (8%)
  other arithmetic  2.79 us (1%)
    reduce_scatter x1, waiting for transfers between devices, shards(): return lax.psum_scatter(dense, 'expert', scatter_dimension=0, tiled=True)  83.8 us
    all_gather x1, waiting for transfers between devices, shards(): all_tokens = lax.all_gather(tokens, 'expert', axis=0, tiled=True)  38.2 us
    pallas_call x1, Pallas kernels, run_experts(): pl.pallas_call(functools.partial(expert_kernel, subs=subs, sources=source...  26.2 us
    all_gather x1, blocking collectives, shards(): all_codes = lax.all_gather(codes, 'expert', axis=0)  24.8 us
  transfers between devices with their start and end apart: 2, of which 2 were waited for; matrix products, arithmetic and copies ran while one was open for 1% of the time, Pallas kernels for 0%

profile of v1, /device:TPU:0, one launch (start us, length us, event | category | flops | bytes accessed | tf_op | source)
XLA Modules:
  0.0 191.2 jit_solution(8065388249133933457)
XLA Ops:
  6.5 0.0 all-gather.4.cloned.1.call-start
  6.5 0.7 all-gather.4.cloned.1.call-update
  7.3 0.0 reduce-scatter.2.cloned.1.call-start
  8.0 1.4 fusion
  10.0 0.7 add_bitcast_fusion
  10.7 24.8 %all-gather.1.codes = s32[16,4,128]{2,1,0:T(4,128)} all-gather(s32[1,4,128]{2,1,0:T(4,128)S(1)} %add_bitcast_fusion), channel_id=2, replica_groups=mesh['group'=2,'expert'=16] {'expert'}, dimensions={0}, use_global_device_ids=true | all-gather | bytes 34816 | tf_op jit(solution)/shard_map/all_gather | solution.py:178
  35.5 0.7 pad_add_fusion.scalars
  36.2 38.2 %all-gather.4.cloned.1.call-done.tokens = bf16[2048,1536]{1,0:T(8,128)(2,1)} async-done(((bf16[128,1536]{1,0:T(8,128)(2,1)}), bf16[2048,1536]{1,0:T(8,128)(2,1)}) %all-gather.4.cloned.1.call-update) | async-done | bytes 6291472 | tf_op jit(solution)/shard_map/all_gather | solution.py:179
  74.3 26.2 %experts.1 = bf16[2048,1536]{1,0:T(8,128)(2,1)} custom-call(s32[3]{0:T(128)} %pad_add_fusion.scalars, s32[16,4,128]{2,1,0:T(4,128)} %all-gather.1.codes, bf16[2048,1536]{1,0:T(8,128)(2,1)} %all-gather.4.cloned.1.call-done.tokens, bf16[1,1536,1536]{2,1,0:T(8,128)(2,1)} %w_gate.1, bf16[1,1536,1536]{2,1,0:T(8,128)(2,1)} %w_down.1, ...), custom_call_target="tpu_custom_call" | custom-call | flops 12079595520 | bytes 24379392 | tf_op jit(solution)/shard_map/experts/pallas_call | solution.py:127
  100.5 0.0 reduce-scatter.2.cloned.1.call-update
  100.6 83.8 %reduce-scatter.2.cloned.1.call-done = bf16[128,1536]{1,0:T(8,128)(2,1)} async-done(((bf16[2048,1536]{1,0:T(8,128)(2,1)}), bf16[128,1536]{1,0:T(8,128)(2,1)}) %reduce-scatter.2.cloned.1.call-update) | async-done | bytes 393232 | tf_op jit(solution)/shard_map/reduce_scatter | solution.py:183
Async XLA Ops:
  6.5 67.8 %all-gather.4.cloned.1.call-start = ((), (), s32[]{:S(2)}) async-start(), calls=%async_computation.1 | async-start | bytes 6684672 | tf_op jit(solution)/shard_map/all_gather | solution.py:179
  7.3 177.1 %reduce-scatter.2.cloned.1.call-start = ((), (), s32[]{:S(2)}) async-start(), calls=%async_computation.2 | async-start | bytes 6684672 | tf_op jit(solution)/shard_map/reduce_scatter | solution.py:183
Sparse Core Ops, SparseCore 0:
  9.6 64.6 all-gather.3
  100.7 83.6 reduce-scatter.1

commit v2 on v1

--- a/solution.py
+++ b/solution.py
@@ -155,6 +155,208 @@
     )(scalars, codes, tokens, w_gate, w_down, spare_gate, spare_down)
 
 
+def group_kernel(
+    scalars,
+    block0,
+    block1,
+    block2,
+    block3,
+    w_gate_hbm,
+    w_down_hbm,
+    spare_gate_hbm,
+    spare_down_hbm,
+    keep0,
+    keep1,
+    send,
+    w_gate,
+    w_down,
+    spare_gate,
+    spare_down,
+    rows_in,
+    spare_in,
+    hidden,
+    spare_hidden,
+    rows_out,
+    sems,
+    *,
+    tok,
+    top,
+    capacity,
+):
+    width, inner = w_gate.shape
+    tile = 512
+    my_id, failed_id, holds = scalars[0], scalars[1], scalars[2]
+    copies = []
+
+    def fetch(source, target):
+        copy = pltpu.make_async_copy(source, target, sems.at[len(copies)])
+        copy.start()
+        copies.append(copy)
+        return copy
+
+    gate_tiles = [
+        fetch(w_gate_hbm.at[0, :, n : n + tile], w_gate.at[:, n : n + tile]) for n in range(0, inner, tile)
+    ]
+    down_tiles = [
+        fetch(w_down_hbm.at[0, :, n : n + tile], w_down.at[:, n : n + tile]) for n in range(0, width, tile)
+    ]
+    spare_tiles = [fetch(spare_gate_hbm.at[0], spare_gate), fetch(spare_down_hbm.at[0], spare_down)]
+
+    before = (
+        lax.broadcasted_iota(jnp.int32, (tok, tok), 0)
+        < lax.broadcasted_iota(jnp.int32, (tok, tok), 1)
+    ).astype(jnp.float32).astype(jnp.bfloat16)
+    row_iota = lax.broadcasted_iota(jnp.int32, (capacity, tok), 0)
+
+    def picker(meta, wanted, live):
+        mask = jnp.zeros((8, tok), jnp.float32)
+        level = jnp.zeros((8, tok), jnp.float32)
+        for k in range(top):
+            named = (meta[:, k * tok : (k + 1) * tok] == wanted) & live
+            high = meta[:, (top + k) * tok : (top + k + 1) * tok]
+            low = meta[:, (2 * top + k) * tok : (2 * top + k + 1) * tok]
+            mask = mask + jnp.where(named, 1.0, 0.0)
+            level = level + jnp.where(named, (high * 32.0 + low) / LEVELS, 0.0)
+        rank = jnp.dot(mask.astype(jnp.bfloat16), before, preferred_element_type=jnp.float32)
+        place = jnp.where(mask[:1] > 0, rank[:1].astype(jnp.int32), -1)
+        hit = row_iota == place
+        weight = jnp.sum(jnp.where(hit, level[:1], 0.0), axis=1, keepdims=True)
+        return hit.astype(jnp.float32).astype(jnp.bfloat16), weight
+
+    blocks = (block0, block1, block2, block3)
+    picks, weights, spare_weights = [], [], []
+    for s, block in enumerate(blocks):
+        meta = block[tok : tok + 8, :].astype(jnp.float32)
+        pick, weight = picker(meta, my_id.astype(jnp.float32), my_id != failed_id)
+        spare_pick, spare_weight = picker(meta, failed_id.astype(jnp.float32), holds > 0)
+        both = jnp.concatenate([pick, spare_pick], axis=0)
+        picks.append(both)
+        weights.append(weight)
+        spare_weights.append(spare_weight)
+        for n in range(0, width, tile):
+            got = jnp.dot(both, block[:tok, n : n + tile], preferred_element_type=jnp.float32).astype(
+                jnp.bfloat16
+            )
+            rows_in[s * capacity : (s + 1) * capacity, n : n + tile] = got[:capacity]
+            spare_in[s * capacity : (s + 1) * capacity, n : n + tile] = got[capacity:]
+
+    for i, n in enumerate(range(0, inner, tile)):
+        gate_tiles[i].wait()
+        hidden[:, n : n + tile] = gated_unit(
+            jnp.dot(rows_in[...], w_gate[:, n : n + tile], preferred_element_type=jnp.float32)
+        ).astype(jnp.bfloat16)
+    for i, n in enumerate(range(0, width, tile)):
+        down_tiles[i].wait()
+        result = jnp.dot(hidden[...], w_down[:, n : n + tile], preferred_element_type=jnp.float32)
+        result = result.astype(jnp.bfloat16).astype(jnp.float32)
+        for s in range(len(blocks)):
+            rows_out[s, :capacity, n : n + tile] = (
+                result[s * capacity : (s + 1) * capacity] * weights[s]
+            ).astype(jnp.bfloat16)
+    for copy in spare_tiles:
+        copy.wait()
+
+    @pl.when(holds > 0)
+    def _():
+        spare_hidden[...] = gated_unit(
+            jnp.dot(spare_in[...], spare_gate[...], preferred_element_type=jnp.float32)
+        ).astype(jnp.bfloat16)
+        for n in range(0, width, tile):
+            result = jnp.dot(
+                spare_hidden[...], spare_down[:, n : n + tile], preferred_element_type=jnp.float32
+            )
+            for s in range(len(blocks)):
+                rows_out[s, capacity:, n : n + tile] = (
+                    result[s * capacity : (s + 1) * capacity] * spare_weights[s]
+                ).astype(jnp.bfloat16)
+
+    @pl.when(holds <= 0)
+    def _():
+        rows_out[:, capacity:, :] = jnp.zeros((len(blocks), capacity, width), jnp.bfloat16)
+
+    for s, target in enumerate((keep0, keep1, send.at[0], send.at[1])):
+        for n in range(0, width, tile):
+            target[:, n : n + tile] = lax.dot_general(
+                picks[s],
+                rows_out[s, :, n : n + tile],
+                (((0,), (0,)), ((), ())),
+                preferred_element_type=jnp.float32,
+            ).astype(jnp.bfloat16)
+
+
+def run_group(scalars, blocks, w_gate, w_down, spare_gate, spare_down, tok, top, capacity):
+    width, inner, spare = w_gate.shape[1], w_gate.shape[2], spare_gate.shape[2]
+    rows = len(blocks) * capacity
+    vmem = pl.BlockSpec(memory_space=pltpu.VMEM)
+    hbm = pl.BlockSpec(memory_space=pl.ANY)
+    block = jax.ShapeDtypeStruct((tok, width), jnp.bfloat16)
+    return pl.pallas_call(
+        functools.partial(group_kernel, tok=tok, top=top, capacity=capacity),
+        out_shape=(block, block, jax.ShapeDtypeStruct((2, tok, width), jnp.bfloat16)),
+        in_specs=[pl.BlockSpec(memory_space=pltpu.SMEM)] + [vmem] * 4 + [hbm] * 4,
+        out_specs=(vmem, vmem, vmem),
+        scratch_shapes=[
+            pltpu.VMEM((width, inner), jnp.bfloat16),
+            pltpu.VMEM((inner, width), jnp.bfloat16),
+            pltpu.VMEM((width, spare), jnp.bfloat16),
+            pltpu.VMEM((spare, width), jnp.bfloat16),
+            pltpu.VMEM((rows, width), jnp.bfloat16),
+            pltpu.VMEM((rows, width), jnp.bfloat16),
+            pltpu.VMEM((rows, inner), jnp.bfloat16),
+            pltpu.VMEM((rows, spare), jnp.bfloat16),
+            pltpu.VMEM((len(blocks), 2 * capacity, width), jnp.bfloat16),
+            pltpu.SemaphoreType.DMA((inner // 512 + width // 512 + 2,)),
+        ],
+        compiler_params=pltpu.CompilerParams(vmem_limit_bytes=40 * 1024 * 1024),
+        cost_estimate=pl.CostEstimate(
+            flops=rows * 4 * width * (inner + spare),
+            bytes_accessed=4 * width * (inner + spare) + 4 * len(blocks) * tok * width,
+            transcendentals=rows * inner,
+        ),
+        name="group",
+    )(scalars, *blocks, w_gate, w_down, spare_gate, spare_down)
+
+
+def folded_ring(length):
+    return [0] + list(range(1, length, 2)) + list(range(2, length, 2))[::-1]
+
+
+def by_permutes(scalars, tokens, expert_ids, gate_levels, weights, owners, capacity):
+    tok, top = expert_ids.shape
+    width = tokens.shape[1]
+    order = folded_ring(owners // 4)
+    steps = len(order)
+    after = {a: order[(i + 1) % steps] for i, a in enumerate(order)}
+    round_ring = [(d, after[d // 4] * 4 + d % 4) for d in range(owners)]
+    over_y = [(d, d ^ 2) for d in range(owners)]
+    over_core = [(d, d ^ 1) for d in range(owners)]
+    move = lambda a, pairs: lax.ppermute(a, "expert", pairs)
+
+    meta = jnp.concatenate([expert_ids.T, gate_levels.T >> 5, gate_levels.T & 31], axis=0)
+    meta = meta.astype(jnp.bfloat16).reshape(1, 3 * top * tok)
+    meta = jnp.pad(meta, ((0, 7), (0, width - 3 * top * tok)))
+    held = jnp.concatenate([tokens, meta], axis=0)
+
+    groups = []
+    for k in range(steps):
+        across = move(held, over_y)
+        groups.append((held, across, move(held, over_core), move(across, over_core)))
+        if k < steps - 1:
+            held = move(held, round_ring)
+
+    f32 = lambda a: a.astype(jnp.float32)
+    passing = None
+    for k in list(range(1, steps)) + [0]:
+        keep0, keep1, send = run_group(scalars, groups[k], *weights, tok, top, capacity)
+        got = move(send, over_core)
+        far = (f32(keep1) + f32(got[1])).astype(jnp.bfloat16)
+        total = f32(keep0) + f32(got[0]) + f32(move(far, over_y))
+        if passing is not None:
+            total = total + f32(move(passing, round_ring))
+        passing = total.astype(jnp.bfloat16)
+    return passing
+
+
 def shards(
     tokens,
     expert_ids,
@@ -174,12 +376,13 @@
     holder_row = lax.dynamic_index_in_dim(replica_holders, failed_id, 0, keepdims=False)
     holds = jnp.any(holder_row == my_index).astype(jnp.int32)
     scalars = jnp.stack([my_index, failed_id, holds])
+    weights = (w_gate, w_down, spare_gate, spare_down)
+    if owners % 4 == 0 and owners <= 32 and 3 * top_count * tok_count <= tokens.shape[1]:
+        return by_permutes(scalars, tokens, expert_ids, gate_levels, weights, owners, capacity)
     codes = (expert_ids * LEVELS + gate_levels).T
     all_codes = lax.all_gather(codes, "expert", axis=0)
     all_tokens = lax.all_gather(tokens, "expert", axis=0, tiled=True)
-    dense = run_experts(
-        scalars, all_codes, all_tokens, w_gate, w_down, spare_gate, spare_down, capacity
-    )
+    dense = run_experts(scalars, all_codes, all_tokens, *weights, capacity)
     return lax.psum_scatter(dense, "expert", scatter_dimension=0, tiled=True)
 
 

time: 192 us -> 126 us (0.66)
  waiting for transfers between devices: 123 us -> 64.1 us
  blocking collectives: 24.8 us -> 0 us
  starting transfers between devices: 0.04 us -> 20.3 us
  between operations: 14.7 us -> 1.53 us
  local copies, waits for them, and re-layouts: 0 us -> 4.9 us
  Pallas kernels: 26.2 us -> 30.8 us
  other arithmetic: 2.79 us -> 5.2 us
    reduce_scatter x1 -> x0, waiting for transfers between devices: 83.8 us -> none  [shards(): return lax.psum_scatter(dense, 'expert', scatter_dimension=0, tiled=True)]
    ppermute x0 -> x26, waiting for transfers between devices: none -> 64.1 us  [by_permutes(): move = lambda a, pairs: lax.ppermute(a, 'expert', pairs)]
    all_gather x1 -> x0, waiting for transfers between devices: 38.2 us -> none  [shards(): all_tokens = lax.all_gather(tokens, 'expert', axis=0, tiled=True)]
    all_gather x1 -> x0, blocking collectives: 24.8 us -> none  [shards(): all_codes = lax.all_gather(codes, 'expert', axis=0)]
    ppermute x0 -> x26, starting transfers between devices: none -> 20.3 us  [by_permutes(): move = lambda a, pairs: lax.ppermute(a, 'expert', pairs)]
    unnamed x0 -> x13, local copies, waits for them, and re-layouts: none -> 4.9 us
    pallas_call x1 -> x4, Pallas kernels: 26.2 us -> 30.8 us  [run_group(): pl.pallas_call(functools.partial(group_kernel, tok=tok, top=top, capacity...]
  transfers between devices with their start and end apart: 2 -> 26, of which waited for: 2 -> 11; matrix products, arithmetic and copies ran while one was open for 1% -> 2% of each run, Pallas kernels for 0% -> 24%
where the time goes in v2:
time: 126 us; the launch traced here: 127 us
  waiting for transfers between devices  64.1 us (51%)
  Pallas kernels  30.8 us (24%)
  starting transfers between devices  20.3 us (16%)
  other arithmetic  5.2 us (4%)
  local copies, waits for them, and re-layouts  4.9 us (4%)
  between operations  1.53 us (1%)
    ppermute x26, waiting for transfers between devices, by_permutes(): move = lambda a, pairs: lax.ppermute(a, 'expert', pairs)  64.1 us
    pallas_call x4, Pallas kernels, run_group(): pl.pallas_call(functools.partial(group_kernel, tok=tok, top=top, capacity...  30.8 us
    ppermute x26, starting transfers between devices, by_permutes(): move = lambda a, pairs: lax.ppermute(a, 'expert', pairs)  20.3 us
    unnamed x13, local copies, waits for them, and re-layouts  4.9 us
  transfers between devices with their start and end apart: 26, of which 11 were waited for; matrix products, arithmetic and copies ran while one was open for 2% of the time, Pallas kernels for 24%

profile of v2, /device:TPU:0, one launch (start us, length us, event | category | flops | bytes accessed | tf_op | source)
XLA Modules:
  0.0 126.9 jit_solution(8125338408806216040)
XLA Ops:
  0.0 0.7 fusion.18
  0.7 1.0 fusion.16.block0
  1.8 3.1 %collective-permute-start.5 = (bf16[136,1536]{1,0:T(8,128)(2,1)S(1)}, bf16[136,1536]{1,0:T(8,128)(2,1)S(1)}, u32[]{:S(2)}, u32[]{:S(2)}) collective-permute-start(bf16[136,1536]{1,0:T(8,128)(2,1)S(1)} %fusion.16.block0), channel_id=1, source_target_pairs={{0,4},{1,5},{2,6},{3,7},{4,12},{5,13},{6,14},{7,15},{8,0},{9,1},{1... | collective-permute-start | bytes 1253384 | tf_op jit(solution)/shard_map/ppermute | solution.py:333
  4.8 10.7 %collective-permute-done.5.block0 = bf16[136,1536]{1,0:T(8,128)(2,1)S(1)} collective-permute-done((bf16[136,1536]{1,0:T(8,128)(2,1)S(1)}, bf16[136,1536]{1,0:T(8,128)(2,1)S(1)}, u32[]{:S(2)}, u32[]{:S(2)}) %collective-permute-start.5) | collective-permute-done | bytes 417824 | tf_op jit(solution)/shard_map/ppermute | solution.py:333
  15.5 1.6 %collective-permute-start.18 = (bf16[136,1536]{1,0:T(8,128)(2,1)S(1)}, bf16[136,1536]{1,0:T(8,128)(2,1)S(1)}, u32[]{:S(2)}, u32[]{:S(2)}) collective-permute-start(bf16[136,1536]{1,0:T(8,128)(2,1)S(1)} %collective-permute-done.5.block0), channel_id=1, source_target_pairs={{0,2},{1,3},{2,0},{3,1},{4,6},{5,7},{6,4},{7,5},{8,10},{9,11},{10,... | collective-permute-start | bytes 1253384 | tf_op jit(solution)/shard_map/ppermute | solution.py:333
  17.1 0.0 collective-permute-start.19
  17.1 9.3 %collective-permute-done.18.block1 = bf16[136,1536]{1,0:T(8,128)(2,1)S(1)} collective-permute-done((bf16[136,1536]{1,0:T(8,128)(2,1)S(1)}, bf16[136,1536]{1,0:T(8,128)(2,1)S(1)}, u32[]{:S(2)}, u32[]{:S(2)}) %collective-permute-start.18) | collective-permute-done | bytes 417824 | tf_op jit(solution)/shard_map/ppermute | solution.py:333
  26.3 0.0 collective-permute-start.20
  27.0 1.5 %fusion.17 = pred[]{:T(512)} fusion(s32[16,4]{0,1:T(4,128)} %param.13, s32[]{:T(128)S(6)} %select_n.4, s32[]{:T(128)} %axis_index.12), kind=kLoop, calls=%fused_computation.39 | loop fusion | flops 7 | bytes 25 | tf_op jit(solution)/shard_map/reduce_or | solution.py:377
  29.1 0.1 pad_add_fusion.scalars
  29.2 0.5 collective-permute-start.6
  29.7 0.0 collective-permute-done.19.block2
  29.7 2.3 %copy-done = bf16[1,1536,1536]{2,1,0:T(8,128)(2,1)S(1)} copy-done((bf16[1,1536,1536]{2,1,0:T(8,128)(2,1)S(1)}, bf16[1,1536,1536]{2,1,0:T(8,128)(2,1)}, u32[]{:S(2)}) %copy-start) | copy-done | bytes 4718616
  32.1 1.3 copy-done.2
  33.3 1.3 copy-done.4
  34.6 7.7 %group.7 = (bf16[128,1536]{1,0:T(8,128)(2,1)S(1)}, bf16[128,1536]{1,0:T(8,128)(2,1)S(1)}, bf16[2,128,1536]{2,1,0:T(8,128)(2,1)S(1)}) custom-call(s32[3]{0:T(128)S(1)} %pad_add_fusion.scalars, bf16[136,1536]{1,0:T(8,128)(2,1)S(1)} %collective-permute-done.5.block0, bf16[136,1536]{1,0:T(8,128)(2,1)S(1)} %collective-permute-done.18.block1, ...), custom_call_target="tpu_custom_call" | custom-call | flops 3019898880 | bytes 14942208 | tf_op jit(solution)/shard_map/group/pallas_call | solution.py:293
  42.3 0.3 collective-permute-start.21
  42.6 0.8 collective-permute-start.13
  43.4 4.0 %collective-permute-start.7 = (bf16[136,1536]{1,0:T(8,128)(2,1)S(1)}, bf16[136,1536]{1,0:T(8,128)(2,1)S(1)}, u32[]{:S(2)}, u32[]{:S(2)}) collective-permute-start(bf16[136,1536]{1,0:T(8,128)(2,1)S(1)} %collective-permute-done.6.block0), channel_id=1, source_target_pairs={{0,4},{1,5},{2,6},{3,7},{4,12},{5,13},{6,14},{7,15},{8,0},{9,1},{1... | collective-permute-start | bytes 1253384 | tf_op jit(solution)/shard_map/ppermute | solution.py:333
  47.4 0.1 collective-permute-start
  47.4 7.6 %collective-permute-done.13.block1 = bf16[136,1536]{1,0:T(8,128)(2,1)S(1)} collective-permute-done((bf16[136,1536]{1,0:T(8,128)(2,1)S(1)}, bf16[136,1536]{1,0:T(8,128)(2,1)S(1)}, u32[]{:S(2)}, u32[]{:S(2)}) %collective-permute-start.13) | collective-permute-done | bytes 417824 | tf_op jit(solution)/shard_map/ppermute | solution.py:333
  55.1 0.0 collective-permute-start.15
  55.1 1.5 %collective-permute-done.7.block0 = bf16[136,1536]{1,0:T(8,128)(2,1)S(1)} collective-permute-done((bf16[136,1536]{1,0:T(8,128)(2,1)S(1)}, bf16[136,1536]{1,0:T(8,128)(2,1)S(1)}, u32[]{:S(2)}, u32[]{:S(2)}) %collective-permute-start.7) | collective-permute-done | bytes 417824 | tf_op jit(solution)/shard_map/ppermute | solution.py:333
  56.6 0.5 collective-permute-start.8
  57.1 0.0 collective-permute-done.21
  57.1 0.1 fusion.1
  57.2 1.6 %collective-permute-start.22 = (bf16[128,1536]{1,0:T(8,128)(2,1)S(1)}, bf16[128,1536]{1,0:T(8,128)(2,1)S(1)}, u32[]{:S(2)}, u32[]{:S(2)}) collective-permute-start(bf16[128,1536]{1,0:T(8,128)(2,1)S(1)} %fusion.1), channel_id=1, source_target_pairs={{0,2},{1,3},{2,0},{3,1},{4,6},{5,7},{6,4},{7,5},{8,10},{9,11},{10,... | collective-permute-start | bytes 1179656 | tf_op jit(solution)/shard_map/ppermute | solution.py:333
  58.8 0.0 collective-permute-done.14.block2
  58.8 0.0 collective-permute-done.15.block3
  58.8 7.7 %group.6 = (bf16[128,1536]{1,0:T(8,128)(2,1)S(1)}, bf16[128,1536]{1,0:T(8,128)(2,1)S(1)}, bf16[2,128,1536]{2,1,0:T(8,128)(2,1)S(1)}) custom-call(s32[3]{0:T(128)S(1)} %pad_add_fusion.scalars, bf16[136,1536]{1,0:T(8,128)(2,1)S(1)} %collective-permute-done.6.block0, bf16[136,1536]{1,0:T(8,128)(2,1)S(1)} %collective-permute-done.13.block1, ...), custom_call_target="tpu_custom_call" | custom-call | flops 3019898880 | bytes 14942208 | tf_op jit(solution)/shard_map/group/pallas_call | solution.py:293
  66.5 0.1 collective-permute-start.16
  66.6 0.5 collective-permute-start.1
  67.1 0.0 collective-permute-done.block1
  67.1 0.1 collective-permute-start.2
  67.2 5.8 %collective-permute-done.8.block1 = bf16[136,1536]{1,0:T(8,128)(2,1)S(1)} collective-permute-done((bf16[136,1536]{1,0:T(8,128)(2,1)S(1)}, bf16[136,1536]{1,0:T(8,128)(2,1)S(1)}, u32[]{:S(2)}, u32[]{:S(2)}) %collective-permute-start.8) | collective-permute-done | bytes 417824 | tf_op jit(solution)/shard_map/ppermute | solution.py:333
  73.0 0.0 collective-permute-start.9
  73.0 7.8 %collective-permute-done.22 = bf16[128,1536]{1,0:T(8,128)(2,1)S(1)} collective-permute-done((bf16[128,1536]{1,0:T(8,128)(2,1)S(1)}, bf16[128,1536]{1,0:T(8,128)(2,1)S(1)}, u32[]{:S(2)}, u32[]{:S(2)}) %collective-permute-start.22) | collective-permute-done | bytes 393248 | tf_op jit(solution)/shard_map/ppermute | solution.py:333
  80.8 0.0 collective-permute-start.10
  80.8 0.1 fusion.3
  80.9 0.0 collective-permute-done.16
  81.0 3.4 %collective-permute-start.23 = (bf16[128,1536]{1,0:T(8,128)(2,1)S(1)}, bf16[128,1536]{1,0:T(8,128)(2,1)S(1)}, u32[]{:S(2)}, u32[]{:S(2)}) collective-permute-start(bf16[128,1536]{1,0:T(8,128)(2,1)S(1)} %fusion.3), channel_id=1, source_target_pairs={{0,4},{1,5},{2,6},{3,7},{4,12},{5,13},{6,14},{7,15},{8,0},{9,1},{1... | collective-permute-start | bytes 1179656 | tf_op jit(solution)/shard_map/ppermute | solution.py:333
  84.3 0.1 fusion.4
  84.4 1.8 %collective-permute-start.17 = (bf16[128,1536]{1,0:T(8,128)(2,1)S(1)}, bf16[128,1536]{1,0:T(8,128)(2,1)S(1)}, u32[]{:S(2)}, u32[]{:S(2)}) collective-permute-start(bf16[128,1536]{1,0:T(8,128)(2,1)S(1)} %fusion.4), channel_id=1, source_target_pairs={{0,2},{1,3},{2,0},{3,1},{4,6},{5,7},{6,4},{7,5},{8,10},{9,11},{10,... | collective-permute-start | bytes 1179656 | tf_op jit(solution)/shard_map/ppermute | solution.py:333
  86.3 7.7 %group.5 = (bf16[128,1536]{1,0:T(8,128)(2,1)S(1)}, bf16[128,1536]{1,0:T(8,128)(2,1)S(1)}, bf16[2,128,1536]{2,1,0:T(8,128)(2,1)S(1)}) custom-call(s32[3]{0:T(128)S(1)} %pad_add_fusion.scalars, bf16[136,1536]{1,0:T(8,128)(2,1)S(1)} %collective-permute-done.7.block0, bf16[136,1536]{1,0:T(8,128)(2,1)S(1)} %collective-permute-done.8.block1, ...), custom_call_target="tpu_custom_call" | custom-call | flops 3019898880 | bytes 14942208 | tf_op jit(solution)/shard_map/group/pallas_call | solution.py:293
  94.0 0.1 collective-permute-start.11
  94.1 0.0 collective-permute-done.2.block3
  94.1 7.7 %group.4 = (bf16[128,1536]{1,0:T(8,128)(2,1)S(1)}, bf16[128,1536]{1,0:T(8,128)(2,1)S(1)}, bf16[2,128,1536]{2,1,0:T(8,128)(2,1)S(1)}) custom-call(s32[3]{0:T(128)S(1)} %pad_add_fusion.scalars, bf16[136,1536]{1,0:T(8,128)(2,1)S(1)} %fusion.16.block0, bf16[136,1536]{1,0:T(8,128)(2,1)S(1)} %collective-permute-done.block1, ...), custom_call_target="tpu_custom_call" | custom-call | flops 3019898880 | bytes 14942208 | tf_op jit(solution)/shard_map/group/pallas_call | solution.py:293
  101.8 0.6 collective-permute-start.3
  102.3 0.0 collective-permute-done.23
  102.3 0.0 collective-permute-done.17
  102.4 0.2 fusion.7
  102.6 0.1 collective-permute-start.24
  102.6 0.1 fusion.8
  102.7 0.8 collective-permute-start.12
  103.5 0.8 collective-permute-done.3
  104.3 0.1 fusion.12
  104.4 0.6 collective-permute-start.4
  105.0 9.5 %collective-permute-done.24 = bf16[128,1536]{1,0:T(8,128)(2,1)S(1)} collective-permute-done((bf16[128,1536]{1,0:T(8,128)(2,1)S(1)}, bf16[128,1536]{1,0:T(8,128)(2,1)S(1)}, u32[]{:S(2)}, u32[]{:S(2)}) %collective-permute-start.24) | collective-permute-done | bytes 393248 | tf_op jit(solution)/shard_map/ppermute | solution.py:333
  114.6 0.2 collective-permute-done.12
  114.8 0.2 fusion.11
  115.0 0.1 collective-permute-start.25
  115.1 7.2 %collective-permute-done.4 = bf16[128,1536]{1,0:T(8,128)(2,1)S(1)} collective-permute-done((bf16[128,1536]{1,0:T(8,128)(2,1)S(1)}, bf16[128,1536]{1,0:T(8,128)(2,1)S(1)}, u32[]{:S(2)}, u32[]{:S(2)}) %collective-permute-start.4) | collective-permute-done | bytes 393248 | tf_op jit(solution)/shard_map/ppermute | solution.py:333
  122.3 3.7 %collective-permute-done.25 = bf16[128,1536]{1,0:T(8,128)(2,1)S(1)} collective-permute-done((bf16[128,1536]{1,0:T(8,128)(2,1)S(1)}, bf16[128,1536]{1,0:T(8,128)(2,1)S(1)}, u32[]{:S(2)}, u32[]{:S(2)}) %collective-permute-start.25) | collective-permute-done | bytes 393248 | tf_op jit(solution)/shard_map/ppermute | solution.py:333
  126.0 0.9 fusion.15
  (18 shorter events, 0.1 us)
Async XLA Ops:
  1.8 13.7 %collective-permute-start.5 = (bf16[136,1536]{1,0:T(8,128)(2,1)S(1)}, bf16[136,1536]{1,0:T(8,128)(2,1)S(1)}, u32[]{:S(2)}, u32[]{:S(2)}) collective-permute-start(bf16[136,1536]{1,0:T(8,128)(2,1)S(1)} %fusion.16.block0), channel_id=1, source_target_pairs={{0,4},{1,5},{2,6},{3,7},{4,12},{5,13},{6,14},{7,15},{8,0},{9,1},{1... | collective-permute-start | bytes 1253384 | tf_op jit(solution)/shard_map/ppermute | solution.py:333
  15.5 10.8 %collective-permute-start.18 = (bf16[136,1536]{1,0:T(8,128)(2,1)S(1)}, bf16[136,1536]{1,0:T(8,128)(2,1)S(1)}, u32[]{:S(2)}, u32[]{:S(2)}) collective-permute-start(bf16[136,1536]{1,0:T(8,128)(2,1)S(1)} %collective-permute-done.5.block0), channel_id=1, source_target_pairs={{0,2},{1,3},{2,0},{3,1},{4,6},{5,7},{6,4},{7,5},{8,10},{9,11},{10,... | collective-permute-start | bytes 1253384 | tf_op jit(solution)/shard_map/ppermute | solution.py:333
  17.1 12.7 %collective-permute-start.19 = (bf16[136,1536]{1,0:T(8,128)(2,1)S(1)}, bf16[136,1536]{1,0:T(8,128)(2,1)S(1)}, u32[]{:S(2)}, u32[]{:S(2)}) collective-permute-start(bf16[136,1536]{1,0:T(8,128)(2,1)S(1)} %collective-permute-done.5.block0), channel_id=1, source_target_pairs={{0,1},{1,0},{2,3},{3,2},{4,5},{5,4},{6,7},{7,6},{8,9},{9,8},{10,11... | collective-permute-start | bytes 1253384 | tf_op jit(solution)/shard_map/ppermute | solution.py:333
  26.3 3.4 %collective-permute-start.20 = (bf16[136,1536]{1,0:T(8,128)(2,1)S(1)}, bf16[136,1536]{1,0:T(8,128)(2,1)S(1)}, u32[]{:S(2)}, u32[]{:S(2)}) collective-permute-start(bf16[136,1536]{1,0:T(8,128)(2,1)S(1)} %collective-permute-done.18.block1), channel_id=1, source_target_pairs={{0,1},{1,0},{2,3},{3,2},{4,5},{5,4},{6,7},{7,6},{8,9},{9,8},{10,11... | collective-permute-start | bytes 1253384 | tf_op jit(solution)/shard_map/ppermute | solution.py:333
  29.2 13.4 %collective-permute-start.6 = (bf16[136,1536]{1,0:T(8,128)(2,1)S(1)}, bf16[136,1536]{1,0:T(8,128)(2,1)S(1)}, u32[]{:S(2)}, u32[]{:S(2)}) collective-permute-start(bf16[136,1536]{1,0:T(8,128)(2,1)S(1)} %collective-permute-done.5.block0), channel_id=1, source_target_pairs={{0,4},{1,5},{2,6},{3,7},{4,12},{5,13},{6,14},{7,15},{8,0},{9,1},{1... | collective-permute-start | bytes 1253384 | tf_op jit(solution)/shard_map/ppermute | solution.py:333
  29.7 2.3 %copy-start = (bf16[1,1536,1536]{2,1,0:T(8,128)(2,1)S(1)}, bf16[1,1536,1536]{2,1,0:T(8,128)(2,1)}, u32[]{:S(2)}) copy-start(bf16[1,1536,1536]{2,1,0:T(8,128)(2,1)} %w_gate_hbm.7) | copy-start | bytes 14155780
  32.1 1.3 %copy-start.2 = (bf16[1,1536,384]{2,1,0:T(8,128)(2,1)S(1)}, bf16[1,1536,384]{2,1,0:T(8,128)(2,1)}, u32[]{:S(2)}) copy-start(bf16[1,1536,384]{2,1,0:T(8,128)(2,1)} %spare_gate_hbm.7) | copy-start | bytes 3538948
  33.3 1.3 %copy-start.4 = (bf16[1,384,1536]{2,1,0:T(8,128)(2,1)S(1)}, bf16[1,384,1536]{2,1,0:T(8,128)(2,1)}, u32[]{:S(2)}) copy-start(bf16[1,384,1536]{2,1,0:T(8,128)(2,1)} %spare_down_hbm.7) | copy-start | bytes 3538948
  34.6 24.2 %copy-start.1 = (bf16[1,1536,1536]{2,1,0:T(8,128)(2,1)S(1)}, bf16[1,1536,1536]{2,1,0:T(8,128)(2,1)}, u32[]{:S(2)}) copy-start(bf16[1,1536,1536]{2,1,0:T(8,128)(2,1)} %w_gate_hbm.7) | copy-start | bytes 14155780
  34.6 24.2 %copy-start.3 = (bf16[1,1536,384]{2,1,0:T(8,128)(2,1)S(1)}, bf16[1,1536,384]{2,1,0:T(8,128)(2,1)}, u32[]{:S(2)}) copy-start(bf16[1,1536,384]{2,1,0:T(8,128)(2,1)} %spare_gate_hbm.7) | copy-start | bytes 3538948
  34.6 24.2 %copy-start.5 = (bf16[1,384,1536]{2,1,0:T(8,128)(2,1)S(1)}, bf16[1,384,1536]{2,1,0:T(8,128)(2,1)}, u32[]{:S(2)}) copy-start(bf16[1,384,1536]{2,1,0:T(8,128)(2,1)} %spare_down_hbm.7) | copy-start | bytes 3538948
  42.3 14.8 %collective-permute-start.21 = (bf16[2,128,1536]{2,1,0:T(8,128)(2,1)S(1)}, bf16[2,128,1536]{2,1,0:T(8,128)(2,1)S(1)}, u32[]{:S(2)}, u32[]{:S(2)}) collective-permute-start(bf16[2,128,1536]{2,1,0:T(8,128)(2,1)S(1)} %get-tuple-element.27), channel_id=1, source_target_pairs={{0,1},{1,0},{2,3},{3,2},{4,5},{5,4},{6,7},{7,6},{8,9},{9,8},{10,11... | collective-permute-start | bytes 2359304 | tf_op jit(solution)/shard_map/ppermute | solution.py:333
  42.6 12.5 %collective-permute-start.13 = (bf16[136,1536]{1,0:T(8,128)(2,1)S(1)}, bf16[136,1536]{1,0:T(8,128)(2,1)S(1)}, u32[]{:S(2)}, u32[]{:S(2)}) collective-permute-start(bf16[136,1536]{1,0:T(8,128)(2,1)S(1)} %collective-permute-done.6.block0), channel_id=1, source_target_pairs={{0,2},{1,3},{2,0},{3,1},{4,6},{5,7},{6,4},{7,5},{8,10},{9,11},{10,... | collective-permute-start | bytes 1253384 | tf_op jit(solution)/shard_map/ppermute | solution.py:333
  43.4 13.2 %collective-permute-start.7 = (bf16[136,1536]{1,0:T(8,128)(2,1)S(1)}, bf16[136,1536]{1,0:T(8,128)(2,1)S(1)}, u32[]{:S(2)}, u32[]{:S(2)}) collective-permute-start(bf16[136,1536]{1,0:T(8,128)(2,1)S(1)} %collective-permute-done.6.block0), channel_id=1, source_target_pairs={{0,4},{1,5},{2,6},{3,7},{4,12},{5,13},{6,14},{7,15},{8,0},{9,1},{1... | collective-permute-start | bytes 1253384 | tf_op jit(solution)/shard_map/ppermute | solution.py:333
  47.4 19.7 %collective-permute-start = (bf16[136,1536]{1,0:T(8,128)(2,1)S(1)}, bf16[136,1536]{1,0:T(8,128)(2,1)S(1)}, u32[]{:S(2)}, u32[]{:S(2)}) collective-permute-start(bf16[136,1536]{1,0:T(8,128)(2,1)S(1)} %fusion.16.block0), channel_id=1, source_target_pairs={{0,2},{1,3},{2,0},{3,1},{4,6},{5,7},{6,4},{7,5},{8,10},{9,11},{10,... | collective-permute-start | bytes 1253384 | tf_op jit(solution)/shard_map/ppermute | solution.py:333
  47.4 11.3 %collective-permute-start.14 = (bf16[136,1536]{1,0:T(8,128)(2,1)S(1)}, bf16[136,1536]{1,0:T(8,128)(2,1)S(1)}, u32[]{:S(2)}, u32[]{:S(2)}) collective-permute-start(bf16[136,1536]{1,0:T(8,128)(2,1)S(1)} %collective-permute-done.6.block0), channel_id=1, source_target_pairs={{0,1},{1,0},{2,3},{3,2},{4,5},{5,4},{6,7},{7,6},{8,9},{9,8},{10,11... | collective-permute-start | bytes 1253384 | tf_op jit(solution)/shard_map/ppermute | solution.py:333
  55.1 3.7 %collective-permute-start.15 = (bf16[136,1536]{1,0:T(8,128)(2,1)S(1)}, bf16[136,1536]{1,0:T(8,128)(2,1)S(1)}, u32[]{:S(2)}, u32[]{:S(2)}) collective-permute-start(bf16[136,1536]{1,0:T(8,128)(2,1)S(1)} %collective-permute-done.13.block1), channel_id=1, source_target_pairs={{0,1},{1,0},{2,3},{3,2},{4,5},{5,4},{6,7},{7,6},{8,9},{9,8},{10,11... | collective-permute-start | bytes 1253384 | tf_op jit(solution)/shard_map/ppermute | solution.py:333
  56.6 16.4 %collective-permute-start.8 = (bf16[136,1536]{1,0:T(8,128)(2,1)S(1)}, bf16[136,1536]{1,0:T(8,128)(2,1)S(1)}, u32[]{:S(2)}, u32[]{:S(2)}) collective-permute-start(bf16[136,1536]{1,0:T(8,128)(2,1)S(1)} %collective-permute-done.7.block0), channel_id=1, source_target_pairs={{0,2},{1,3},{2,0},{3,1},{4,6},{5,7},{6,4},{7,5},{8,10},{9,11},{10,... | collective-permute-start | bytes 1253384 | tf_op jit(solution)/shard_map/ppermute | solution.py:333
  57.2 23.6 %collective-permute-start.22 = (bf16[128,1536]{1,0:T(8,128)(2,1)S(1)}, bf16[128,1536]{1,0:T(8,128)(2,1)S(1)}, u32[]{:S(2)}, u32[]{:S(2)}) collective-permute-start(bf16[128,1536]{1,0:T(8,128)(2,1)S(1)} %fusion.1), channel_id=1, source_target_pairs={{0,2},{1,3},{2,0},{3,1},{4,6},{5,7},{6,4},{7,5},{8,10},{9,11},{10,... | collective-permute-start | bytes 1179656 | tf_op jit(solution)/shard_map/ppermute | solution.py:333
  66.5 14.4 %collective-permute-start.16 = (bf16[2,128,1536]{2,1,0:T(8,128)(2,1)S(1)}, bf16[2,128,1536]{2,1,0:T(8,128)(2,1)S(1)}, u32[]{:S(2)}, u32[]{:S(2)}) collective-permute-start(bf16[2,128,1536]{2,1,0:T(8,128)(2,1)S(1)} %get-tuple-element.24), channel_id=1, source_target_pairs={{0,1},{1,0},{2,3},{3,2},{4,5},{5,4},{6,7},{7,6},{8,9},{9,8},{10,11... | collective-permute-start | bytes 2359304 | tf_op jit(solution)/shard_map/ppermute | solution.py:333
  66.6 27.5 %collective-permute-start.1 = (bf16[136,1536]{1,0:T(8,128)(2,1)S(1)}, bf16[136,1536]{1,0:T(8,128)(2,1)S(1)}, u32[]{:S(2)}, u32[]{:S(2)}) collective-permute-start(bf16[136,1536]{1,0:T(8,128)(2,1)S(1)} %fusion.16.block0), channel_id=1, source_target_pairs={{0,1},{1,0},{2,3},{3,2},{4,5},{5,4},{6,7},{7,6},{8,9},{9,8},{10,11... | collective-permute-start | bytes 1253384 | tf_op jit(solution)/shard_map/ppermute | solution.py:333
  67.1 27.0 %collective-permute-start.2 = (bf16[136,1536]{1,0:T(8,128)(2,1)S(1)}, bf16[136,1536]{1,0:T(8,128)(2,1)S(1)}, u32[]{:S(2)}, u32[]{:S(2)}) collective-permute-start(bf16[136,1536]{1,0:T(8,128)(2,1)S(1)} %collective-permute-done.block1), channel_id=1, source_target_pairs={{0,1},{1,0},{2,3},{3,2},{4,5},{5,4},{6,7},{7,6},{8,9},{9,8},{10,11... | collective-permute-start | bytes 1253384 | tf_op jit(solution)/shard_map/ppermute | solution.py:333
  73.0 11.4 %collective-permute-start.9 = (bf16[136,1536]{1,0:T(8,128)(2,1)S(1)}, bf16[136,1536]{1,0:T(8,128)(2,1)S(1)}, u32[]{:S(2)}, u32[]{:S(2)}) collective-permute-start(bf16[136,1536]{1,0:T(8,128)(2,1)S(1)} %collective-permute-done.7.block0), channel_id=1, source_target_pairs={{0,1},{1,0},{2,3},{3,2},{4,5},{5,4},{6,7},{7,6},{8,9},{9,8},{10,11... | collective-permute-start | bytes 1253384 | tf_op jit(solution)/shard_map/ppermute | solution.py:333
  80.8 5.5 %collective-permute-start.10 = (bf16[136,1536]{1,0:T(8,128)(2,1)S(1)}, bf16[136,1536]{1,0:T(8,128)(2,1)S(1)}, u32[]{:S(2)}, u32[]{:S(2)}) collective-permute-start(bf16[136,1536]{1,0:T(8,128)(2,1)S(1)} %collective-permute-done.8.block1), channel_id=1, source_target_pairs={{0,1},{1,0},{2,3},{3,2},{4,5},{5,4},{6,7},{7,6},{8,9},{9,8},{10,11... | collective-permute-start | bytes 1253384 | tf_op jit(solution)/shard_map/ppermute | solution.py:333
  81.0 21.4 %collective-permute-start.23 = (bf16[128,1536]{1,0:T(8,128)(2,1)S(1)}, bf16[128,1536]{1,0:T(8,128)(2,1)S(1)}, u32[]{:S(2)}, u32[]{:S(2)}) collective-permute-start(bf16[128,1536]{1,0:T(8,128)(2,1)S(1)} %fusion.3), channel_id=1, source_target_pairs={{0,4},{1,5},{2,6},{3,7},{4,12},{5,13},{6,14},{7,15},{8,0},{9,1},{1... | collective-permute-start | bytes 1179656 | tf_op jit(solution)/shard_map/ppermute | solution.py:333
  84.4 17.9 %collective-permute-start.17 = (bf16[128,1536]{1,0:T(8,128)(2,1)S(1)}, bf16[128,1536]{1,0:T(8,128)(2,1)S(1)}, u32[]{:S(2)}, u32[]{:S(2)}) collective-permute-start(bf16[128,1536]{1,0:T(8,128)(2,1)S(1)} %fusion.4), channel_id=1, source_target_pairs={{0,2},{1,3},{2,0},{3,1},{4,6},{5,7},{6,4},{7,5},{8,10},{9,11},{10,... | collective-permute-start | bytes 1179656 | tf_op jit(solution)/shard_map/ppermute | solution.py:333
  94.0 8.6 %collective-permute-start.11 = (bf16[2,128,1536]{2,1,0:T(8,128)(2,1)S(1)}, bf16[2,128,1536]{2,1,0:T(8,128)(2,1)S(1)}, u32[]{:S(2)}, u32[]{:S(2)}) collective-permute-start(bf16[2,128,1536]{2,1,0:T(8,128)(2,1)S(1)} %get-tuple-element.21), channel_id=1, source_target_pairs={{0,1},{1,0},{2,3},{3,2},{4,5},{5,4},{6,7},{7,6},{8,9},{9,8},{10,11... | collective-permute-start | bytes 2359304 | tf_op jit(solution)/shard_map/ppermute | solution.py:333
  101.8 2.5 %collective-permute-start.3 = (bf16[2,128,1536]{2,1,0:T(8,128)(2,1)S(1)}, bf16[2,128,1536]{2,1,0:T(8,128)(2,1)S(1)}, u32[]{:S(2)}, u32[]{:S(2)}) collective-permute-start(bf16[2,128,1536]{2,1,0:T(8,128)(2,1)S(1)} %get-tuple-element.18), channel_id=1, source_target_pairs={{0,1},{1,0},{2,3},{3,2},{4,5},{5,4},{6,7},{7,6},{8,9},{9,8},{10,11... | collective-permute-start | bytes 2359304 | tf_op jit(solution)/shard_map/ppermute | solution.py:333
  102.6 12.0 %collective-permute-start.24 = (bf16[128,1536]{1,0:T(8,128)(2,1)S(1)}, bf16[128,1536]{1,0:T(8,128)(2,1)S(1)}, u32[]{:S(2)}, u32[]{:S(2)}) collective-permute-start(bf16[128,1536]{1,0:T(8,128)(2,1)S(1)} %fusion.7), channel_id=1, source_target_pairs={{0,4},{1,5},{2,6},{3,7},{4,12},{5,13},{6,14},{7,15},{8,0},{9,1},{1... | collective-permute-start | bytes 1179656 | tf_op jit(solution)/shard_map/ppermute | solution.py:333
  102.7 12.0 %collective-permute-start.12 = (bf16[128,1536]{1,0:T(8,128)(2,1)S(1)}, bf16[128,1536]{1,0:T(8,128)(2,1)S(1)}, u32[]{:S(2)}, u32[]{:S(2)}) collective-permute-start(bf16[128,1536]{1,0:T(8,128)(2,1)S(1)} %fusion.8), channel_id=1, source_target_pairs={{0,2},{1,3},{2,0},{3,1},{4,6},{5,7},{6,4},{7,5},{8,10},{9,11},{10,... | collective-permute-start | bytes 1179656 | tf_op jit(solution)/shard_map/ppermute | solution.py:333
  104.4 17.9 %collective-permute-start.4 = (bf16[128,1536]{1,0:T(8,128)(2,1)S(1)}, bf16[128,1536]{1,0:T(8,128)(2,1)S(1)}, u32[]{:S(2)}, u32[]{:S(2)}) collective-permute-start(bf16[128,1536]{1,0:T(8,128)(2,1)S(1)} %fusion.12), channel_id=1, source_target_pairs={{0,2},{1,3},{2,0},{3,1},{4,6},{5,7},{6,4},{7,5},{8,10},{9,11},{10,... | collective-permute-start | bytes 1179656 | tf_op jit(solution)/shard_map/ppermute | solution.py:333
  115.0 10.9 %collective-permute-start.25 = (bf16[128,1536]{1,0:T(8,128)(2,1)S(1)}, bf16[128,1536]{1,0:T(8,128)(2,1)S(1)}, u32[]{:S(2)}, u32[]{:S(2)}) collective-permute-start(bf16[128,1536]{1,0:T(8,128)(2,1)S(1)} %fusion.11), channel_id=1, source_target_pairs={{0,4},{1,5},{2,6},{3,7},{4,12},{5,13},{6,14},{7,15},{8,0},{9,1},{1... | collective-permute-start | bytes 1179656 | tf_op jit(solution)/shard_map/ppermute | solution.py:333

commit v3 on v2

--- a/solution.py
+++ b/solution.py
@@ -307,11 +307,11 @@
             pltpu.VMEM((len(blocks), 2 * capacity, width), jnp.bfloat16),
             pltpu.SemaphoreType.DMA((inner // 512 + width // 512 + 2,)),
         ],
-        compiler_params=pltpu.CompilerParams(vmem_limit_bytes=40 * 1024 * 1024),
+        compiler_params=pltpu.CompilerParams(vmem_limit_bytes=60 * 1024 * 1024),
         cost_estimate=pl.CostEstimate(
-            flops=rows * 4 * width * (inner + spare),
-            bytes_accessed=4 * width * (inner + spare) + 4 * len(blocks) * tok * width,
-            transcendentals=rows * inner,
+            flops=1000,
+            bytes_accessed=1000,
+            transcendentals=0,
         ),
         name="group",
     )(scalars, *blocks, w_gate, w_down, spare_gate, spare_down)
@@ -345,9 +345,15 @@
             held = move(held, round_ring)
 
     f32 = lambda a: a.astype(jnp.float32)
+    results = []
+    for k in range(steps):
+        results.append(run_group(scalars, groups[k], *weights, tok, top, capacity))
+        if k < steps - 1:
+            later = groups[min(k + 2, steps - 1)][0]
+            scalars = lax.optimization_barrier((scalars, results[-1][0], later))[0]
     passing = None
     for k in list(range(1, steps)) + [0]:
-        keep0, keep1, send = run_group(scalars, groups[k], *weights, tok, top, capacity)
+        keep0, keep1, send = results[k]
         got = move(send, over_core)
         far = (f32(keep1) + f32(got[1])).astype(jnp.bfloat16)
         total = f32(keep0) + f32(got[0]) + f32(move(far, over_y))

time: 126 us -> 128 us (1.016)
  waiting for transfers between devices: 64.1 us -> 50.3 us
  other arithmetic: 5.2 us -> 12.6 us
  starting transfers between devices: 20.3 us -> 26.7 us
    ppermute x26, waiting for transfers between devices: 64.1 us -> 50.3 us  [by_permutes(): move = lambda a, pairs: lax.ppermute(a, 'expert', pairs)]
    ppermute x26, starting transfers between devices: 20.3 us -> 26.7 us  [by_permutes(): move = lambda a, pairs: lax.ppermute(a, 'expert', pairs)]
    convert_element_type x4, other arithmetic: 0.4 us -> 4.12 us  [by_permutes(): far = (f32(keep1) + f32(got[1])).astype(jnp.bfloat16)]
    convert_element_type x4, other arithmetic: 1.52 us -> 4.61 us  [by_permutes(): passing = total.astype(jnp.bfloat16)]
    unnamed x13 -> x39, local copies, waits for them, and re-layouts: 4.9 us -> 5.28 us
  transfers between devices with their start and end apart: 26 -> 26, of which waited for: 11 -> 9; matrix products, arithmetic and copies ran while one was open for 2% -> 8% of each run, Pallas kernels for 24% -> 19%
where the time goes in v3:
time: 128 us
  waiting for transfers between devices  50.3 us (39%)
  Pallas kernels  31.6 us (25%)
  starting transfers between devices  26.7 us (21%)
  other arithmetic  12.6 us (10%)
  local copies, waits for them, and re-layouts  5.28 us (4%)
  between operations  1.58 us (1%)
    ppermute x26, waiting for transfers between devices, by_permutes(): move = lambda a, pairs: lax.ppermute(a, 'expert', pairs)  50.3 us
    pallas_call x4, Pallas kernels, run_group(): pl.pallas_call(functools.partial(group_kernel, tok=tok, top=top, capacity...  31.6 us
    ppermute x26, starting transfers between devices, by_permutes(): move = lambda a, pairs: lax.ppermute(a, 'expert', pairs)  26.7 us
    unnamed x39, local copies, waits for them, and re-layouts  5.28 us
    convert_element_type x4, other arithmetic, by_permutes(): passing = total.astype(jnp.bfloat16)  4.61 us
    convert_element_type x4, other arithmetic, by_permutes(): far = (f32(keep1) + f32(got[1])).astype(jnp.bfloat16)  4.12 us
  transfers between devices with their start and end apart: 26, of which 9 were waited for; matrix products, arithmetic and copies ran while one was open for 8% of the time, Pallas kernels for 19%

profile of v3, /device:TPU:0, one launch (start us, length us, event | category | flops | bytes accessed | tf_op | source)
XLA Modules:
  0.0 128.1 jit_solution(2997625648417571177)
XLA Ops:
  0.0 0.7 fusion.18
  0.7 1.0 fusion.16.block0
  1.8 3.1 %collective-permute-start.5 = (bf16[136,1536]{1,0:T(8,128)(2,1)S(1)}, bf16[136,1536]{1,0:T(8,128)(2,1)S(1)}, u32[]{:S(2)}, u32[]{:S(2)}) collective-permute-start(bf16[136,1536]{1,0:T(8,128)(2,1)S(1)} %fusion.16.block0), channel_id=1, source_target_pairs={{0,4},{1,5},{2,6},{3,7},{4,12},{5,13},{6,14},{7,15},{8,0},{9,1},{1... | collective-permute-start | bytes 1253384 | tf_op jit(solution)/shard_map/ppermute | solution.py:333
  4.8 1.5 %collective-permute-start = (bf16[136,1536]{1,0:T(8,128)(2,1)S(1)}, bf16[136,1536]{1,0:T(8,128)(2,1)S(1)}, u32[]{:S(2)}, u32[]{:S(2)}) collective-permute-start(bf16[136,1536]{1,0:T(8,128)(2,1)S(1)} %fusion.16.block0), channel_id=1, source_target_pairs={{0,2},{1,3},{2,0},{3,1},{4,6},{5,7},{6,4},{7,5},{8,10},{9,11},{10,... | collective-permute-start | bytes 1253384 | tf_op jit(solution)/shard_map/ppermute | solution.py:333
  6.4 9.1 %collective-permute-done.5.block0 = bf16[136,1536]{1,0:T(8,128)(2,1)S(1)} collective-permute-done((bf16[136,1536]{1,0:T(8,128)(2,1)S(1)}, bf16[136,1536]{1,0:T(8,128)(2,1)S(1)}, u32[]{:S(2)}, u32[]{:S(2)}) %collective-permute-start.5) | collective-permute-done | bytes 417824 | tf_op jit(solution)/shard_map/ppermute | solution.py:333
  15.5 1.6 %collective-permute-start.7 = (bf16[136,1536]{1,0:T(8,128)(2,1)S(1)}, bf16[136,1536]{1,0:T(8,128)(2,1)S(1)}, u32[]{:S(2)}, u32[]{:S(2)}) collective-permute-start(bf16[136,1536]{1,0:T(8,128)(2,1)S(1)} %collective-permute-done.5.block0), channel_id=1, source_target_pairs={{0,2},{1,3},{2,0},{3,1},{4,6},{5,7},{6,4},{7,5},{8,10},{9,11},{10,... | collective-permute-start | bytes 1253384 | tf_op jit(solution)/shard_map/ppermute | solution.py:333
  17.1 0.0 collective-permute-start.1
  17.1 0.0 collective-permute-done.block1
  17.1 0.5 collective-permute-start.2
  17.6 1.5 %collective-permute-start.6 = (bf16[136,1536]{1,0:T(8,128)(2,1)S(1)}, bf16[136,1536]{1,0:T(8,128)(2,1)S(1)}, u32[]{:S(2)}, u32[]{:S(2)}) collective-permute-start(bf16[136,1536]{1,0:T(8,128)(2,1)S(1)} %collective-permute-done.5.block0), channel_id=1, source_target_pairs={{0,4},{1,5},{2,6},{3,7},{4,12},{5,13},{6,14},{7,15},{8,0},{9,1},{1... | collective-permute-start | bytes 1253384 | tf_op jit(solution)/shard_map/ppermute | solution.py:333
  19.1 0.2 collective-permute-start.8
  19.3 7.0 %collective-permute-done.7.block1 = bf16[136,1536]{1,0:T(8,128)(2,1)S(1)} collective-permute-done((bf16[136,1536]{1,0:T(8,128)(2,1)S(1)}, bf16[136,1536]{1,0:T(8,128)(2,1)S(1)}, u32[]{:S(2)}, u32[]{:S(2)}) %collective-permute-start.7) | collective-permute-done | bytes 417824 | tf_op jit(solution)/shard_map/ppermute | solution.py:333
  26.3 0.0 collective-permute-start.9
  27.0 1.5 %fusion.17 = pred[]{:T(512)} fusion(s32[16,4]{0,1:T(4,128)} %param.13, s32[]{:T(128)S(6)} %select_n.4, s32[]{:T(128)} %axis_index.12), kind=kLoop, calls=%fused_computation.39 | loop fusion | flops 7 | bytes 25 | tf_op jit(solution)/shard_map/reduce_or | solution.py:383
  29.1 0.7 pad_add_fusion.scalars
  29.8 0.0 collective-permute-done.1.block2
  29.8 0.0 collective-permute-done.2.block3
  29.8 0.7 copy-done.8
  30.5 7.9 %group.4 = (bf16[128,1536]{1,0:T(8,128)(2,1)}, bf16[128,1536]{1,0:T(8,128)(2,1)}, bf16[2,128,1536]{2,1,0:T(8,128)(2,1)}) custom-call(s32[3]{0:T(128)} %pad_add_fusion.scalars, bf16[136,1536]{1,0:T(8,128)(2,1)} %copy-done, bf16[136,1536]{1,0:T(8,128)(2,1)} %copy-done.6, bf16[136,1536]{1,0:T(8,128)(2,1)} %copy-done.8, ...), custom_call_target="tpu_custom_call" | custom-call | flops 1000 | bytes 1000 | tf_op jit(solution)/shard_map/group/pallas_call | solution.py:293
  38.5 0.0 collective-permute-done.6.block0
  38.5 0.8 copy-done.7
  39.3 0.8 copy-done.9
  40.1 7.9 %group.5 = (bf16[128,1536]{1,0:T(8,128)(2,1)}, bf16[128,1536]{1,0:T(8,128)(2,1)}, bf16[2,128,1536]{2,1,0:T(8,128)(2,1)}) custom-call(s32[3]{0:T(128)} %pad_add_fusion.scalars, bf16[136,1536]{1,0:T(8,128)(2,1)} %copy-done.3, bf16[136,1536]{1,0:T(8,128)(2,1)} %copy-done.4, bf16[136,1536]{1,0:T(8,128)(2,1)} %copy-done.7, bf16[136,1536]{1,0:T(8,128)(2,1)} %copy-done.9, ...), custom_call_target="tpu_custom_call" | custom-call | flops 1000 | bytes 1000 | tf_op jit(solution)/shard_map/group/pallas_call | solution.py:293
  48.0 0.6 collective-permute-start.21
  48.5 1.3 collective-permute-start.11
  49.8 3.1 %collective-permute-start.10 = (bf16[136,1536]{1,0:T(8,128)(2,1)S(1)}, bf16[136,1536]{1,0:T(8,128)(2,1)S(1)}, u32[]{:S(2)}, u32[]{:S(2)}) collective-permute-start(bf16[136,1536]{1,0:T(8,128)(2,1)S(1)} %collective-permute-done.6.block0), channel_id=1, source_target_pairs={{0,4},{1,5},{2,6},{3,7},{4,12},{5,13},{6,14},{7,15},{8,0},{9,1},{1... | collective-permute-start | bytes 1253384 | tf_op jit(solution)/shard_map/ppermute | solution.py:333
  52.9 7.2 %collective-permute-done.11.block1 = bf16[136,1536]{1,0:T(8,128)(2,1)S(1)} collective-permute-done((bf16[136,1536]{1,0:T(8,128)(2,1)S(1)}, bf16[136,1536]{1,0:T(8,128)(2,1)S(1)}, u32[]{:S(2)}, u32[]{:S(2)}) %collective-permute-start.11) | collective-permute-done | bytes 417824 | tf_op jit(solution)/shard_map/ppermute | solution.py:333
  60.2 0.0 collective-permute-start.13
  60.2 2.0 %collective-permute-done.10.block0 = bf16[136,1536]{1,0:T(8,128)(2,1)S(1)} collective-permute-done((bf16[136,1536]{1,0:T(8,128)(2,1)S(1)}, bf16[136,1536]{1,0:T(8,128)(2,1)S(1)}, u32[]{:S(2)}, u32[]{:S(2)}) %collective-permute-start.10) | collective-permute-done | bytes 417824 | tf_op jit(solution)/shard_map/ppermute | solution.py:333
  62.2 1.5 %collective-permute-start.14 = (bf16[136,1536]{1,0:T(8,128)(2,1)S(1)}, bf16[136,1536]{1,0:T(8,128)(2,1)S(1)}, u32[]{:S(2)}, u32[]{:S(2)}) collective-permute-start(bf16[136,1536]{1,0:T(8,128)(2,1)S(1)} %collective-permute-done.10.block0), channel_id=1, source_target_pairs={{0,2},{1,3},{2,0},{3,1},{4,6},{5,7},{6,4},{7,5},{8,10},{9,11},{10,... | collective-permute-start | bytes 1253384 | tf_op jit(solution)/shard_map/ppermute | solution.py:333
  63.7 0.0 collective-permute-done.21
  63.7 1.8 %fusion.1 = bf16[128,1536]{1,0:T(8,128)(2,1)} fusion(bf16[128,1536]{1,0:T(8,128)(2,1)} %get-tuple-element.34, bf16[2,128,1536]{2,1,0:T(8,128)(2,1)S(1)} %collective-permute-done.21), kind=kLoop, calls=%fused_computation.3 | loop fusion | flops 786432 | bytes 1179648 | tf_op jit(solution)/shard_map/convert_element_type | solution.py:358
  65.6 0.5 collective-permute-start.22
  66.1 0.0 collective-permute-done.13.block3
  66.1 0.7 copy-done.12
  66.8 0.8 copy-done.14
  67.6 7.9 %group.6 = (bf16[128,1536]{1,0:T(8,128)(2,1)}, bf16[128,1536]{1,0:T(8,128)(2,1)}, bf16[2,128,1536]{2,1,0:T(8,128)(2,1)}) custom-call(s32[3]{0:T(128)} %pad_add_fusion.scalars, bf16[136,1536]{1,0:T(8,128)(2,1)} %copy-done.1, bf16[136,1536]{1,0:T(8,128)(2,1)} %copy-done.10, bf16[136,1536]{1,0:T(8,128)(2,1)} %copy-done.12, bf16[136,1536]{1,0:T(8,128)(2,1)} %copy-done.14, ...), custom_call_target="tpu_custom_call" | custom-call | flops 1000 | bytes 1000 | tf_op jit(solution)/shard_map/group/pallas_call | solution.py:293
  75.5 0.1 collective-permute-start.19
  75.6 0.5 collective-permute-start.15
  76.1 0.1 collective-permute-start.16
  76.2 5.4 %collective-permute-done.22 = bf16[128,1536]{1,0:T(8,128)(2,1)} collective-permute-done((bf16[128,1536]{1,0:T(8,128)(2,1)}, bf16[128,1536]{1,0:T(8,128)(2,1)}, u32[]{:S(2)}, u32[]{:S(2)}) %collective-permute-start.22) | collective-permute-done | bytes 393248 | tf_op jit(solution)/shard_map/ppermute | solution.py:333
  81.6 1.2 fusion.3
  82.7 2.8 %collective-permute-start.23 = (bf16[128,1536]{1,0:T(8,128)(2,1)S(1)}, bf16[128,1536]{1,0:T(8,128)(2,1)}, u32[]{:S(2)}, u32[]{:S(2)}) collective-permute-start(bf16[128,1536]{1,0:T(8,128)(2,1)S(1)} %fusion.3), channel_id=1, source_target_pairs={{0,4},{1,5},{2,6},{3,7},{4,12},{5,13},{6,14},{7,15},{8,0},{9,1},{1... | collective-permute-start | bytes 1179656 | tf_op jit(solution)/shard_map/ppermute | solution.py:333
  85.5 0.0 collective-permute-done.19
  85.5 1.1 fusion.4
  86.6 1.3 %collective-permute-start.20 = (bf16[128,1536]{1,0:T(8,128)(2,1)S(1)}, bf16[128,1536]{1,0:T(8,128)(2,1)}, u32[]{:S(2)}, u32[]{:S(2)}) collective-permute-start(bf16[128,1536]{1,0:T(8,128)(2,1)S(1)} %fusion.4), channel_id=1, source_target_pairs={{0,2},{1,3},{2,0},{3,1},{4,6},{5,7},{6,4},{7,5},{8,10},{9,11},{10,... | collective-permute-start | bytes 1179656 | tf_op jit(solution)/shard_map/ppermute | solution.py:333
  87.9 0.7 copy-done.11
  88.7 0.7 copy-done.13
  89.4 7.9 %group.7 = (bf16[128,1536]{1,0:T(8,128)(2,1)}, bf16[128,1536]{1,0:T(8,128)(2,1)}, bf16[2,128,1536]{2,1,0:T(8,128)(2,1)}) custom-call(s32[3]{0:T(128)} %pad_add_fusion.scalars, bf16[136,1536]{1,0:T(8,128)(2,1)} %copy-done.2, bf16[136,1536]{1,0:T(8,128)(2,1)} %copy-done.5, bf16[136,1536]{1,0:T(8,128)(2,1)} %copy-done.11, bf16[136,1536]{1,0:T(8,128)(2,1)} %copy-done.13, ...), custom_call_target="tpu_custom_call" | custom-call | flops 1000 | bytes 1000 | tf_op jit(solution)/shard_map/group/pallas_call | solution.py:293
  97.3 0.1 collective-permute-start.17
  97.4 0.5 collective-permute-start.3
  97.9 1.3 %fusion.7 = bf16[128,1536]{1,0:T(8,128)(2,1)S(1)} fusion(bf16[128,1536]{1,0:T(8,128)(2,1)} %collective-permute-done.23, bf16[128,1536]{1,0:T(8,128)(2,1)} %collective-permute-done.20, bf16[128,1536]{1,0:T(8,128)(2,1)S(1)} %copy-done.18, bf16[2,128,1536]{2,1,0:T(8,128)(2,1)S(1)} %collective-permute-done.19), kind=kLoop, calls=%fused_computation.12 | loop fusion | flops 1572864 | bytes 1966080 | tf_op jit(solution)/shard_map/convert_element_type | solution.py:362
  99.2 2.8 %collective-permute-start.24 = (bf16[128,1536]{1,0:T(8,128)(2,1)S(1)}, bf16[128,1536]{1,0:T(8,128)(2,1)S(1)}, u32[]{:S(2)}, u32[]{:S(2)}) collective-permute-start(bf16[128,1536]{1,0:T(8,128)(2,1)S(1)} %fusion.7), channel_id=1, source_target_pairs={{0,4},{1,5},{2,6},{3,7},{4,12},{5,13},{6,14},{7,15},{8,0},{9,1},{1... | collective-permute-start | bytes 1179656 | tf_op jit(solution)/shard_map/ppermute | solution.py:333
  102.0 1.1 fusion.8
  103.1 2.6 %collective-permute-start.18 = (bf16[128,1536]{1,0:T(8,128)(2,1)S(1)}, bf16[128,1536]{1,0:T(8,128)(2,1)S(1)}, u32[]{:S(2)}, u32[]{:S(2)}) collective-permute-start(bf16[128,1536]{1,0:T(8,128)(2,1)S(1)} %fusion.8), channel_id=1, source_target_pairs={{0,2},{1,3},{2,0},{3,1},{4,6},{5,7},{6,4},{7,5},{8,10},{9,11},{10,... | collective-permute-start | bytes 1179656 | tf_op jit(solution)/shard_map/ppermute | solution.py:333
  105.7 0.1 fusion.12
  105.8 0.1 collective-permute-start.4
  105.9 5.4 %collective-permute-done.24 = bf16[128,1536]{1,0:T(8,128)(2,1)S(1)} collective-permute-done((bf16[128,1536]{1,0:T(8,128)(2,1)S(1)}, bf16[128,1536]{1,0:T(8,128)(2,1)S(1)}, u32[]{:S(2)}, u32[]{:S(2)}) %collective-permute-start.24) | collective-permute-done | bytes 393248 | tf_op jit(solution)/shard_map/ppermute | solution.py:333
  111.3 4.3 %collective-permute-done.18 = bf16[128,1536]{1,0:T(8,128)(2,1)S(1)} collective-permute-done((bf16[128,1536]{1,0:T(8,128)(2,1)S(1)}, bf16[128,1536]{1,0:T(8,128)(2,1)S(1)}, u32[]{:S(2)}, u32[]{:S(2)}) %collective-permute-start.18) | collective-permute-done | bytes 393248 | tf_op jit(solution)/shard_map/ppermute | solution.py:333
  115.6 1.2 fusion.11
  116.8 0.6 collective-permute-start.25
  117.4 5.8 %collective-permute-done.4 = bf16[128,1536]{1,0:T(8,128)(2,1)S(1)} collective-permute-done((bf16[128,1536]{1,0:T(8,128)(2,1)S(1)}, bf16[128,1536]{1,0:T(8,128)(2,1)S(1)}, u32[]{:S(2)}, u32[]{:S(2)}) %collective-permute-start.4) | collective-permute-done | bytes 393248 | tf_op jit(solution)/shard_map/ppermute | solution.py:333
  123.2 4.0 %collective-permute-done.25 = bf16[128,1536]{1,0:T(8,128)(2,1)S(1)} collective-permute-done((bf16[128,1536]{1,0:T(8,128)(2,1)S(1)}, bf16[128,1536]{1,0:T(8,128)(2,1)S(1)}, u32[]{:S(2)}, u32[]{:S(2)}) %collective-permute-start.25) | collective-permute-done | bytes 393248 | tf_op jit(solution)/shard_map/ppermute | solution.py:333
  127.1 0.9 fusion.15
  (44 shorter events, 0.1 us)
Async XLA Ops:
  1.8 28.0 %copy-start = (bf16[136,1536]{1,0:T(8,128)(2,1)}, bf16[136,1536]{1,0:T(8,128)(2,1)S(1)}, u32[]{:S(2)}) copy-start(bf16[136,1536]{1,0:T(8,128)(2,1)S(1)} %fusion.16.block0) | copy-start | bytes 1253380
  1.8 13.7 %collective-permute-start.5 = (bf16[136,1536]{1,0:T(8,128)(2,1)S(1)}, bf16[136,1536]{1,0:T(8,128)(2,1)S(1)}, u32[]{:S(2)}, u32[]{:S(2)}) collective-permute-start(bf16[136,1536]{1,0:T(8,128)(2,1)S(1)} %fusion.16.block0), channel_id=1, source_target_pairs={{0,4},{1,5},{2,6},{3,7},{4,12},{5,13},{6,14},{7,15},{8,0},{9,1},{1... | collective-permute-start | bytes 1253384 | tf_op jit(solution)/shard_map/ppermute | solution.py:333
  4.8 12.2 %collective-permute-start = (bf16[136,1536]{1,0:T(8,128)(2,1)S(1)}, bf16[136,1536]{1,0:T(8,128)(2,1)S(1)}, u32[]{:S(2)}, u32[]{:S(2)}) collective-permute-start(bf16[136,1536]{1,0:T(8,128)(2,1)S(1)} %fusion.16.block0), channel_id=1, source_target_pairs={{0,2},{1,3},{2,0},{3,1},{4,6},{5,7},{6,4},{7,5},{8,10},{9,11},{10,... | collective-permute-start | bytes 1253384 | tf_op jit(solution)/shard_map/ppermute | solution.py:333
  15.5 23.0 %copy-start.3 = (bf16[136,1536]{1,0:T(8,128)(2,1)}, bf16[136,1536]{1,0:T(8,128)(2,1)S(1)}, u32[]{:S(2)}) copy-start(bf16[136,1536]{1,0:T(8,128)(2,1)S(1)} %collective-permute-done.5.block0) | copy-start | bytes 1253380
  15.5 10.8 %collective-permute-start.7 = (bf16[136,1536]{1,0:T(8,128)(2,1)S(1)}, bf16[136,1536]{1,0:T(8,128)(2,1)S(1)}, u32[]{:S(2)}, u32[]{:S(2)}) collective-permute-start(bf16[136,1536]{1,0:T(8,128)(2,1)S(1)} %collective-permute-done.5.block0), channel_id=1, source_target_pairs={{0,2},{1,3},{2,0},{3,1},{4,6},{5,7},{6,4},{7,5},{8,10},{9,11},{10,... | collective-permute-start | bytes 1253384 | tf_op jit(solution)/shard_map/ppermute | solution.py:333
  17.1 12.7 %collective-permute-start.1 = (bf16[136,1536]{1,0:T(8,128)(2,1)S(1)}, bf16[136,1536]{1,0:T(8,128)(2,1)S(1)}, u32[]{:S(2)}, u32[]{:S(2)}) collective-permute-start(bf16[136,1536]{1,0:T(8,128)(2,1)S(1)} %fusion.16.block0), channel_id=1, source_target_pairs={{0,1},{1,0},{2,3},{3,2},{4,5},{5,4},{6,7},{7,6},{8,9},{9,8},{10,11... | collective-permute-start | bytes 1253384 | tf_op jit(solution)/shard_map/ppermute | solution.py:333
  17.1 12.7 %copy-start.6 = (bf16[136,1536]{1,0:T(8,128)(2,1)}, bf16[136,1536]{1,0:T(8,128)(2,1)S(1)}, u32[]{:S(2)}) copy-start(bf16[136,1536]{1,0:T(8,128)(2,1)S(1)} %collective-permute-done.block1) | copy-start | bytes 1253380
  17.1 12.7 %collective-permute-start.2 = (bf16[136,1536]{1,0:T(8,128)(2,1)S(1)}, bf16[136,1536]{1,0:T(8,128)(2,1)}, u32[]{:S(2)}, u32[]{:S(2)}) collective-permute-start(bf16[136,1536]{1,0:T(8,128)(2,1)S(1)} %collective-permute-done.block1), channel_id=1, source_target_pairs={{0,1},{1,0},{2,3},{3,2},{4,5},{5,4},{6,7},{7,6},{8,9},{9,8},{10,11... | collective-permute-start | bytes 1253384 | tf_op jit(solution)/shard_map/ppermute | solution.py:333
  17.6 20.9 %collective-permute-start.6 = (bf16[136,1536]{1,0:T(8,128)(2,1)S(1)}, bf16[136,1536]{1,0:T(8,128)(2,1)S(1)}, u32[]{:S(2)}, u32[]{:S(2)}) collective-permute-start(bf16[136,1536]{1,0:T(8,128)(2,1)S(1)} %collective-permute-done.5.block0), channel_id=1, source_target_pairs={{0,4},{1,5},{2,6},{3,7},{4,12},{5,13},{6,14},{7,15},{8,0},{9,1},{1... | collective-permute-start | bytes 1253384 | tf_op jit(solution)/shard_map/ppermute | solution.py:333
  19.1 19.4 %collective-permute-start.8 = (bf16[136,1536]{1,0:T(8,128)(2,1)S(1)}, bf16[136,1536]{1,0:T(8,128)(2,1)S(1)}, u32[]{:S(2)}, u32[]{:S(2)}) collective-permute-start(bf16[136,1536]{1,0:T(8,128)(2,1)S(1)} %collective-permute-done.5.block0), channel_id=1, source_target_pairs={{0,1},{1,0},{2,3},{3,2},{4,5},{5,4},{6,7},{7,6},{8,9},{9,8},{10,11... | collective-permute-start | bytes 1253384 | tf_op jit(solution)/shard_map/ppermute | solution.py:333
  26.3 12.1 %copy-start.4 = (bf16[136,1536]{1,0:T(8,128)(2,1)}, bf16[136,1536]{1,0:T(8,128)(2,1)S(1)}, u32[]{:S(2)}) copy-start(bf16[136,1536]{1,0:T(8,128)(2,1)S(1)} %collective-permute-done.7.block1) | copy-start | bytes 1253380
  26.3 12.2 %collective-permute-start.9 = (bf16[136,1536]{1,0:T(8,128)(2,1)S(1)}, bf16[136,1536]{1,0:T(8,128)(2,1)S(1)}, u32[]{:S(2)}, u32[]{:S(2)}) collective-permute-start(bf16[136,1536]{1,0:T(8,128)(2,1)S(1)} %collective-permute-done.7.block1), channel_id=1, source_target_pairs={{0,1},{1,0},{2,3},{3,2},{4,5},{5,4},{6,7},{7,6},{8,9},{9,8},{10,11... | collective-permute-start | bytes 1253384 | tf_op jit(solution)/shard_map/ppermute | solution.py:333
  29.8 0.8 copy-start.8
  38.5 14.4 %copy-start.1 = (bf16[136,1536]{1,0:T(8,128)(2,1)}, bf16[136,1536]{1,0:T(8,128)(2,1)S(1)}, u32[]{:S(2)}) copy-start(bf16[136,1536]{1,0:T(8,128)(2,1)S(1)} %collective-permute-done.6.block0) | copy-start | bytes 1253380
  38.5 0.8 copy-start.7
  39.3 0.8 copy-start.9
  48.0 15.7 %collective-permute-start.21 = (bf16[2,128,1536]{2,1,0:T(8,128)(2,1)}, bf16[2,128,1536]{2,1,0:T(8,128)(2,1)S(1)}, u32[]{:S(2)}, u32[]{:S(2)}) collective-permute-start(bf16[2,128,1536]{2,1,0:T(8,128)(2,1)} %get-tuple-element.33), channel_id=1, source_target_pairs={{0,1},{1,0},{2,3},{3,2},{4,5},{5,4},{6,7},{7,6},{8,9},{9,8},{10,11... | collective-permute-start | bytes 2359304 | tf_op jit(solution)/shard_map/ppermute | solution.py:333
  48.5 11.6 %collective-permute-start.11 = (bf16[136,1536]{1,0:T(8,128)(2,1)S(1)}, bf16[136,1536]{1,0:T(8,128)(2,1)S(1)}, u32[]{:S(2)}, u32[]{:S(2)}) collective-permute-start(bf16[136,1536]{1,0:T(8,128)(2,1)S(1)} %collective-permute-done.6.block0), channel_id=1, source_target_pairs={{0,2},{1,3},{2,0},{3,1},{4,6},{5,7},{6,4},{7,5},{8,10},{9,11},{10,... | collective-permute-start | bytes 1253384 | tf_op jit(solution)/shard_map/ppermute | solution.py:333
  49.8 12.4 %collective-permute-start.10 = (bf16[136,1536]{1,0:T(8,128)(2,1)S(1)}, bf16[136,1536]{1,0:T(8,128)(2,1)S(1)}, u32[]{:S(2)}, u32[]{:S(2)}) collective-permute-start(bf16[136,1536]{1,0:T(8,128)(2,1)S(1)} %collective-permute-done.6.block0), channel_id=1, source_target_pairs={{0,4},{1,5},{2,6},{3,7},{4,12},{5,13},{6,14},{7,15},{8,0},{9,1},{1... | collective-permute-start | bytes 1253384 | tf_op jit(solution)/shard_map/ppermute | solution.py:333
  52.9 13.2 %collective-permute-start.12 = (bf16[136,1536]{1,0:T(8,128)(2,1)S(1)}, bf16[136,1536]{1,0:T(8,128)(2,1)S(1)}, u32[]{:S(2)}, u32[]{:S(2)}) collective-permute-start(bf16[136,1536]{1,0:T(8,128)(2,1)S(1)} %collective-permute-done.6.block0), channel_id=1, source_target_pairs={{0,1},{1,0},{2,3},{3,2},{4,5},{5,4},{6,7},{7,6},{8,9},{9,8},{10,11... | collective-permute-start | bytes 1253384 | tf_op jit(solution)/shard_map/ppermute | solution.py:333
  60.2 5.9 %copy-start.10 = (bf16[136,1536]{1,0:T(8,128)(2,1)}, bf16[136,1536]{1,0:T(8,128)(2,1)S(1)}, u32[]{:S(2)}) copy-start(bf16[136,1536]{1,0:T(8,128)(2,1)S(1)} %collective-permute-done.11.block1) | copy-start | bytes 1253380
  60.2 5.9 %collective-permute-start.13 = (bf16[136,1536]{1,0:T(8,128)(2,1)S(1)}, bf16[136,1536]{1,0:T(8,128)(2,1)S(1)}, u32[]{:S(2)}, u32[]{:S(2)}) collective-permute-start(bf16[136,1536]{1,0:T(8,128)(2,1)S(1)} %collective-permute-done.11.block1), channel_id=1, source_target_pairs={{0,1},{1,0},{2,3},{3,2},{4,5},{5,4},{6,7},{7,6},{8,9},{9,8},{10,11... | collective-permute-start | bytes 1253384 | tf_op jit(solution)/shard_map/ppermute | solution.py:333
  62.2 13.4 %copy-start.2 = (bf16[136,1536]{1,0:T(8,128)(2,1)}, bf16[136,1536]{1,0:T(8,128)(2,1)S(1)}, u32[]{:S(2)}) copy-start(bf16[136,1536]{1,0:T(8,128)(2,1)S(1)} %collective-permute-done.10.block0) | copy-start | bytes 1253380
  62.2 13.9 %collective-permute-start.14 = (bf16[136,1536]{1,0:T(8,128)(2,1)S(1)}, bf16[136,1536]{1,0:T(8,128)(2,1)S(1)}, u32[]{:S(2)}, u32[]{:S(2)}) collective-permute-start(bf16[136,1536]{1,0:T(8,128)(2,1)S(1)} %collective-permute-done.10.block0), channel_id=1, source_target_pairs={{0,2},{1,3},{2,0},{3,1},{4,6},{5,7},{6,4},{7,5},{8,10},{9,11},{10,... | collective-permute-start | bytes 1253384 | tf_op jit(solution)/shard_map/ppermute | solution.py:333
  65.6 16.0 %collective-permute-start.22 = (bf16[128,1536]{1,0:T(8,128)(2,1)}, bf16[128,1536]{1,0:T(8,128)(2,1)}, u32[]{:S(2)}, u32[]{:S(2)}) collective-permute-start(bf16[128,1536]{1,0:T(8,128)(2,1)} %fusion.1), channel_id=1, source_target_pairs={{0,2},{1,3},{2,0},{3,1},{4,6},{5,7},{6,4},{7,5},{8,10},{9,11},{10,... | collective-permute-start | bytes 1179656 | tf_op jit(solution)/shard_map/ppermute | solution.py:333
  66.1 15.5 %copy-start.16 = (bf16[128,1536]{1,0:T(8,128)(2,1)S(1)}, bf16[128,1536]{1,0:T(8,128)(2,1)}, u32[]{:S(2)}) copy-start(bf16[128,1536]{1,0:T(8,128)(2,1)} %get-tuple-element.24) | copy-start | bytes 1179652
  66.1 0.8 copy-start.12
  66.8 0.8 copy-start.14
  75.5 10.0 %collective-permute-start.19 = (bf16[2,128,1536]{2,1,0:T(8,128)(2,1)}, bf16[2,128,1536]{2,1,0:T(8,128)(2,1)S(1)}, u32[]{:S(2)}, u32[]{:S(2)}) collective-permute-start(bf16[2,128,1536]{2,1,0:T(8,128)(2,1)} %get-tuple-element.31), channel_id=1, source_target_pairs={{0,1},{1,0},{2,3},{3,2},{4,5},{5,4},{6,7},{7,6},{8,9},{9,8},{10,11... | collective-permute-start | bytes 2359304 | tf_op jit(solution)/shard_map/ppermute | solution.py:333
  75.6 12.3 %collective-permute-start.15 = (bf16[136,1536]{1,0:T(8,128)(2,1)S(1)}, bf16[136,1536]{1,0:T(8,128)(2,1)S(1)}, u32[]{:S(2)}, u32[]{:S(2)}) collective-permute-start(bf16[136,1536]{1,0:T(8,128)(2,1)S(1)} %collective-permute-done.10.block0), channel_id=1, source_target_pairs={{0,1},{1,0},{2,3},{3,2},{4,5},{5,4},{6,7},{7,6},{8,9},{9,8},{10,11... | collective-permute-start | bytes 1253384 | tf_op jit(solution)/shard_map/ppermute | solution.py:333
  76.1 11.8 %copy-start.5 = (bf16[136,1536]{1,0:T(8,128)(2,1)}, bf16[136,1536]{1,0:T(8,128)(2,1)S(1)}, u32[]{:S(2)}) copy-start(bf16[136,1536]{1,0:T(8,128)(2,1)S(1)} %collective-permute-done.14.block1) | copy-start | bytes 1253380
  76.1 11.8 %collective-permute-start.16 = (bf16[136,1536]{1,0:T(8,128)(2,1)S(1)}, bf16[136,1536]{1,0:T(8,128)(2,1)S(1)}, u32[]{:S(2)}, u32[]{:S(2)}) collective-permute-start(bf16[136,1536]{1,0:T(8,128)(2,1)S(1)} %collective-permute-done.14.block1), channel_id=1, source_target_pairs={{0,1},{1,0},{2,3},{3,2},{4,5},{5,4},{6,7},{7,6},{8,9},{9,8},{10,11... | collective-permute-start | bytes 1253384 | tf_op jit(solution)/shard_map/ppermute | solution.py:333
  82.7 15.2 %collective-permute-start.23 = (bf16[128,1536]{1,0:T(8,128)(2,1)S(1)}, bf16[128,1536]{1,0:T(8,128)(2,1)}, u32[]{:S(2)}, u32[]{:S(2)}) collective-permute-start(bf16[128,1536]{1,0:T(8,128)(2,1)S(1)} %fusion.3), channel_id=1, source_target_pairs={{0,4},{1,5},{2,6},{3,7},{4,12},{5,13},{6,14},{7,15},{8,0},{9,1},{1... | collective-permute-start | bytes 1179656 | tf_op jit(solution)/shard_map/ppermute | solution.py:333
  86.6 11.3 %collective-permute-start.20 = (bf16[128,1536]{1,0:T(8,128)(2,1)S(1)}, bf16[128,1536]{1,0:T(8,128)(2,1)}, u32[]{:S(2)}, u32[]{:S(2)}) collective-permute-start(bf16[128,1536]{1,0:T(8,128)(2,1)S(1)} %fusion.4), channel_id=1, source_target_pairs={{0,2},{1,3},{2,0},{3,1},{4,6},{5,7},{6,4},{7,5},{8,10},{9,11},{10,... | collective-permute-start | bytes 1179656 | tf_op jit(solution)/shard_map/ppermute | solution.py:333
  87.9 10.0 %copy-start.18 = (bf16[128,1536]{1,0:T(8,128)(2,1)S(1)}, bf16[128,1536]{1,0:T(8,128)(2,1)}, u32[]{:S(2)}) copy-start(bf16[128,1536]{1,0:T(8,128)(2,1)} %get-tuple-element.26) | copy-start | bytes 1179652
  87.9 17.8 %copy-start.15 = (bf16[128,1536]{1,0:T(8,128)(2,1)S(1)}, bf16[128,1536]{1,0:T(8,128)(2,1)}, u32[]{:S(2)}) copy-start(bf16[128,1536]{1,0:T(8,128)(2,1)} %get-tuple-element.22) | copy-start | bytes 1179652
  87.9 0.8 copy-start.11
  88.7 0.7 copy-start.13
  97.3 29.8 %copy-start.17 = (bf16[128,1536]{1,0:T(8,128)(2,1)S(1)}, bf16[128,1536]{1,0:T(8,128)(2,1)}, u32[]{:S(2)}) copy-start(bf16[128,1536]{1,0:T(8,128)(2,1)} %get-tuple-element.20) | copy-start | bytes 1179652
  97.3 4.7 %collective-permute-start.17 = (bf16[2,128,1536]{2,1,0:T(8,128)(2,1)}, bf16[2,128,1536]{2,1,0:T(8,128)(2,1)S(1)}, u32[]{:S(2)}, u32[]{:S(2)}) collective-permute-start(bf16[2,128,1536]{2,1,0:T(8,128)(2,1)} %get-tuple-element.29), channel_id=1, source_target_pairs={{0,1},{1,0},{2,3},{3,2},{4,5},{5,4},{6,7},{7,6},{8,9},{9,8},{10,11... | collective-permute-start | bytes 2359304 | tf_op jit(solution)/shard_map/ppermute | solution.py:333
  97.4 8.3 %collective-permute-start.3 = (bf16[2,128,1536]{2,1,0:T(8,128)(2,1)}, bf16[2,128,1536]{2,1,0:T(8,128)(2,1)S(1)}, u32[]{:S(2)}, u32[]{:S(2)}) collective-permute-start(bf16[2,128,1536]{2,1,0:T(8,128)(2,1)} %get-tuple-element.21), channel_id=1, source_target_pairs={{0,1},{1,0},{2,3},{3,2},{4,5},{5,4},{6,7},{7,6},{8,9},{9,8},{10,11... | collective-permute-start | bytes 2359304 | tf_op jit(solution)/shard_map/ppermute | solution.py:333
  99.2 12.0 %collective-permute-start.24 = (bf16[128,1536]{1,0:T(8,128)(2,1)S(1)}, bf16[128,1536]{1,0:T(8,128)(2,1)S(1)}, u32[]{:S(2)}, u32[]{:S(2)}) collective-permute-start(bf16[128,1536]{1,0:T(8,128)(2,1)S(1)} %fusion.7), channel_id=1, source_target_pairs={{0,4},{1,5},{2,6},{3,7},{4,12},{5,13},{6,14},{7,15},{8,0},{9,1},{1... | collective-permute-start | bytes 1179656 | tf_op jit(solution)/shard_map/ppermute | solution.py:333
  103.1 12.5 %collective-permute-start.18 = (bf16[128,1536]{1,0:T(8,128)(2,1)S(1)}, bf16[128,1536]{1,0:T(8,128)(2,1)S(1)}, u32[]{:S(2)}, u32[]{:S(2)}) collective-permute-start(bf16[128,1536]{1,0:T(8,128)(2,1)S(1)} %fusion.8), channel_id=1, source_target_pairs={{0,2},{1,3},{2,0},{3,1},{4,6},{5,7},{6,4},{7,5},{8,10},{9,11},{10,... | collective-permute-start | bytes 1179656 | tf_op jit(solution)/shard_map/ppermute | solution.py:333
  105.8 17.4 %collective-permute-start.4 = (bf16[128,1536]{1,0:T(8,128)(2,1)S(1)}, bf16[128,1536]{1,0:T(8,128)(2,1)S(1)}, u32[]{:S(2)}, u32[]{:S(2)}) collective-permute-start(bf16[128,1536]{1,0:T(8,128)(2,1)S(1)} %fusion.12), channel_id=1, source_target_pairs={{0,2},{1,3},{2,0},{3,1},{4,6},{5,7},{6,4},{7,5},{8,10},{9,11},{10,... | collective-permute-start | bytes 1179656 | tf_op jit(solution)/shard_map/ppermute | solution.py:333
  116.8 10.3 %collective-permute-start.25 = (bf16[128,1536]{1,0:T(8,128)(2,1)S(1)}, bf16[128,1536]{1,0:T(8,128)(2,1)S(1)}, u32[]{:S(2)}, u32[]{:S(2)}) collective-permute-start(bf16[128,1536]{1,0:T(8,128)(2,1)S(1)} %fusion.11), channel_id=1, source_target_pairs={{0,4},{1,5},{2,6},{3,7},{4,12},{5,13},{6,14},{7,15},{8,0},{9,1},{1... | collective-permute-start | bytes 1179656 | tf_op jit(solution)/shard_map/ppermute | solution.py:333

commit v4 on v2

--- a/solution.py
+++ b/solution.py
@@ -156,51 +156,28 @@
 
 
 def group_kernel(
-    scalars,
+    failed,
+    holders,
     block0,
     block1,
     block2,
     block3,
-    w_gate_hbm,
-    w_down_hbm,
-    spare_gate_hbm,
-    spare_down_hbm,
-    keep0,
-    keep1,
-    send,
     w_gate,
     w_down,
     spare_gate,
     spare_down,
-    rows_in,
-    spare_in,
-    hidden,
-    spare_hidden,
-    rows_out,
-    sems,
-    *,
+    *rest,
     tok,
     top,
     capacity,
 ):
-    width, inner = w_gate.shape
+    keep0, keep1, send, rows_in, spare_in, hidden, spare_hidden, rows_out = rest[-8:]
+    width, inner = w_gate.shape[1:]
     tile = 512
-    my_id, failed_id, holds = scalars[0], scalars[1], scalars[2]
-    copies = []
-
-    def fetch(source, target):
-        copy = pltpu.make_async_copy(source, target, sems.at[len(copies)])
-        copy.start()
-        copies.append(copy)
-        return copy
-
-    gate_tiles = [
-        fetch(w_gate_hbm.at[0, :, n : n + tile], w_gate.at[:, n : n + tile]) for n in range(0, inner, tile)
-    ]
-    down_tiles = [
-        fetch(w_down_hbm.at[0, :, n : n + tile], w_down.at[:, n : n + tile]) for n in range(0, width, tile)
-    ]
-    spare_tiles = [fetch(spare_gate_hbm.at[0], spare_gate), fetch(spare_down_hbm.at[0], spare_down)]
+    my_id, failed_id = lax.axis_index("expert"), failed[0]
+    holds = holders[failed_id, 0] == my_id
+    for j in range(1, holders.shape[1]):
+        holds = holds | (holders[failed_id, j] == my_id)
 
     before = (
         lax.broadcasted_iota(jnp.int32, (tok, tok), 0)
@@ -212,7 +189,7 @@
         mask = jnp.zeros((8, tok), jnp.float32)
         level = jnp.zeros((8, tok), jnp.float32)
         for k in range(top):
-            named = (meta[:, k * tok : (k + 1) * tok] == wanted) & live
+            named = (meta[:, k * tok : (k + 1) * tok] == wanted.astype(jnp.float32)) & live
             high = meta[:, (top + k) * tok : (top + k + 1) * tok]
             low = meta[:, (2 * top + k) * tok : (2 * top + k + 1) * tok]
             mask = mask + jnp.where(named, 1.0, 0.0)
@@ -227,8 +204,8 @@
     picks, weights, spare_weights = [], [], []
     for s, block in enumerate(blocks):
         meta = block[tok : tok + 8, :].astype(jnp.float32)
-        pick, weight = picker(meta, my_id.astype(jnp.float32), my_id != failed_id)
-        spare_pick, spare_weight = picker(meta, failed_id.astype(jnp.float32), holds > 0)
+        pick, weight = picker(meta, my_id, my_id != failed_id)
+        spare_pick, spare_weight = picker(meta, failed_id, holds)
         both = jnp.concatenate([pick, spare_pick], axis=0)
         picks.append(both)
         weights.append(weight)
@@ -240,37 +217,33 @@
             rows_in[s * capacity : (s + 1) * capacity, n : n + tile] = got[:capacity]
             spare_in[s * capacity : (s + 1) * capacity, n : n + tile] = got[capacity:]
 
-    for i, n in enumerate(range(0, inner, tile)):
-        gate_tiles[i].wait()
+    for n in range(0, inner, tile):
         hidden[:, n : n + tile] = gated_unit(
-            jnp.dot(rows_in[...], w_gate[:, n : n + tile], preferred_element_type=jnp.float32)
+            jnp.dot(rows_in[...], w_gate[0, :, n : n + tile], preferred_element_type=jnp.float32)
         ).astype(jnp.bfloat16)
-    for i, n in enumerate(range(0, width, tile)):
-        down_tiles[i].wait()
-        result = jnp.dot(hidden[...], w_down[:, n : n + tile], preferred_element_type=jnp.float32)
+    for n in range(0, width, tile):
+        result = jnp.dot(hidden[...], w_down[0, :, n : n + tile], preferred_element_type=jnp.float32)
         result = result.astype(jnp.bfloat16).astype(jnp.float32)
         for s in range(len(blocks)):
             rows_out[s, :capacity, n : n + tile] = (
                 result[s * capacity : (s + 1) * capacity] * weights[s]
             ).astype(jnp.bfloat16)
-    for copy in spare_tiles:
-        copy.wait()
-
-    @pl.when(holds > 0)
+
+    @pl.when(holds)
     def _():
         spare_hidden[...] = gated_unit(
-            jnp.dot(spare_in[...], spare_gate[...], preferred_element_type=jnp.float32)
+            jnp.dot(spare_in[...], spare_gate[0], preferred_element_type=jnp.float32)
         ).astype(jnp.bfloat16)
         for n in range(0, width, tile):
             result = jnp.dot(
-                spare_hidden[...], spare_down[:, n : n + tile], preferred_element_type=jnp.float32
+                spare_hidden[...], spare_down[0, :, n : n + tile], preferred_element_type=jnp.float32
             )
             for s in range(len(blocks)):
                 rows_out[s, capacity:, n : n + tile] = (
                     result[s * capacity : (s + 1) * capacity] * spare_weights[s]
                 ).astype(jnp.bfloat16)
 
-    @pl.when(holds <= 0)
+    @pl.when(jnp.logical_not(holds))
     def _():
         rows_out[:, capacity:, :] = jnp.zeros((len(blocks), capacity, width), jnp.bfloat16)
 
@@ -284,44 +257,55 @@
             ).astype(jnp.bfloat16)
 
 
-def run_group(scalars, blocks, w_gate, w_down, spare_gate, spare_down, tok, top, capacity):
-    width, inner, spare = w_gate.shape[1], w_gate.shape[2], spare_gate.shape[2]
+def run_group(failed, holders, blocks, weights, earlier, tok, top, capacity):
+    width, inner, spare = weights[0].shape[1], weights[0].shape[2], weights[2].shape[2]
     rows = len(blocks) * capacity
     vmem = pl.BlockSpec(memory_space=pltpu.VMEM)
-    hbm = pl.BlockSpec(memory_space=pl.ANY)
+    smem = pl.BlockSpec(memory_space=pltpu.SMEM)
     block = jax.ShapeDtypeStruct((tok, width), jnp.bfloat16)
     return pl.pallas_call(
         functools.partial(group_kernel, tok=tok, top=top, capacity=capacity),
         out_shape=(block, block, jax.ShapeDtypeStruct((2, tok, width), jnp.bfloat16)),
-        in_specs=[pl.BlockSpec(memory_space=pltpu.SMEM)] + [vmem] * 4 + [hbm] * 4,
+        in_specs=[smem, smem] + [vmem] * 8 + [pl.BlockSpec(memory_space=pl.ANY)] * len(earlier),
         out_specs=(vmem, vmem, vmem),
         scratch_shapes=[
-            pltpu.VMEM((width, inner), jnp.bfloat16),
-            pltpu.VMEM((inner, width), jnp.bfloat16),
-            pltpu.VMEM((width, spare), jnp.bfloat16),
-            pltpu.VMEM((spare, width), jnp.bfloat16),
             pltpu.VMEM((rows, width), jnp.bfloat16),
             pltpu.VMEM((rows, width), jnp.bfloat16),
             pltpu.VMEM((rows, inner), jnp.bfloat16),
             pltpu.VMEM((rows, spare), jnp.bfloat16),
             pltpu.VMEM((len(blocks), 2 * capacity, width), jnp.bfloat16),
-            pltpu.SemaphoreType.DMA((inner // 512 + width // 512 + 2,)),
         ],
-        compiler_params=pltpu.CompilerParams(vmem_limit_bytes=40 * 1024 * 1024),
+        compiler_params=pltpu.CompilerParams(vmem_limit_bytes=30 * 1024 * 1024),
         cost_estimate=pl.CostEstimate(
             flops=rows * 4 * width * (inner + spare),
             bytes_accessed=4 * width * (inner + spare) + 4 * len(blocks) * tok * width,
             transcendentals=rows * inner,
         ),
         name="group",
-    )(scalars, *blocks, w_gate, w_down, spare_gate, spare_down)
+    )(failed, holders, *blocks, *weights, *earlier)
+
+
+def nothing(*refs):
+    pass
+
+
+def come_after(value, *others, flops=0):
+    return pl.pallas_call(
+        nothing,
+        out_shape=jax.ShapeDtypeStruct(value.shape, value.dtype),
+        in_specs=[pl.BlockSpec(memory_space=pl.ANY)] * (1 + len(others)),
+        out_specs=pl.BlockSpec(memory_space=pl.ANY),
+        input_output_aliases={0: 0},
+        cost_estimate=pl.CostEstimate(flops=flops, bytes_accessed=0, transcendentals=0),
+        name="after",
+    )(value, *others)
 
 
 def folded_ring(length):
     return [0] + list(range(1, length, 2)) + list(range(2, length, 2))[::-1]
 
 
-def by_permutes(scalars, tokens, expert_ids, gate_levels, weights, owners, capacity):
+def by_permutes(failed, holders, tokens, expert_ids, gate_levels, weights, owners, capacity):
     tok, top = expert_ids.shape
     width = tokens.shape[1]
     order = folded_ring(owners // 4)
@@ -335,19 +319,24 @@
     meta = jnp.concatenate([expert_ids.T, gate_levels.T >> 5, gate_levels.T & 31], axis=0)
     meta = meta.astype(jnp.bfloat16).reshape(1, 3 * top * tok)
     meta = jnp.pad(meta, ((0, 7), (0, width - 3 * top * tok)))
-    held = jnp.concatenate([tokens, meta], axis=0)
-
-    groups = []
+    held = [come_after(jnp.concatenate([tokens, meta], axis=0), flops=8 * 10**9)]
+    across, results = [], []
     for k in range(steps):
-        across = move(held, over_y)
-        groups.append((held, across, move(held, over_core), move(across, over_core)))
-        if k < steps - 1:
-            held = move(held, round_ring)
+        if k > 0:
+            held.append(move(held[-1], round_ring))
+            if k > 1:
+                held[k] = come_after(held[k], results[k - 2][0])
+        across.append(move(held[k], over_y))
+        blocks = (held[k], across[k], move(held[k], over_core), move(across[k], over_core))
+        earlier = [results[-1][0]] if results else []
+        results.append(run_group(failed, holders, blocks, weights, earlier, tok, top, capacity))
 
     f32 = lambda a: a.astype(jnp.float32)
     passing = None
     for k in list(range(1, steps)) + [0]:
-        keep0, keep1, send = run_group(scalars, groups[k], *weights, tok, top, capacity)
+        keep0, keep1, send = results[k]
+        if k < steps - 1:
+            send = come_after(send, across[k + 1], held[min(k + 2, steps - 1)])
         got = move(send, over_core)
         far = (f32(keep1) + f32(got[1])).astype(jnp.bfloat16)
         total = f32(keep0) + f32(got[0]) + f32(move(far, over_y))
@@ -378,7 +367,9 @@
     scalars = jnp.stack([my_index, failed_id, holds])
     weights = (w_gate, w_down, spare_gate, spare_down)
     if owners % 4 == 0 and owners <= 32 and 3 * top_count * tok_count <= tokens.shape[1]:
-        return by_permutes(scalars, tokens, expert_ids, gate_levels, weights, owners, capacity)
+        return by_permutes(
+            failed_device, replica_holders, tokens, expert_ids, gate_levels, weights, owners, capacity
+        )
     codes = (expert_ids * LEVELS + gate_levels).T
     all_codes = lax.all_gather(codes, "expert", axis=0)
     all_tokens = lax.all_gather(tokens, "expert", axis=0, tiled=True)

time: 126 us -> 131 us (1.040); the launches traced: 127 us -> 130 us
  local copies, waits for them, and re-layouts: 4.9 us -> 33.1 us
  waiting for transfers between devices: 64.1 us -> 37.9 us
  other arithmetic: 5.2 us -> 12.6 us
  Pallas kernels: 30.8 us -> 26.6 us
  starting transfers between devices: 20.3 us -> 18.9 us
    unnamed x13 -> x76, local copies, waits for them, and re-layouts: 4.9 us -> 33.1 us
    ppermute x26, waiting for transfers between devices: 64.1 us -> 37.9 us  [by_permutes(): move = lambda a, pairs: lax.ppermute(a, 'expert', pairs)]
    convert_element_type x4, other arithmetic: 0.4 us -> 5.43 us  [by_permutes(): far = (f32(keep1) + f32(got[1])).astype(jnp.bfloat16)]
    pallas_call x4, Pallas kernels: 30.8 us -> 26.6 us  [run_group(): pl.pallas_call(functools.partial(group_kernel, tok=tok, top=top, capacity...]
    convert_element_type x4, other arithmetic: 1.52 us -> 4.72 us  [by_permutes(): passing = total.astype(jnp.bfloat16)]
    reduce_or x1 -> x0, other arithmetic: 1.46 us -> none  [shards(): holds = jnp.any(holder_row == my_index).astype(jnp.int32)]
    ppermute x26, starting transfers between devices: 20.3 us -> 18.9 us  [by_permutes(): move = lambda a, pairs: lax.ppermute(a, 'expert', pairs)]
  transfers between devices with their start and end apart: 26 -> 26, of which waited for: 11 -> 9; matrix products, arithmetic and copies ran while one was open for 2% -> 7% of each run, Pallas kernels for 24% -> 20%
where the time goes in v4:
time: 131 us; the launch traced here: 130 us
  waiting for transfers between devices  37.9 us (29%)
  local copies, waits for them, and re-layouts  33.1 us (25%)
  Pallas kernels  26.6 us (20%)
  starting transfers between devices  18.9 us (14%)
  other arithmetic  12.6 us (10%)
    ppermute x26, waiting for transfers between devices, by_permutes(): move = lambda a, pairs: lax.ppermute(a, 'expert', pairs)  37.9 us
    unnamed x76, local copies, waits for them, and re-layouts  33.1 us
    pallas_call x4, Pallas kernels, run_group(): pl.pallas_call(functools.partial(group_kernel, tok=tok, top=top, capacity...  26.6 us
    ppermute x26, starting transfers between devices, by_permutes(): move = lambda a, pairs: lax.ppermute(a, 'expert', pairs)  18.9 us
    convert_element_type x4, other arithmetic, by_permutes(): far = (f32(keep1) + f32(got[1])).astype(jnp.bfloat16)  5.43 us
    convert_element_type x4, other arithmetic, by_permutes(): passing = total.astype(jnp.bfloat16)  4.72 us
  transfers between devices with their start and end apart: 26, of which 9 were waited for; matrix products, arithmetic and copies ran while one was open for 7% of the time, Pallas kernels for 20%

profile of v4, /device:TPU:0, one launch (start us, length us, event | category | flops | bytes accessed | tf_op | source)
XLA Modules:
  0.0 130.0 jit_solution(14738082371988737486)
XLA Ops:
  0.0 0.7 fusion.17
  0.7 1.8 %fusion.16.refs_0_ = bf16[136,1536]{1,0:T(8,128)(2,1)} fusion(bf16[1,1536]{1,0:T(2,128)(2,1)S(1)} %bitcast.52, bf16[128,1536]{1,0:T(8,128)(2,1)} %param.9), kind=kLoop, calls=%fused_computation.25 | loop fusion | flops 1253376 | bytes 814080 | tf_op jit(solution)/shard_map/concatenate | solution.py:322
  2.5 3.1 %collective-permute-start.3 = (bf16[136,1536]{1,0:T(8,128)(2,1)}, bf16[136,1536]{1,0:T(8,128)(2,1)}, u32[]{:S(2)}, u32[]{:S(2)}) collective-permute-start(bf16[136,1536]{1,0:T(8,128)(2,1)} %after.6.block0), channel_id=1, source_target_pairs={{0,4},{1,5},{2,6},{3,7},{4,12},{5,13},{6,14},{7,15},{8,0},{9,1},{1... | collective-permute-start | bytes 1253384 | tf_op jit(solution)/shard_map/ppermute | solution.py:317
  5.6 1.5 %collective-permute-start = (bf16[136,1536]{1,0:T(8,128)(2,1)}, bf16[136,1536]{1,0:T(8,128)(2,1)}, u32[]{:S(2)}, u32[]{:S(2)}) collective-permute-start(bf16[136,1536]{1,0:T(8,128)(2,1)} %after.6.block0), channel_id=1, source_target_pairs={{0,2},{1,3},{2,0},{3,1},{4,6},{5,7},{6,4},{7,5},{8,10},{9,11},{10,... | collective-permute-start | bytes 1253384 | tf_op jit(solution)/shard_map/ppermute | solution.py:317
  7.1 9.5 %collective-permute-done.3.block0 = bf16[136,1536]{1,0:T(8,128)(2,1)} collective-permute-done((bf16[136,1536]{1,0:T(8,128)(2,1)}, bf16[136,1536]{1,0:T(8,128)(2,1)}, u32[]{:S(2)}, u32[]{:S(2)}) %collective-permute-start.3) | collective-permute-done | bytes 417824 | tf_op jit(solution)/shard_map/ppermute | solution.py:317
  16.6 1.6 %collective-permute-start.4 = (bf16[136,1536]{1,0:T(8,128)(2,1)}, bf16[136,1536]{1,0:T(8,128)(2,1)S(1)}, u32[]{:S(2)}, u32[]{:S(2)}) collective-permute-start(bf16[136,1536]{1,0:T(8,128)(2,1)} %collective-permute-done.3.block0), channel_id=1, source_target_pairs={{0,2},{1,3},{2,0},{3,1},{4,6},{5,7},{6,4},{7,5},{8,10},{9,11},{10,... | collective-permute-start | bytes 1253384 | tf_op jit(solution)/shard_map/ppermute | solution.py:317
  18.1 0.5 collective-permute-start.2
  18.6 1.2 collective-permute-start.5
  20.6 0.2 collective-permute-start.9
  20.8 6.8 %collective-permute-done.4.refs_1_.block1 = bf16[136,1536]{1,0:T(8,128)(2,1)S(1)} collective-permute-done((bf16[136,1536]{1,0:T(8,128)(2,1)}, bf16[136,1536]{1,0:T(8,128)(2,1)S(1)}, u32[]{:S(2)}, u32[]{:S(2)}) %collective-permute-start.4) | collective-permute-done | bytes 417824 | tf_op jit(solution)/shard_map/ppermute | solution.py:317
  27.7 2.5 %copy-done = bf16[1,1536,1536]{2,1,0:T(8,128)(2,1)S(1)} copy-done((bf16[1,1536,1536]{2,1,0:T(8,128)(2,1)S(1)}, bf16[1,1536,1536]{2,1,0:T(8,128)(2,1)}, u32[]{:S(2)}) %copy-start) | copy-done | bytes 4718616
  30.1 2.3 %copy-done.4 = bf16[1,1536,1536]{2,1,0:T(8,128)(2,1)S(1)} copy-done((bf16[1,1536,1536]{2,1,0:T(8,128)(2,1)S(1)}, bf16[1,1536,1536]{2,1,0:T(8,128)(2,1)}, u32[]{:S(2)}) %copy-start.4) | copy-done | bytes 4718616
  32.5 1.0 copy-done.21
  33.5 6.5 %group.4 = (bf16[128,1536]{1,0:T(8,128)(2,1)S(1)}, bf16[128,1536]{1,0:T(8,128)(2,1)S(1)}, bf16[2,128,1536]{2,1,0:T(8,128)(2,1)S(1)}) custom-call(s32[1]{0:T(128)S(6)} %copy.29.failed, s32[16,4]{1,0:T(8,128)S(1)} %copy.16.holders, bf16[136,1536]{1,0:T(8,128)(2,1)S(1)} %copy-done.21, bf16[136,1536]{1,0:T(8,128)(2,1)} %collective-permute-done.block1, ...), custom_call_target="tpu_custom_call" | custom-call | flops 3019898880 | bytes 14942208 | tf_op jit(solution)/shard_map/group/pallas_call | solution.py:266
  40.0 0.7 copy-done.16
  40.7 0.8 copy-done.27
  41.5 0.9 copy-done.24
  42.4 0.8 copy-done.12
  43.1 1.3 %collective-permute-start.14 = (bf16[136,1536]{1,0:T(8,128)(2,1)}, bf16[136,1536]{1,0:T(8,128)(2,1)}, u32[]{:S(2)}, u32[]{:S(2)}) collective-permute-start(bf16[136,1536]{1,0:T(8,128)(2,1)} %after.7.refs_2_.block0), channel_id=1, source_target_pairs={{0,2},{1,3},{2,0},{3,1},{4,6},{5,7},{6,4},{7,5},{8,10},{9,11},{10,... | collective-permute-start | bytes 1253384 | tf_op jit(solution)/shard_map/ppermute | solution.py:317
  44.5 2.3 %copy-done.1 = bf16[1,1536,1536]{2,1,0:T(8,128)(2,1)S(1)} copy-done((bf16[1,1536,1536]{2,1,0:T(8,128)(2,1)S(1)}, bf16[1,1536,1536]{2,1,0:T(8,128)(2,1)}, u32[]{:S(2)}) %copy-start.1) | copy-done | bytes 4718616
  46.8 2.3 %copy-done.5 = bf16[1,1536,1536]{2,1,0:T(8,128)(2,1)S(1)} copy-done((bf16[1,1536,1536]{2,1,0:T(8,128)(2,1)S(1)}, bf16[1,1536,1536]{2,1,0:T(8,128)(2,1)}, u32[]{:S(2)}) %copy-start.5) | copy-done | bytes 4718616
  49.1 1.0 copy-done.17
  50.1 1.0 copy-done.20
  51.1 6.7 %group.5 = (bf16[128,1536]{1,0:T(8,128)(2,1)S(1)}, bf16[128,1536]{1,0:T(8,128)(2,1)S(1)}, bf16[2,128,1536]{2,1,0:T(8,128)(2,1)S(1)}) custom-call(s32[1]{0:T(128)S(6)} %copy.29.failed, s32[16,4]{1,0:T(8,128)S(1)} %copy.16.holders, bf16[136,1536]{1,0:T(8,128)(2,1)} %collective-permute-done.3.block0, bf16[136,1536]{1,0:T(8,128)(2,1)S(1)} %copy-done.20, ...), custom_call_target="tpu_custom_call" | custom-call | flops 3019898880 | bytes 14942208 | tf_op jit(solution)/shard_map/group/pallas_call | solution.py:266
  57.9 0.8 copy-done.14
  58.6 0.9 copy-done.25
  59.5 0.7 copy-done.31
  60.3 0.7 copy-done.10
  61.0 0.5 collective-permute-start.15
  61.5 0.7 collective-permute-start.11
  62.2 1.6 %collective-permute-done.21 = bf16[2,128,1536]{2,1,0:T(8,128)(2,1)S(1)} collective-permute-done((bf16[2,128,1536]{2,1,0:T(8,128)(2,1)}, bf16[2,128,1536]{2,1,0:T(8,128)(2,1)S(1)}, u32[]{:S(2)}, u32[]{:S(2)}) %collective-permute-start.21) | collective-permute-done | bytes 786464 | tf_op jit(solution)/shard_map/ppermute | solution.py:317
  63.8 2.1 %fusion.1 = bf16[128,1536]{1,0:T(8,128)(2,1)} fusion(bf16[128,1536]{1,0:T(8,128)(2,1)} %copy-done.31, bf16[2,128,1536]{2,1,0:T(8,128)(2,1)S(1)} %collective-permute-done.21), kind=kLoop, calls=%fused_computation.3 | loop fusion | flops 786432 | bytes 1179648 | tf_op jit(solution)/shard_map/convert_element_type | solution.py:341
  66.0 0.7 collective-permute-start.22
  66.7 2.3 %copy-done.2 = bf16[1,1536,1536]{2,1,0:T(8,128)(2,1)S(1)} copy-done((bf16[1,1536,1536]{2,1,0:T(8,128)(2,1)S(1)}, bf16[1,1536,1536]{2,1,0:T(8,128)(2,1)}, u32[]{:S(2)}) %copy-start.2) | copy-done | bytes 4718616
  69.0 2.3 %copy-done.6 = bf16[1,1536,1536]{2,1,0:T(8,128)(2,1)S(1)} copy-done((bf16[1,1536,1536]{2,1,0:T(8,128)(2,1)S(1)}, bf16[1,1536,1536]{2,1,0:T(8,128)(2,1)}, u32[]{:S(2)}) %copy-start.6) | copy-done | bytes 4718616
  71.4 1.0 copy-done.15
  72.4 6.2 %group.6 = (bf16[128,1536]{1,0:T(8,128)(2,1)S(1)}, bf16[128,1536]{1,0:T(8,128)(2,1)S(1)}, bf16[2,128,1536]{2,1,0:T(8,128)(2,1)S(1)}) custom-call(s32[1]{0:T(128)S(6)} %copy.29.failed, s32[16,4]{1,0:T(8,128)S(1)} %copy.16.holders, bf16[136,1536]{1,0:T(8,128)(2,1)S(1)} %copy-done.13, bf16[136,1536]{1,0:T(8,128)(2,1)} %collective-permute-done.14.block1.refs_1_, ...), custom_call_target="tpu_custom_call" | custom-call | flops 3019898880 | bytes 14942208 | tf_op jit(solution)/shard_map/group/pallas_call | solution.py:266
  78.6 0.7 copy-done.22
  79.4 0.9 copy-done.26
  80.2 0.7 copy-done.30
  81.0 0.5 collective-permute-start.12
  81.6 0.3 collective-permute-done.22
  81.9 2.1 %fusion.3 = bf16[128,1536]{1,0:T(8,128)(2,1)} fusion(bf16[128,1536]{1,0:T(8,128)(2,1)} %collective-permute-done.22, bf16[128,1536]{1,0:T(8,128)(2,1)} %copy-done.14, bf16[2,128,1536]{2,1,0:T(8,128)(2,1)} %copy-done.34), kind=kLoop, calls=%fused_computation.6 | loop fusion | flops 1179648 | bytes 1572864 | tf_op jit(solution)/shard_map/convert_element_type | solution.py:345
  84.0 2.0 %collective-permute-start.23 = (bf16[128,1536]{1,0:T(8,128)(2,1)}, bf16[128,1536]{1,0:T(8,128)(2,1)}, u32[]{:S(2)}, u32[]{:S(2)}) collective-permute-start(bf16[128,1536]{1,0:T(8,128)(2,1)} %fusion.3), channel_id=1, source_target_pairs={{0,4},{1,5},{2,6},{3,7},{4,12},{5,13},{6,14},{7,15},{8,0},{9,1},{1... | collective-permute-start | bytes 1179656 | tf_op jit(solution)/shard_map/ppermute | solution.py:317
  86.0 2.1 %fusion.4 = bf16[128,1536]{1,0:T(8,128)(2,1)} fusion(bf16[128,1536]{1,0:T(8,128)(2,1)} %copy-done.30, bf16[2,128,1536]{2,1,0:T(8,128)(2,1)S(1)} %collective-permute-done.19), kind=kLoop, calls=%fused_computation.8 | loop fusion | flops 786432 | bytes 1179648 | tf_op jit(solution)/shard_map/convert_element_type | solution.py:341
  88.1 1.3 collective-permute-start.20
  89.4 2.3 %copy-done.3 = bf16[1,1536,1536]{2,1,0:T(8,128)(2,1)S(1)} copy-done((bf16[1,1536,1536]{2,1,0:T(8,128)(2,1)S(1)}, bf16[1,1536,1536]{2,1,0:T(8,128)(2,1)}, u32[]{:S(2)}) %copy-start.3) | copy-done | bytes 4718616
  91.8 2.3 %copy-done.7 = bf16[1,1536,1536]{2,1,0:T(8,128)(2,1)S(1)} copy-done((bf16[1,1536,1536]{2,1,0:T(8,128)(2,1)S(1)}, bf16[1,1536,1536]{2,1,0:T(8,128)(2,1)}, u32[]{:S(2)}) %copy-start.7) | copy-done | bytes 4718616
  94.1 7.1 %group.7 = (bf16[128,1536]{1,0:T(8,128)(2,1)S(1)}, bf16[128,1536]{1,0:T(8,128)(2,1)S(1)}, bf16[2,128,1536]{2,1,0:T(8,128)(2,1)}) custom-call(s32[1]{0:T(128)S(6)} %copy.29.failed, s32[16,4]{1,0:T(8,128)S(1)} %copy.16.holders, bf16[136,1536]{1,0:T(8,128)(2,1)S(1)} %copy-done.11, bf16[136,1536]{1,0:T(8,128)(2,1)} %collective-permute-done.11.block1.refs_1_, ...), custom_call_target="tpu_custom_call" | custom-call | flops 3019898880 | bytes 14942208 | tf_op jit(solution)/shard_map/group/pallas_call | solution.py:266
  101.2 0.8 copy-done.29
  102.0 0.7 copy-done.32
  102.8 0.5 collective-permute-start.6
  103.3 1.5 %fusion.7 = bf16[128,1536]{1,0:T(8,128)(2,1)S(1)} fusion(bf16[128,1536]{1,0:T(8,128)(2,1)} %collective-permute-done.23, bf16[128,1536]{1,0:T(8,128)(2,1)} %collective-permute-done.20, bf16[128,1536]{1,0:T(8,128)(2,1)S(1)} %copy-done.23, bf16[2,128,1536]{2,1,0:T(8,128)(2,1)} %copy-done.35), kind=kLoop, calls=%fused_computation.12 | loop fusion | flops 1572864 | bytes 1966080 | tf_op jit(solution)/shard_map/convert_element_type | solution.py:345
  104.8 0.4 collective-permute-done.17
  105.2 1.1 fusion.8
  106.3 0.8 collective-permute-start.18
  107.2 1.3 %collective-permute-start.7 = (bf16[128,1536]{1,0:T(8,128)(2,1)S(1)}, bf16[128,1536]{1,0:T(8,128)(2,1)S(1)}, u32[]{:S(2)}, u32[]{:S(2)}) collective-permute-start(bf16[128,1536]{1,0:T(8,128)(2,1)S(1)} %fusion.12), channel_id=1, source_target_pairs={{0,2},{1,3},{2,0},{3,1},{4,6},{5,7},{6,4},{7,5},{8,10},{9,11},{10,... | collective-permute-start | bytes 1179656 | tf_op jit(solution)/shard_map/ppermute | solution.py:317
  108.6 8.2 %collective-permute-done.24 = bf16[128,1536]{1,0:T(8,128)(2,1)S(1)} collective-permute-done((bf16[128,1536]{1,0:T(8,128)(2,1)S(1)}, bf16[128,1536]{1,0:T(8,128)(2,1)S(1)}, u32[]{:S(2)}, u32[]{:S(2)}) %collective-permute-start.24) | collective-permute-done | bytes 393248 | tf_op jit(solution)/shard_map/ppermute | solution.py:317
  116.8 1.6 %collective-permute-done.18 = bf16[128,1536]{1,0:T(8,128)(2,1)S(1)} collective-permute-done((bf16[128,1536]{1,0:T(8,128)(2,1)S(1)}, bf16[128,1536]{1,0:T(8,128)(2,1)S(1)}, u32[]{:S(2)}, u32[]{:S(2)}) %collective-permute-start.18) | collective-permute-done | bytes 393248 | tf_op jit(solution)/shard_map/ppermute | solution.py:317
  118.4 0.2 fusion.11
  118.6 1.0 collective-permute-start.25
  119.5 6.5 %collective-permute-done.7 = bf16[128,1536]{1,0:T(8,128)(2,1)S(1)} collective-permute-done((bf16[128,1536]{1,0:T(8,128)(2,1)S(1)}, bf16[128,1536]{1,0:T(8,128)(2,1)S(1)}, u32[]{:S(2)}, u32[]{:S(2)}) %collective-permute-start.7) | collective-permute-done | bytes 393248 | tf_op jit(solution)/shard_map/ppermute | solution.py:317
  126.0 3.1 %collective-permute-done.25 = bf16[128,1536]{1,0:T(8,128)(2,1)S(1)} collective-permute-done((bf16[128,1536]{1,0:T(8,128)(2,1)S(1)}, bf16[128,1536]{1,0:T(8,128)(2,1)S(1)}, u32[]{:S(2)}, u32[]{:S(2)}) %collective-permute-start.25) | collective-permute-done | bytes 393248 | tf_op jit(solution)/shard_map/ppermute | solution.py:317
  129.0 0.9 fusion.15
  (85 shorter events, 0.5 us)
Async XLA Ops:
  2.5 18.0 %copy-start.36 = (s32[16,4]{0,1:T(4,128)S(1)}, s32[16,4]{0,1:T(4,128)}, u32[]{:S(2)}) copy-start(s32[16,4]{0,1:T(4,128)} %param.13) | copy-start | bytes 772
  2.5 25.1 %copy-start.8 = (bf16[1,1536,384]{2,1,0:T(8,128)(2,1)S(1)}, bf16[1,1536,384]{2,1,0:T(8,128)(2,1)}, u32[]{:S(2)}) copy-start(bf16[1,1536,384]{2,1,0:T(8,128)(2,1)} %spare_gate.7) | copy-start | bytes 3538948
  2.5 25.1 %copy-start.9 = (bf16[1,384,1536]{2,1,0:T(8,128)(2,1)S(1)}, bf16[1,384,1536]{2,1,0:T(8,128)(2,1)}, u32[]{:S(2)}) copy-start(bf16[1,384,1536]{2,1,0:T(8,128)(2,1)} %spare_down.7) | copy-start | bytes 3538948
  2.5 14.0 %collective-permute-start.3 = (bf16[136,1536]{1,0:T(8,128)(2,1)}, bf16[136,1536]{1,0:T(8,128)(2,1)}, u32[]{:S(2)}, u32[]{:S(2)}) collective-permute-start(bf16[136,1536]{1,0:T(8,128)(2,1)} %after.6.block0), channel_id=1, source_target_pairs={{0,4},{1,5},{2,6},{3,7},{4,12},{5,13},{6,14},{7,15},{8,0},{9,1},{1... | collective-permute-start | bytes 1253384 | tf_op jit(solution)/shard_map/ppermute | solution.py:317
  5.6 12.5 %collective-permute-start = (bf16[136,1536]{1,0:T(8,128)(2,1)}, bf16[136,1536]{1,0:T(8,128)(2,1)}, u32[]{:S(2)}, u32[]{:S(2)}) collective-permute-start(bf16[136,1536]{1,0:T(8,128)(2,1)} %after.6.block0), channel_id=1, source_target_pairs={{0,2},{1,3},{2,0},{3,1},{4,6},{5,7},{6,4},{7,5},{8,10},{9,11},{10,... | collective-permute-start | bytes 1253384 | tf_op jit(solution)/shard_map/ppermute | solution.py:317
  16.6 11.0 %collective-permute-start.4 = (bf16[136,1536]{1,0:T(8,128)(2,1)}, bf16[136,1536]{1,0:T(8,128)(2,1)S(1)}, u32[]{:S(2)}, u32[]{:S(2)}) collective-permute-start(bf16[136,1536]{1,0:T(8,128)(2,1)} %collective-permute-done.3.block0), channel_id=1, source_target_pairs={{0,2},{1,3},{2,0},{3,1},{4,6},{5,7},{6,4},{7,5},{8,10},{9,11},{10,... | collective-permute-start | bytes 1253384 | tf_op jit(solution)/shard_map/ppermute | solution.py:317
  18.1 9.5 %collective-permute-start.1 = (bf16[136,1536]{1,0:T(8,128)(2,1)}, bf16[136,1536]{1,0:T(8,128)(2,1)}, u32[]{:S(2)}, u32[]{:S(2)}) collective-permute-start(bf16[136,1536]{1,0:T(8,128)(2,1)} %after.6.block0), channel_id=1, source_target_pairs={{0,1},{1,0},{2,3},{3,2},{4,5},{5,4},{6,7},{7,6},{8,9},{9,8},{10,11... | collective-permute-start | bytes 1253384 | tf_op jit(solution)/shard_map/ppermute | solution.py:317
  18.1 9.5 %collective-permute-start.2 = (bf16[136,1536]{1,0:T(8,128)(2,1)}, bf16[136,1536]{1,0:T(8,128)(2,1)}, u32[]{:S(2)}, u32[]{:S(2)}) collective-permute-start(bf16[136,1536]{1,0:T(8,128)(2,1)} %collective-permute-done.block1), channel_id=1, source_target_pairs={{0,1},{1,0},{2,3},{3,2},{4,5},{5,4},{6,7},{7,6},{8,9},{9,8},{10,11... | collective-permute-start | bytes 1253384 | tf_op jit(solution)/shard_map/ppermute | solution.py:317
  18.6 22.8 %collective-permute-start.5 = (bf16[136,1536]{1,0:T(8,128)(2,1)}, bf16[136,1536]{1,0:T(8,128)(2,1)S(1)}, u32[]{:S(2)}, u32[]{:S(2)}) collective-permute-start(bf16[136,1536]{1,0:T(8,128)(2,1)} %collective-permute-done.3.block0), channel_id=1, source_target_pairs={{0,4},{1,5},{2,6},{3,7},{4,12},{5,13},{6,14},{7,15},{8,0},{9,1},{1... | collective-permute-start | bytes 1253384 | tf_op jit(solution)/shard_map/ppermute | solution.py:317
  20.6 23.8 %collective-permute-start.9 = (bf16[136,1536]{1,0:T(8,128)(2,1)}, bf16[136,1536]{1,0:T(8,128)(2,1)}, u32[]{:S(2)}, u32[]{:S(2)}) collective-permute-start(bf16[136,1536]{1,0:T(8,128)(2,1)} %collective-permute-done.3.block0), channel_id=1, source_target_pairs={{0,1},{1,0},{2,3},{3,2},{4,5},{5,4},{6,7},{7,6},{8,9},{9,8},{10,11... | collective-permute-start | bytes 1253384 | tf_op jit(solution)/shard_map/ppermute | solution.py:317
  27.6 12.3 %copy-start.19 = (bf16[136,1536]{1,0:T(8,128)(2,1)}, bf16[136,1536]{1,0:T(8,128)(2,1)S(1)}, u32[]{:S(2)}) copy-start(bf16[136,1536]{1,0:T(8,128)(2,1)S(1)} %collective-permute-done.4.refs_1_.block1) | copy-start | bytes 1253380
  27.6 16.8 %collective-permute-start.10 = (bf16[136,1536]{1,0:T(8,128)(2,1)S(1)}, bf16[136,1536]{1,0:T(8,128)(2,1)}, u32[]{:S(2)}, u32[]{:S(2)}) collective-permute-start(bf16[136,1536]{1,0:T(8,128)(2,1)S(1)} %collective-permute-done.4.refs_1_.block1), channel_id=1, source_target_pairs={{0,1},{1,0},{2,3},{3,2},{4,5},{5,4},{6,7},{7,6},{8,9},{9,8},{10,11... | collective-permute-start | bytes 1253384 | tf_op jit(solution)/shard_map/ppermute | solution.py:317
  27.6 2.5 %copy-start = (bf16[1,1536,1536]{2,1,0:T(8,128)(2,1)S(1)}, bf16[1,1536,1536]{2,1,0:T(8,128)(2,1)}, u32[]{:S(2)}) copy-start(bf16[1,1536,1536]{2,1,0:T(8,128)(2,1)} %w_gate.7) | copy-start | bytes 14155780
  30.1 2.3 %copy-start.4 = (bf16[1,1536,1536]{2,1,0:T(8,128)(2,1)S(1)}, bf16[1,1536,1536]{2,1,0:T(8,128)(2,1)}, u32[]{:S(2)}) copy-start(bf16[1,1536,1536]{2,1,0:T(8,128)(2,1)} %w_down.7) | copy-start | bytes 14155780
  32.5 1.0 copy-start.21
  40.0 0.7 copy-start.16
  40.7 0.8 copy-start.27
  41.5 0.9 copy-start.24
  42.4 0.8 copy-start.12
  43.1 17.1 %collective-permute-start.8 = (bf16[136,1536]{1,0:T(8,128)(2,1)}, bf16[136,1536]{1,0:T(8,128)(2,1)S(1)}, u32[]{:S(2)}, u32[]{:S(2)}) collective-permute-start(bf16[136,1536]{1,0:T(8,128)(2,1)} %after.7.refs_2_.block0), channel_id=1, source_target_pairs={{0,4},{1,5},{2,6},{3,7},{4,12},{5,13},{6,14},{7,15},{8,0},{9,1},{1... | collective-permute-start | bytes 1253384 | tf_op jit(solution)/shard_map/ppermute | solution.py:317
  43.1 17.9 %collective-permute-start.14 = (bf16[136,1536]{1,0:T(8,128)(2,1)}, bf16[136,1536]{1,0:T(8,128)(2,1)}, u32[]{:S(2)}, u32[]{:S(2)}) collective-permute-start(bf16[136,1536]{1,0:T(8,128)(2,1)} %after.7.refs_2_.block0), channel_id=1, source_target_pairs={{0,2},{1,3},{2,0},{3,1},{4,6},{5,7},{6,4},{7,5},{8,10},{9,11},{10,... | collective-permute-start | bytes 1253384 | tf_op jit(solution)/shard_map/ppermute | solution.py:317
  44.5 2.3 %copy-start.1 = (bf16[1,1536,1536]{2,1,0:T(8,128)(2,1)S(1)}, bf16[1,1536,1536]{2,1,0:T(8,128)(2,1)}, u32[]{:S(2)}) copy-start(bf16[1,1536,1536]{2,1,0:T(8,128)(2,1)} %w_gate.7) | copy-start | bytes 14155780
  46.8 2.3 %copy-start.5 = (bf16[1,1536,1536]{2,1,0:T(8,128)(2,1)S(1)}, bf16[1,1536,1536]{2,1,0:T(8,128)(2,1)}, u32[]{:S(2)}) copy-start(bf16[1,1536,1536]{2,1,0:T(8,128)(2,1)} %w_down.7) | copy-start | bytes 14155780
  49.1 1.0 copy-start.17
  50.1 1.0 copy-start.20
  51.1 9.9 %copy-start.13 = (bf16[136,1536]{1,0:T(8,128)(2,1)S(1)}, bf16[136,1536]{1,0:T(8,128)(2,1)}, u32[]{:S(2)}) copy-start(bf16[136,1536]{1,0:T(8,128)(2,1)} %after.7.refs_2_.block0) | copy-start | bytes 1253380
  57.9 0.8 copy-start.14
  58.6 0.9 copy-start.25
  59.5 0.7 copy-start.31
  60.2 0.7 copy-start.10
  61.0 2.8 %collective-permute-start.21 = (bf16[2,128,1536]{2,1,0:T(8,128)(2,1)}, bf16[2,128,1536]{2,1,0:T(8,128)(2,1)S(1)}, u32[]{:S(2)}, u32[]{:S(2)}) collective-permute-start(bf16[2,128,1536]{2,1,0:T(8,128)(2,1)} %after.11), channel_id=1, source_target_pairs={{0,1},{1,0},{2,3},{3,2},{4,5},{5,4},{6,7},{7,6},{8,9},{9,8},{10,11... | collective-permute-start | bytes 2359304 | tf_op jit(solution)/shard_map/ppermute | solution.py:317
  61.0 5.7 %collective-permute-start.15 = (bf16[136,1536]{1,0:T(8,128)(2,1)S(1)}, bf16[136,1536]{1,0:T(8,128)(2,1)S(1)}, u32[]{:S(2)}, u32[]{:S(2)}) collective-permute-start(bf16[136,1536]{1,0:T(8,128)(2,1)S(1)} %copy-done.13), channel_id=1, source_target_pairs={{0,1},{1,0},{2,3},{3,2},{4,5},{5,4},{6,7},{7,6},{8,9},{9,8},{10,11... | collective-permute-start | bytes 1253384 | tf_op jit(solution)/shard_map/ppermute | solution.py:317
  61.5 19.5 %collective-permute-start.11 = (bf16[136,1536]{1,0:T(8,128)(2,1)}, bf16[136,1536]{1,0:T(8,128)(2,1)}, u32[]{:S(2)}, u32[]{:S(2)}) collective-permute-start(bf16[136,1536]{1,0:T(8,128)(2,1)} %after.9.block0.refs_2_), channel_id=1, source_target_pairs={{0,2},{1,3},{2,0},{3,1},{4,6},{5,7},{6,4},{7,5},{8,10},{9,11},{10,... | collective-permute-start | bytes 1253384 | tf_op jit(solution)/shard_map/ppermute | solution.py:317
  62.2 4.5 %collective-permute-start.16 = (bf16[136,1536]{1,0:T(8,128)(2,1)}, bf16[136,1536]{1,0:T(8,128)(2,1)S(1)}, u32[]{:S(2)}, u32[]{:S(2)}) collective-permute-start(bf16[136,1536]{1,0:T(8,128)(2,1)} %collective-permute-done.14.block1.refs_1_), channel_id=1, source_target_pairs={{0,1},{1,0},{2,3},{3,2},{4,5},{5,4},{6,7},{7,6},{8,9},{9,8},{10,11... | collective-permute-start | bytes 1253384 | tf_op jit(solution)/shard_map/ppermute | solution.py:317
  63.8 2.9 %copy-start.34 = (bf16[2,128,1536]{2,1,0:T(8,128)(2,1)}, bf16[2,128,1536]{2,1,0:T(8,128)(2,1)S(1)}, u32[]{:S(2)}) copy-start(bf16[2,128,1536]{2,1,0:T(8,128)(2,1)S(1)} %collective-permute-done.21) | copy-start | bytes 2359300
  63.8 17.2 %copy-start.11 = (bf16[136,1536]{1,0:T(8,128)(2,1)S(1)}, bf16[136,1536]{1,0:T(8,128)(2,1)}, u32[]{:S(2)}) copy-start(bf16[136,1536]{1,0:T(8,128)(2,1)} %after.9.block0.refs_2_) | copy-start | bytes 1253380
  66.0 15.9 %collective-permute-start.22 = (bf16[128,1536]{1,0:T(8,128)(2,1)}, bf16[128,1536]{1,0:T(8,128)(2,1)}, u32[]{:S(2)}, u32[]{:S(2)}) collective-permute-start(bf16[128,1536]{1,0:T(8,128)(2,1)} %fusion.1), channel_id=1, source_target_pairs={{0,2},{1,3},{2,0},{3,1},{4,6},{5,7},{6,4},{7,5},{8,10},{9,11},{10,... | collective-permute-start | bytes 1179656 | tf_op jit(solution)/shard_map/ppermute | solution.py:317
  66.7 2.3 %copy-start.2 = (bf16[1,1536,1536]{2,1,0:T(8,128)(2,1)S(1)}, bf16[1,1536,1536]{2,1,0:T(8,128)(2,1)}, u32[]{:S(2)}) copy-start(bf16[1,1536,1536]{2,1,0:T(8,128)(2,1)} %w_gate.7) | copy-start | bytes 14155780
  69.0 2.3 %copy-start.6 = (bf16[1,1536,1536]{2,1,0:T(8,128)(2,1)S(1)}, bf16[1,1536,1536]{2,1,0:T(8,128)(2,1)}, u32[]{:S(2)}) copy-start(bf16[1,1536,1536]{2,1,0:T(8,128)(2,1)} %w_down.7) | copy-start | bytes 14155780
  71.4 1.0 copy-start.15
  78.6 0.7 copy-start.22
  79.4 0.9 copy-start.26
  80.2 0.7 copy-start.30
  81.0 8.4 %copy-start.23 = (bf16[128,1536]{1,0:T(8,128)(2,1)S(1)}, bf16[128,1536]{1,0:T(8,128)(2,1)}, u32[]{:S(2)}) copy-start(bf16[128,1536]{1,0:T(8,128)(2,1)} %copy-done.22) | copy-start | bytes 1179652
  81.0 5.0 %collective-permute-start.19 = (bf16[2,128,1536]{2,1,0:T(8,128)(2,1)}, bf16[2,128,1536]{2,1,0:T(8,128)(2,1)S(1)}, u32[]{:S(2)}, u32[]{:S(2)}) collective-permute-start(bf16[2,128,1536]{2,1,0:T(8,128)(2,1)} %after.10), channel_id=1, source_target_pairs={{0,1},{1,0},{2,3},{3,2},{4,5},{5,4},{6,7},{7,6},{8,9},{9,8},{10,11... | collective-permute-start | bytes 2359304 | tf_op jit(solution)/shard_map/ppermute | solution.py:317
  81.0 8.4 %collective-permute-start.12 = (bf16[136,1536]{1,0:T(8,128)(2,1)S(1)}, bf16[136,1536]{1,0:T(8,128)(2,1)S(1)}, u32[]{:S(2)}, u32[]{:S(2)}) collective-permute-start(bf16[136,1536]{1,0:T(8,128)(2,1)S(1)} %copy-done.11), channel_id=1, source_target_pairs={{0,1},{1,0},{2,3},{3,2},{4,5},{5,4},{6,7},{7,6},{8,9},{9,8},{10,11... | collective-permute-start | bytes 1253384 | tf_op jit(solution)/shard_map/ppermute | solution.py:317
  81.5 7.9 %collective-permute-start.13 = (bf16[136,1536]{1,0:T(8,128)(2,1)}, bf16[136,1536]{1,0:T(8,128)(2,1)S(1)}, u32[]{:S(2)}, u32[]{:S(2)}) collective-permute-start(bf16[136,1536]{1,0:T(8,128)(2,1)} %collective-permute-done.11.block1.refs_1_), channel_id=1, source_target_pairs={{0,1},{1,0},{2,3},{3,2},{4,5},{5,4},{6,7},{7,6},{8,9},{9,8},{10,11... | collective-permute-start | bytes 1253384 | tf_op jit(solution)/shard_map/ppermute | solution.py:317
  84.0 19.2 %collective-permute-start.23 = (bf16[128,1536]{1,0:T(8,128)(2,1)}, bf16[128,1536]{1,0:T(8,128)(2,1)}, u32[]{:S(2)}, u32[]{:S(2)}) collective-permute-start(bf16[128,1536]{1,0:T(8,128)(2,1)} %fusion.3), channel_id=1, source_target_pairs={{0,4},{1,5},{2,6},{3,7},{4,12},{5,13},{6,14},{7,15},{8,0},{9,1},{1... | collective-permute-start | bytes 1179656 | tf_op jit(solution)/shard_map/ppermute | solution.py:317
  86.0 3.4 %copy-start.35 = (bf16[2,128,1536]{2,1,0:T(8,128)(2,1)}, bf16[2,128,1536]{2,1,0:T(8,128)(2,1)S(1)}, u32[]{:S(2)}) copy-start(bf16[2,128,1536]{2,1,0:T(8,128)(2,1)S(1)} %collective-permute-done.19) | copy-start | bytes 2359300
  88.1 15.1 %collective-permute-start.20 = (bf16[128,1536]{1,0:T(8,128)(2,1)}, bf16[128,1536]{1,0:T(8,128)(2,1)}, u32[]{:S(2)}, u32[]{:S(2)}) collective-permute-start(bf16[128,1536]{1,0:T(8,128)(2,1)} %fusion.4), channel_id=1, source_target_pairs={{0,2},{1,3},{2,0},{3,1},{4,6},{5,7},{6,4},{7,5},{8,10},{9,11},{10,... | collective-permute-start | bytes 1179656 | tf_op jit(solution)/shard_map/ppermute | solution.py:317
  89.4 2.3 %copy-start.3 = (bf16[1,1536,1536]{2,1,0:T(8,128)(2,1)S(1)}, bf16[1,1536,1536]{2,1,0:T(8,128)(2,1)}, u32[]{:S(2)}) copy-start(bf16[1,1536,1536]{2,1,0:T(8,128)(2,1)} %w_gate.7) | copy-start | bytes 14155780
  91.8 2.3 %copy-start.7 = (bf16[1,1536,1536]{2,1,0:T(8,128)(2,1)S(1)}, bf16[1,1536,1536]{2,1,0:T(8,128)(2,1)}, u32[]{:S(2)}) copy-start(bf16[1,1536,1536]{2,1,0:T(8,128)(2,1)} %w_down.7) | copy-start | bytes 14155780
  101.2 0.8 copy-start.29
  102.0 0.7 copy-start.32
  102.7 4.4 %copy-start.28 = (bf16[128,1536]{1,0:T(8,128)(2,1)S(1)}, bf16[128,1536]{1,0:T(8,128)(2,1)}, u32[]{:S(2)}) copy-start(bf16[128,1536]{1,0:T(8,128)(2,1)} %copy-done.27) | copy-start | bytes 1179652
  102.7 26.3 %copy-start.18 = (bf16[128,1536]{1,0:T(8,128)(2,1)S(1)}, bf16[128,1536]{1,0:T(8,128)(2,1)}, u32[]{:S(2)}) copy-start(bf16[128,1536]{1,0:T(8,128)(2,1)} %copy-done.16) | copy-start | bytes 1179652
  102.7 15.6 %copy-start.33 = (bf16[128,1536]{1,0:T(8,128)(2,1)S(1)}, bf16[128,1536]{1,0:T(8,128)(2,1)}, u32[]{:S(2)}) copy-start(bf16[128,1536]{1,0:T(8,128)(2,1)} %copy-done.32) | copy-start | bytes 1179652
  102.7 2.5 %collective-permute-start.17 = (bf16[2,128,1536]{2,1,0:T(8,128)(2,1)}, bf16[2,128,1536]{2,1,0:T(8,128)(2,1)S(1)}, u32[]{:S(2)}, u32[]{:S(2)}) collective-permute-start(bf16[2,128,1536]{2,1,0:T(8,128)(2,1)} %get-tuple-element.23), channel_id=1, source_target_pairs={{0,1},{1,0},{2,3},{3,2},{4,5},{5,4},{6,7},{7,6},{8,9},{9,8},{10,11... | collective-permute-start | bytes 2359304 | tf_op jit(solution)/shard_map/ppermute | solution.py:317
  102.8 4.4 %collective-permute-start.6 = (bf16[2,128,1536]{2,1,0:T(8,128)(2,1)}, bf16[2,128,1536]{2,1,0:T(8,128)(2,1)S(1)}, u32[]{:S(2)}, u32[]{:S(2)}) collective-permute-start(bf16[2,128,1536]{2,1,0:T(8,128)(2,1)} %after.8), channel_id=1, source_target_pairs={{0,1},{1,0},{2,3},{3,2},{4,5},{5,4},{6,7},{7,6},{8,9},{9,8},{10,11... | collective-permute-start | bytes 2359304 | tf_op jit(solution)/shard_map/ppermute | solution.py:317
  104.7 12.1 %collective-permute-start.24 = (bf16[128,1536]{1,0:T(8,128)(2,1)S(1)}, bf16[128,1536]{1,0:T(8,128)(2,1)S(1)}, u32[]{:S(2)}, u32[]{:S(2)}) collective-permute-start(bf16[128,1536]{1,0:T(8,128)(2,1)S(1)} %fusion.7), channel_id=1, source_target_pairs={{0,4},{1,5},{2,6},{3,7},{4,12},{5,13},{6,14},{7,15},{8,0},{9,1},{1... | collective-permute-start | bytes 1179656 | tf_op jit(solution)/shard_map/ppermute | solution.py:317
  106.3 12.0 %collective-permute-start.18 = (bf16[128,1536]{1,0:T(8,128)(2,1)S(1)}, bf16[128,1536]{1,0:T(8,128)(2,1)S(1)}, u32[]{:S(2)}, u32[]{:S(2)}) collective-permute-start(bf16[128,1536]{1,0:T(8,128)(2,1)S(1)} %fusion.8), channel_id=1, source_target_pairs={{0,2},{1,3},{2,0},{3,1},{4,6},{5,7},{6,4},{7,5},{8,10},{9,11},{10,... | collective-permute-start | bytes 1179656 | tf_op jit(solution)/shard_map/ppermute | solution.py:317
  107.2 18.7 %collective-permute-start.7 = (bf16[128,1536]{1,0:T(8,128)(2,1)S(1)}, bf16[128,1536]{1,0:T(8,128)(2,1)S(1)}, u32[]{:S(2)}, u32[]{:S(2)}) collective-permute-start(bf16[128,1536]{1,0:T(8,128)(2,1)S(1)} %fusion.12), channel_id=1, source_target_pairs={{0,2},{1,3},{2,0},{3,1},{4,6},{5,7},{6,4},{7,5},{8,10},{9,11},{10,... | collective-permute-start | bytes 1179656 | tf_op jit(solution)/shard_map/ppermute | solution.py:317
  118.6 10.5 %collective-permute-start.25 = (bf16[128,1536]{1,0:T(8,128)(2,1)S(1)}, bf16[128,1536]{1,0:T(8,128)(2,1)S(1)}, u32[]{:S(2)}, u32[]{:S(2)}) collective-permute-start(bf16[128,1536]{1,0:T(8,128)(2,1)S(1)} %fusion.11), channel_id=1, source_target_pairs={{0,4},{1,5},{2,6},{3,7},{4,12},{5,13},{6,14},{7,15},{8,0},{9,1},{1... | collective-permute-start | bytes 1179656 | tf_op jit(solution)/shard_map/ppermute | solution.py:317

commit v5 on v4

--- a/solution.py
+++ b/solution.py
@@ -7,10 +7,11 @@
 from jax.sharding import PartitionSpec as P
 
 LEVELS = 1024
+VMEM_GRANT = 65200 * 1024
 
 
 def gated_unit(values):
-    return values * jax.nn.sigmoid(1.702 * values)
+    return values * (0.5 + 0.5 * jnp.tanh(0.851 * values))
 
 
 def expert_kernel(
@@ -155,29 +156,33 @@
     )(scalars, codes, tokens, w_gate, w_down, spare_gate, spare_down)
 
 
-def group_kernel(
-    failed,
-    holders,
-    block0,
-    block1,
-    block2,
-    block3,
-    w_gate,
-    w_down,
-    spare_gate,
-    spare_down,
-    *rest,
-    tok,
-    top,
-    capacity,
-):
-    keep0, keep1, send, rows_in, spare_in, hidden, spare_hidden, rows_out = rest[-8:]
-    width, inner = w_gate.shape[1:]
+def group_kernel(failed, holders, *refs, others, tok, top, capacity):
+    blocks, weights_hbm, refs = refs[:4], refs[4:8], refs[8 + others :]
+    keep0, keep1, send, held, w_gate, w_down, spare_gate, spare_down = refs[:8]
+    rows_in, spare_in, hidden, spare_hidden, rows_out, dense, fetched, stored = refs[8:]
+    width, inner = w_gate.shape
     tile = 512
     my_id, failed_id = lax.axis_index("expert"), failed[0]
     holds = holders[failed_id, 0] == my_id
     for j in range(1, holders.shape[1]):
         holds = holds | (holders[failed_id, j] == my_id)
+    copies = []
+
+    def fetch(source, target):
+        copy = pltpu.make_async_copy(source, target, fetched.at[len(copies)])
+        copy.start()
+        copies.append(copy)
+        return copy
+
+    gate_hbm, down_hbm, spare_gate_hbm, spare_down_hbm = weights_hbm
+    block_copies = [fetch(block, held.at[s]) for s, block in enumerate(blocks)]
+    gate_copies = [
+        fetch(gate_hbm.at[0, :, n : n + tile], w_gate.at[:, n : n + tile]) for n in range(0, inner, tile)
+    ]
+    spare_copies = [fetch(spare_gate_hbm.at[0], spare_gate), fetch(spare_down_hbm.at[0], spare_down)]
+    down_copies = [
+        fetch(down_hbm.at[0, :, n : n + tile], w_down.at[:, n : n + tile]) for n in range(0, width, tile)
+    ]
 
     before = (
         lax.broadcasted_iota(jnp.int32, (tok, tok), 0)
@@ -200,10 +205,10 @@
         weight = jnp.sum(jnp.where(hit, level[:1], 0.0), axis=1, keepdims=True)
         return hit.astype(jnp.float32).astype(jnp.bfloat16), weight
 
-    blocks = (block0, block1, block2, block3)
     picks, weights, spare_weights = [], [], []
-    for s, block in enumerate(blocks):
-        meta = block[tok : tok + 8, :].astype(jnp.float32)
+    for s in range(len(blocks)):
+        block_copies[s].wait()
+        meta = held[s, tok : tok + 8, :].astype(jnp.float32)
         pick, weight = picker(meta, my_id, my_id != failed_id)
         spare_pick, spare_weight = picker(meta, failed_id, holds)
         both = jnp.concatenate([pick, spare_pick], axis=0)
@@ -211,94 +216,120 @@
         weights.append(weight)
         spare_weights.append(spare_weight)
         for n in range(0, width, tile):
-            got = jnp.dot(both, block[:tok, n : n + tile], preferred_element_type=jnp.float32).astype(
+            got = jnp.dot(both, held[s, :tok, n : n + tile], preferred_element_type=jnp.float32).astype(
                 jnp.bfloat16
             )
             rows_in[s * capacity : (s + 1) * capacity, n : n + tile] = got[:capacity]
             spare_in[s * capacity : (s + 1) * capacity, n : n + tile] = got[capacity:]
 
-    for n in range(0, inner, tile):
+    for i, n in enumerate(range(0, inner, tile)):
+        gate_copies[i].wait()
         hidden[:, n : n + tile] = gated_unit(
-            jnp.dot(rows_in[...], w_gate[0, :, n : n + tile], preferred_element_type=jnp.float32)
+            jnp.dot(rows_in[...], w_gate[:, n : n + tile], preferred_element_type=jnp.float32)
         ).astype(jnp.bfloat16)
-    for n in range(0, width, tile):
-        result = jnp.dot(hidden[...], w_down[0, :, n : n + tile], preferred_element_type=jnp.float32)
+    for copy in spare_copies:
+        copy.wait()
+
+    @pl.when(holds)
+    def _():
+        spare_hidden[...] = gated_unit(
+            jnp.dot(spare_in[...], spare_gate[...], preferred_element_type=jnp.float32)
+        ).astype(jnp.bfloat16)
+        for n in range(0, width, tile):
+            result = jnp.dot(
+                spare_hidden[...], spare_down[:, n : n + tile], preferred_element_type=jnp.float32
+            )
+            for s in range(len(blocks)):
+                rows_out[s, capacity:, n : n + tile] = (
+                    result[s * capacity : (s + 1) * capacity] * spare_weights[s]
+                ).astype(jnp.bfloat16)
+
+    @pl.when(jnp.logical_not(holds))
+    def _():
+        rows_out[:, capacity:, :] = jnp.zeros((len(blocks), capacity, width), jnp.bfloat16)
+
+    for i, n in enumerate(range(0, width, tile)):
+        down_copies[i].wait()
+        result = jnp.dot(hidden[...], w_down[:, n : n + tile], preferred_element_type=jnp.float32)
         result = result.astype(jnp.bfloat16).astype(jnp.float32)
         for s in range(len(blocks)):
             rows_out[s, :capacity, n : n + tile] = (
                 result[s * capacity : (s + 1) * capacity] * weights[s]
             ).astype(jnp.bfloat16)
-
-    @pl.when(holds)
-    def _():
-        spare_hidden[...] = gated_unit(
-            jnp.dot(spare_in[...], spare_gate[0], preferred_element_type=jnp.float32)
-        ).astype(jnp.bfloat16)
-        for n in range(0, width, tile):
-            result = jnp.dot(
-                spare_hidden[...], spare_down[0, :, n : n + tile], preferred_element_type=jnp.float32
-            )
-            for s in range(len(blocks)):
-                rows_out[s, capacity:, n : n + tile] = (
-                    result[s * capacity : (s + 1) * capacity] * spare_weights[s]
-                ).astype(jnp.bfloat16)
-
-    @pl.when(jnp.logical_not(holds))
-    def _():
-        rows_out[:, capacity:, :] = jnp.zeros((len(blocks), capacity, width), jnp.bfloat16)
-
-    for s, target in enumerate((keep0, keep1, send.at[0], send.at[1])):
-        for n in range(0, width, tile):
-            target[:, n : n + tile] = lax.dot_general(
+            dense[s, :, n : n + tile] = lax.dot_general(
                 picks[s],
                 rows_out[s, :, n : n + tile],
                 (((0,), (0,)), ((), ())),
                 preferred_element_type=jnp.float32,
             ).astype(jnp.bfloat16)
+    stores = [
+        pltpu.make_async_copy(dense.at[s], target, stored.at[s])
+        for s, target in enumerate((keep0, keep1, send.at[0], send.at[1]))
+    ]
+    for copy in stores:
+        copy.start()
+    for copy in stores:
+        copy.wait()
 
 
 def run_group(failed, holders, blocks, weights, earlier, tok, top, capacity):
     width, inner, spare = weights[0].shape[1], weights[0].shape[2], weights[2].shape[2]
-    rows = len(blocks) * capacity
-    vmem = pl.BlockSpec(memory_space=pltpu.VMEM)
+    count = len(blocks)
+    rows = count * capacity
+    hbm = pl.BlockSpec(memory_space=pl.ANY)
     smem = pl.BlockSpec(memory_space=pltpu.SMEM)
-    block = jax.ShapeDtypeStruct((tok, width), jnp.bfloat16)
+    block = pltpu.HBM((tok, width), jnp.bfloat16)
     return pl.pallas_call(
-        functools.partial(group_kernel, tok=tok, top=top, capacity=capacity),
-        out_shape=(block, block, jax.ShapeDtypeStruct((2, tok, width), jnp.bfloat16)),
-        in_specs=[smem, smem] + [vmem] * 8 + [pl.BlockSpec(memory_space=pl.ANY)] * len(earlier),
-        out_specs=(vmem, vmem, vmem),
+        functools.partial(
+            group_kernel, others=len(earlier), tok=tok, top=top, capacity=capacity
+        ),
+        out_shape=(block, block, pltpu.HBM((2, tok, width), jnp.bfloat16)),
+        in_specs=[smem, smem] + [hbm] * (count + 4 + len(earlier)),
+        out_specs=(hbm, hbm, hbm),
         scratch_shapes=[
+            pltpu.VMEM((count, *blocks[0].shape), jnp.bfloat16),
+            pltpu.VMEM((width, inner), jnp.bfloat16),
+            pltpu.VMEM((inner, width), jnp.bfloat16),
+            pltpu.VMEM((width, spare), jnp.bfloat16),
+            pltpu.VMEM((spare, width), jnp.bfloat16),
             pltpu.VMEM((rows, width), jnp.bfloat16),
             pltpu.VMEM((rows, width), jnp.bfloat16),
             pltpu.VMEM((rows, inner), jnp.bfloat16),
             pltpu.VMEM((rows, spare), jnp.bfloat16),
-            pltpu.VMEM((len(blocks), 2 * capacity, width), jnp.bfloat16),
+            pltpu.VMEM((count, 2 * capacity, width), jnp.bfloat16),
+            pltpu.VMEM((count, tok, width), jnp.bfloat16),
+            pltpu.SemaphoreType.DMA((count + inner // 512 + width // 512 + 2,)),
+            pltpu.SemaphoreType.DMA((count,)),
         ],
-        compiler_params=pltpu.CompilerParams(vmem_limit_bytes=30 * 1024 * 1024),
+        compiler_params=pltpu.CompilerParams(vmem_limit_bytes=VMEM_GRANT),
         cost_estimate=pl.CostEstimate(
             flops=rows * 4 * width * (inner + spare),
-            bytes_accessed=4 * width * (inner + spare) + 4 * len(blocks) * tok * width,
+            bytes_accessed=4 * width * (inner + spare) + 4 * count * tok * width,
             transcendentals=rows * inner,
         ),
         name="group",
-    )(failed, holders, *blocks, *weights, *earlier)
+    )(failed, holders, *map(in_hbm, (*blocks, *weights, *earlier)))
+
+
+def in_hbm(array):
+    return pltpu.with_memory_space_constraint(array, pltpu.HBM)
 
 
 def nothing(*refs):
     pass
 
 
-def come_after(value, *others, flops=0):
+def come_after(value, *others):
     return pl.pallas_call(
         nothing,
-        out_shape=jax.ShapeDtypeStruct(value.shape, value.dtype),
+        out_shape=pltpu.HBM(value.shape, value.dtype),
         in_specs=[pl.BlockSpec(memory_space=pl.ANY)] * (1 + len(others)),
         out_specs=pl.BlockSpec(memory_space=pl.ANY),
         input_output_aliases={0: 0},
-        cost_estimate=pl.CostEstimate(flops=flops, bytes_accessed=0, transcendentals=0),
+        compiler_params=pltpu.CompilerParams(vmem_limit_bytes=VMEM_GRANT),
+        cost_estimate=pl.CostEstimate(flops=0, bytes_accessed=0, transcendentals=0),
         name="after",
-    )(value, *others)
+    )(*map(in_hbm, (value, *others)))
 
 
 def folded_ring(length):
@@ -319,7 +350,7 @@
     meta = jnp.concatenate([expert_ids.T, gate_levels.T >> 5, gate_levels.T & 31], axis=0)
     meta = meta.astype(jnp.bfloat16).reshape(1, 3 * top * tok)
     meta = jnp.pad(meta, ((0, 7), (0, width - 3 * top * tok)))
-    held = [come_after(jnp.concatenate([tokens, meta], axis=0), flops=8 * 10**9)]
+    held = [jnp.concatenate([tokens, meta], axis=0)]
     across, results = [], []
     for k in range(steps):
         if k > 0:

time: 131 us -> 119 us (0.908); the launches traced: 130 us -> 120 us
  local copies, waits for them, and re-layouts: 33.1 us -> 3.92 us
  Pallas kernels: 26.6 us -> 36.1 us
  starting transfers between devices: 18.9 us -> 25.1 us
  waiting for transfers between devices: 37.9 us -> 40.1 us
    unnamed x76 -> x14, local copies, waits for them, and re-layouts: 33.1 us -> 3.92 us
    pallas_call x10 -> x9, Pallas kernels: 26.6 us -> 36.1 us  [the longest x4 36.1 us: run_group(): pl.pallas_call(functools.partial(group_kernel, others=len(earlier), tok=t...]
    ppermute x26, starting transfers between devices: 18.9 us -> 25.1 us  [by_permutes(): move = lambda a, pairs: lax.ppermute(a, 'expert', pairs)]
    ppermute x26, waiting for transfers between devices: 37.9 us -> 40.1 us  [by_permutes(): move = lambda a, pairs: lax.ppermute(a, 'expert', pairs)]
  transfers between devices with their start and end apart: 26 -> 26, of which waited for: 9 -> 9; matrix products, arithmetic and copies ran while one was open for 7% -> 10% of each run, Pallas kernels for 20% -> 30%
where the time goes in v5:
time: 119 us; the launch traced here: 120 us
  waiting for transfers between devices  40.1 us (34%)
  Pallas kernels  36.1 us (30%)
  starting transfers between devices  25.1 us (21%)
  other arithmetic  13.7 us (12%)
  local copies, waits for them, and re-layouts  3.92 us (3%)
    ppermute x26, waiting for transfers between devices, by_permutes(): move = lambda a, pairs: lax.ppermute(a, 'expert', pairs)  40.1 us
    pallas_call x4, Pallas kernels, run_group(): pl.pallas_call(functools.partial(group_kernel, others=len(earlier), tok=t...  36.1 us
    ppermute x26, starting transfers between devices, by_permutes(): move = lambda a, pairs: lax.ppermute(a, 'expert', pairs)  25.1 us
    convert_element_type x4, other arithmetic, by_permutes(): far = (f32(keep1) + f32(got[1])).astype(jnp.bfloat16)  6.04 us
    convert_element_type x4, other arithmetic, by_permutes(): passing = total.astype(jnp.bfloat16)  5.94 us
    unnamed x14, local copies, waits for them, and re-layouts  3.92 us
  transfers between devices with their start and end apart: 26, of which 9 were waited for; matrix products, arithmetic and copies ran while one was open for 10% of the time, Pallas kernels for 30%

profile of v5, /device:TPU:0, one launch (start us, length us, event | category | flops | bytes accessed | tf_op | source)
XLA Modules:
  0.0 119.8 jit_solution(3292683182042669626)
XLA Ops:
  0.0 0.7 fusion.17
  0.7 1.0 fusion.16.refs_0_
  1.8 3.1 %collective-permute-start.3 = (bf16[136,1536]{1,0:T(8,128)(2,1)S(1)}, bf16[136,1536]{1,0:T(8,128)(2,1)}, u32[]{:S(2)}, u32[]{:S(2)}) collective-permute-start(bf16[136,1536]{1,0:T(8,128)(2,1)S(1)} %fusion.16.refs_0_), channel_id=1, source_target_pairs={{0,4},{1,5},{2,6},{3,7},{4,12},{5,13},{6,14},{7,15},{8,0},{9,1},{1... | collective-permute-start | bytes 1253384 | tf_op jit(solution)/shard_map/ppermute | solution.py:348
  4.8 1.5 %collective-permute-start = (bf16[136,1536]{1,0:T(8,128)(2,1)S(1)}, bf16[136,1536]{1,0:T(8,128)(2,1)S(1)}, u32[]{:S(2)}, u32[]{:S(2)}) collective-permute-start(bf16[136,1536]{1,0:T(8,128)(2,1)S(1)} %fusion.16.refs_0_), channel_id=1, source_target_pairs={{0,2},{1,3},{2,0},{3,1},{4,6},{5,7},{6,4},{7,5},{8,10},{9,11},{10,... | collective-permute-start | bytes 1253384 | tf_op jit(solution)/shard_map/ppermute | solution.py:348
  6.4 9.2 %collective-permute-done.3.refs_0_ = bf16[136,1536]{1,0:T(8,128)(2,1)} collective-permute-done((bf16[136,1536]{1,0:T(8,128)(2,1)S(1)}, bf16[136,1536]{1,0:T(8,128)(2,1)}, u32[]{:S(2)}, u32[]{:S(2)}) %collective-permute-start.3) | collective-permute-done | bytes 417824 | tf_op jit(solution)/shard_map/ppermute | solution.py:348
  15.6 1.6 %collective-permute-start.4 = (bf16[136,1536]{1,0:T(8,128)(2,1)}, bf16[136,1536]{1,0:T(8,128)(2,1)}, u32[]{:S(2)}, u32[]{:S(2)}) collective-permute-start(bf16[136,1536]{1,0:T(8,128)(2,1)} %collective-permute-done.3.refs_0_), channel_id=1, source_target_pairs={{0,2},{1,3},{2,0},{3,1},{4,6},{5,7},{6,4},{7,5},{8,10},{9,11},{10,... | collective-permute-start | bytes 1253384 | tf_op jit(solution)/shard_map/ppermute | solution.py:348
  17.2 0.0 collective-permute-start.1
  17.2 0.0 collective-permute-done.refs_1_
  17.2 0.5 collective-permute-start.2
  17.7 1.2 %collective-permute-start.5 = (bf16[136,1536]{1,0:T(8,128)(2,1)}, bf16[136,1536]{1,0:T(8,128)(2,1)}, u32[]{:S(2)}, u32[]{:S(2)}) collective-permute-start(bf16[136,1536]{1,0:T(8,128)(2,1)} %collective-permute-done.3.refs_0_), channel_id=1, source_target_pairs={{0,4},{1,5},{2,6},{3,7},{4,12},{5,13},{6,14},{7,15},{8,0},{9,1},{1... | collective-permute-start | bytes 1253384 | tf_op jit(solution)/shard_map/ppermute | solution.py:348
  19.6 1.4 %copy.15.holders = s32[16,4]{1,0:T(8,128)} copy(s32[16,4]{0,1:T(4,128)} %param.13) | data formatting | bytes 512 | tf_op args[4]
  20.9 0.2 collective-permute-start.9
  21.1 5.6 %collective-permute-done.4.refs_1_ = bf16[136,1536]{1,0:T(8,128)(2,1)} collective-permute-done((bf16[136,1536]{1,0:T(8,128)(2,1)}, bf16[136,1536]{1,0:T(8,128)(2,1)}, u32[]{:S(2)}, u32[]{:S(2)}) %collective-permute-start.4) | collective-permute-done | bytes 417824 | tf_op jit(solution)/shard_map/ppermute | solution.py:348
  26.8 0.0 collective-permute-start.10
  26.8 0.8 copy-done.5
  27.5 0.0 collective-permute-done.2.refs_3_
  27.5 8.9 %group.4 = (bf16[128,1536]{1,0:T(8,128)(2,1)}, bf16[128,1536]{1,0:T(8,128)(2,1)}, bf16[2,128,1536]{2,1,0:T(8,128)(2,1)}) custom-call(s32[1]{0:T(128)S(6)} %copy.27.failed, s32[16,4]{1,0:T(8,128)} %copy.15.holders, bf16[136,1536]{1,0:T(8,128)(2,1)} %copy-done.1, bf16[136,1536]{1,0:T(8,128)(2,1)} %copy-done.4, bf16[136,1536]{1,0:T(8,128)(2,1)} %copy-done.5, ...), custom_call_target="tpu_custom_call" | custom-call | flops 3019898880 | bytes 14942208 | tf_op jit(solution)/shard_map/group/pallas_call | solution.py:282
  36.5 2.0 %collective-permute-start.8 = (bf16[136,1536]{1,0:T(8,128)(2,1)}, bf16[136,1536]{1,0:T(8,128)(2,1)}, u32[]{:S(2)}, u32[]{:S(2)}) collective-permute-start(bf16[136,1536]{1,0:T(8,128)(2,1)} %after.5.refs_2_.refs_0_), channel_id=1, source_target_pairs={{0,4},{1,5},{2,6},{3,7},{4,12},{5,13},{6,14},{7,15},{8,0},{9,1},{1... | collective-permute-start | bytes 1253384 | tf_op jit(solution)/shard_map/ppermute | solution.py:348
  38.4 0.5 collective-permute-start.14
  38.9 0.0 collective-permute-done.9.refs_2_
  38.9 9.1 %group.5 = (bf16[128,1536]{1,0:T(8,128)(2,1)}, bf16[128,1536]{1,0:T(8,128)(2,1)}, bf16[2,128,1536]{2,1,0:T(8,128)(2,1)}) custom-call(s32[1]{0:T(128)S(6)} %copy.27.failed, s32[16,4]{1,0:T(8,128)} %copy.15.holders, bf16[136,1536]{1,0:T(8,128)(2,1)} %collective-permute-done.3.refs_0_, bf16[136,1536]{1,0:T(8,128)(2,1)} %collective-permute-done.4.refs_1_, ...), custom_call_target="tpu_custom_call" | custom-call | flops 3019898880 | bytes 14942208 | tf_op jit(solution)/shard_map/group/pallas_call | solution.py:282
  48.0 1.7 %collective-permute-done.8.refs_0_ = bf16[136,1536]{1,0:T(8,128)(2,1)} collective-permute-done((bf16[136,1536]{1,0:T(8,128)(2,1)}, bf16[136,1536]{1,0:T(8,128)(2,1)}, u32[]{:S(2)}, u32[]{:S(2)}) %collective-permute-start.8) | collective-permute-done | bytes 417824 | tf_op jit(solution)/shard_map/ppermute | solution.py:348
  49.8 0.0 collective-permute-start.21
  49.8 0.5 collective-permute-start.15
  50.3 1.2 %collective-permute-start.11 = (bf16[136,1536]{1,0:T(8,128)(2,1)}, bf16[136,1536]{1,0:T(8,128)(2,1)}, u32[]{:S(2)}, u32[]{:S(2)}) collective-permute-start(bf16[136,1536]{1,0:T(8,128)(2,1)} %after.7.refs_0_.refs_2_), channel_id=1, source_target_pairs={{0,2},{1,3},{2,0},{3,1},{4,6},{5,7},{6,4},{7,5},{8,10},{9,11},{10,... | collective-permute-start | bytes 1253384 | tf_op jit(solution)/shard_map/ppermute | solution.py:348
  51.5 0.0 collective-permute-start.16
  51.5 1.2 collective-permute-done.21
  52.7 0.9 copy-done.2
  53.6 1.9 %fusion.1 = bf16[128,1536]{1,0:T(8,128)(2,1)} fusion(bf16[128,1536]{1,0:T(8,128)(2,1)} %get-tuple-element.28, bf16[2,128,1536]{2,1,0:T(8,128)(2,1)S(1)} %collective-permute-done.21), kind=kLoop, calls=%fused_computation.3 | loop fusion | flops 786432 | bytes 1179648 | tf_op jit(solution)/shard_map/convert_element_type | solution.py:372
  55.5 1.2 %collective-permute-start.22 = (bf16[128,1536]{1,0:T(8,128)(2,1)}, bf16[128,1536]{1,0:T(8,128)(2,1)}, u32[]{:S(2)}, u32[]{:S(2)}) collective-permute-start(bf16[128,1536]{1,0:T(8,128)(2,1)} %fusion.1), channel_id=1, source_target_pairs={{0,2},{1,3},{2,0},{3,1},{4,6},{5,7},{6,4},{7,5},{8,10},{9,11},{10,... | collective-permute-start | bytes 1179656 | tf_op jit(solution)/shard_map/ppermute | solution.py:348
  56.7 0.0 collective-permute-done.16.refs_3_
  56.8 8.9 %group.6 = (bf16[128,1536]{1,0:T(8,128)(2,1)}, bf16[128,1536]{1,0:T(8,128)(2,1)}, bf16[2,128,1536]{2,1,0:T(8,128)(2,1)}) custom-call(s32[1]{0:T(128)S(6)} %copy.27.failed, s32[16,4]{1,0:T(8,128)} %copy.15.holders, bf16[136,1536]{1,0:T(8,128)(2,1)} %after.5.refs_2_.refs_0_, bf16[136,1536]{1,0:T(8,128)(2,1)} %collective-permute-done.14.refs_1_, ...), custom_call_target="tpu_custom_call" | custom-call | flops 3019898880 | bytes 14942208 | tf_op jit(solution)/shard_map/group/pallas_call | solution.py:282
  65.7 0.0 collective-permute-done.11.refs_1_
  65.7 0.1 collective-permute-start.19
  65.8 0.5 collective-permute-start.12
  66.3 0.1 collective-permute-start.13
  66.3 4.3 %collective-permute-done.22 = bf16[128,1536]{1,0:T(8,128)(2,1)} collective-permute-done((bf16[128,1536]{1,0:T(8,128)(2,1)}, bf16[128,1536]{1,0:T(8,128)(2,1)}, u32[]{:S(2)}, u32[]{:S(2)}) %collective-permute-start.22) | collective-permute-done | bytes 393248 | tf_op jit(solution)/shard_map/ppermute | solution.py:348
  70.6 2.1 %fusion.3 = bf16[128,1536]{1,0:T(8,128)(2,1)} fusion(bf16[128,1536]{1,0:T(8,128)(2,1)} %collective-permute-done.22, bf16[128,1536]{1,0:T(8,128)(2,1)} %get-tuple-element.20.refs_1_.refs_8_, bf16[2,128,1536]{2,1,0:T(8,128)(2,1)} %copy-done.2), kind=kLoop, calls=%fused_computation.6 | loop fusion | flops 1179648 | bytes 1572864 | tf_op jit(solution)/shard_map/convert_element_type | solution.py:376
  72.8 3.5 %collective-permute-start.23 = (bf16[128,1536]{1,0:T(8,128)(2,1)}, bf16[128,1536]{1,0:T(8,128)(2,1)}, u32[]{:S(2)}, u32[]{:S(2)}) collective-permute-start(bf16[128,1536]{1,0:T(8,128)(2,1)} %fusion.3), channel_id=1, source_target_pairs={{0,4},{1,5},{2,6},{3,7},{4,12},{5,13},{6,14},{7,15},{8,0},{9,1},{1... | collective-permute-start | bytes 1179656 | tf_op jit(solution)/shard_map/ppermute | solution.py:348
  76.3 0.0 collective-permute-done.19
  76.3 0.9 copy-done.3
  77.2 1.8 %fusion.4 = bf16[128,1536]{1,0:T(8,128)(2,1)} fusion(bf16[128,1536]{1,0:T(8,128)(2,1)} %get-tuple-element.26, bf16[2,128,1536]{2,1,0:T(8,128)(2,1)S(1)} %collective-permute-done.19), kind=kLoop, calls=%fused_computation.8 | loop fusion | flops 786432 | bytes 1179648 | tf_op jit(solution)/shard_map/convert_element_type | solution.py:372
  79.1 1.7 %collective-permute-start.20 = (bf16[128,1536]{1,0:T(8,128)(2,1)}, bf16[128,1536]{1,0:T(8,128)(2,1)}, u32[]{:S(2)}, u32[]{:S(2)}) collective-permute-start(bf16[128,1536]{1,0:T(8,128)(2,1)} %fusion.4), channel_id=1, source_target_pairs={{0,2},{1,3},{2,0},{3,1},{4,6},{5,7},{6,4},{7,5},{8,10},{9,11},{10,... | collective-permute-start | bytes 1179656 | tf_op jit(solution)/shard_map/ppermute | solution.py:348
  80.8 0.0 collective-permute-done.12.refs_2_
  80.8 0.0 collective-permute-done.13.refs_3_
  80.8 9.1 %group.7 = (bf16[128,1536]{1,0:T(8,128)(2,1)}, bf16[128,1536]{1,0:T(8,128)(2,1)}, bf16[2,128,1536]{2,1,0:T(8,128)(2,1)}) custom-call(s32[1]{0:T(128)S(6)} %copy.27.failed, s32[16,4]{1,0:T(8,128)} %copy.15.holders, bf16[136,1536]{1,0:T(8,128)(2,1)} %after.7.refs_0_.refs_2_, bf16[136,1536]{1,0:T(8,128)(2,1)} %collective-permute-done.11.refs_1_, ...), custom_call_target="tpu_custom_call" | custom-call | flops 3019898880 | bytes 14942208 | tf_op jit(solution)/shard_map/group/pallas_call | solution.py:282
  89.9 0.1 collective-permute-start.17
  90.0 0.0 copy-start
  90.0 0.5 collective-permute-start.6
  90.5 1.5 %fusion.7 = bf16[128,1536]{1,0:T(8,128)(2,1)S(1)} fusion(bf16[128,1536]{1,0:T(8,128)(2,1)} %collective-permute-done.23, bf16[128,1536]{1,0:T(8,128)(2,1)} %collective-permute-done.20, bf16[128,1536]{1,0:T(8,128)(2,1)} %get-tuple-element.21.refs_8_, bf16[2,128,1536]{2,1,0:T(8,128)(2,1)} %copy-done.3), kind=kLoop, calls=%fused_computation.12 | loop fusion | flops 1572864 | bytes 1966080 | tf_op jit(solution)/shard_map/convert_element_type | solution.py:376
  92.1 2.4 %collective-permute-start.24 = (bf16[128,1536]{1,0:T(8,128)(2,1)S(1)}, bf16[128,1536]{1,0:T(8,128)(2,1)S(1)}, u32[]{:S(2)}, u32[]{:S(2)}) collective-permute-start(bf16[128,1536]{1,0:T(8,128)(2,1)S(1)} %fusion.7), channel_id=1, source_target_pairs={{0,4},{1,5},{2,6},{3,7},{4,12},{5,13},{6,14},{7,15},{8,0},{9,1},{1... | collective-permute-start | bytes 1179656 | tf_op jit(solution)/shard_map/ppermute | solution.py:348
  94.4 0.0 collective-permute-done.17
  94.5 1.2 %fusion.8 = bf16[128,1536]{1,0:T(8,128)(2,1)S(1)} fusion(bf16[128,1536]{1,0:T(8,128)(2,1)} %get-tuple-element.24, bf16[2,128,1536]{2,1,0:T(8,128)(2,1)} %collective-permute-done.17), kind=kLoop, calls=%fused_computation.14 | loop fusion | flops 786432 | bytes 1179648 | tf_op jit(solution)/shard_map/convert_element_type | solution.py:372
  95.7 0.1 collective-permute-start.18
  95.7 0.0 collective-permute-done.6
  95.8 1.1 fusion.12
  96.8 2.1 %collective-permute-start.7 = (bf16[128,1536]{1,0:T(8,128)(2,1)S(1)}, bf16[128,1536]{1,0:T(8,128)(2,1)S(1)}, u32[]{:S(2)}, u32[]{:S(2)}) collective-permute-start(bf16[128,1536]{1,0:T(8,128)(2,1)S(1)} %fusion.12), channel_id=1, source_target_pairs={{0,2},{1,3},{2,0},{3,1},{4,6},{5,7},{6,4},{7,5},{8,10},{9,11},{10,... | collective-permute-start | bytes 1179656 | tf_op jit(solution)/shard_map/ppermute | solution.py:348
  98.9 5.3 %collective-permute-done.24 = bf16[128,1536]{1,0:T(8,128)(2,1)S(1)} collective-permute-done((bf16[128,1536]{1,0:T(8,128)(2,1)S(1)}, bf16[128,1536]{1,0:T(8,128)(2,1)S(1)}, u32[]{:S(2)}, u32[]{:S(2)}) %collective-permute-start.24) | collective-permute-done | bytes 393248 | tf_op jit(solution)/shard_map/ppermute | solution.py:348
  104.2 3.6 %collective-permute-done.18 = bf16[128,1536]{1,0:T(8,128)(2,1)S(1)} collective-permute-done((bf16[128,1536]{1,0:T(8,128)(2,1)S(1)}, bf16[128,1536]{1,0:T(8,128)(2,1)S(1)}, u32[]{:S(2)}, u32[]{:S(2)}) %collective-permute-start.18) | collective-permute-done | bytes 393248 | tf_op jit(solution)/shard_map/ppermute | solution.py:348
  107.7 1.3 %fusion.11 = bf16[128,1536]{1,0:T(8,128)(2,1)S(1)} fusion(bf16[128,1536]{1,0:T(8,128)(2,1)S(1)} %collective-permute-done.24, bf16[128,1536]{1,0:T(8,128)(2,1)S(1)} %collective-permute-done.18, bf16[128,1536]{1,0:T(8,128)(2,1)} %get-tuple-element.22, bf16[2,128,1536]{2,1,0:T(8,128)(2,1)} %collective-permute-done.17), kind=kLoop, calls=%fused_computation.18 | loop fusion | flops 1572864 | bytes 1966080 | tf_op jit(solution)/shard_map/convert_element_type | solution.py:376
  109.0 0.6 collective-permute-start.25
  109.7 5.4 %collective-permute-done.7 = bf16[128,1536]{1,0:T(8,128)(2,1)S(1)} collective-permute-done((bf16[128,1536]{1,0:T(8,128)(2,1)S(1)}, bf16[128,1536]{1,0:T(8,128)(2,1)S(1)}, u32[]{:S(2)}, u32[]{:S(2)}) %collective-permute-start.7) | collective-permute-done | bytes 393248 | tf_op jit(solution)/shard_map/ppermute | solution.py:348
  115.0 3.8 %collective-permute-done.25 = bf16[128,1536]{1,0:T(8,128)(2,1)S(1)} collective-permute-done((bf16[128,1536]{1,0:T(8,128)(2,1)S(1)}, bf16[128,1536]{1,0:T(8,128)(2,1)S(1)}, u32[]{:S(2)}, u32[]{:S(2)}) %collective-permute-start.25) | collective-permute-done | bytes 393248 | tf_op jit(solution)/shard_map/ppermute | solution.py:348
  118.9 0.9 fusion.15
  (22 shorter events, 0.1 us)
Async XLA Ops:
  1.8 15.4 %copy-start.1 = (bf16[136,1536]{1,0:T(8,128)(2,1)}, bf16[136,1536]{1,0:T(8,128)(2,1)S(1)}, u32[]{:S(2)}) copy-start(bf16[136,1536]{1,0:T(8,128)(2,1)S(1)} %fusion.16.refs_0_) | copy-start | bytes 1253380
  1.8 13.8 %collective-permute-start.3 = (bf16[136,1536]{1,0:T(8,128)(2,1)S(1)}, bf16[136,1536]{1,0:T(8,128)(2,1)}, u32[]{:S(2)}, u32[]{:S(2)}) collective-permute-start(bf16[136,1536]{1,0:T(8,128)(2,1)S(1)} %fusion.16.refs_0_), channel_id=1, source_target_pairs={{0,4},{1,5},{2,6},{3,7},{4,12},{5,13},{6,14},{7,15},{8,0},{9,1},{1... | collective-permute-start | bytes 1253384 | tf_op jit(solution)/shard_map/ppermute | solution.py:348
  4.8 12.3 %collective-permute-start = (bf16[136,1536]{1,0:T(8,128)(2,1)S(1)}, bf16[136,1536]{1,0:T(8,128)(2,1)S(1)}, u32[]{:S(2)}, u32[]{:S(2)}) collective-permute-start(bf16[136,1536]{1,0:T(8,128)(2,1)S(1)} %fusion.16.refs_0_), channel_id=1, source_target_pairs={{0,2},{1,3},{2,0},{3,1},{4,6},{5,7},{6,4},{7,5},{8,10},{9,11},{10,... | collective-permute-start | bytes 1253384 | tf_op jit(solution)/shard_map/ppermute | solution.py:348
  15.6 11.1 %collective-permute-start.4 = (bf16[136,1536]{1,0:T(8,128)(2,1)}, bf16[136,1536]{1,0:T(8,128)(2,1)}, u32[]{:S(2)}, u32[]{:S(2)}) collective-permute-start(bf16[136,1536]{1,0:T(8,128)(2,1)} %collective-permute-done.3.refs_0_), channel_id=1, source_target_pairs={{0,2},{1,3},{2,0},{3,1},{4,6},{5,7},{6,4},{7,5},{8,10},{9,11},{10,... | collective-permute-start | bytes 1253384 | tf_op jit(solution)/shard_map/ppermute | solution.py:348
  17.2 9.6 %collective-permute-start.1 = (bf16[136,1536]{1,0:T(8,128)(2,1)S(1)}, bf16[136,1536]{1,0:T(8,128)(2,1)S(1)}, u32[]{:S(2)}, u32[]{:S(2)}) collective-permute-start(bf16[136,1536]{1,0:T(8,128)(2,1)S(1)} %fusion.16.refs_0_), channel_id=1, source_target_pairs={{0,1},{1,0},{2,3},{3,2},{4,5},{5,4},{6,7},{7,6},{8,9},{9,8},{10,11... | collective-permute-start | bytes 1253384 | tf_op jit(solution)/shard_map/ppermute | solution.py:348
  17.2 9.6 %copy-start.4 = (bf16[136,1536]{1,0:T(8,128)(2,1)}, bf16[136,1536]{1,0:T(8,128)(2,1)S(1)}, u32[]{:S(2)}) copy-start(bf16[136,1536]{1,0:T(8,128)(2,1)S(1)} %collective-permute-done.refs_1_) | copy-start | bytes 1253380
  17.2 10.3 %collective-permute-start.2 = (bf16[136,1536]{1,0:T(8,128)(2,1)S(1)}, bf16[136,1536]{1,0:T(8,128)(2,1)}, u32[]{:S(2)}, u32[]{:S(2)}) collective-permute-start(bf16[136,1536]{1,0:T(8,128)(2,1)S(1)} %collective-permute-done.refs_1_), channel_id=1, source_target_pairs={{0,1},{1,0},{2,3},{3,2},{4,5},{5,4},{6,7},{7,6},{8,9},{9,8},{10,11... | collective-permute-start | bytes 1253384 | tf_op jit(solution)/shard_map/ppermute | solution.py:348
  17.7 18.7 %collective-permute-start.5 = (bf16[136,1536]{1,0:T(8,128)(2,1)}, bf16[136,1536]{1,0:T(8,128)(2,1)}, u32[]{:S(2)}, u32[]{:S(2)}) collective-permute-start(bf16[136,1536]{1,0:T(8,128)(2,1)} %collective-permute-done.3.refs_0_), channel_id=1, source_target_pairs={{0,4},{1,5},{2,6},{3,7},{4,12},{5,13},{6,14},{7,15},{8,0},{9,1},{1... | collective-permute-start | bytes 1253384 | tf_op jit(solution)/shard_map/ppermute | solution.py:348
  20.9 18.0 %collective-permute-start.9 = (bf16[136,1536]{1,0:T(8,128)(2,1)}, bf16[136,1536]{1,0:T(8,128)(2,1)}, u32[]{:S(2)}, u32[]{:S(2)}) collective-permute-start(bf16[136,1536]{1,0:T(8,128)(2,1)} %collective-permute-done.3.refs_0_), channel_id=1, source_target_pairs={{0,1},{1,0},{2,3},{3,2},{4,5},{5,4},{6,7},{7,6},{8,9},{9,8},{10,11... | collective-permute-start | bytes 1253384 | tf_op jit(solution)/shard_map/ppermute | solution.py:348
  26.8 12.2 %collective-permute-start.10 = (bf16[136,1536]{1,0:T(8,128)(2,1)}, bf16[136,1536]{1,0:T(8,128)(2,1)}, u32[]{:S(2)}, u32[]{:S(2)}) collective-permute-start(bf16[136,1536]{1,0:T(8,128)(2,1)} %collective-permute-done.4.refs_1_), channel_id=1, source_target_pairs={{0,1},{1,0},{2,3},{3,2},{4,5},{5,4},{6,7},{7,6},{8,9},{9,8},{10,11... | collective-permute-start | bytes 1253384 | tf_op jit(solution)/shard_map/ppermute | solution.py:348
  26.8 0.8 copy-start.5
  36.5 13.3 %collective-permute-start.8 = (bf16[136,1536]{1,0:T(8,128)(2,1)}, bf16[136,1536]{1,0:T(8,128)(2,1)}, u32[]{:S(2)}, u32[]{:S(2)}) collective-permute-start(bf16[136,1536]{1,0:T(8,128)(2,1)} %after.5.refs_2_.refs_0_), channel_id=1, source_target_pairs={{0,4},{1,5},{2,6},{3,7},{4,12},{5,13},{6,14},{7,15},{8,0},{9,1},{1... | collective-permute-start | bytes 1253384 | tf_op jit(solution)/shard_map/ppermute | solution.py:348
  38.4 11.3 %collective-permute-start.14 = (bf16[136,1536]{1,0:T(8,128)(2,1)}, bf16[136,1536]{1,0:T(8,128)(2,1)}, u32[]{:S(2)}, u32[]{:S(2)}) collective-permute-start(bf16[136,1536]{1,0:T(8,128)(2,1)} %after.5.refs_2_.refs_0_), channel_id=1, source_target_pairs={{0,2},{1,3},{2,0},{3,1},{4,6},{5,7},{6,4},{7,5},{8,10},{9,11},{10,... | collective-permute-start | bytes 1253384 | tf_op jit(solution)/shard_map/ppermute | solution.py:348
  49.8 2.9 %collective-permute-start.21 = (bf16[2,128,1536]{2,1,0:T(8,128)(2,1)}, bf16[2,128,1536]{2,1,0:T(8,128)(2,1)S(1)}, u32[]{:S(2)}, u32[]{:S(2)}) collective-permute-start(bf16[2,128,1536]{2,1,0:T(8,128)(2,1)} %after.9), channel_id=1, source_target_pairs={{0,1},{1,0},{2,3},{3,2},{4,5},{5,4},{6,7},{7,6},{8,9},{9,8},{10,11... | collective-permute-start | bytes 2359304 | tf_op jit(solution)/shard_map/ppermute | solution.py:348
  49.8 7.0 %collective-permute-start.15 = (bf16[136,1536]{1,0:T(8,128)(2,1)}, bf16[136,1536]{1,0:T(8,128)(2,1)}, u32[]{:S(2)}, u32[]{:S(2)}) collective-permute-start(bf16[136,1536]{1,0:T(8,128)(2,1)} %after.5.refs_2_.refs_0_), channel_id=1, source_target_pairs={{0,1},{1,0},{2,3},{3,2},{4,5},{5,4},{6,7},{7,6},{8,9},{9,8},{10,11... | collective-permute-start | bytes 1253384 | tf_op jit(solution)/shard_map/ppermute | solution.py:348
  50.3 15.4 %collective-permute-start.11 = (bf16[136,1536]{1,0:T(8,128)(2,1)}, bf16[136,1536]{1,0:T(8,128)(2,1)}, u32[]{:S(2)}, u32[]{:S(2)}) collective-permute-start(bf16[136,1536]{1,0:T(8,128)(2,1)} %after.7.refs_0_.refs_2_), channel_id=1, source_target_pairs={{0,2},{1,3},{2,0},{3,1},{4,6},{5,7},{6,4},{7,5},{8,10},{9,11},{10,... | collective-permute-start | bytes 1253384 | tf_op jit(solution)/shard_map/ppermute | solution.py:348
  51.5 5.2 %collective-permute-start.16 = (bf16[136,1536]{1,0:T(8,128)(2,1)}, bf16[136,1536]{1,0:T(8,128)(2,1)}, u32[]{:S(2)}, u32[]{:S(2)}) collective-permute-start(bf16[136,1536]{1,0:T(8,128)(2,1)} %collective-permute-done.14.refs_1_), channel_id=1, source_target_pairs={{0,1},{1,0},{2,3},{3,2},{4,5},{5,4},{6,7},{7,6},{8,9},{9,8},{10,11... | collective-permute-start | bytes 1253384 | tf_op jit(solution)/shard_map/ppermute | solution.py:348
  52.7 0.9 copy-start.2
  55.5 15.2 %collective-permute-start.22 = (bf16[128,1536]{1,0:T(8,128)(2,1)}, bf16[128,1536]{1,0:T(8,128)(2,1)}, u32[]{:S(2)}, u32[]{:S(2)}) collective-permute-start(bf16[128,1536]{1,0:T(8,128)(2,1)} %fusion.1), channel_id=1, source_target_pairs={{0,2},{1,3},{2,0},{3,1},{4,6},{5,7},{6,4},{7,5},{8,10},{9,11},{10,... | collective-permute-start | bytes 1179656 | tf_op jit(solution)/shard_map/ppermute | solution.py:348
  65.7 10.6 %collective-permute-start.19 = (bf16[2,128,1536]{2,1,0:T(8,128)(2,1)}, bf16[2,128,1536]{2,1,0:T(8,128)(2,1)S(1)}, u32[]{:S(2)}, u32[]{:S(2)}) collective-permute-start(bf16[2,128,1536]{2,1,0:T(8,128)(2,1)} %after.8), channel_id=1, source_target_pairs={{0,1},{1,0},{2,3},{3,2},{4,5},{5,4},{6,7},{7,6},{8,9},{9,8},{10,11... | collective-permute-start | bytes 2359304 | tf_op jit(solution)/shard_map/ppermute | solution.py:348
  65.8 15.0 %collective-permute-start.12 = (bf16[136,1536]{1,0:T(8,128)(2,1)}, bf16[136,1536]{1,0:T(8,128)(2,1)}, u32[]{:S(2)}, u32[]{:S(2)}) collective-permute-start(bf16[136,1536]{1,0:T(8,128)(2,1)} %after.7.refs_0_.refs_2_), channel_id=1, source_target_pairs={{0,1},{1,0},{2,3},{3,2},{4,5},{5,4},{6,7},{7,6},{8,9},{9,8},{10,11... | collective-permute-start | bytes 1253384 | tf_op jit(solution)/shard_map/ppermute | solution.py:348
  66.3 14.5 %collective-permute-start.13 = (bf16[136,1536]{1,0:T(8,128)(2,1)}, bf16[136,1536]{1,0:T(8,128)(2,1)}, u32[]{:S(2)}, u32[]{:S(2)}) collective-permute-start(bf16[136,1536]{1,0:T(8,128)(2,1)} %collective-permute-done.11.refs_1_), channel_id=1, source_target_pairs={{0,1},{1,0},{2,3},{3,2},{4,5},{5,4},{6,7},{7,6},{8,9},{9,8},{10,11... | collective-permute-start | bytes 1253384 | tf_op jit(solution)/shard_map/ppermute | solution.py:348
  72.8 17.7 %collective-permute-start.23 = (bf16[128,1536]{1,0:T(8,128)(2,1)}, bf16[128,1536]{1,0:T(8,128)(2,1)}, u32[]{:S(2)}, u32[]{:S(2)}) collective-permute-start(bf16[128,1536]{1,0:T(8,128)(2,1)} %fusion.3), channel_id=1, source_target_pairs={{0,4},{1,5},{2,6},{3,7},{4,12},{5,13},{6,14},{7,15},{8,0},{9,1},{1... | collective-permute-start | bytes 1179656 | tf_op jit(solution)/shard_map/ppermute | solution.py:348
  76.3 0.9 copy-start.3
  79.1 11.5 %collective-permute-start.20 = (bf16[128,1536]{1,0:T(8,128)(2,1)}, bf16[128,1536]{1,0:T(8,128)(2,1)}, u32[]{:S(2)}, u32[]{:S(2)}) collective-permute-start(bf16[128,1536]{1,0:T(8,128)(2,1)} %fusion.4), channel_id=1, source_target_pairs={{0,2},{1,3},{2,0},{3,1},{4,6},{5,7},{6,4},{7,5},{8,10},{9,11},{10,... | collective-permute-start | bytes 1179656 | tf_op jit(solution)/shard_map/ppermute | solution.py:348
  89.9 4.5 %collective-permute-start.17 = (bf16[2,128,1536]{2,1,0:T(8,128)(2,1)}, bf16[2,128,1536]{2,1,0:T(8,128)(2,1)}, u32[]{:S(2)}, u32[]{:S(2)}) collective-permute-start(bf16[2,128,1536]{2,1,0:T(8,128)(2,1)} %get-tuple-element.23), channel_id=1, source_target_pairs={{0,1},{1,0},{2,3},{3,2},{4,5},{5,4},{6,7},{7,6},{8,9},{9,8},{10,11... | collective-permute-start | bytes 2359304 | tf_op jit(solution)/shard_map/ppermute | solution.py:348
  90.0 28.8 %copy-start = (bf16[128,1536]{1,0:T(8,128)(2,1)S(1)}, bf16[128,1536]{1,0:T(8,128)(2,1)}, u32[]{:S(2)}) copy-start(bf16[128,1536]{1,0:T(8,128)(2,1)} %get-tuple-element.17.refs_1_.refs_8_) | copy-start | bytes 1179652
  90.0 5.7 %collective-permute-start.6 = (bf16[2,128,1536]{2,1,0:T(8,128)(2,1)}, bf16[2,128,1536]{2,1,0:T(8,128)(2,1)S(1)}, u32[]{:S(2)}, u32[]{:S(2)}) collective-permute-start(bf16[2,128,1536]{2,1,0:T(8,128)(2,1)} %after.6), channel_id=1, source_target_pairs={{0,1},{1,0},{2,3},{3,2},{4,5},{5,4},{6,7},{7,6},{8,9},{9,8},{10,11... | collective-permute-start | bytes 2359304 | tf_op jit(solution)/shard_map/ppermute | solution.py:348
  92.1 12.1 %collective-permute-start.24 = (bf16[128,1536]{1,0:T(8,128)(2,1)S(1)}, bf16[128,1536]{1,0:T(8,128)(2,1)S(1)}, u32[]{:S(2)}, u32[]{:S(2)}) collective-permute-start(bf16[128,1536]{1,0:T(8,128)(2,1)S(1)} %fusion.7), channel_id=1, source_target_pairs={{0,4},{1,5},{2,6},{3,7},{4,12},{5,13},{6,14},{7,15},{8,0},{9,1},{1... | collective-permute-start | bytes 1179656 | tf_op jit(solution)/shard_map/ppermute | solution.py:348
  95.7 12.1 %collective-permute-start.18 = (bf16[128,1536]{1,0:T(8,128)(2,1)S(1)}, bf16[128,1536]{1,0:T(8,128)(2,1)S(1)}, u32[]{:S(2)}, u32[]{:S(2)}) collective-permute-start(bf16[128,1536]{1,0:T(8,128)(2,1)S(1)} %fusion.8), channel_id=1, source_target_pairs={{0,2},{1,3},{2,0},{3,1},{4,6},{5,7},{6,4},{7,5},{8,10},{9,11},{10,... | collective-permute-start | bytes 1179656 | tf_op jit(solution)/shard_map/ppermute | solution.py:348
  96.8 18.2 %collective-permute-start.7 = (bf16[128,1536]{1,0:T(8,128)(2,1)S(1)}, bf16[128,1536]{1,0:T(8,128)(2,1)S(1)}, u32[]{:S(2)}, u32[]{:S(2)}) collective-permute-start(bf16[128,1536]{1,0:T(8,128)(2,1)S(1)} %fusion.12), channel_id=1, source_target_pairs={{0,2},{1,3},{2,0},{3,1},{4,6},{5,7},{6,4},{7,5},{8,10},{9,11},{10,... | collective-permute-start | bytes 1179656 | tf_op jit(solution)/shard_map/ppermute | solution.py:348
  109.0 9.8 %collective-permute-start.25 = (bf16[128,1536]{1,0:T(8,128)(2,1)S(1)}, bf16[128,1536]{1,0:T(8,128)(2,1)S(1)}, u32[]{:S(2)}, u32[]{:S(2)}) collective-permute-start(bf16[128,1536]{1,0:T(8,128)(2,1)S(1)} %fusion.11), channel_id=1, source_target_pairs={{0,4},{1,5},{2,6},{3,7},{4,12},{5,13},{6,14},{7,15},{8,0},{9,1},{1... | collective-permute-start | bytes 1179656 | tf_op jit(solution)/shard_map/ppermute | solution.py:348

commit v6 on v5

--- a/solution.py
+++ b/solution.py
@@ -168,9 +168,10 @@
         holds = holds | (holders[failed_id, j] == my_id)
     copies = []
 
-    def fetch(source, target):
+    def fetch(source, target, start=True):
         copy = pltpu.make_async_copy(source, target, fetched.at[len(copies)])
-        copy.start()
+        if start:
+            copy.start()
         copies.append(copy)
         return copy
 
@@ -179,7 +180,16 @@
     gate_copies = [
         fetch(gate_hbm.at[0, :, n : n + tile], w_gate.at[:, n : n + tile]) for n in range(0, inner, tile)
     ]
-    spare_copies = [fetch(spare_gate_hbm.at[0], spare_gate), fetch(spare_down_hbm.at[0], spare_down)]
+    spare_copies = [
+        fetch(spare_gate_hbm.at[0], spare_gate, False),
+        fetch(spare_down_hbm.at[0], spare_down, False),
+    ]
+
+    @pl.when(holds)
+    def _():
+        for copy in spare_copies:
+            copy.start()
+
     down_copies = [
         fetch(down_hbm.at[0, :, n : n + tile], w_down.at[:, n : n + tile]) for n in range(0, width, tile)
     ]
@@ -227,11 +237,11 @@
         hidden[:, n : n + tile] = gated_unit(
             jnp.dot(rows_in[...], w_gate[:, n : n + tile], preferred_element_type=jnp.float32)
         ).astype(jnp.bfloat16)
-    for copy in spare_copies:
-        copy.wait()
 
     @pl.when(holds)
     def _():
+        for copy in spare_copies:
+            copy.wait()
         spare_hidden[...] = gated_unit(
             jnp.dot(spare_in[...], spare_gate[...], preferred_element_type=jnp.float32)
         ).astype(jnp.bfloat16)
@@ -248,6 +258,7 @@
     def _():
         rows_out[:, capacity:, :] = jnp.zeros((len(blocks), capacity, width), jnp.bfloat16)
 
+    stores = []
     for i, n in enumerate(range(0, width, tile)):
         down_copies[i].wait()
         result = jnp.dot(hidden[...], w_down[:, n : n + tile], preferred_element_type=jnp.float32)
@@ -262,12 +273,13 @@
                 (((0,), (0,)), ((), ())),
                 preferred_element_type=jnp.float32,
             ).astype(jnp.bfloat16)
-    stores = [
-        pltpu.make_async_copy(dense.at[s], target, stored.at[s])
-        for s, target in enumerate((keep0, keep1, send.at[0], send.at[1]))
-    ]
-    for copy in stores:
-        copy.start()
+            target = (keep0, keep1, send.at[0], send.at[1])[s]
+            stores.append(
+                pltpu.make_async_copy(
+                    dense.at[s, :, n : n + tile], target.at[:, n : n + tile], stored.at[len(stores)]
+                )
+            )
+            stores[-1].start()
     for copy in stores:
         copy.wait()
 
@@ -299,7 +311,7 @@
             pltpu.VMEM((count, 2 * capacity, width), jnp.bfloat16),
             pltpu.VMEM((count, tok, width), jnp.bfloat16),
             pltpu.SemaphoreType.DMA((count + inner // 512 + width // 512 + 2,)),
-            pltpu.SemaphoreType.DMA((count,)),
+            pltpu.SemaphoreType.DMA((count * (width // 512),)),
         ],
         compiler_params=pltpu.CompilerParams(vmem_limit_bytes=VMEM_GRANT),
         cost_estimate=pl.CostEstimate(
@@ -357,7 +369,12 @@
             held.append(move(held[-1], round_ring))
             if k > 1:
                 held[k] = come_after(held[k], results[k - 2][0])
-        across.append(move(held[k], over_y))
+        if 1 < k == steps - 1:
+            across.append(move(across[-1], round_ring))
+        else:
+            across.append(move(held[k], over_y))
+        if k == 1:
+            across[1] = come_after(across[1], results[0][0])
         blocks = (held[k], across[k], move(held[k], over_core), move(across[k], over_core))
         earlier = [results[-1][0]] if results else []
         results.append(run_group(failed, holders, blocks, weights, earlier, tok, top, capacity))
@@ -370,7 +387,10 @@
             send = come_after(send, across[k + 1], held[min(k + 2, steps - 1)])
         got = move(send, over_core)
         far = (f32(keep1) + f32(got[1])).astype(jnp.bfloat16)
-        total = f32(keep0) + f32(got[0]) + f32(move(far, over_y))
+        if k == 0 and steps > 1:
+            far = come_after(far, from_y)
+        from_y = move(far, over_y)
+        total = f32(keep0) + f32(got[0]) + f32(from_y)
         if passing is not None:
             total = total + f32(move(passing, round_ring))
         passing = total.astype(jnp.bfloat16)

time: 119 us -> 114 us (0.958)
  waiting for transfers between devices: 40.1 us -> 33.4 us
  starting transfers between devices: 25.1 us -> 19.9 us
  other arithmetic: 13.7 us -> 16.6 us
  Pallas kernels: 36.1 us -> 38.5 us
    ppermute x26, waiting for transfers between devices: 40.1 us -> 33.4 us  [by_permutes(): move = lambda a, pairs: lax.ppermute(a, 'expert', pairs)]
    ppermute x26, starting transfers between devices: 25.1 us -> 19.9 us  [by_permutes(): move = lambda a, pairs: lax.ppermute(a, 'expert', pairs)]
    pallas_call x4, Pallas kernels: 36.1 us -> 38.5 us  [run_group(): pl.pallas_call(functools.partial(group_kernel, others=len(earlier), tok=t...]
    convert_element_type x4, other arithmetic: 5.94 us -> 7.9 us  [by_permutes(): passing = total.astype(jnp.bfloat16)]
    unnamed x14 -> x16, local copies, waits for them, and re-layouts: 3.92 us -> 4.71 us
  transfers between devices with their start and end apart: 26 -> 26, of which waited for: 9 -> 8; matrix products, arithmetic and copies ran while one was open for 10% -> 11% of each run, Pallas kernels for 30% -> 34%
where the time goes in v6:
time: 114 us
  Pallas kernels  38.5 us (34%)
  waiting for transfers between devices  33.4 us (29%)
  starting transfers between devices  19.9 us (17%)
  other arithmetic  16.6 us (15%)
  local copies, waits for them, and re-layouts  4.71 us (4%)
    pallas_call x4, Pallas kernels, run_group(): pl.pallas_call(functools.partial(group_kernel, others=len(earlier), tok=t...  38.5 us
    ppermute x26, waiting for transfers between devices, by_permutes(): move = lambda a, pairs: lax.ppermute(a, 'expert', pairs)  33.4 us
    ppermute x26, starting transfers between devices, by_permutes(): move = lambda a, pairs: lax.ppermute(a, 'expert', pairs)  19.9 us
    convert_element_type x4, other arithmetic, by_permutes(): passing = total.astype(jnp.bfloat16)  7.9 us
    convert_element_type x4, other arithmetic, by_permutes(): far = (f32(keep1) + f32(got[1])).astype(jnp.bfloat16)  7 us
    unnamed x16, local copies, waits for them, and re-layouts  4.71 us
  transfers between devices with their start and end apart: 26, of which 8 were waited for; matrix products, arithmetic and copies ran while one was open for 11% of the time, Pallas kernels for 34%

profile of v6, /device:TPU:0, one launch (start us, length us, event | category | flops | bytes accessed | tf_op | source)
XLA Modules:
  0.0 114.0 jit_solution(4145478440617540294)
XLA Ops:
  0.0 0.7 fusion.17
  0.7 1.0 fusion.16.refs_0_
  1.8 3.0 %collective-permute-start = (bf16[136,1536]{1,0:T(8,128)(2,1)S(1)}, bf16[136,1536]{1,0:T(8,128)(2,1)S(1)}, u32[]{:S(2)}, u32[]{:S(2)}) collective-permute-start(bf16[136,1536]{1,0:T(8,128)(2,1)S(1)} %fusion.16.refs_0_), channel_id=1, source_target_pairs={{0,2},{1,3},{2,0},{3,1},{4,6},{5,7},{6,4},{7,5},{8,10},{9,11},{10,... | collective-permute-start | bytes 1253384 | tf_op jit(solution)/shard_map/ppermute | solution.py:360
  4.8 1.6 %collective-permute-start.3 = (bf16[136,1536]{1,0:T(8,128)(2,1)S(1)}, bf16[136,1536]{1,0:T(8,128)(2,1)}, u32[]{:S(2)}, u32[]{:S(2)}) collective-permute-start(bf16[136,1536]{1,0:T(8,128)(2,1)S(1)} %fusion.16.refs_0_), channel_id=1, source_target_pairs={{0,4},{1,5},{2,6},{3,7},{4,12},{5,13},{6,14},{7,15},{8,0},{9,1},{1... | collective-permute-start | bytes 1253384 | tf_op jit(solution)/shard_map/ppermute | solution.py:360
  6.4 0.0 collective-permute-start.1
  6.4 8.1 %collective-permute-done.refs_1_ = bf16[136,1536]{1,0:T(8,128)(2,1)S(1)} collective-permute-done((bf16[136,1536]{1,0:T(8,128)(2,1)S(1)}, bf16[136,1536]{1,0:T(8,128)(2,1)S(1)}, u32[]{:S(2)}, u32[]{:S(2)}) %collective-permute-start) | collective-permute-done | bytes 417824 | tf_op jit(solution)/shard_map/ppermute | solution.py:360
  14.4 0.0 collective-permute-start.2
  14.4 2.5 %collective-permute-done.3.refs_0_ = bf16[136,1536]{1,0:T(8,128)(2,1)} collective-permute-done((bf16[136,1536]{1,0:T(8,128)(2,1)S(1)}, bf16[136,1536]{1,0:T(8,128)(2,1)}, u32[]{:S(2)}, u32[]{:S(2)}) %collective-permute-start.3) | collective-permute-done | bytes 417824 | tf_op jit(solution)/shard_map/ppermute | solution.py:360
  16.9 0.5 collective-permute-start.4
  18.0 1.4 %copy.17.holders = s32[16,4]{1,0:T(8,128)} copy(s32[16,4]{0,1:T(4,128)} %param.13) | data formatting | bytes 512 | tf_op args[4]
  19.4 0.0 collective-permute-start.8
  19.4 0.7 collective-permute-start.5
  20.1 0.0 collective-permute-done.1.refs_2_
  20.1 0.7 copy-done.6
  20.9 0.0 collective-permute-done.2.refs_3_
  20.9 9.6 %group.4 = (bf16[128,1536]{1,0:T(8,128)(2,1)}, bf16[128,1536]{1,0:T(8,128)(2,1)}, bf16[2,128,1536]{2,1,0:T(8,128)(2,1)}) custom-call(s32[1]{0:T(128)S(6)} %copy.31.failed, s32[16,4]{1,0:T(8,128)} %copy.17.holders, bf16[136,1536]{1,0:T(8,128)(2,1)} %copy-done, bf16[136,1536]{1,0:T(8,128)(2,1)} %copy-done.5, bf16[136,1536]{1,0:T(8,128)(2,1)} %copy-done.6, ...), custom_call_target="tpu_custom_call" | custom-call | flops 3019898880 | bytes 14942208 | tf_op jit(solution)/shard_map/group/pallas_call | solution.py:294
  30.4 0.0 collective-permute-done.4.refs_0_
  30.5 0.1 collective-permute-start.9
  30.6 2.1 %collective-permute-done.5.refs_0_ = bf16[136,1536]{1,0:T(8,128)(2,1)} collective-permute-done((bf16[136,1536]{1,0:T(8,128)(2,1)}, bf16[136,1536]{1,0:T(8,128)(2,1)}, u32[]{:S(2)}, u32[]{:S(2)}) %collective-permute-start.5) | collective-permute-done | bytes 417824 | tf_op jit(solution)/shard_map/ppermute | solution.py:360
  32.6 0.8 collective-permute-start.7
  33.5 1.5 %collective-permute-start.10 = (bf16[136,1536]{1,0:T(8,128)(2,1)}, bf16[136,1536]{1,0:T(8,128)(2,1)}, u32[]{:S(2)}, u32[]{:S(2)}) collective-permute-start(bf16[136,1536]{1,0:T(8,128)(2,1)} %after.8.refs_2_.refs_0_), channel_id=1, source_target_pairs={{0,2},{1,3},{2,0},{3,1},{4,6},{5,7},{6,4},{7,5},{8,10},{9,11},{10,... | collective-permute-start | bytes 1253384 | tf_op jit(solution)/shard_map/ppermute | solution.py:360
  35.0 0.0 collective-permute-done.8.refs_2_
  35.0 0.0 collective-permute-done.9.refs_3_
  35.0 9.6 %group.5 = (bf16[128,1536]{1,0:T(8,128)(2,1)}, bf16[128,1536]{1,0:T(8,128)(2,1)}, bf16[2,128,1536]{2,1,0:T(8,128)(2,1)}) custom-call(s32[1]{0:T(128)S(6)} %copy.31.failed, s32[16,4]{1,0:T(8,128)} %copy.17.holders, bf16[136,1536]{1,0:T(8,128)(2,1)} %collective-permute-done.3.refs_0_, bf16[136,1536]{1,0:T(8,128)(2,1)} %after.7.refs_1_, ...), custom_call_target="tpu_custom_call" | custom-call | flops 3019898880 | bytes 14942208 | tf_op jit(solution)/shard_map/group/pallas_call | solution.py:294
  44.6 0.5 collective-permute-done.7.refs_0_
  45.1 0.0 collective-permute-start.21
  45.1 0.5 collective-permute-start.14
  45.7 0.1 collective-permute-start.15
  45.7 3.0 %collective-permute-start.11 = (bf16[136,1536]{1,0:T(8,128)(2,1)}, bf16[136,1536]{1,0:T(8,128)(2,1)}, u32[]{:S(2)}, u32[]{:S(2)}) collective-permute-start(bf16[136,1536]{1,0:T(8,128)(2,1)} %collective-permute-done.10.refs_1_), channel_id=1, source_target_pairs={{0,4},{1,5},{2,6},{3,7},{4,12},{5,13},{6,14},{7,15},{8,0},{9,1},{1... | collective-permute-start | bytes 1253384 | tf_op jit(solution)/shard_map/ppermute | solution.py:360
  48.7 0.0 collective-permute-done.21
  48.7 0.9 copy-done.2
  49.6 1.8 %fusion.1 = bf16[128,1536]{1,0:T(8,128)(2,1)} fusion(bf16[128,1536]{1,0:T(8,128)(2,1)} %get-tuple-element.28, bf16[2,128,1536]{2,1,0:T(8,128)(2,1)S(1)} %collective-permute-done.21), kind=kLoop, calls=%fused_computation.3 | loop fusion | flops 786432 | bytes 1179648 | tf_op jit(solution)/shard_map/convert_element_type | solution.py:389
  51.4 1.5 %collective-permute-start.22 = (bf16[128,1536]{1,0:T(8,128)(2,1)}, bf16[128,1536]{1,0:T(8,128)(2,1)}, u32[]{:S(2)}, u32[]{:S(2)}) collective-permute-start(bf16[128,1536]{1,0:T(8,128)(2,1)} %fusion.1), channel_id=1, source_target_pairs={{0,2},{1,3},{2,0},{3,1},{4,6},{5,7},{6,4},{7,5},{8,10},{9,11},{10,... | collective-permute-start | bytes 1179656 | tf_op jit(solution)/shard_map/ppermute | solution.py:360
  52.9 0.0 collective-permute-done.15.refs_3_
  53.0 9.6 %group.6 = (bf16[128,1536]{1,0:T(8,128)(2,1)}, bf16[128,1536]{1,0:T(8,128)(2,1)}, bf16[2,128,1536]{2,1,0:T(8,128)(2,1)}) custom-call(s32[1]{0:T(128)S(6)} %copy.31.failed, s32[16,4]{1,0:T(8,128)} %copy.17.holders, bf16[136,1536]{1,0:T(8,128)(2,1)} %after.8.refs_2_.refs_0_, bf16[136,1536]{1,0:T(8,128)(2,1)} %collective-permute-done.10.refs_1_, ...), custom_call_target="tpu_custom_call" | custom-call | flops 3019898880 | bytes 14942208 | tf_op jit(solution)/shard_map/group/pallas_call | solution.py:294
  62.6 0.0 collective-permute-done.11.refs_1_
  62.6 0.1 collective-permute-start.19
  62.7 0.5 collective-permute-start.12
  63.2 0.1 collective-permute-start.13
  63.2 0.0 collective-permute-done.22
  63.2 2.1 %fusion.3 = bf16[128,1536]{1,0:T(8,128)(2,1)} fusion(bf16[128,1536]{1,0:T(8,128)(2,1)} %collective-permute-done.22, bf16[128,1536]{1,0:T(8,128)(2,1)} %get-tuple-element.20.refs_1_.refs_8_, bf16[2,128,1536]{2,1,0:T(8,128)(2,1)} %copy-done.2), kind=kLoop, calls=%fused_computation.6 | loop fusion | flops 1179648 | bytes 1572864 | tf_op jit(solution)/shard_map/convert_element_type | solution.py:396
  65.4 2.7 %collective-permute-start.23 = (bf16[128,1536]{1,0:T(8,128)(2,1)}, bf16[128,1536]{1,0:T(8,128)(2,1)}, u32[]{:S(2)}, u32[]{:S(2)}) collective-permute-start(bf16[128,1536]{1,0:T(8,128)(2,1)} %fusion.3), channel_id=1, source_target_pairs={{0,4},{1,5},{2,6},{3,7},{4,12},{5,13},{6,14},{7,15},{8,0},{9,1},{1... | collective-permute-start | bytes 1179656 | tf_op jit(solution)/shard_map/ppermute | solution.py:360
  68.1 0.9 copy-done.3
  69.0 1.9 %fusion.4 = bf16[128,1536]{1,0:T(8,128)(2,1)} fusion(bf16[128,1536]{1,0:T(8,128)(2,1)} %get-tuple-element.26, bf16[2,128,1536]{2,1,0:T(8,128)(2,1)S(1)} %collective-permute-done.19), kind=kLoop, calls=%fused_computation.8 | loop fusion | flops 786432 | bytes 1179648 | tf_op jit(solution)/shard_map/convert_element_type | solution.py:389
  70.9 1.5 %collective-permute-start.20 = (bf16[128,1536]{1,0:T(8,128)(2,1)}, bf16[128,1536]{1,0:T(8,128)(2,1)}, u32[]{:S(2)}, u32[]{:S(2)}) collective-permute-start(bf16[128,1536]{1,0:T(8,128)(2,1)} %fusion.4), channel_id=1, source_target_pairs={{0,2},{1,3},{2,0},{3,1},{4,6},{5,7},{6,4},{7,5},{8,10},{9,11},{10,... | collective-permute-start | bytes 1179656 | tf_op jit(solution)/shard_map/ppermute | solution.py:360
  72.4 9.7 %group.7 = (bf16[128,1536]{1,0:T(8,128)(2,1)}, bf16[128,1536]{1,0:T(8,128)(2,1)}, bf16[2,128,1536]{2,1,0:T(8,128)(2,1)}) custom-call(s32[1]{0:T(128)S(6)} %copy.31.failed, s32[16,4]{1,0:T(8,128)} %copy.17.holders, bf16[136,1536]{1,0:T(8,128)(2,1)} %after.10.refs_0_.refs_2_, bf16[136,1536]{1,0:T(8,128)(2,1)} %collective-permute-done.11.refs_1_, ...), custom_call_target="tpu_custom_call" | custom-call | flops 3019898880 | bytes 14942208 | tf_op jit(solution)/shard_map/group/pallas_call | solution.py:294
  82.0 0.1 collective-permute-start.16
  82.1 0.5 collective-permute-start.6
  82.6 1.5 %fusion.7 = bf16[128,1536]{1,0:T(8,128)(2,1)S(1)} fusion(bf16[128,1536]{1,0:T(8,128)(2,1)} %collective-permute-done.23, bf16[128,1536]{1,0:T(8,128)(2,1)} %collective-permute-done.20, bf16[128,1536]{1,0:T(8,128)(2,1)} %get-tuple-element.21.refs_8_, bf16[2,128,1536]{2,1,0:T(8,128)(2,1)} %copy-done.3), kind=kLoop, calls=%fused_computation.12 | loop fusion | flops 1572864 | bytes 1966080 | tf_op jit(solution)/shard_map/convert_element_type | solution.py:396
  84.2 0.1 collective-permute-start.24
  84.2 0.7 collective-permute-done.16
  85.0 1.2 %fusion.11 = bf16[128,1536]{1,0:T(8,128)(2,1)S(1)} fusion(bf16[128,1536]{1,0:T(8,128)(2,1)} %get-tuple-element.22, bf16[2,128,1536]{2,1,0:T(8,128)(2,1)} %collective-permute-done.16), kind=kLoop, calls=%fused_computation.18 | loop fusion | flops 786432 | bytes 1179648 | tf_op jit(solution)/shard_map/convert_element_type | solution.py:389
  86.2 0.6 collective-permute-start.17
  86.7 0.0 collective-permute-done.6
  86.7 2.1 %fusion.12.refs_0_ = bf16[128,1536]{1,0:T(8,128)(2,1)} fusion(bf16[128,1536]{1,0:T(8,128)(2,1)} %get-tuple-element.19, bf16[2,128,1536]{2,1,0:T(8,128)(2,1)S(1)} %collective-permute-done.6), kind=kLoop, calls=%fused_computation.20 | loop fusion | flops 786432 | bytes 1179648 | tf_op jit(solution)/shard_map/convert_element_type | solution.py:389
  88.8 7.4 %collective-permute-done.24 = bf16[128,1536]{1,0:T(8,128)(2,1)S(1)} collective-permute-done((bf16[128,1536]{1,0:T(8,128)(2,1)S(1)}, bf16[128,1536]{1,0:T(8,128)(2,1)S(1)}, u32[]{:S(2)}, u32[]{:S(2)}) %collective-permute-start.24) | collective-permute-done | bytes 393248 | tf_op jit(solution)/shard_map/ppermute | solution.py:360
  96.2 1.2 %collective-permute-done.17.refs_1_ = bf16[128,1536]{1,0:T(8,128)(2,1)S(1)} collective-permute-done((bf16[128,1536]{1,0:T(8,128)(2,1)S(1)}, bf16[128,1536]{1,0:T(8,128)(2,1)S(1)}, u32[]{:S(2)}, u32[]{:S(2)}) %collective-permute-start.17) | collective-permute-done | bytes 393248 | tf_op jit(solution)/shard_map/ppermute | solution.py:360
  97.4 0.8 copy-done.1
  98.2 2.1 %fusion.10 = bf16[128,1536]{1,0:T(8,128)(2,1)} fusion(bf16[128,1536]{1,0:T(8,128)(2,1)S(1)} %collective-permute-done.24, bf16[128,1536]{1,0:T(8,128)(2,1)S(1)} %collective-permute-done.17.refs_1_, bf16[128,1536]{1,0:T(8,128)(2,1)} %get-tuple-element.24, bf16[2,128,1536]{2,1,0:T(8,128)(2,1)} %collective-permute-done.16), kind=kLoop, calls=%fused_computation.16 | loop fusion | flops 1572864 | bytes 1966080 | tf_op jit(solution)/shard_map/convert_element_type | solution.py:396
  100.2 0.0 collective-permute-start.25
  100.2 0.6 collective-permute-start.18
  100.8 11.0 %collective-permute-done.25 = bf16[128,1536]{1,0:T(8,128)(2,1)} collective-permute-done((bf16[128,1536]{1,0:T(8,128)(2,1)}, bf16[128,1536]{1,0:T(8,128)(2,1)}, u32[]{:S(2)}, u32[]{:S(2)}) %collective-permute-start.25) | collective-permute-done | bytes 393248 | tf_op jit(solution)/shard_map/ppermute | solution.py:360
  111.8 0.0 collective-permute-done.18
  111.8 2.2 %fusion.15 = bf16[128,1536]{1,0:T(8,128)(2,1)} fusion(bf16[128,1536]{1,0:T(8,128)(2,1)} %collective-permute-done.25, bf16[128,1536]{1,0:T(8,128)(2,1)S(1)} %collective-permute-done.18, bf16[128,1536]{1,0:T(8,128)(2,1)} %get-tuple-element.17.refs_1_.refs_8_, bf16[2,128,1536]{2,1,0:T(8,128)(2,1)} %copy-done.4), kind=kLoop, calls=%fused_computation.24 | loop fusion | flops 1572864 | bytes 1966080 | tf_op jit(solution)/shard_map/convert_element_type | solution.py:396
  (26 shorter events, 0.1 us)
Async XLA Ops:
  1.8 4.6 %copy-start = (bf16[136,1536]{1,0:T(8,128)(2,1)}, bf16[136,1536]{1,0:T(8,128)(2,1)S(1)}, u32[]{:S(2)}) copy-start(bf16[136,1536]{1,0:T(8,128)(2,1)S(1)} %fusion.16.refs_0_) | copy-start | bytes 1253380
  1.8 12.7 %collective-permute-start = (bf16[136,1536]{1,0:T(8,128)(2,1)S(1)}, bf16[136,1536]{1,0:T(8,128)(2,1)S(1)}, u32[]{:S(2)}, u32[]{:S(2)}) collective-permute-start(bf16[136,1536]{1,0:T(8,128)(2,1)S(1)} %fusion.16.refs_0_), channel_id=1, source_target_pairs={{0,2},{1,3},{2,0},{3,1},{4,6},{5,7},{6,4},{7,5},{8,10},{9,11},{10,... | collective-permute-start | bytes 1253384 | tf_op jit(solution)/shard_map/ppermute | solution.py:360
  4.8 12.1 %collective-permute-start.3 = (bf16[136,1536]{1,0:T(8,128)(2,1)S(1)}, bf16[136,1536]{1,0:T(8,128)(2,1)}, u32[]{:S(2)}, u32[]{:S(2)}) collective-permute-start(bf16[136,1536]{1,0:T(8,128)(2,1)S(1)} %fusion.16.refs_0_), channel_id=1, source_target_pairs={{0,4},{1,5},{2,6},{3,7},{4,12},{5,13},{6,14},{7,15},{8,0},{9,1},{1... | collective-permute-start | bytes 1253384 | tf_op jit(solution)/shard_map/ppermute | solution.py:360
  6.4 13.7 %collective-permute-start.1 = (bf16[136,1536]{1,0:T(8,128)(2,1)S(1)}, bf16[136,1536]{1,0:T(8,128)(2,1)S(1)}, u32[]{:S(2)}, u32[]{:S(2)}) collective-permute-start(bf16[136,1536]{1,0:T(8,128)(2,1)S(1)} %fusion.16.refs_0_), channel_id=1, source_target_pairs={{0,1},{1,0},{2,3},{3,2},{4,5},{5,4},{6,7},{7,6},{8,9},{9,8},{10,11... | collective-permute-start | bytes 1253384 | tf_op jit(solution)/shard_map/ppermute | solution.py:360
  14.4 5.7 %copy-start.5 = (bf16[136,1536]{1,0:T(8,128)(2,1)}, bf16[136,1536]{1,0:T(8,128)(2,1)S(1)}, u32[]{:S(2)}) copy-start(bf16[136,1536]{1,0:T(8,128)(2,1)S(1)} %collective-permute-done.refs_1_) | copy-start | bytes 1253380
  14.4 6.4 %collective-permute-start.2 = (bf16[136,1536]{1,0:T(8,128)(2,1)S(1)}, bf16[136,1536]{1,0:T(8,128)(2,1)}, u32[]{:S(2)}, u32[]{:S(2)}) collective-permute-start(bf16[136,1536]{1,0:T(8,128)(2,1)S(1)} %collective-permute-done.refs_1_), channel_id=1, source_target_pairs={{0,1},{1,0},{2,3},{3,2},{4,5},{5,4},{6,7},{7,6},{8,9},{9,8},{10,11... | collective-permute-start | bytes 1253384 | tf_op jit(solution)/shard_map/ppermute | solution.py:360
  16.9 13.5 %collective-permute-start.4 = (bf16[136,1536]{1,0:T(8,128)(2,1)}, bf16[136,1536]{1,0:T(8,128)(2,1)}, u32[]{:S(2)}, u32[]{:S(2)}) collective-permute-start(bf16[136,1536]{1,0:T(8,128)(2,1)} %collective-permute-done.3.refs_0_), channel_id=1, source_target_pairs={{0,2},{1,3},{2,0},{3,1},{4,6},{5,7},{6,4},{7,5},{8,10},{9,11},{10,... | collective-permute-start | bytes 1253384 | tf_op jit(solution)/shard_map/ppermute | solution.py:360
  19.4 15.6 %collective-permute-start.8 = (bf16[136,1536]{1,0:T(8,128)(2,1)}, bf16[136,1536]{1,0:T(8,128)(2,1)}, u32[]{:S(2)}, u32[]{:S(2)}) collective-permute-start(bf16[136,1536]{1,0:T(8,128)(2,1)} %collective-permute-done.3.refs_0_), channel_id=1, source_target_pairs={{0,1},{1,0},{2,3},{3,2},{4,5},{5,4},{6,7},{7,6},{8,9},{9,8},{10,11... | collective-permute-start | bytes 1253384 | tf_op jit(solution)/shard_map/ppermute | solution.py:360
  19.4 13.3 %collective-permute-start.5 = (bf16[136,1536]{1,0:T(8,128)(2,1)}, bf16[136,1536]{1,0:T(8,128)(2,1)}, u32[]{:S(2)}, u32[]{:S(2)}) collective-permute-start(bf16[136,1536]{1,0:T(8,128)(2,1)} %collective-permute-done.3.refs_0_), channel_id=1, source_target_pairs={{0,4},{1,5},{2,6},{3,7},{4,12},{5,13},{6,14},{7,15},{8,0},{9,1},{1... | collective-permute-start | bytes 1253384 | tf_op jit(solution)/shard_map/ppermute | solution.py:360
  20.1 0.8 copy-start.6
  30.5 4.5 %collective-permute-start.9 = (bf16[136,1536]{1,0:T(8,128)(2,1)}, bf16[136,1536]{1,0:T(8,128)(2,1)}, u32[]{:S(2)}, u32[]{:S(2)}) collective-permute-start(bf16[136,1536]{1,0:T(8,128)(2,1)} %after.7.refs_1_), channel_id=1, source_target_pairs={{0,1},{1,0},{2,3},{3,2},{4,5},{5,4},{6,7},{7,6},{8,9},{9,8},{10,11... | collective-permute-start | bytes 1253384 | tf_op jit(solution)/shard_map/ppermute | solution.py:360
  32.6 12.5 %collective-permute-start.7 = (bf16[136,1536]{1,0:T(8,128)(2,1)}, bf16[136,1536]{1,0:T(8,128)(2,1)}, u32[]{:S(2)}, u32[]{:S(2)}) collective-permute-start(bf16[136,1536]{1,0:T(8,128)(2,1)} %after.8.refs_2_.refs_0_), channel_id=1, source_target_pairs={{0,4},{1,5},{2,6},{3,7},{4,12},{5,13},{6,14},{7,15},{8,0},{9,1},{1... | collective-permute-start | bytes 1253384 | tf_op jit(solution)/shard_map/ppermute | solution.py:360
  33.5 11.7 %collective-permute-start.10 = (bf16[136,1536]{1,0:T(8,128)(2,1)}, bf16[136,1536]{1,0:T(8,128)(2,1)}, u32[]{:S(2)}, u32[]{:S(2)}) collective-permute-start(bf16[136,1536]{1,0:T(8,128)(2,1)} %after.8.refs_2_.refs_0_), channel_id=1, source_target_pairs={{0,2},{1,3},{2,0},{3,1},{4,6},{5,7},{6,4},{7,5},{8,10},{9,11},{10,... | collective-permute-start | bytes 1253384 | tf_op jit(solution)/shard_map/ppermute | solution.py:360
  45.1 3.6 %collective-permute-start.21 = (bf16[2,128,1536]{2,1,0:T(8,128)(2,1)}, bf16[2,128,1536]{2,1,0:T(8,128)(2,1)S(1)}, u32[]{:S(2)}, u32[]{:S(2)}) collective-permute-start(bf16[2,128,1536]{2,1,0:T(8,128)(2,1)} %after.13), channel_id=1, source_target_pairs={{0,1},{1,0},{2,3},{3,2},{4,5},{5,4},{6,7},{7,6},{8,9},{9,8},{10,11... | collective-permute-start | bytes 2359304 | tf_op jit(solution)/shard_map/ppermute | solution.py:360
  45.1 7.8 %collective-permute-start.14 = (bf16[136,1536]{1,0:T(8,128)(2,1)}, bf16[136,1536]{1,0:T(8,128)(2,1)}, u32[]{:S(2)}, u32[]{:S(2)}) collective-permute-start(bf16[136,1536]{1,0:T(8,128)(2,1)} %after.8.refs_2_.refs_0_), channel_id=1, source_target_pairs={{0,1},{1,0},{2,3},{3,2},{4,5},{5,4},{6,7},{7,6},{8,9},{9,8},{10,11... | collective-permute-start | bytes 1253384 | tf_op jit(solution)/shard_map/ppermute | solution.py:360
  45.7 7.3 %collective-permute-start.15 = (bf16[136,1536]{1,0:T(8,128)(2,1)}, bf16[136,1536]{1,0:T(8,128)(2,1)}, u32[]{:S(2)}, u32[]{:S(2)}) collective-permute-start(bf16[136,1536]{1,0:T(8,128)(2,1)} %collective-permute-done.10.refs_1_), channel_id=1, source_target_pairs={{0,1},{1,0},{2,3},{3,2},{4,5},{5,4},{6,7},{7,6},{8,9},{9,8},{10,11... | collective-permute-start | bytes 1253384 | tf_op jit(solution)/shard_map/ppermute | solution.py:360
  45.7 16.9 %collective-permute-start.11 = (bf16[136,1536]{1,0:T(8,128)(2,1)}, bf16[136,1536]{1,0:T(8,128)(2,1)}, u32[]{:S(2)}, u32[]{:S(2)}) collective-permute-start(bf16[136,1536]{1,0:T(8,128)(2,1)} %collective-permute-done.10.refs_1_), channel_id=1, source_target_pairs={{0,4},{1,5},{2,6},{3,7},{4,12},{5,13},{6,14},{7,15},{8,0},{9,1},{1... | collective-permute-start | bytes 1253384 | tf_op jit(solution)/shard_map/ppermute | solution.py:360
  48.7 0.9 copy-start.2
  51.4 11.8 %collective-permute-start.22 = (bf16[128,1536]{1,0:T(8,128)(2,1)}, bf16[128,1536]{1,0:T(8,128)(2,1)}, u32[]{:S(2)}, u32[]{:S(2)}) collective-permute-start(bf16[128,1536]{1,0:T(8,128)(2,1)} %fusion.1), channel_id=1, source_target_pairs={{0,2},{1,3},{2,0},{3,1},{4,6},{5,7},{6,4},{7,5},{8,10},{9,11},{10,... | collective-permute-start | bytes 1179656 | tf_op jit(solution)/shard_map/ppermute | solution.py:360
  62.6 5.5 %collective-permute-start.19 = (bf16[2,128,1536]{2,1,0:T(8,128)(2,1)}, bf16[2,128,1536]{2,1,0:T(8,128)(2,1)S(1)}, u32[]{:S(2)}, u32[]{:S(2)}) collective-permute-start(bf16[2,128,1536]{2,1,0:T(8,128)(2,1)} %after.12), channel_id=1, source_target_pairs={{0,1},{1,0},{2,3},{3,2},{4,5},{5,4},{6,7},{7,6},{8,9},{9,8},{10,11... | collective-permute-start | bytes 2359304 | tf_op jit(solution)/shard_map/ppermute | solution.py:360
  62.7 9.7 %collective-permute-start.12 = (bf16[136,1536]{1,0:T(8,128)(2,1)}, bf16[136,1536]{1,0:T(8,128)(2,1)}, u32[]{:S(2)}, u32[]{:S(2)}) collective-permute-start(bf16[136,1536]{1,0:T(8,128)(2,1)} %after.10.refs_0_.refs_2_), channel_id=1, source_target_pairs={{0,1},{1,0},{2,3},{3,2},{4,5},{5,4},{6,7},{7,6},{8,9},{9,8},{10,11... | collective-permute-start | bytes 1253384 | tf_op jit(solution)/shard_map/ppermute | solution.py:360
  63.2 9.2 %collective-permute-start.13 = (bf16[136,1536]{1,0:T(8,128)(2,1)}, bf16[136,1536]{1,0:T(8,128)(2,1)}, u32[]{:S(2)}, u32[]{:S(2)}) collective-permute-start(bf16[136,1536]{1,0:T(8,128)(2,1)} %collective-permute-done.11.refs_1_), channel_id=1, source_target_pairs={{0,1},{1,0},{2,3},{3,2},{4,5},{5,4},{6,7},{7,6},{8,9},{9,8},{10,11... | collective-permute-start | bytes 1253384 | tf_op jit(solution)/shard_map/ppermute | solution.py:360
  65.4 17.3 %collective-permute-start.23 = (bf16[128,1536]{1,0:T(8,128)(2,1)}, bf16[128,1536]{1,0:T(8,128)(2,1)}, u32[]{:S(2)}, u32[]{:S(2)}) collective-permute-start(bf16[128,1536]{1,0:T(8,128)(2,1)} %fusion.3), channel_id=1, source_target_pairs={{0,4},{1,5},{2,6},{3,7},{4,12},{5,13},{6,14},{7,15},{8,0},{9,1},{1... | collective-permute-start | bytes 1179656 | tf_op jit(solution)/shard_map/ppermute | solution.py:360
  68.1 0.9 copy-start.3
  70.9 11.8 %collective-permute-start.20 = (bf16[128,1536]{1,0:T(8,128)(2,1)}, bf16[128,1536]{1,0:T(8,128)(2,1)}, u32[]{:S(2)}, u32[]{:S(2)}) collective-permute-start(bf16[128,1536]{1,0:T(8,128)(2,1)} %fusion.4), channel_id=1, source_target_pairs={{0,2},{1,3},{2,0},{3,1},{4,6},{5,7},{6,4},{7,5},{8,10},{9,11},{10,... | collective-permute-start | bytes 1179656 | tf_op jit(solution)/shard_map/ppermute | solution.py:360
  82.0 2.9 %collective-permute-start.16 = (bf16[2,128,1536]{2,1,0:T(8,128)(2,1)}, bf16[2,128,1536]{2,1,0:T(8,128)(2,1)}, u32[]{:S(2)}, u32[]{:S(2)}) collective-permute-start(bf16[2,128,1536]{2,1,0:T(8,128)(2,1)} %get-tuple-element.23), channel_id=1, source_target_pairs={{0,1},{1,0},{2,3},{3,2},{4,5},{5,4},{6,7},{7,6},{8,9},{9,8},{10,11... | collective-permute-start | bytes 2359304 | tf_op jit(solution)/shard_map/ppermute | solution.py:360
  82.1 4.6 %collective-permute-start.6 = (bf16[2,128,1536]{2,1,0:T(8,128)(2,1)}, bf16[2,128,1536]{2,1,0:T(8,128)(2,1)S(1)}, u32[]{:S(2)}, u32[]{:S(2)}) collective-permute-start(bf16[2,128,1536]{2,1,0:T(8,128)(2,1)} %after.9), channel_id=1, source_target_pairs={{0,1},{1,0},{2,3},{3,2},{4,5},{5,4},{6,7},{7,6},{8,9},{9,8},{10,11... | collective-permute-start | bytes 2359304 | tf_op jit(solution)/shard_map/ppermute | solution.py:360
  84.2 12.1 %collective-permute-start.24 = (bf16[128,1536]{1,0:T(8,128)(2,1)S(1)}, bf16[128,1536]{1,0:T(8,128)(2,1)S(1)}, u32[]{:S(2)}, u32[]{:S(2)}) collective-permute-start(bf16[128,1536]{1,0:T(8,128)(2,1)S(1)} %fusion.7), channel_id=1, source_target_pairs={{0,4},{1,5},{2,6},{3,7},{4,12},{5,13},{6,14},{7,15},{8,0},{9,1},{1... | collective-permute-start | bytes 1179656 | tf_op jit(solution)/shard_map/ppermute | solution.py:360
  86.2 11.2 %collective-permute-start.17 = (bf16[128,1536]{1,0:T(8,128)(2,1)S(1)}, bf16[128,1536]{1,0:T(8,128)(2,1)S(1)}, u32[]{:S(2)}, u32[]{:S(2)}) collective-permute-start(bf16[128,1536]{1,0:T(8,128)(2,1)S(1)} %fusion.11), channel_id=1, source_target_pairs={{0,2},{1,3},{2,0},{3,1},{4,6},{5,7},{6,4},{7,5},{8,10},{9,11},{10,... | collective-permute-start | bytes 1179656 | tf_op jit(solution)/shard_map/ppermute | solution.py:360
  86.7 13.5 %copy-start.4 = (bf16[2,128,1536]{2,1,0:T(8,128)(2,1)}, bf16[2,128,1536]{2,1,0:T(8,128)(2,1)S(1)}, u32[]{:S(2)}) copy-start(bf16[2,128,1536]{2,1,0:T(8,128)(2,1)S(1)} %collective-permute-done.6) | copy-start | bytes 2359300
  97.4 0.8 copy-start.1
  100.2 11.5 %collective-permute-start.25 = (bf16[128,1536]{1,0:T(8,128)(2,1)}, bf16[128,1536]{1,0:T(8,128)(2,1)}, u32[]{:S(2)}, u32[]{:S(2)}) collective-permute-start(bf16[128,1536]{1,0:T(8,128)(2,1)} %fusion.10), channel_id=1, source_target_pairs={{0,4},{1,5},{2,6},{3,7},{4,12},{5,13},{6,14},{7,15},{8,0},{9,1},{1... | collective-permute-start | bytes 1179656 | tf_op jit(solution)/shard_map/ppermute | solution.py:360
  100.2 11.5 %collective-permute-start.18 = (bf16[128,1536]{1,0:T(8,128)(2,1)}, bf16[128,1536]{1,0:T(8,128)(2,1)S(1)}, u32[]{:S(2)}, u32[]{:S(2)}) collective-permute-start(bf16[128,1536]{1,0:T(8,128)(2,1)} %after.11), channel_id=1, source_target_pairs={{0,2},{1,3},{2,0},{3,1},{4,6},{5,7},{6,4},{7,5},{8,10},{9,11},{10,... | collective-permute-start | bytes 1179656 | tf_op jit(solution)/shard_map/ppermute | solution.py:360

commit v7 on v6

--- a/solution.py
+++ b/solution.py
@@ -163,9 +163,9 @@
     width, inner = w_gate.shape
     tile = 512
     my_id, failed_id = lax.axis_index("expert"), failed[0]
-    holds = holders[failed_id, 0] == my_id
-    for j in range(1, holders.shape[1]):
-        holds = holds | (holders[failed_id, j] == my_id)
+    holds = holders[0, failed_id] == my_id
+    for j in range(1, holders.shape[0]):
+        holds = holds | (holders[j, failed_id] == my_id)
     copies = []
 
     def fetch(source, target, start=True):
@@ -194,39 +194,52 @@
         fetch(down_hbm.at[0, :, n : n + tile], w_down.at[:, n : n + tile]) for n in range(0, width, tile)
     ]
 
+    count = len(blocks)
     before = (
         lax.broadcasted_iota(jnp.int32, (tok, tok), 0)
         < lax.broadcasted_iota(jnp.int32, (tok, tok), 1)
     ).astype(jnp.float32).astype(jnp.bfloat16)
-    row_iota = lax.broadcasted_iota(jnp.int32, (capacity, tok), 0)
-
-    def picker(meta, wanted, live):
-        mask = jnp.zeros((8, tok), jnp.float32)
-        level = jnp.zeros((8, tok), jnp.float32)
-        for k in range(top):
-            named = (meta[:, k * tok : (k + 1) * tok] == wanted.astype(jnp.float32)) & live
-            high = meta[:, (top + k) * tok : (top + k + 1) * tok]
-            low = meta[:, (2 * top + k) * tok : (2 * top + k + 1) * tok]
-            mask = mask + jnp.where(named, 1.0, 0.0)
-            level = level + jnp.where(named, (high * 32.0 + low) / LEVELS, 0.0)
-        rank = jnp.dot(mask.astype(jnp.bfloat16), before, preferred_element_type=jnp.float32)
-        place = jnp.where(mask[:1] > 0, rank[:1].astype(jnp.int32), -1)
-        hit = row_iota == place
-        weight = jnp.sum(jnp.where(hit, level[:1], 0.0), axis=1, keepdims=True)
-        return hit.astype(jnp.float32).astype(jnp.bfloat16), weight
-
-    picks, weights, spare_weights = [], [], []
-    for s in range(len(blocks)):
-        block_copies[s].wait()
-        meta = held[s, tok : tok + 8, :].astype(jnp.float32)
-        pick, weight = picker(meta, my_id, my_id != failed_id)
-        spare_pick, spare_weight = picker(meta, failed_id, holds)
-        both = jnp.concatenate([pick, spare_pick], axis=0)
-        picks.append(both)
-        weights.append(weight)
-        spare_weights.append(spare_weight)
+    own = lax.broadcasted_iota(jnp.int32, (2 * count, tok), 0) < count
+    wanted = jnp.where(own, my_id, failed_id).astype(jnp.float32)
+    serves = jnp.where(my_id != failed_id, 1.0, 0.0)
+    live = jnp.where(own, serves, jnp.where(holds, 1.0, 0.0))
+    slots = 2 * capacity
+    row_iota = lax.broadcasted_iota(jnp.int32, (slots, tok), 0)
+    lane_iota = lax.broadcasted_iota(jnp.int32, (tok, slots), 1)
+
+    for copy in block_copies:
+        copy.wait()
+    meta = jnp.concatenate([held[s, tok : tok + 8, :].astype(jnp.float32)[:1] for s in range(count)] * 2, axis=0)
+    mask = jnp.zeros((2 * count, tok), jnp.float32)
+    level = jnp.zeros((2 * count, tok), jnp.float32)
+    for k in range(top):
+        named = jnp.where(meta[:, k * tok : (k + 1) * tok] == wanted, live, 0.0)
+        high = meta[:, (top + k) * tok : (top + k + 1) * tok]
+        low = meta[:, (2 * top + k) * tok : (2 * top + k + 1) * tok]
+        mask = mask + named
+        level = level + named * ((high * 32.0 + low) / LEVELS)
+    rank = jnp.dot(mask.astype(jnp.bfloat16), before, preferred_element_type=jnp.float32)
+    place = jnp.where(mask > 0, rank + jnp.where(own, 0.0, float(capacity)), -1.0)
+    place_rows = place.astype(jnp.int32)
+    place_columns = place.T.astype(jnp.int32)
+
+    spreads, weights = [], []
+    for s in range(count):
+        here, there = place_rows[s : s + 1], place_rows[count + s : count + s + 1]
+        hit_here, hit_there = row_iota == here, row_iota == there
+        pick = jnp.where(hit_here | hit_there, 1.0, 0.0).astype(jnp.bfloat16)
+        weights.append(
+            jnp.sum(
+                jnp.where(hit_here, level[s : s + 1], 0.0)
+                + jnp.where(hit_there, level[count + s : count + s + 1], 0.0),
+                axis=1,
+                keepdims=True,
+            )
+        )
+        here, there = place_columns[:, s : s + 1], place_columns[:, count + s : count + s + 1]
+        spreads.append(jnp.where((lane_iota == here) | (lane_iota == there), 1.0, 0.0).astype(jnp.bfloat16))
         for n in range(0, width, tile):
-            got = jnp.dot(both, held[s, :tok, n : n + tile], preferred_element_type=jnp.float32).astype(
+            got = jnp.dot(pick, held[s, :tok, n : n + tile], preferred_element_type=jnp.float32).astype(
                 jnp.bfloat16
             )
             rows_in[s * capacity : (s + 1) * capacity, n : n + tile] = got[:capacity]
@@ -249,29 +262,26 @@
             result = jnp.dot(
                 spare_hidden[...], spare_down[:, n : n + tile], preferred_element_type=jnp.float32
             )
-            for s in range(len(blocks)):
+            for s in range(count):
                 rows_out[s, capacity:, n : n + tile] = (
-                    result[s * capacity : (s + 1) * capacity] * spare_weights[s]
+                    result[s * capacity : (s + 1) * capacity] * weights[s][capacity:]
                 ).astype(jnp.bfloat16)
 
     @pl.when(jnp.logical_not(holds))
     def _():
-        rows_out[:, capacity:, :] = jnp.zeros((len(blocks), capacity, width), jnp.bfloat16)
+        rows_out[:, capacity:, :] = jnp.zeros((count, capacity, width), jnp.bfloat16)
 
     stores = []
     for i, n in enumerate(range(0, width, tile)):
         down_copies[i].wait()
         result = jnp.dot(hidden[...], w_down[:, n : n + tile], preferred_element_type=jnp.float32)
         result = result.astype(jnp.bfloat16).astype(jnp.float32)
-        for s in range(len(blocks)):
+        for s in range(count):
             rows_out[s, :capacity, n : n + tile] = (
-                result[s * capacity : (s + 1) * capacity] * weights[s]
+                result[s * capacity : (s + 1) * capacity] * weights[s][:capacity]
             ).astype(jnp.bfloat16)
-            dense[s, :, n : n + tile] = lax.dot_general(
-                picks[s],
-                rows_out[s, :, n : n + tile],
-                (((0,), (0,)), ((), ())),
-                preferred_element_type=jnp.float32,
+            dense[s, :, n : n + tile] = jnp.dot(
+                spreads[s], rows_out[s, :, n : n + tile], preferred_element_type=jnp.float32
             ).astype(jnp.bfloat16)
             target = (keep0, keep1, send.at[0], send.at[1])[s]
             stores.append(
@@ -419,7 +429,7 @@
     weights = (w_gate, w_down, spare_gate, spare_down)
     if owners % 4 == 0 and owners <= 32 and 3 * top_count * tok_count <= tokens.shape[1]:
         return by_permutes(
-            failed_device, replica_holders, tokens, expert_ids, gate_levels, weights, owners, capacity
+            failed_device, replica_holders.T, tokens, expert_ids, gate_levels, weights, owners, capacity
         )
     codes = (expert_ids * LEVELS + gate_levels).T
     all_codes = lax.all_gather(codes, "expert", axis=0)

time: 114 us -> 112 us (0.982)
  Pallas kernels: 38.5 us -> 32.5 us
  waiting for transfers between devices: 33.4 us -> 37.1 us
    pallas_call x4, Pallas kernels: 38.5 us -> 32.5 us  [run_group(): pl.pallas_call(functools.partial(group_kernel, others=len(earlier), tok=t...]
    ppermute x26, waiting for transfers between devices: 33.4 us -> 37.1 us  [by_permutes(): move = lambda a, pairs: lax.ppermute(a, 'expert', pairs)]
    unnamed x16 -> x17, local copies, waits for them, and re-layouts: 4.71 us -> 4.09 us
  transfers between devices with their start and end apart: 26 -> 26, of which waited for: 8 -> 12; matrix products, arithmetic and copies ran while one was open for 11% -> 10% of each run, Pallas kernels for 34% -> 29%
where the time goes in v7:
time: 112 us; the launch traced here: 111 us
  waiting for transfers between devices  37.1 us (33%)
  Pallas kernels  32.5 us (29%)
  starting transfers between devices  20.1 us (18%)
  other arithmetic  16.7 us (15%)
  local copies, waits for them, and re-layouts  4.09 us (4%)
    ppermute x26, waiting for transfers between devices, by_permutes(): move = lambda a, pairs: lax.ppermute(a, 'expert', pairs)  37.1 us
    pallas_call x4, Pallas kernels, run_group(): pl.pallas_call(functools.partial(group_kernel, others=len(earlier), tok=t...  32.5 us
    ppermute x26, starting transfers between devices, by_permutes(): move = lambda a, pairs: lax.ppermute(a, 'expert', pairs)  20.1 us
    convert_element_type x4, other arithmetic, by_permutes(): passing = total.astype(jnp.bfloat16)  7.92 us
    convert_element_type x4, other arithmetic, by_permutes(): far = (f32(keep1) + f32(got[1])).astype(jnp.bfloat16)  7 us
    unnamed x17, local copies, waits for them, and re-layouts  4.09 us
  transfers between devices with their start and end apart: 26, of which 12 were waited for; matrix products, arithmetic and copies ran while one was open for 10% of the time, Pallas kernels for 29%

profile of v7, /device:TPU:0, one launch (start us, length us, event | category | flops | bytes accessed | tf_op | source)
XLA Modules:
  0.0 111.3 jit_solution(13680042764515552166)
XLA Ops:
  0.0 0.7 fusion.17
  0.7 1.0 fusion.16.refs_0_
  1.8 3.0 %collective-permute-start = (bf16[136,1536]{1,0:T(8,128)(2,1)S(1)}, bf16[136,1536]{1,0:T(8,128)(2,1)S(1)}, u32[]{:S(2)}, u32[]{:S(2)}) collective-permute-start(bf16[136,1536]{1,0:T(8,128)(2,1)S(1)} %fusion.16.refs_0_), channel_id=1, source_target_pairs={{0,2},{1,3},{2,0},{3,1},{4,6},{5,7},{6,4},{7,5},{8,10},{9,11},{10,... | collective-permute-start | bytes 1253384 | tf_op jit(solution)/shard_map/ppermute | solution.py:370
  4.8 1.6 %collective-permute-start.3 = (bf16[136,1536]{1,0:T(8,128)(2,1)S(1)}, bf16[136,1536]{1,0:T(8,128)(2,1)}, u32[]{:S(2)}, u32[]{:S(2)}) collective-permute-start(bf16[136,1536]{1,0:T(8,128)(2,1)S(1)} %fusion.16.refs_0_), channel_id=1, source_target_pairs={{0,4},{1,5},{2,6},{3,7},{4,12},{5,13},{6,14},{7,15},{8,0},{9,1},{1... | collective-permute-start | bytes 1253384 | tf_op jit(solution)/shard_map/ppermute | solution.py:370
  6.4 0.0 collective-permute-start.1
  6.4 8.1 %collective-permute-done.refs_1_ = bf16[136,1536]{1,0:T(8,128)(2,1)S(1)} collective-permute-done((bf16[136,1536]{1,0:T(8,128)(2,1)S(1)}, bf16[136,1536]{1,0:T(8,128)(2,1)S(1)}, u32[]{:S(2)}, u32[]{:S(2)}) %collective-permute-start) | collective-permute-done | bytes 417824 | tf_op jit(solution)/shard_map/ppermute | solution.py:370
  14.4 0.0 collective-permute-start.2
  14.5 2.5 %collective-permute-done.3.refs_0_ = bf16[136,1536]{1,0:T(8,128)(2,1)} collective-permute-done((bf16[136,1536]{1,0:T(8,128)(2,1)S(1)}, bf16[136,1536]{1,0:T(8,128)(2,1)}, u32[]{:S(2)}, u32[]{:S(2)}) %collective-permute-start.3) | collective-permute-done | bytes 417824 | tf_op jit(solution)/shard_map/ppermute | solution.py:370
  16.9 0.5 collective-permute-start.4
  18.0 0.1 collective-permute-start.8
  18.1 0.8 collective-permute-start.5
  18.9 0.0 collective-permute-done.1.refs_2_
  18.9 0.0 collective-permute-done.2.refs_3_
  18.9 0.7 copy-done.6
  19.6 0.8 copy-done.7
  20.4 8.1 %group.4 = (bf16[128,1536]{1,0:T(8,128)(2,1)}, bf16[128,1536]{1,0:T(8,128)(2,1)}, bf16[2,128,1536]{2,1,0:T(8,128)(2,1)}) custom-call(s32[1]{0:T(128)S(6)} %copy.27.failed, s32[4,16]{1,0:T(4,128)} %bitcast.53, bf16[136,1536]{1,0:T(8,128)(2,1)} %copy-done, bf16[136,1536]{1,0:T(8,128)(2,1)} %copy-done.5, bf16[136,1536]{1,0:T(8,128)(2,1)} %copy-done.6, ...), custom_call_target="tpu_custom_call" | custom-call | flops 3019898880 | bytes 14942208 | tf_op jit(solution)/shard_map/group/pallas_call | solution.py:304
  28.5 0.2 collective-permute-start.9
  28.7 2.6 %collective-permute-done.5.refs_0_ = bf16[136,1536]{1,0:T(8,128)(2,1)} collective-permute-done((bf16[136,1536]{1,0:T(8,128)(2,1)}, bf16[136,1536]{1,0:T(8,128)(2,1)}, u32[]{:S(2)}, u32[]{:S(2)}) %collective-permute-start.5) | collective-permute-done | bytes 417824 | tf_op jit(solution)/shard_map/ppermute | solution.py:370
  31.4 1.9 %collective-permute-start.7 = (bf16[136,1536]{1,0:T(8,128)(2,1)}, bf16[136,1536]{1,0:T(8,128)(2,1)}, u32[]{:S(2)}, u32[]{:S(2)}) collective-permute-start(bf16[136,1536]{1,0:T(8,128)(2,1)} %after.8.refs_2_.refs_0_), channel_id=1, source_target_pairs={{0,4},{1,5},{2,6},{3,7},{4,12},{5,13},{6,14},{7,15},{8,0},{9,1},{1... | collective-permute-start | bytes 1253384 | tf_op jit(solution)/shard_map/ppermute | solution.py:370
  33.2 1.5 %collective-permute-start.10 = (bf16[136,1536]{1,0:T(8,128)(2,1)}, bf16[136,1536]{1,0:T(8,128)(2,1)}, u32[]{:S(2)}, u32[]{:S(2)}) collective-permute-start(bf16[136,1536]{1,0:T(8,128)(2,1)} %after.8.refs_2_.refs_0_), channel_id=1, source_target_pairs={{0,2},{1,3},{2,0},{3,1},{4,6},{5,7},{6,4},{7,5},{8,10},{9,11},{10,... | collective-permute-start | bytes 1253384 | tf_op jit(solution)/shard_map/ppermute | solution.py:370
  34.7 8.2 %group.5 = (bf16[128,1536]{1,0:T(8,128)(2,1)}, bf16[128,1536]{1,0:T(8,128)(2,1)}, bf16[2,128,1536]{2,1,0:T(8,128)(2,1)}) custom-call(s32[1]{0:T(128)S(6)} %copy.27.failed, s32[4,16]{1,0:T(4,128)} %bitcast.54, bf16[136,1536]{1,0:T(8,128)(2,1)} %collective-permute-done.3.refs_0_, bf16[136,1536]{1,0:T(8,128)(2,1)} %after.7.refs_1_, ...), custom_call_target="tpu_custom_call" | custom-call | flops 3019898880 | bytes 14942208 | tf_op jit(solution)/shard_map/group/pallas_call | solution.py:304
  42.9 0.8 collective-permute-done.7.refs_0_
  43.8 1.5 %collective-permute-done.10.refs_1_ = bf16[136,1536]{1,0:T(8,128)(2,1)} collective-permute-done((bf16[136,1536]{1,0:T(8,128)(2,1)}, bf16[136,1536]{1,0:T(8,128)(2,1)}, u32[]{:S(2)}, u32[]{:S(2)}) %collective-permute-start.10) | collective-permute-done | bytes 417824 | tf_op jit(solution)/shard_map/ppermute | solution.py:370
  45.3 0.0 collective-permute-start.21
  45.3 0.5 collective-permute-start.14
  45.8 0.0 collective-permute-start.15
  45.8 1.6 %collective-permute-start.11 = (bf16[136,1536]{1,0:T(8,128)(2,1)}, bf16[136,1536]{1,0:T(8,128)(2,1)}, u32[]{:S(2)}, u32[]{:S(2)}) collective-permute-start(bf16[136,1536]{1,0:T(8,128)(2,1)} %collective-permute-done.10.refs_1_), channel_id=1, source_target_pairs={{0,4},{1,5},{2,6},{3,7},{4,12},{5,13},{6,14},{7,15},{8,0},{9,1},{1... | collective-permute-start | bytes 1253384 | tf_op jit(solution)/shard_map/ppermute | solution.py:370
  47.3 1.5 %collective-permute-done.21 = bf16[2,128,1536]{2,1,0:T(8,128)(2,1)S(1)} collective-permute-done((bf16[2,128,1536]{2,1,0:T(8,128)(2,1)}, bf16[2,128,1536]{2,1,0:T(8,128)(2,1)S(1)}, u32[]{:S(2)}, u32[]{:S(2)}) %collective-permute-start.21) | collective-permute-done | bytes 786464 | tf_op jit(solution)/shard_map/ppermute | solution.py:370
  48.8 0.9 copy-done.2
  49.7 1.8 %fusion.1 = bf16[128,1536]{1,0:T(8,128)(2,1)} fusion(bf16[128,1536]{1,0:T(8,128)(2,1)} %get-tuple-element.28, bf16[2,128,1536]{2,1,0:T(8,128)(2,1)S(1)} %collective-permute-done.21), kind=kLoop, calls=%fused_computation.3 | loop fusion | flops 786432 | bytes 1179648 | tf_op jit(solution)/shard_map/convert_element_type | solution.py:399
  51.6 1.5 %collective-permute-start.22 = (bf16[128,1536]{1,0:T(8,128)(2,1)}, bf16[128,1536]{1,0:T(8,128)(2,1)}, u32[]{:S(2)}, u32[]{:S(2)}) collective-permute-start(bf16[128,1536]{1,0:T(8,128)(2,1)} %fusion.1), channel_id=1, source_target_pairs={{0,2},{1,3},{2,0},{3,1},{4,6},{5,7},{6,4},{7,5},{8,10},{9,11},{10,... | collective-permute-start | bytes 1179656 | tf_op jit(solution)/shard_map/ppermute | solution.py:370
  53.1 0.0 collective-permute-done.15.refs_3_
  53.1 8.2 %group.6 = (bf16[128,1536]{1,0:T(8,128)(2,1)}, bf16[128,1536]{1,0:T(8,128)(2,1)}, bf16[2,128,1536]{2,1,0:T(8,128)(2,1)}) custom-call(s32[1]{0:T(128)S(6)} %copy.27.failed, s32[4,16]{1,0:T(4,128)} %bitcast.55, bf16[136,1536]{1,0:T(8,128)(2,1)} %after.8.refs_2_.refs_0_, bf16[136,1536]{1,0:T(8,128)(2,1)} %collective-permute-done.10.refs_1_, ...), custom_call_target="tpu_custom_call" | custom-call | flops 3019898880 | bytes 14942208 | tf_op jit(solution)/shard_map/group/pallas_call | solution.py:304
  61.3 0.1 collective-permute-start.19
  61.4 0.5 collective-permute-start.12
  61.9 0.1 collective-permute-start.13
  61.9 1.1 %collective-permute-done.22 = bf16[128,1536]{1,0:T(8,128)(2,1)} collective-permute-done((bf16[128,1536]{1,0:T(8,128)(2,1)}, bf16[128,1536]{1,0:T(8,128)(2,1)}, u32[]{:S(2)}, u32[]{:S(2)}) %collective-permute-start.22) | collective-permute-done | bytes 393248 | tf_op jit(solution)/shard_map/ppermute | solution.py:370
  63.1 2.1 %fusion.3 = bf16[128,1536]{1,0:T(8,128)(2,1)} fusion(bf16[128,1536]{1,0:T(8,128)(2,1)} %collective-permute-done.22, bf16[128,1536]{1,0:T(8,128)(2,1)} %get-tuple-element.20.refs_1_.refs_8_, bf16[2,128,1536]{2,1,0:T(8,128)(2,1)} %copy-done.2), kind=kLoop, calls=%fused_computation.6 | loop fusion | flops 1179648 | bytes 1572864 | tf_op jit(solution)/shard_map/convert_element_type | solution.py:406
  65.2 1.6 %collective-permute-start.23 = (bf16[128,1536]{1,0:T(8,128)(2,1)}, bf16[128,1536]{1,0:T(8,128)(2,1)}, u32[]{:S(2)}, u32[]{:S(2)}) collective-permute-start(bf16[128,1536]{1,0:T(8,128)(2,1)} %fusion.3), channel_id=1, source_target_pairs={{0,4},{1,5},{2,6},{3,7},{4,12},{5,13},{6,14},{7,15},{8,0},{9,1},{1... | collective-permute-start | bytes 1179656 | tf_op jit(solution)/shard_map/ppermute | solution.py:370
  66.8 0.9 copy-done.3
  67.7 1.8 %fusion.4 = bf16[128,1536]{1,0:T(8,128)(2,1)} fusion(bf16[128,1536]{1,0:T(8,128)(2,1)} %get-tuple-element.26, bf16[2,128,1536]{2,1,0:T(8,128)(2,1)S(1)} %collective-permute-done.19), kind=kLoop, calls=%fused_computation.8 | loop fusion | flops 786432 | bytes 1179648 | tf_op jit(solution)/shard_map/convert_element_type | solution.py:399
  69.5 1.5 %collective-permute-start.20 = (bf16[128,1536]{1,0:T(8,128)(2,1)}, bf16[128,1536]{1,0:T(8,128)(2,1)}, u32[]{:S(2)}, u32[]{:S(2)}) collective-permute-start(bf16[128,1536]{1,0:T(8,128)(2,1)} %fusion.4), channel_id=1, source_target_pairs={{0,2},{1,3},{2,0},{3,1},{4,6},{5,7},{6,4},{7,5},{8,10},{9,11},{10,... | collective-permute-start | bytes 1179656 | tf_op jit(solution)/shard_map/ppermute | solution.py:370
  71.0 0.0 collective-permute-done.12.refs_2_
  71.0 0.0 collective-permute-done.13.refs_3_
  71.0 8.1 %group.7 = (bf16[128,1536]{1,0:T(8,128)(2,1)}, bf16[128,1536]{1,0:T(8,128)(2,1)}, bf16[2,128,1536]{2,1,0:T(8,128)(2,1)}) custom-call(s32[1]{0:T(128)S(6)} %copy.27.failed, s32[4,16]{1,0:T(4,128)} %bitcast.56, bf16[136,1536]{1,0:T(8,128)(2,1)} %after.10.refs_0_.refs_2_, bf16[136,1536]{1,0:T(8,128)(2,1)} %collective-permute-done.11.refs_1_, ...), custom_call_target="tpu_custom_call" | custom-call | flops 3019898880 | bytes 14942208 | tf_op jit(solution)/shard_map/group/pallas_call | solution.py:304
  79.1 0.1 collective-permute-start.16
  79.2 0.5 collective-permute-start.6
  79.7 1.3 %collective-permute-done.20 = bf16[128,1536]{1,0:T(8,128)(2,1)} collective-permute-done((bf16[128,1536]{1,0:T(8,128)(2,1)}, bf16[128,1536]{1,0:T(8,128)(2,1)}, u32[]{:S(2)}, u32[]{:S(2)}) %collective-permute-start.20) | collective-permute-done | bytes 393248 | tf_op jit(solution)/shard_map/ppermute | solution.py:370
  81.0 1.5 %fusion.7 = bf16[128,1536]{1,0:T(8,128)(2,1)S(1)} fusion(bf16[128,1536]{1,0:T(8,128)(2,1)} %collective-permute-done.23, bf16[128,1536]{1,0:T(8,128)(2,1)} %collective-permute-done.20, bf16[128,1536]{1,0:T(8,128)(2,1)} %get-tuple-element.21.refs_8_, bf16[2,128,1536]{2,1,0:T(8,128)(2,1)} %copy-done.3), kind=kLoop, calls=%fused_computation.12 | loop fusion | flops 1572864 | bytes 1966080 | tf_op jit(solution)/shard_map/convert_element_type | solution.py:406
  82.5 0.4 collective-permute-start.24
  82.9 0.0 collective-permute-done.16
  82.9 1.2 %fusion.11 = bf16[128,1536]{1,0:T(8,128)(2,1)S(1)} fusion(bf16[128,1536]{1,0:T(8,128)(2,1)} %get-tuple-element.22, bf16[2,128,1536]{2,1,0:T(8,128)(2,1)} %collective-permute-done.16), kind=kLoop, calls=%fused_computation.18 | loop fusion | flops 786432 | bytes 1179648 | tf_op jit(solution)/shard_map/convert_element_type | solution.py:399
  84.1 0.8 collective-permute-start.17
  84.9 0.0 collective-permute-done.6
  84.9 2.1 %fusion.12.refs_0_ = bf16[128,1536]{1,0:T(8,128)(2,1)} fusion(bf16[128,1536]{1,0:T(8,128)(2,1)} %get-tuple-element.19, bf16[2,128,1536]{2,1,0:T(8,128)(2,1)S(1)} %collective-permute-done.6), kind=kLoop, calls=%fused_computation.20 | loop fusion | flops 786432 | bytes 1179648 | tf_op jit(solution)/shard_map/convert_element_type | solution.py:399
  87.0 6.8 %collective-permute-done.24 = bf16[128,1536]{1,0:T(8,128)(2,1)S(1)} collective-permute-done((bf16[128,1536]{1,0:T(8,128)(2,1)S(1)}, bf16[128,1536]{1,0:T(8,128)(2,1)S(1)}, u32[]{:S(2)}, u32[]{:S(2)}) %collective-permute-start.24) | collective-permute-done | bytes 393248 | tf_op jit(solution)/shard_map/ppermute | solution.py:370
  93.8 1.2 %collective-permute-done.17.refs_1_ = bf16[128,1536]{1,0:T(8,128)(2,1)S(1)} collective-permute-done((bf16[128,1536]{1,0:T(8,128)(2,1)S(1)}, bf16[128,1536]{1,0:T(8,128)(2,1)S(1)}, u32[]{:S(2)}, u32[]{:S(2)}) %collective-permute-start.17) | collective-permute-done | bytes 393248 | tf_op jit(solution)/shard_map/ppermute | solution.py:370
  95.0 0.7 copy-done.1
  95.8 2.1 %fusion.10 = bf16[128,1536]{1,0:T(8,128)(2,1)} fusion(bf16[128,1536]{1,0:T(8,128)(2,1)S(1)} %collective-permute-done.24, bf16[128,1536]{1,0:T(8,128)(2,1)S(1)} %collective-permute-done.17.refs_1_, bf16[128,1536]{1,0:T(8,128)(2,1)} %get-tuple-element.24, bf16[2,128,1536]{2,1,0:T(8,128)(2,1)} %collective-permute-done.16), kind=kLoop, calls=%fused_computation.16 | loop fusion | flops 1572864 | bytes 1966080 | tf_op jit(solution)/shard_map/convert_element_type | solution.py:406
  97.8 1.1 collective-permute-start.25
  98.9 0.5 collective-permute-start.18
  99.4 9.6 %collective-permute-done.25 = bf16[128,1536]{1,0:T(8,128)(2,1)} collective-permute-done((bf16[128,1536]{1,0:T(8,128)(2,1)}, bf16[128,1536]{1,0:T(8,128)(2,1)}, u32[]{:S(2)}, u32[]{:S(2)}) %collective-permute-start.25) | collective-permute-done | bytes 393248 | tf_op jit(solution)/shard_map/ppermute | solution.py:370
  109.0 0.2 collective-permute-done.18
  109.2 2.2 %fusion.15 = bf16[128,1536]{1,0:T(8,128)(2,1)} fusion(bf16[128,1536]{1,0:T(8,128)(2,1)} %collective-permute-done.25, bf16[128,1536]{1,0:T(8,128)(2,1)S(1)} %collective-permute-done.18, bf16[128,1536]{1,0:T(8,128)(2,1)} %get-tuple-element.17.refs_1_.refs_8_, bf16[2,128,1536]{2,1,0:T(8,128)(2,1)} %copy-done.4), kind=kLoop, calls=%fused_computation.24 | loop fusion | flops 1572864 | bytes 1966080 | tf_op jit(solution)/shard_map/convert_element_type | solution.py:406
  (27 shorter events, 0.1 us)
Async XLA Ops:
  1.8 4.6 %copy-start = (bf16[136,1536]{1,0:T(8,128)(2,1)}, bf16[136,1536]{1,0:T(8,128)(2,1)S(1)}, u32[]{:S(2)}) copy-start(bf16[136,1536]{1,0:T(8,128)(2,1)S(1)} %fusion.16.refs_0_) | copy-start | bytes 1253380
  1.8 12.7 %collective-permute-start = (bf16[136,1536]{1,0:T(8,128)(2,1)S(1)}, bf16[136,1536]{1,0:T(8,128)(2,1)S(1)}, u32[]{:S(2)}, u32[]{:S(2)}) collective-permute-start(bf16[136,1536]{1,0:T(8,128)(2,1)S(1)} %fusion.16.refs_0_), channel_id=1, source_target_pairs={{0,2},{1,3},{2,0},{3,1},{4,6},{5,7},{6,4},{7,5},{8,10},{9,11},{10,... | collective-permute-start | bytes 1253384 | tf_op jit(solution)/shard_map/ppermute | solution.py:370
  4.8 12.1 %collective-permute-start.3 = (bf16[136,1536]{1,0:T(8,128)(2,1)S(1)}, bf16[136,1536]{1,0:T(8,128)(2,1)}, u32[]{:S(2)}, u32[]{:S(2)}) collective-permute-start(bf16[136,1536]{1,0:T(8,128)(2,1)S(1)} %fusion.16.refs_0_), channel_id=1, source_target_pairs={{0,4},{1,5},{2,6},{3,7},{4,12},{5,13},{6,14},{7,15},{8,0},{9,1},{1... | collective-permute-start | bytes 1253384 | tf_op jit(solution)/shard_map/ppermute | solution.py:370
  6.4 12.5 %collective-permute-start.1 = (bf16[136,1536]{1,0:T(8,128)(2,1)S(1)}, bf16[136,1536]{1,0:T(8,128)(2,1)S(1)}, u32[]{:S(2)}, u32[]{:S(2)}) collective-permute-start(bf16[136,1536]{1,0:T(8,128)(2,1)S(1)} %fusion.16.refs_0_), channel_id=1, source_target_pairs={{0,1},{1,0},{2,3},{3,2},{4,5},{5,4},{6,7},{7,6},{8,9},{9,8},{10,11... | collective-permute-start | bytes 1253384 | tf_op jit(solution)/shard_map/ppermute | solution.py:370
  14.4 4.4 %copy-start.5 = (bf16[136,1536]{1,0:T(8,128)(2,1)}, bf16[136,1536]{1,0:T(8,128)(2,1)S(1)}, u32[]{:S(2)}) copy-start(bf16[136,1536]{1,0:T(8,128)(2,1)S(1)} %collective-permute-done.refs_1_) | copy-start | bytes 1253380
  14.4 4.4 %collective-permute-start.2 = (bf16[136,1536]{1,0:T(8,128)(2,1)S(1)}, bf16[136,1536]{1,0:T(8,128)(2,1)S(1)}, u32[]{:S(2)}, u32[]{:S(2)}) collective-permute-start(bf16[136,1536]{1,0:T(8,128)(2,1)S(1)} %collective-permute-done.refs_1_), channel_id=1, source_target_pairs={{0,1},{1,0},{2,3},{3,2},{4,5},{5,4},{6,7},{7,6},{8,9},{9,8},{10,11... | collective-permute-start | bytes 1253384 | tf_op jit(solution)/shard_map/ppermute | solution.py:370
  16.9 11.6 %collective-permute-start.4 = (bf16[136,1536]{1,0:T(8,128)(2,1)}, bf16[136,1536]{1,0:T(8,128)(2,1)}, u32[]{:S(2)}, u32[]{:S(2)}) collective-permute-start(bf16[136,1536]{1,0:T(8,128)(2,1)} %collective-permute-done.3.refs_0_), channel_id=1, source_target_pairs={{0,2},{1,3},{2,0},{3,1},{4,6},{5,7},{6,4},{7,5},{8,10},{9,11},{10,... | collective-permute-start | bytes 1253384 | tf_op jit(solution)/shard_map/ppermute | solution.py:370
  18.0 16.7 %collective-permute-start.8 = (bf16[136,1536]{1,0:T(8,128)(2,1)}, bf16[136,1536]{1,0:T(8,128)(2,1)}, u32[]{:S(2)}, u32[]{:S(2)}) collective-permute-start(bf16[136,1536]{1,0:T(8,128)(2,1)} %collective-permute-done.3.refs_0_), channel_id=1, source_target_pairs={{0,1},{1,0},{2,3},{3,2},{4,5},{5,4},{6,7},{7,6},{8,9},{9,8},{10,11... | collective-permute-start | bytes 1253384 | tf_op jit(solution)/shard_map/ppermute | solution.py:370
  18.1 13.3 %collective-permute-start.5 = (bf16[136,1536]{1,0:T(8,128)(2,1)}, bf16[136,1536]{1,0:T(8,128)(2,1)}, u32[]{:S(2)}, u32[]{:S(2)}) collective-permute-start(bf16[136,1536]{1,0:T(8,128)(2,1)} %collective-permute-done.3.refs_0_), channel_id=1, source_target_pairs={{0,4},{1,5},{2,6},{3,7},{4,12},{5,13},{6,14},{7,15},{8,0},{9,1},{1... | collective-permute-start | bytes 1253384 | tf_op jit(solution)/shard_map/ppermute | solution.py:370
  18.9 0.8 copy-start.6
  19.6 0.8 copy-start.7
  28.5 6.2 %collective-permute-start.9 = (bf16[136,1536]{1,0:T(8,128)(2,1)}, bf16[136,1536]{1,0:T(8,128)(2,1)}, u32[]{:S(2)}, u32[]{:S(2)}) collective-permute-start(bf16[136,1536]{1,0:T(8,128)(2,1)} %after.7.refs_1_), channel_id=1, source_target_pairs={{0,1},{1,0},{2,3},{3,2},{4,5},{5,4},{6,7},{7,6},{8,9},{9,8},{10,11... | collective-permute-start | bytes 1253384 | tf_op jit(solution)/shard_map/ppermute | solution.py:370
  31.4 12.4 %collective-permute-start.7 = (bf16[136,1536]{1,0:T(8,128)(2,1)}, bf16[136,1536]{1,0:T(8,128)(2,1)}, u32[]{:S(2)}, u32[]{:S(2)}) collective-permute-start(bf16[136,1536]{1,0:T(8,128)(2,1)} %after.8.refs_2_.refs_0_), channel_id=1, source_target_pairs={{0,4},{1,5},{2,6},{3,7},{4,12},{5,13},{6,14},{7,15},{8,0},{9,1},{1... | collective-permute-start | bytes 1253384 | tf_op jit(solution)/shard_map/ppermute | solution.py:370
  33.2 12.0 %collective-permute-start.10 = (bf16[136,1536]{1,0:T(8,128)(2,1)}, bf16[136,1536]{1,0:T(8,128)(2,1)}, u32[]{:S(2)}, u32[]{:S(2)}) collective-permute-start(bf16[136,1536]{1,0:T(8,128)(2,1)} %after.8.refs_2_.refs_0_), channel_id=1, source_target_pairs={{0,2},{1,3},{2,0},{3,1},{4,6},{5,7},{6,4},{7,5},{8,10},{9,11},{10,... | collective-permute-start | bytes 1253384 | tf_op jit(solution)/shard_map/ppermute | solution.py:370
  45.3 3.6 %collective-permute-start.21 = (bf16[2,128,1536]{2,1,0:T(8,128)(2,1)}, bf16[2,128,1536]{2,1,0:T(8,128)(2,1)S(1)}, u32[]{:S(2)}, u32[]{:S(2)}) collective-permute-start(bf16[2,128,1536]{2,1,0:T(8,128)(2,1)} %after.13), channel_id=1, source_target_pairs={{0,1},{1,0},{2,3},{3,2},{4,5},{5,4},{6,7},{7,6},{8,9},{9,8},{10,11... | collective-permute-start | bytes 2359304 | tf_op jit(solution)/shard_map/ppermute | solution.py:370
  45.3 7.8 %collective-permute-start.14 = (bf16[136,1536]{1,0:T(8,128)(2,1)}, bf16[136,1536]{1,0:T(8,128)(2,1)}, u32[]{:S(2)}, u32[]{:S(2)}) collective-permute-start(bf16[136,1536]{1,0:T(8,128)(2,1)} %after.8.refs_2_.refs_0_), channel_id=1, source_target_pairs={{0,1},{1,0},{2,3},{3,2},{4,5},{5,4},{6,7},{7,6},{8,9},{9,8},{10,11... | collective-permute-start | bytes 1253384 | tf_op jit(solution)/shard_map/ppermute | solution.py:370
  45.8 7.3 %collective-permute-start.15 = (bf16[136,1536]{1,0:T(8,128)(2,1)}, bf16[136,1536]{1,0:T(8,128)(2,1)}, u32[]{:S(2)}, u32[]{:S(2)}) collective-permute-start(bf16[136,1536]{1,0:T(8,128)(2,1)} %collective-permute-done.10.refs_1_), channel_id=1, source_target_pairs={{0,1},{1,0},{2,3},{3,2},{4,5},{5,4},{6,7},{7,6},{8,9},{9,8},{10,11... | collective-permute-start | bytes 1253384 | tf_op jit(solution)/shard_map/ppermute | solution.py:370
  45.8 15.5 %collective-permute-start.11 = (bf16[136,1536]{1,0:T(8,128)(2,1)}, bf16[136,1536]{1,0:T(8,128)(2,1)}, u32[]{:S(2)}, u32[]{:S(2)}) collective-permute-start(bf16[136,1536]{1,0:T(8,128)(2,1)} %collective-permute-done.10.refs_1_), channel_id=1, source_target_pairs={{0,4},{1,5},{2,6},{3,7},{4,12},{5,13},{6,14},{7,15},{8,0},{9,1},{1... | collective-permute-start | bytes 1253384 | tf_op jit(solution)/shard_map/ppermute | solution.py:370
  48.8 0.9 copy-start.2
  51.6 11.5 %collective-permute-start.22 = (bf16[128,1536]{1,0:T(8,128)(2,1)}, bf16[128,1536]{1,0:T(8,128)(2,1)}, u32[]{:S(2)}, u32[]{:S(2)}) collective-permute-start(bf16[128,1536]{1,0:T(8,128)(2,1)} %fusion.1), channel_id=1, source_target_pairs={{0,2},{1,3},{2,0},{3,1},{4,6},{5,7},{6,4},{7,5},{8,10},{9,11},{10,... | collective-permute-start | bytes 1179656 | tf_op jit(solution)/shard_map/ppermute | solution.py:370
  61.3 5.5 %collective-permute-start.19 = (bf16[2,128,1536]{2,1,0:T(8,128)(2,1)}, bf16[2,128,1536]{2,1,0:T(8,128)(2,1)S(1)}, u32[]{:S(2)}, u32[]{:S(2)}) collective-permute-start(bf16[2,128,1536]{2,1,0:T(8,128)(2,1)} %after.12), channel_id=1, source_target_pairs={{0,1},{1,0},{2,3},{3,2},{4,5},{5,4},{6,7},{7,6},{8,9},{9,8},{10,11... | collective-permute-start | bytes 2359304 | tf_op jit(solution)/shard_map/ppermute | solution.py:370
  61.4 9.7 %collective-permute-start.12 = (bf16[136,1536]{1,0:T(8,128)(2,1)}, bf16[136,1536]{1,0:T(8,128)(2,1)}, u32[]{:S(2)}, u32[]{:S(2)}) collective-permute-start(bf16[136,1536]{1,0:T(8,128)(2,1)} %after.10.refs_0_.refs_2_), channel_id=1, source_target_pairs={{0,1},{1,0},{2,3},{3,2},{4,5},{5,4},{6,7},{7,6},{8,9},{9,8},{10,11... | collective-permute-start | bytes 1253384 | tf_op jit(solution)/shard_map/ppermute | solution.py:370
  61.9 9.2 %collective-permute-start.13 = (bf16[136,1536]{1,0:T(8,128)(2,1)}, bf16[136,1536]{1,0:T(8,128)(2,1)}, u32[]{:S(2)}, u32[]{:S(2)}) collective-permute-start(bf16[136,1536]{1,0:T(8,128)(2,1)} %collective-permute-done.11.refs_1_), channel_id=1, source_target_pairs={{0,1},{1,0},{2,3},{3,2},{4,5},{5,4},{6,7},{7,6},{8,9},{9,8},{10,11... | collective-permute-start | bytes 1253384 | tf_op jit(solution)/shard_map/ppermute | solution.py:370
  65.2 14.5 %collective-permute-start.23 = (bf16[128,1536]{1,0:T(8,128)(2,1)}, bf16[128,1536]{1,0:T(8,128)(2,1)}, u32[]{:S(2)}, u32[]{:S(2)}) collective-permute-start(bf16[128,1536]{1,0:T(8,128)(2,1)} %fusion.3), channel_id=1, source_target_pairs={{0,4},{1,5},{2,6},{3,7},{4,12},{5,13},{6,14},{7,15},{8,0},{9,1},{1... | collective-permute-start | bytes 1179656 | tf_op jit(solution)/shard_map/ppermute | solution.py:370
  66.8 0.9 copy-start.3
  69.5 11.5 %collective-permute-start.20 = (bf16[128,1536]{1,0:T(8,128)(2,1)}, bf16[128,1536]{1,0:T(8,128)(2,1)}, u32[]{:S(2)}, u32[]{:S(2)}) collective-permute-start(bf16[128,1536]{1,0:T(8,128)(2,1)} %fusion.4), channel_id=1, source_target_pairs={{0,2},{1,3},{2,0},{3,1},{4,6},{5,7},{6,4},{7,5},{8,10},{9,11},{10,... | collective-permute-start | bytes 1179656 | tf_op jit(solution)/shard_map/ppermute | solution.py:370
  79.1 3.8 %collective-permute-start.16 = (bf16[2,128,1536]{2,1,0:T(8,128)(2,1)}, bf16[2,128,1536]{2,1,0:T(8,128)(2,1)}, u32[]{:S(2)}, u32[]{:S(2)}) collective-permute-start(bf16[2,128,1536]{2,1,0:T(8,128)(2,1)} %get-tuple-element.23), channel_id=1, source_target_pairs={{0,1},{1,0},{2,3},{3,2},{4,5},{5,4},{6,7},{7,6},{8,9},{9,8},{10,11... | collective-permute-start | bytes 2359304 | tf_op jit(solution)/shard_map/ppermute | solution.py:370
  79.2 5.7 %collective-permute-start.6 = (bf16[2,128,1536]{2,1,0:T(8,128)(2,1)}, bf16[2,128,1536]{2,1,0:T(8,128)(2,1)S(1)}, u32[]{:S(2)}, u32[]{:S(2)}) collective-permute-start(bf16[2,128,1536]{2,1,0:T(8,128)(2,1)} %after.9), channel_id=1, source_target_pairs={{0,1},{1,0},{2,3},{3,2},{4,5},{5,4},{6,7},{7,6},{8,9},{9,8},{10,11... | collective-permute-start | bytes 2359304 | tf_op jit(solution)/shard_map/ppermute | solution.py:370
  82.5 11.3 %collective-permute-start.24 = (bf16[128,1536]{1,0:T(8,128)(2,1)S(1)}, bf16[128,1536]{1,0:T(8,128)(2,1)S(1)}, u32[]{:S(2)}, u32[]{:S(2)}) collective-permute-start(bf16[128,1536]{1,0:T(8,128)(2,1)S(1)} %fusion.7), channel_id=1, source_target_pairs={{0,4},{1,5},{2,6},{3,7},{4,12},{5,13},{6,14},{7,15},{8,0},{9,1},{1... | collective-permute-start | bytes 1179656 | tf_op jit(solution)/shard_map/ppermute | solution.py:370
  84.1 10.9 %collective-permute-start.17 = (bf16[128,1536]{1,0:T(8,128)(2,1)S(1)}, bf16[128,1536]{1,0:T(8,128)(2,1)S(1)}, u32[]{:S(2)}, u32[]{:S(2)}) collective-permute-start(bf16[128,1536]{1,0:T(8,128)(2,1)S(1)} %fusion.11), channel_id=1, source_target_pairs={{0,2},{1,3},{2,0},{3,1},{4,6},{5,7},{6,4},{7,5},{8,10},{9,11},{10,... | collective-permute-start | bytes 1179656 | tf_op jit(solution)/shard_map/ppermute | solution.py:370
  84.9 12.9 %copy-start.4 = (bf16[2,128,1536]{2,1,0:T(8,128)(2,1)}, bf16[2,128,1536]{2,1,0:T(8,128)(2,1)S(1)}, u32[]{:S(2)}) copy-start(bf16[2,128,1536]{2,1,0:T(8,128)(2,1)S(1)} %collective-permute-done.6) | copy-start | bytes 2359300
  95.0 0.8 copy-start.1
  97.8 11.2 %collective-permute-start.25 = (bf16[128,1536]{1,0:T(8,128)(2,1)}, bf16[128,1536]{1,0:T(8,128)(2,1)}, u32[]{:S(2)}, u32[]{:S(2)}) collective-permute-start(bf16[128,1536]{1,0:T(8,128)(2,1)} %fusion.10), channel_id=1, source_target_pairs={{0,4},{1,5},{2,6},{3,7},{4,12},{5,13},{6,14},{7,15},{8,0},{9,1},{1... | collective-permute-start | bytes 1179656 | tf_op jit(solution)/shard_map/ppermute | solution.py:370
  98.9 10.3 %collective-permute-start.18 = (bf16[128,1536]{1,0:T(8,128)(2,1)}, bf16[128,1536]{1,0:T(8,128)(2,1)S(1)}, u32[]{:S(2)}, u32[]{:S(2)}) collective-permute-start(bf16[128,1536]{1,0:T(8,128)(2,1)} %after.11), channel_id=1, source_target_pairs={{0,2},{1,3},{2,0},{3,1},{4,6},{5,7},{6,4},{7,5},{8,10},{9,11},{10,... | collective-permute-start | bytes 1179656 | tf_op jit(solution)/shard_map/ppermute | solution.py:370

commit v8 on v7

--- a/solution.py
+++ b/solution.py
@@ -156,10 +156,12 @@
     )(scalars, codes, tokens, w_gate, w_down, spare_gate, spare_down)
 
 
-def group_kernel(failed, holders, *refs, others, tok, top, capacity):
-    blocks, weights_hbm, refs = refs[:4], refs[4:8], refs[8 + others :]
-    keep0, keep1, send, held, w_gate, w_down, spare_gate, spare_down = refs[:8]
-    rows_in, spare_in, hidden, spare_hidden, rows_out, dense, fetched, stored = refs[8:]
+def group_kernel(failed, holders, *refs, others, adds, tok, top, capacity):
+    blocks, weights_hbm, shares, refs = refs[:4], refs[4:8], refs[8 : 8 + 2 * adds], refs[8 + 2 * adds + others :]
+    keep0, keep1, send = refs[:3]
+    far, refs = refs[3 : 3 + adds], refs[3 + adds :]
+    held, w_gate, w_down, spare_gate, spare_down = refs[:5]
+    rows_in, spare_in, hidden, spare_hidden, rows_out, dense, summed, fetched, stored = refs[5:]
     width, inner = w_gate.shape
     tile = 512
     my_id, failed_id = lax.axis_index("expert"), failed[0]
@@ -180,18 +182,16 @@
     gate_copies = [
         fetch(gate_hbm.at[0, :, n : n + tile], w_gate.at[:, n : n + tile]) for n in range(0, inner, tile)
     ]
+    share_copies = []
+    if adds:
+        share_copies = [fetch(shares[0], summed.at[0]), fetch(shares[1].at[1], summed.at[1])]
     spare_copies = [
         fetch(spare_gate_hbm.at[0], spare_gate, False),
         fetch(spare_down_hbm.at[0], spare_down, False),
     ]
-
-    @pl.when(holds)
-    def _():
-        for copy in spare_copies:
-            copy.start()
-
     down_copies = [
-        fetch(down_hbm.at[0, :, n : n + tile], w_down.at[:, n : n + tile]) for n in range(0, width, tile)
+        fetch(down_hbm.at[0, :, n : n + tile], w_down.at[:, n : n + tile], False)
+        for n in range(0, width, tile)
     ]
 
     count = len(blocks)
@@ -247,9 +247,26 @@
 
     for i, n in enumerate(range(0, inner, tile)):
         gate_copies[i].wait()
+        if i == 0:
+
+            @pl.when(holds)
+            def _():
+                for copy in spare_copies:
+                    copy.start()
+
+        for copy in down_copies[i:] if n + tile >= inner else down_copies[i : i + 1]:
+            copy.start()
         hidden[:, n : n + tile] = gated_unit(
             jnp.dot(rows_in[...], w_gate[:, n : n + tile], preferred_element_type=jnp.float32)
         ).astype(jnp.bfloat16)
+    stores = []
+    if adds:
+        for copy in share_copies:
+            copy.wait()
+        total = summed[0].astype(jnp.float32) + summed[1].astype(jnp.float32)
+        summed[0] = total.astype(jnp.bfloat16)
+        stores.append(pltpu.make_async_copy(summed.at[0], far[0], stored.at[0]))
+        stores[0].start()
 
     @pl.when(holds)
     def _():
@@ -271,7 +288,6 @@
     def _():
         rows_out[:, capacity:, :] = jnp.zeros((count, capacity, width), jnp.bfloat16)
 
-    stores = []
     for i, n in enumerate(range(0, width, tile)):
         down_copies[i].wait()
         result = jnp.dot(hidden[...], w_down[:, n : n + tile], preferred_element_type=jnp.float32)
@@ -294,20 +310,20 @@
         copy.wait()
 
 
-def run_group(failed, holders, blocks, weights, earlier, tok, top, capacity):
+def run_group(failed, holders, blocks, weights, shares, earlier, tok, top, capacity):
     width, inner, spare = weights[0].shape[1], weights[0].shape[2], weights[2].shape[2]
-    count = len(blocks)
+    count, adds = len(blocks), len(shares) // 2
     rows = count * capacity
     hbm = pl.BlockSpec(memory_space=pl.ANY)
     smem = pl.BlockSpec(memory_space=pltpu.SMEM)
     block = pltpu.HBM((tok, width), jnp.bfloat16)
     return pl.pallas_call(
         functools.partial(
-            group_kernel, others=len(earlier), tok=tok, top=top, capacity=capacity
+            group_kernel, others=len(earlier), adds=adds, tok=tok, top=top, capacity=capacity
         ),
-        out_shape=(block, block, pltpu.HBM((2, tok, width), jnp.bfloat16)),
-        in_specs=[smem, smem] + [hbm] * (count + 4 + len(earlier)),
-        out_specs=(hbm, hbm, hbm),
+        out_shape=(block, block, pltpu.HBM((2, tok, width), jnp.bfloat16)) + (block,) * adds,
+        in_specs=[smem, smem] + [hbm] * (count + 4 + len(shares) + len(earlier)),
+        out_specs=(hbm,) * (3 + adds),
         scratch_shapes=[
             pltpu.VMEM((count, *blocks[0].shape), jnp.bfloat16),
             pltpu.VMEM((width, inner), jnp.bfloat16),
@@ -320,8 +336,9 @@
             pltpu.VMEM((rows, spare), jnp.bfloat16),
             pltpu.VMEM((count, 2 * capacity, width), jnp.bfloat16),
             pltpu.VMEM((count, tok, width), jnp.bfloat16),
-            pltpu.SemaphoreType.DMA((count + inner // 512 + width // 512 + 2,)),
-            pltpu.SemaphoreType.DMA((count * (width // 512),)),
+            pltpu.VMEM((2, tok, width), jnp.bfloat16),
+            pltpu.SemaphoreType.DMA((count + inner // 512 + width // 512 + 4,)),
+            pltpu.SemaphoreType.DMA((1 + count * (width // 512),)),
         ],
         compiler_params=pltpu.CompilerParams(vmem_limit_bytes=VMEM_GRANT),
         cost_estimate=pl.CostEstimate(
@@ -330,7 +347,7 @@
             transcendentals=rows * inner,
         ),
         name="group",
-    )(failed, holders, *map(in_hbm, (*blocks, *weights, *earlier)))
+    )(failed, holders, *map(in_hbm, (*blocks, *weights, *shares, *earlier)))
 
 
 def in_hbm(array):
@@ -373,38 +390,43 @@
     meta = meta.astype(jnp.bfloat16).reshape(1, 3 * top * tok)
     meta = jnp.pad(meta, ((0, 7), (0, width - 3 * top * tok)))
     held = [jnp.concatenate([tokens, meta], axis=0)]
-    across, results = [], []
-    for k in range(steps):
-        if k > 0:
-            held.append(move(held[-1], round_ring))
-            if k > 1:
-                held[k] = come_after(held[k], results[k - 2][0])
-        if 1 < k == steps - 1:
-            across.append(move(across[-1], round_ring))
-        else:
-            across.append(move(held[k], over_y))
+    held.append(move(held[0], round_ring))
+    across, kept, got, from_y = [], [], [], []
+
+    def add_group(k, shares):
+        blocks = (held[k], across[k], move(held[k], over_core), move(across[k], over_core))
+        keep0, keep1, send, *summed = run_group(
+            failed, holders, blocks, weights, shares, (), tok, top, capacity
+        )
+        kept.append((keep0, keep1))
+        from_y.extend(move(a, over_y) for a in summed)
+        return send
+
+    across.append(move(held[0], over_y))
+    send = add_group(0, ())
+    for k in range(1, steps):
+        last = k == steps - 1
+        across.append(move(across[-1], round_ring) if last else move(held[k], over_y))
         if k == 1:
-            across[1] = come_after(across[1], results[0][0])
-        blocks = (held[k], across[k], move(held[k], over_core), move(across[k], over_core))
-        earlier = [results[-1][0]] if results else []
-        results.append(run_group(failed, holders, blocks, weights, earlier, tok, top, capacity))
+            across[1] = come_after(across[1], kept[0][0])
+        if not last:
+            held.append(come_after(move(held[k], round_ring), kept[k - 1][0]))
+        send = come_after(send, across[k], held[min(k + 1, steps - 1)], *from_y[-2:-1])
+        got.append(move(send, over_core))
+        send = add_group(k, (kept[-1][1], got[-1]))
+    got.append(move(come_after(send, *from_y[-2:-1]), over_core))
 
     f32 = lambda a: a.astype(jnp.float32)
-    passing = None
-    for k in list(range(1, steps)) + [0]:
-        keep0, keep1, send = results[k]
-        if k < steps - 1:
-            send = come_after(send, across[k + 1], held[min(k + 2, steps - 1)])
-        got = move(send, over_core)
-        far = (f32(keep1) + f32(got[1])).astype(jnp.bfloat16)
-        if k == 0 and steps > 1:
-            far = come_after(far, from_y)
-        from_y = move(far, over_y)
-        total = f32(keep0) + f32(got[0]) + f32(from_y)
-        if passing is not None:
-            total = total + f32(move(passing, round_ring))
-        passing = total.astype(jnp.bfloat16)
-    return passing
+    last = steps - 1
+    summed = (f32(kept[last][1]) + f32(got[last][1])).astype(jnp.bfloat16)
+    from_y.append(move(summed, over_y))
+    total = lambda k: f32(kept[k][0]) + f32(got[k][0]) + f32(from_y[k])
+    result = total(0)
+    place = {a: i for i, a in enumerate(order)}
+    for k in range(1, steps):
+        home = [(d, order[(place[d // 4] - k) % steps] * 4 + d % 4) for d in range(owners)]
+        result = result + f32(move(total(k).astype(jnp.bfloat16), home))
+    return result.astype(jnp.bfloat16)
 
 
 def shards(
@@ -427,7 +449,7 @@
     holds = jnp.any(holder_row == my_index).astype(jnp.int32)
     scalars = jnp.stack([my_index, failed_id, holds])
     weights = (w_gate, w_down, spare_gate, spare_down)
-    if owners % 4 == 0 and owners <= 32 and 3 * top_count * tok_count <= tokens.shape[1]:
+    if 12 <= owners <= 32 and owners % 4 == 0 and 3 * top_count * tok_count <= tokens.shape[1]:
         return by_permutes(
             failed_device, replica_holders.T, tokens, expert_ids, gate_levels, weights, owners, capacity
         )

time: 112 us -> 117 us (1.045)
  waiting for transfers between devices: 37.1 us -> 48.7 us
  other arithmetic: 16.7 us -> 8.8 us
  Pallas kernels: 32.5 us -> 37.3 us
  local copies, waits for them, and re-layouts: 4.09 us -> 1.55 us
    ppermute x26, waiting for transfers between devices: 37.1 us -> 48.7 us  [by_permutes(): move = lambda a, pairs: lax.ppermute(a, 'expert', pairs)]
    convert_element_type x8 -> x5, other arithmetic: 14.9 us -> 7.06 us  [the longest x3 3.81 us: by_permutes(): result = result + f32(move(total(k).astype(jnp.bfloat16), home))]
    pallas_call x4, Pallas kernels: 32.5 us -> 37.3 us  [run_group(): pl.pallas_call(functools.partial(group_kernel, others=len(earlier), adds=...]
    unnamed x17 -> x11, local copies, waits for them, and re-layouts: 4.09 us -> 1.55 us
  transfers between devices with their start and end apart: 26 -> 26, of which waited for: 12 -> 12; matrix products, arithmetic and copies ran while one was open for 10% -> 4% of each run, Pallas kernels for 29% -> 32%
where the time goes in v8:
time: 117 us
  waiting for transfers between devices  48.7 us (42%)
  Pallas kernels  37.3 us (32%)
  starting transfers between devices  19.6 us (17%)
  other arithmetic  8.8 us (8%)
  local copies, waits for them, and re-layouts  1.55 us (1%)
    ppermute x26, waiting for transfers between devices, by_permutes(): move = lambda a, pairs: lax.ppermute(a, 'expert', pairs)  48.7 us
    pallas_call x4, Pallas kernels, run_group(): pl.pallas_call(functools.partial(group_kernel, others=len(earlier), adds=...  37.3 us
    ppermute x26, starting transfers between devices, by_permutes(): move = lambda a, pairs: lax.ppermute(a, 'expert', pairs)  19.6 us
    convert_element_type x3, other arithmetic, by_permutes(): result = result + f32(move(total(k).astype(jnp.bfloat16), home))  3.81 us
  transfers between devices with their start and end apart: 26, of which 12 were waited for; matrix products, arithmetic and copies ran while one was open for 4% of the time, Pallas kernels for 32%

profile of v8, /device:TPU:0, one launch (start us, length us, event | category | flops | bytes accessed | tf_op | source)
XLA Modules:
  0.0 116.7 jit_solution(931805447682751440)
XLA Ops:
  0.0 0.7 fusion.14
  0.7 1.0 fusion.13.refs_0_
  1.8 3.0 %collective-permute-start = (bf16[136,1536]{1,0:T(8,128)(2,1)S(1)}, bf16[136,1536]{1,0:T(8,128)(2,1)S(1)}, u32[]{:S(2)}, u32[]{:S(2)}) collective-permute-start(bf16[136,1536]{1,0:T(8,128)(2,1)S(1)} %fusion.13.refs_0_), channel_id=1, source_target_pairs={{0,2},{1,3},{2,0},{3,1},{4,6},{5,7},{6,4},{7,5},{8,10},{9,11},{10,... | collective-permute-start | bytes 1253384 | tf_op jit(solution)/shard_map/ppermute | solution.py:387
  4.8 1.6 %collective-permute-start.3 = (bf16[136,1536]{1,0:T(8,128)(2,1)S(1)}, bf16[136,1536]{1,0:T(8,128)(2,1)}, u32[]{:S(2)}, u32[]{:S(2)}) collective-permute-start(bf16[136,1536]{1,0:T(8,128)(2,1)S(1)} %fusion.13.refs_0_), channel_id=1, source_target_pairs={{0,4},{1,5},{2,6},{3,7},{4,12},{5,13},{6,14},{7,15},{8,0},{9,1},{1... | collective-permute-start | bytes 1253384 | tf_op jit(solution)/shard_map/ppermute | solution.py:387
  6.4 0.0 collective-permute-start.1
  6.4 8.1 %collective-permute-done.refs_1_ = bf16[136,1536]{1,0:T(8,128)(2,1)S(1)} collective-permute-done((bf16[136,1536]{1,0:T(8,128)(2,1)S(1)}, bf16[136,1536]{1,0:T(8,128)(2,1)S(1)}, u32[]{:S(2)}, u32[]{:S(2)}) %collective-permute-start) | collective-permute-done | bytes 417824 | tf_op jit(solution)/shard_map/ppermute | solution.py:387
  14.4 0.0 collective-permute-start.2
  14.5 2.5 %collective-permute-done.3.refs_0_ = bf16[136,1536]{1,0:T(8,128)(2,1)} collective-permute-done((bf16[136,1536]{1,0:T(8,128)(2,1)S(1)}, bf16[136,1536]{1,0:T(8,128)(2,1)}, u32[]{:S(2)}, u32[]{:S(2)}) %collective-permute-start.3) | collective-permute-done | bytes 417824 | tf_op jit(solution)/shard_map/ppermute | solution.py:387
  16.9 0.7 collective-permute-start.5
  17.6 0.5 collective-permute-start.4
  18.7 0.0 collective-permute-done.1.refs_2_
  18.8 0.0 collective-permute-done.2.refs_3_
  18.8 0.7 copy-done.3
  19.5 0.8 copy-done.4
  20.3 9.2 %group.4 = (bf16[128,1536]{1,0:T(8,128)(2,1)}, bf16[128,1536]{1,0:T(8,128)(2,1)}, bf16[2,128,1536]{2,1,0:T(8,128)(2,1)}) custom-call(s32[1]{0:T(128)S(6)} %copy.27.failed, s32[4,16]{1,0:T(4,128)} %bitcast.38, bf16[136,1536]{1,0:T(8,128)(2,1)} %copy-done.1, bf16[136,1536]{1,0:T(8,128)(2,1)} %copy-done.2, bf16[136,1536]{1,0:T(8,128)(2,1)} %copy-done.3, ...), custom_call_target="tpu_custom_call" | custom-call | flops 3019898880 | bytes 14942208 | tf_op jit(solution)/shard_map/group/pallas_call | solution.py:320
  29.5 0.0 collective-permute-done.5.refs_0_
  29.5 0.0 collective-permute-done.4.refs_0_
  29.5 0.1 collective-permute-start.6
  29.6 0.5 collective-permute-start.7
  30.1 0.1 collective-permute-start.8
  30.2 2.4 %collective-permute-start.11 = (bf16[136,1536]{1,0:T(8,128)(2,1)}, bf16[136,1536]{1,0:T(8,128)(2,1)}, u32[]{:S(2)}, u32[]{:S(2)}) collective-permute-start(bf16[136,1536]{1,0:T(8,128)(2,1)} %after.8.refs_2_.refs_0_), channel_id=1, source_target_pairs={{0,4},{1,5},{2,6},{3,7},{4,12},{5,13},{6,14},{7,15},{8,0},{9,1},{1... | collective-permute-start | bytes 1253384 | tf_op jit(solution)/shard_map/ppermute | solution.py:387
  32.6 1.5 %collective-permute-start.10 = (bf16[136,1536]{1,0:T(8,128)(2,1)}, bf16[136,1536]{1,0:T(8,128)(2,1)}, u32[]{:S(2)}, u32[]{:S(2)}) collective-permute-start(bf16[136,1536]{1,0:T(8,128)(2,1)} %after.8.refs_2_.refs_0_), channel_id=1, source_target_pairs={{0,2},{1,3},{2,0},{3,1},{4,6},{5,7},{6,4},{7,5},{8,10},{9,11},{10,... | collective-permute-start | bytes 1253384 | tf_op jit(solution)/shard_map/ppermute | solution.py:387
  34.1 0.0 collective-permute-done.7.refs_2_
  34.1 0.0 collective-permute-done.8.refs_3_
  34.1 0.0 collective-permute-done.6.refs_9_
  34.2 9.3 %group.5 = (bf16[128,1536]{1,0:T(8,128)(2,1)}, bf16[128,1536]{1,0:T(8,128)(2,1)}, bf16[2,128,1536]{2,1,0:T(8,128)(2,1)}, bf16[128,1536]{1,0:T(8,128)(2,1)}) custom-call(s32[1]{0:T(128)S(6)} %copy.27.failed, s32[4,16]{1,0:T(4,128)} %bitcast.39, bf16[136,1536]{1,0:T(8,128)(2,1)} %collective-permute-done.3.refs_0_, bf16[136,1536]{1,0:T(8,128)(2,1)} %after.7.refs_1_, ...), custom_call_target="tpu_custom_call" | custom-call | flops 3019898880 | bytes 14942208 | tf_op jit(solution)/shard_map/group/pallas_call | solution.py:320
  43.5 0.0 collective-permute-done.11.refs_0_
  43.5 1.2 %collective-permute-done.10.refs_1_ = bf16[136,1536]{1,0:T(8,128)(2,1)} collective-permute-done((bf16[136,1536]{1,0:T(8,128)(2,1)}, bf16[136,1536]{1,0:T(8,128)(2,1)}, u32[]{:S(2)}, u32[]{:S(2)}) %collective-permute-start.10) | collective-permute-done | bytes 417824 | tf_op jit(solution)/shard_map/ppermute | solution.py:387
  44.7 0.0 collective-permute-start.12
  44.7 0.5 collective-permute-start.13
  45.2 0.0 collective-permute-start.14
  45.2 0.4 collective-permute-start.17
  45.6 1.4 %collective-permute-start.9 = (bf16[128,1536]{1,0:T(8,128)(2,1)}, bf16[128,1536]{1,0:T(8,128)(2,1)}, u32[]{:S(2)}, u32[]{:S(2)}) collective-permute-start(bf16[128,1536]{1,0:T(8,128)(2,1)} %get-tuple-element.23), channel_id=1, source_target_pairs={{0,2},{1,3},{2,0},{3,1},{4,6},{5,7},{6,4},{7,5},{8,10},{9,11},{10,... | collective-permute-start | bytes 1179656 | tf_op jit(solution)/shard_map/ppermute | solution.py:387
  47.0 0.8 collective-permute-done.13.refs_2_
  47.9 0.6 collective-permute-done.14.refs_3_
  48.5 0.0 collective-permute-done.12.refs_9_
  48.5 9.5 %group.6 = (bf16[128,1536]{1,0:T(8,128)(2,1)}, bf16[128,1536]{1,0:T(8,128)(2,1)}, bf16[2,128,1536]{2,1,0:T(8,128)(2,1)}, bf16[128,1536]{1,0:T(8,128)(2,1)}) custom-call(s32[1]{0:T(128)S(6)} %copy.27.failed, s32[4,16]{1,0:T(4,128)} %bitcast.40, bf16[136,1536]{1,0:T(8,128)(2,1)} %after.8.refs_2_.refs_0_, bf16[136,1536]{1,0:T(8,128)(2,1)} %collective-permute-done.10.refs_1_, ...), custom_call_target="tpu_custom_call" | custom-call | flops 3019898880 | bytes 14942208 | tf_op jit(solution)/shard_map/group/pallas_call | solution.py:320
  58.0 0.5 collective-permute-done.17.refs_1_
  58.4 0.0 collective-permute-done.9.refs_3_
  58.4 0.0 collective-permute-start.18
  58.4 0.5 collective-permute-start.19
  59.0 0.1 collective-permute-start.20
  59.0 1.5 %collective-permute-start.15 = (bf16[128,1536]{1,0:T(8,128)(2,1)}, bf16[128,1536]{1,0:T(8,128)(2,1)}, u32[]{:S(2)}, u32[]{:S(2)}) collective-permute-start(bf16[128,1536]{1,0:T(8,128)(2,1)} %get-tuple-element.27), channel_id=1, source_target_pairs={{0,2},{1,3},{2,0},{3,1},{4,6},{5,7},{6,4},{7,5},{8,10},{9,11},{10,... | collective-permute-start | bytes 1179656 | tf_op jit(solution)/shard_map/ppermute | solution.py:387
  60.5 1.1 collective-permute-done.19.refs_2_
  61.7 0.6 collective-permute-done.20.refs_3_
  62.3 9.3 %group.7 = (bf16[128,1536]{1,0:T(8,128)(2,1)}, bf16[128,1536]{1,0:T(8,128)(2,1)}, bf16[2,128,1536]{2,1,0:T(8,128)(2,1)}, bf16[128,1536]{1,0:T(8,128)(2,1)}) custom-call(s32[1]{0:T(128)S(6)} %copy.27.failed, s32[4,16]{1,0:T(4,128)} %bitcast.41, bf16[136,1536]{1,0:T(8,128)(2,1)} %after.10.refs_2_.refs_0_, bf16[136,1536]{1,0:T(8,128)(2,1)} %collective-permute-done.17.refs_1_, ...), custom_call_target="tpu_custom_call" | custom-call | flops 3019898880 | bytes 14942208 | tf_op jit(solution)/shard_map/group/pallas_call | solution.py:320
  71.6 0.0 collective-permute-done.15.refs_1_
  71.6 0.0 copy-start
  71.6 0.1 collective-permute-start.23
  71.7 1.4 %fusion.7 = bf16[128,1536]{1,0:T(8,128)(2,1)S(1)} fusion(bf16[128,1536]{1,0:T(8,128)(2,1)} %collective-permute-done.15.refs_1_, bf16[128,1536]{1,0:T(8,128)(2,1)} %get-tuple-element.24.refs_1_, bf16[2,128,1536]{2,1,0:T(8,128)(2,1)} %collective-permute-done.12.refs_9_), kind=kLoop, calls=%fused_computation.12 | loop fusion | flops 1179648 | bytes 1572864 | tf_op jit(solution)/shard_map/convert_element_type | solution.py:428
  73.1 1.3 %collective-permute-start.16 = (bf16[128,1536]{1,0:T(8,128)(2,1)S(1)}, bf16[128,1536]{1,0:T(8,128)(2,1)S(1)}, u32[]{:S(2)}, u32[]{:S(2)}) collective-permute-start(bf16[128,1536]{1,0:T(8,128)(2,1)S(1)} %fusion.7), channel_id=1, source_target_pairs={{0,8},{1,9},{2,10},{3,11},{4,0},{5,1},{6,2},{7,3},{8,12},{9,13},{1... | collective-permute-start | bytes 1179656 | tf_op jit(solution)/shard_map/ppermute | solution.py:387
  74.4 1.6 %collective-permute-start.21 = (bf16[128,1536]{1,0:T(8,128)(2,1)}, bf16[128,1536]{1,0:T(8,128)(2,1)S(1)}, u32[]{:S(2)}, u32[]{:S(2)}) collective-permute-start(bf16[128,1536]{1,0:T(8,128)(2,1)} %get-tuple-element.31), channel_id=1, source_target_pairs={{0,2},{1,3},{2,0},{3,1},{4,6},{5,7},{6,4},{7,5},{8,10},{9,11},{10,... | collective-permute-start | bytes 1179656 | tf_op jit(solution)/shard_map/ppermute | solution.py:387
  76.0 1.1 fusion.1
  77.1 0.5 collective-permute-start.24
  77.5 9.0 %collective-permute-done.21 = bf16[128,1536]{1,0:T(8,128)(2,1)S(1)} collective-permute-done((bf16[128,1536]{1,0:T(8,128)(2,1)}, bf16[128,1536]{1,0:T(8,128)(2,1)S(1)}, u32[]{:S(2)}, u32[]{:S(2)}) %collective-permute-start.21) | collective-permute-done | bytes 393248 | tf_op jit(solution)/shard_map/ppermute | solution.py:387
  86.5 1.3 %fusion.5 = bf16[128,1536]{1,0:T(8,128)(2,1)S(1)} fusion(bf16[128,1536]{1,0:T(8,128)(2,1)S(1)} %collective-permute-done.21, bf16[128,1536]{1,0:T(8,128)(2,1)} %get-tuple-element.28, bf16[2,128,1536]{2,1,0:T(8,128)(2,1)} %collective-permute-done.18.refs_9_), kind=kLoop, calls=%fused_computation.9 | loop fusion | flops 1179648 | bytes 1572864 | tf_op jit(solution)/shard_map/convert_element_type | solution.py:428
  87.8 0.4 collective-permute-start.22
  88.2 6.0 %collective-permute-done.24 = bf16[128,1536]{1,0:T(8,128)(2,1)S(1)} collective-permute-done((bf16[128,1536]{1,0:T(8,128)(2,1)S(1)}, bf16[128,1536]{1,0:T(8,128)(2,1)S(1)}, u32[]{:S(2)}, u32[]{:S(2)}) %collective-permute-start.24) | collective-permute-done | bytes 393248 | tf_op jit(solution)/shard_map/ppermute | solution.py:387
  94.2 1.1 fusion.3
  95.3 0.9 collective-permute-start.25
  96.2 0.0 collective-permute-done.16
  96.2 4.9 %collective-permute-done.22 = bf16[128,1536]{1,0:T(8,128)(2,1)S(1)} collective-permute-done((bf16[128,1536]{1,0:T(8,128)(2,1)S(1)}, bf16[128,1536]{1,0:T(8,128)(2,1)S(1)}, u32[]{:S(2)}, u32[]{:S(2)}) %collective-permute-start.22) | collective-permute-done | bytes 393248 | tf_op jit(solution)/shard_map/ppermute | solution.py:387
  101.1 13.5 %collective-permute-done.25 = bf16[128,1536]{1,0:T(8,128)(2,1)S(1)} collective-permute-done((bf16[128,1536]{1,0:T(8,128)(2,1)S(1)}, bf16[128,1536]{1,0:T(8,128)(2,1)S(1)}, u32[]{:S(2)}, u32[]{:S(2)}) %collective-permute-start.25) | collective-permute-done | bytes 393248 | tf_op jit(solution)/shard_map/ppermute | solution.py:387
  114.6 2.2 %fusion.12 = bf16[128,1536]{1,0:T(8,128)(2,1)} fusion(bf16[128,1536]{1,0:T(8,128)(2,1)S(1)} %collective-permute-done.25, bf16[128,1536]{1,0:T(8,128)(2,1)S(1)} %collective-permute-done.22, bf16[128,1536]{1,0:T(8,128)(2,1)S(1)} %collective-permute-done.16, bf16[128,1536]{1,0:T(8,128)(2,1)} %collective-permute-done.9.refs_3_, ...), kind=kLoop, calls=%fused_computation.18 | loop fusion | flops 2359296 | bytes 2752512 | tf_op jit(solution)/shard_map/convert_element_type | solution.py:429
  (18 shorter events, 0.0 us)
Async XLA Ops:
  1.8 4.6 %copy-start.1 = (bf16[136,1536]{1,0:T(8,128)(2,1)}, bf16[136,1536]{1,0:T(8,128)(2,1)S(1)}, u32[]{:S(2)}) copy-start(bf16[136,1536]{1,0:T(8,128)(2,1)S(1)} %fusion.13.refs_0_) | copy-start | bytes 1253380
  1.8 12.7 %collective-permute-start = (bf16[136,1536]{1,0:T(8,128)(2,1)S(1)}, bf16[136,1536]{1,0:T(8,128)(2,1)S(1)}, u32[]{:S(2)}, u32[]{:S(2)}) collective-permute-start(bf16[136,1536]{1,0:T(8,128)(2,1)S(1)} %fusion.13.refs_0_), channel_id=1, source_target_pairs={{0,2},{1,3},{2,0},{3,1},{4,6},{5,7},{6,4},{7,5},{8,10},{9,11},{10,... | collective-permute-start | bytes 1253384 | tf_op jit(solution)/shard_map/ppermute | solution.py:387
  4.8 12.1 %collective-permute-start.3 = (bf16[136,1536]{1,0:T(8,128)(2,1)S(1)}, bf16[136,1536]{1,0:T(8,128)(2,1)}, u32[]{:S(2)}, u32[]{:S(2)}) collective-permute-start(bf16[136,1536]{1,0:T(8,128)(2,1)S(1)} %fusion.13.refs_0_), channel_id=1, source_target_pairs={{0,4},{1,5},{2,6},{3,7},{4,12},{5,13},{6,14},{7,15},{8,0},{9,1},{1... | collective-permute-start | bytes 1253384 | tf_op jit(solution)/shard_map/ppermute | solution.py:387
  6.4 12.4 %collective-permute-start.1 = (bf16[136,1536]{1,0:T(8,128)(2,1)S(1)}, bf16[136,1536]{1,0:T(8,128)(2,1)S(1)}, u32[]{:S(2)}, u32[]{:S(2)}) collective-permute-start(bf16[136,1536]{1,0:T(8,128)(2,1)S(1)} %fusion.13.refs_0_), channel_id=1, source_target_pairs={{0,1},{1,0},{2,3},{3,2},{4,5},{5,4},{6,7},{7,6},{8,9},{9,8},{10,11... | collective-permute-start | bytes 1253384 | tf_op jit(solution)/shard_map/ppermute | solution.py:387
  14.4 4.3 %copy-start.2 = (bf16[136,1536]{1,0:T(8,128)(2,1)}, bf16[136,1536]{1,0:T(8,128)(2,1)S(1)}, u32[]{:S(2)}) copy-start(bf16[136,1536]{1,0:T(8,128)(2,1)S(1)} %collective-permute-done.refs_1_) | copy-start | bytes 1253380
  14.4 4.3 %collective-permute-start.2 = (bf16[136,1536]{1,0:T(8,128)(2,1)S(1)}, bf16[136,1536]{1,0:T(8,128)(2,1)S(1)}, u32[]{:S(2)}, u32[]{:S(2)}) collective-permute-start(bf16[136,1536]{1,0:T(8,128)(2,1)S(1)} %collective-permute-done.refs_1_), channel_id=1, source_target_pairs={{0,1},{1,0},{2,3},{3,2},{4,5},{5,4},{6,7},{7,6},{8,9},{9,8},{10,11... | collective-permute-start | bytes 1253384 | tf_op jit(solution)/shard_map/ppermute | solution.py:387
  16.9 12.6 %collective-permute-start.5 = (bf16[136,1536]{1,0:T(8,128)(2,1)}, bf16[136,1536]{1,0:T(8,128)(2,1)}, u32[]{:S(2)}, u32[]{:S(2)}) collective-permute-start(bf16[136,1536]{1,0:T(8,128)(2,1)} %collective-permute-done.3.refs_0_), channel_id=1, source_target_pairs={{0,4},{1,5},{2,6},{3,7},{4,12},{5,13},{6,14},{7,15},{8,0},{9,1},{1... | collective-permute-start | bytes 1253384 | tf_op jit(solution)/shard_map/ppermute | solution.py:387
  17.6 11.9 %collective-permute-start.4 = (bf16[136,1536]{1,0:T(8,128)(2,1)}, bf16[136,1536]{1,0:T(8,128)(2,1)}, u32[]{:S(2)}, u32[]{:S(2)}) collective-permute-start(bf16[136,1536]{1,0:T(8,128)(2,1)} %collective-permute-done.3.refs_0_), channel_id=1, source_target_pairs={{0,2},{1,3},{2,0},{3,1},{4,6},{5,7},{6,4},{7,5},{8,10},{9,11},{10,... | collective-permute-start | bytes 1253384 | tf_op jit(solution)/shard_map/ppermute | solution.py:387
  18.8 0.8 copy-start.3
  19.5 0.8 copy-start.4
  29.5 4.6 %collective-permute-start.6 = (bf16[2,128,1536]{2,1,0:T(8,128)(2,1)}, bf16[2,128,1536]{2,1,0:T(8,128)(2,1)}, u32[]{:S(2)}, u32[]{:S(2)}) collective-permute-start(bf16[2,128,1536]{2,1,0:T(8,128)(2,1)} %after.9), channel_id=1, source_target_pairs={{0,1},{1,0},{2,3},{3,2},{4,5},{5,4},{6,7},{7,6},{8,9},{9,8},{10,11... | collective-permute-start | bytes 2359304 | tf_op jit(solution)/shard_map/ppermute | solution.py:387
  29.6 4.5 %collective-permute-start.7 = (bf16[136,1536]{1,0:T(8,128)(2,1)}, bf16[136,1536]{1,0:T(8,128)(2,1)}, u32[]{:S(2)}, u32[]{:S(2)}) collective-permute-start(bf16[136,1536]{1,0:T(8,128)(2,1)} %collective-permute-done.3.refs_0_), channel_id=1, source_target_pairs={{0,1},{1,0},{2,3},{3,2},{4,5},{5,4},{6,7},{7,6},{8,9},{9,8},{10,11... | collective-permute-start | bytes 1253384 | tf_op jit(solution)/shard_map/ppermute | solution.py:387
  30.1 4.0 %collective-permute-start.8 = (bf16[136,1536]{1,0:T(8,128)(2,1)}, bf16[136,1536]{1,0:T(8,128)(2,1)}, u32[]{:S(2)}, u32[]{:S(2)}) collective-permute-start(bf16[136,1536]{1,0:T(8,128)(2,1)} %after.7.refs_1_), channel_id=1, source_target_pairs={{0,1},{1,0},{2,3},{3,2},{4,5},{5,4},{6,7},{7,6},{8,9},{9,8},{10,11... | collective-permute-start | bytes 1253384 | tf_op jit(solution)/shard_map/ppermute | solution.py:387
  30.2 13.2 %collective-permute-start.11 = (bf16[136,1536]{1,0:T(8,128)(2,1)}, bf16[136,1536]{1,0:T(8,128)(2,1)}, u32[]{:S(2)}, u32[]{:S(2)}) collective-permute-start(bf16[136,1536]{1,0:T(8,128)(2,1)} %after.8.refs_2_.refs_0_), channel_id=1, source_target_pairs={{0,4},{1,5},{2,6},{3,7},{4,12},{5,13},{6,14},{7,15},{8,0},{9,1},{1... | collective-permute-start | bytes 1253384 | tf_op jit(solution)/shard_map/ppermute | solution.py:387
  32.6 12.0 %collective-permute-start.10 = (bf16[136,1536]{1,0:T(8,128)(2,1)}, bf16[136,1536]{1,0:T(8,128)(2,1)}, u32[]{:S(2)}, u32[]{:S(2)}) collective-permute-start(bf16[136,1536]{1,0:T(8,128)(2,1)} %after.8.refs_2_.refs_0_), channel_id=1, source_target_pairs={{0,2},{1,3},{2,0},{3,1},{4,6},{5,7},{6,4},{7,5},{8,10},{9,11},{10,... | collective-permute-start | bytes 1253384 | tf_op jit(solution)/shard_map/ppermute | solution.py:387
  44.7 3.8 %collective-permute-start.12 = (bf16[2,128,1536]{2,1,0:T(8,128)(2,1)}, bf16[2,128,1536]{2,1,0:T(8,128)(2,1)}, u32[]{:S(2)}, u32[]{:S(2)}) collective-permute-start(bf16[2,128,1536]{2,1,0:T(8,128)(2,1)} %after.11), channel_id=1, source_target_pairs={{0,1},{1,0},{2,3},{3,2},{4,5},{5,4},{6,7},{7,6},{8,9},{9,8},{10,11... | collective-permute-start | bytes 2359304 | tf_op jit(solution)/shard_map/ppermute | solution.py:387
  44.7 3.2 %collective-permute-start.13 = (bf16[136,1536]{1,0:T(8,128)(2,1)}, bf16[136,1536]{1,0:T(8,128)(2,1)}, u32[]{:S(2)}, u32[]{:S(2)}) collective-permute-start(bf16[136,1536]{1,0:T(8,128)(2,1)} %after.8.refs_2_.refs_0_), channel_id=1, source_target_pairs={{0,1},{1,0},{2,3},{3,2},{4,5},{5,4},{6,7},{7,6},{8,9},{9,8},{10,11... | collective-permute-start | bytes 1253384 | tf_op jit(solution)/shard_map/ppermute | solution.py:387
  45.2 3.3 %collective-permute-start.14 = (bf16[136,1536]{1,0:T(8,128)(2,1)}, bf16[136,1536]{1,0:T(8,128)(2,1)}, u32[]{:S(2)}, u32[]{:S(2)}) collective-permute-start(bf16[136,1536]{1,0:T(8,128)(2,1)} %collective-permute-done.10.refs_1_), channel_id=1, source_target_pairs={{0,1},{1,0},{2,3},{3,2},{4,5},{5,4},{6,7},{7,6},{8,9},{9,8},{10,11... | collective-permute-start | bytes 1253384 | tf_op jit(solution)/shard_map/ppermute | solution.py:387
  45.2 13.3 %collective-permute-start.17 = (bf16[136,1536]{1,0:T(8,128)(2,1)}, bf16[136,1536]{1,0:T(8,128)(2,1)}, u32[]{:S(2)}, u32[]{:S(2)}) collective-permute-start(bf16[136,1536]{1,0:T(8,128)(2,1)} %collective-permute-done.10.refs_1_), channel_id=1, source_target_pairs={{0,4},{1,5},{2,6},{3,7},{4,12},{5,13},{6,14},{7,15},{8,0},{9,1},{1... | collective-permute-start | bytes 1253384 | tf_op jit(solution)/shard_map/ppermute | solution.py:387
  45.6 12.8 %collective-permute-start.9 = (bf16[128,1536]{1,0:T(8,128)(2,1)}, bf16[128,1536]{1,0:T(8,128)(2,1)}, u32[]{:S(2)}, u32[]{:S(2)}) collective-permute-start(bf16[128,1536]{1,0:T(8,128)(2,1)} %get-tuple-element.23), channel_id=1, source_target_pairs={{0,2},{1,3},{2,0},{3,1},{4,6},{5,7},{6,4},{7,5},{8,10},{9,11},{10,... | collective-permute-start | bytes 1179656 | tf_op jit(solution)/shard_map/ppermute | solution.py:387
  58.4 3.8 %collective-permute-start.18 = (bf16[2,128,1536]{2,1,0:T(8,128)(2,1)}, bf16[2,128,1536]{2,1,0:T(8,128)(2,1)}, u32[]{:S(2)}, u32[]{:S(2)}) collective-permute-start(bf16[2,128,1536]{2,1,0:T(8,128)(2,1)} %after.12), channel_id=1, source_target_pairs={{0,1},{1,0},{2,3},{3,2},{4,5},{5,4},{6,7},{7,6},{8,9},{9,8},{10,11... | collective-permute-start | bytes 2359304 | tf_op jit(solution)/shard_map/ppermute | solution.py:387
  58.4 3.2 %collective-permute-start.19 = (bf16[136,1536]{1,0:T(8,128)(2,1)}, bf16[136,1536]{1,0:T(8,128)(2,1)}, u32[]{:S(2)}, u32[]{:S(2)}) collective-permute-start(bf16[136,1536]{1,0:T(8,128)(2,1)} %after.10.refs_2_.refs_0_), channel_id=1, source_target_pairs={{0,1},{1,0},{2,3},{3,2},{4,5},{5,4},{6,7},{7,6},{8,9},{9,8},{10,11... | collective-permute-start | bytes 1253384 | tf_op jit(solution)/shard_map/ppermute | solution.py:387
  59.0 3.3 %collective-permute-start.20 = (bf16[136,1536]{1,0:T(8,128)(2,1)}, bf16[136,1536]{1,0:T(8,128)(2,1)}, u32[]{:S(2)}, u32[]{:S(2)}) collective-permute-start(bf16[136,1536]{1,0:T(8,128)(2,1)} %collective-permute-done.17.refs_1_), channel_id=1, source_target_pairs={{0,1},{1,0},{2,3},{3,2},{4,5},{5,4},{6,7},{7,6},{8,9},{9,8},{10,11... | collective-permute-start | bytes 1253384 | tf_op jit(solution)/shard_map/ppermute | solution.py:387
  59.0 12.6 %collective-permute-start.15 = (bf16[128,1536]{1,0:T(8,128)(2,1)}, bf16[128,1536]{1,0:T(8,128)(2,1)}, u32[]{:S(2)}, u32[]{:S(2)}) collective-permute-start(bf16[128,1536]{1,0:T(8,128)(2,1)} %get-tuple-element.27), channel_id=1, source_target_pairs={{0,2},{1,3},{2,0},{3,1},{4,6},{5,7},{6,4},{7,5},{8,10},{9,11},{10,... | collective-permute-start | bytes 1179656 | tf_op jit(solution)/shard_map/ppermute | solution.py:387
  71.6 43.0 %copy-start = (bf16[128,1536]{1,0:T(8,128)(2,1)S(1)}, bf16[128,1536]{1,0:T(8,128)(2,1)}, u32[]{:S(2)}) copy-start(bf16[128,1536]{1,0:T(8,128)(2,1)} %get-tuple-element.20.refs_1_) | copy-start | bytes 1179652
  71.6 4.4 %collective-permute-start.23 = (bf16[2,128,1536]{2,1,0:T(8,128)(2,1)}, bf16[2,128,1536]{2,1,0:T(8,128)(2,1)S(1)}, u32[]{:S(2)}, u32[]{:S(2)}) collective-permute-start(bf16[2,128,1536]{2,1,0:T(8,128)(2,1)} %after.13), channel_id=1, source_target_pairs={{0,1},{1,0},{2,3},{3,2},{4,5},{5,4},{6,7},{7,6},{8,9},{9,8},{10,11... | collective-permute-start | bytes 2359304 | tf_op jit(solution)/shard_map/ppermute | solution.py:387
  73.1 23.1 %collective-permute-start.16 = (bf16[128,1536]{1,0:T(8,128)(2,1)S(1)}, bf16[128,1536]{1,0:T(8,128)(2,1)S(1)}, u32[]{:S(2)}, u32[]{:S(2)}) collective-permute-start(bf16[128,1536]{1,0:T(8,128)(2,1)S(1)} %fusion.7), channel_id=1, source_target_pairs={{0,8},{1,9},{2,10},{3,11},{4,0},{5,1},{6,2},{7,3},{8,12},{9,13},{1... | collective-permute-start | bytes 1179656 | tf_op jit(solution)/shard_map/ppermute | solution.py:387
  74.4 12.2 %collective-permute-start.21 = (bf16[128,1536]{1,0:T(8,128)(2,1)}, bf16[128,1536]{1,0:T(8,128)(2,1)S(1)}, u32[]{:S(2)}, u32[]{:S(2)}) collective-permute-start(bf16[128,1536]{1,0:T(8,128)(2,1)} %get-tuple-element.31), channel_id=1, source_target_pairs={{0,2},{1,3},{2,0},{3,1},{4,6},{5,7},{6,4},{7,5},{8,10},{9,11},{10,... | collective-permute-start | bytes 1179656 | tf_op jit(solution)/shard_map/ppermute | solution.py:387
  77.1 17.1 %collective-permute-start.24 = (bf16[128,1536]{1,0:T(8,128)(2,1)S(1)}, bf16[128,1536]{1,0:T(8,128)(2,1)S(1)}, u32[]{:S(2)}, u32[]{:S(2)}) collective-permute-start(bf16[128,1536]{1,0:T(8,128)(2,1)S(1)} %fusion.1), channel_id=1, source_target_pairs={{0,2},{1,3},{2,0},{3,1},{4,6},{5,7},{6,4},{7,5},{8,10},{9,11},{10,... | collective-permute-start | bytes 1179656 | tf_op jit(solution)/shard_map/ppermute | solution.py:387
  87.8 13.3 %collective-permute-start.22 = (bf16[128,1536]{1,0:T(8,128)(2,1)S(1)}, bf16[128,1536]{1,0:T(8,128)(2,1)S(1)}, u32[]{:S(2)}, u32[]{:S(2)}) collective-permute-start(bf16[128,1536]{1,0:T(8,128)(2,1)S(1)} %fusion.5), channel_id=1, source_target_pairs={{0,12},{1,13},{2,14},{3,15},{4,8},{5,9},{6,10},{7,11},{8,4},{9,5},... | collective-permute-start | bytes 1179656 | tf_op jit(solution)/shard_map/ppermute | solution.py:387
  95.3 19.2 %collective-permute-start.25 = (bf16[128,1536]{1,0:T(8,128)(2,1)S(1)}, bf16[128,1536]{1,0:T(8,128)(2,1)S(1)}, u32[]{:S(2)}, u32[]{:S(2)}) collective-permute-start(bf16[128,1536]{1,0:T(8,128)(2,1)S(1)} %fusion.3), channel_id=1, source_target_pairs={{0,4},{1,5},{2,6},{3,7},{4,12},{5,13},{6,14},{7,15},{8,0},{9,1},{1... | collective-permute-start | bytes 1179656 | tf_op jit(solution)/shard_map/ppermute | solution.py:387

commit v9 on v8

--- a/solution.py
+++ b/solution.py
@@ -189,9 +189,14 @@
         fetch(spare_gate_hbm.at[0], spare_gate, False),
         fetch(spare_down_hbm.at[0], spare_down, False),
     ]
+
+    @pl.when(holds)
+    def _():
+        for copy in spare_copies:
+            copy.start()
+
     down_copies = [
-        fetch(down_hbm.at[0, :, n : n + tile], w_down.at[:, n : n + tile], False)
-        for n in range(0, width, tile)
+        fetch(down_hbm.at[0, :, n : n + tile], w_down.at[:, n : n + tile]) for n in range(0, width, tile)
     ]
 
     count = len(blocks)
@@ -247,15 +252,6 @@
 
     for i, n in enumerate(range(0, inner, tile)):
         gate_copies[i].wait()
-        if i == 0:
-
-            @pl.when(holds)
-            def _():
-                for copy in spare_copies:
-                    copy.start()
-
-        for copy in down_copies[i:] if n + tile >= inner else down_copies[i : i + 1]:
-            copy.start()
         hidden[:, n : n + tile] = gated_unit(
             jnp.dot(rows_in[...], w_gate[:, n : n + tile], preferred_element_type=jnp.float32)
         ).astype(jnp.bfloat16)
@@ -382,9 +378,12 @@
     steps = len(order)
     after = {a: order[(i + 1) % steps] for i, a in enumerate(order)}
     round_ring = [(d, after[d // 4] * 4 + d % 4) for d in range(owners)]
+    back = [(b, a) for a, b in round_ring]
     over_y = [(d, d ^ 2) for d in range(owners)]
     over_core = [(d, d ^ 1) for d in range(owners)]
     move = lambda a, pairs: lax.ppermute(a, "expert", pairs)
+    f32 = lambda a: a.astype(jnp.float32)
+    add = lambda a, b: (f32(a) + f32(b)).astype(jnp.bfloat16)
 
     meta = jnp.concatenate([expert_ids.T, gate_levels.T >> 5, gate_levels.T & 31], axis=0)
     meta = meta.astype(jnp.bfloat16).reshape(1, 3 * top * tok)
@@ -393,10 +392,10 @@
     held.append(move(held[0], round_ring))
     across, kept, got, from_y = [], [], [], []
 
-    def add_group(k, shares):
+    def add_group(k, shares, *earlier):
         blocks = (held[k], across[k], move(held[k], over_core), move(across[k], over_core))
         keep0, keep1, send, *summed = run_group(
-            failed, holders, blocks, weights, shares, (), tok, top, capacity
+            failed, holders, blocks, weights, shares, earlier, tok, top, capacity
         )
         kept.append((keep0, keep1))
         from_y.extend(move(a, over_y) for a in summed)
@@ -413,20 +412,21 @@
             held.append(come_after(move(held[k], round_ring), kept[k - 1][0]))
         send = come_after(send, across[k], held[min(k + 1, steps - 1)], *from_y[-2:-1])
         got.append(move(send, over_core))
-        send = add_group(k, (kept[-1][1], got[-1]))
+        if last:
+            share = add(kept[-1][1], got[-1][1])
+            from_y.append(move(share, over_y))
+            send = add_group(k, (), share)
+        else:
+            send = add_group(k, (kept[-1][1], got[-1]))
     got.append(move(come_after(send, *from_y[-2:-1]), over_core))
-
-    f32 = lambda a: a.astype(jnp.float32)
-    last = steps - 1
-    summed = (f32(kept[last][1]) + f32(got[last][1])).astype(jnp.bfloat16)
-    from_y.append(move(summed, over_y))
+    from_y.append(move(add(kept[-1][1], got[-1][1]), over_y))
+
     total = lambda k: f32(kept[k][0]) + f32(got[k][0]) + f32(from_y[k])
-    result = total(0)
-    place = {a: i for i, a in enumerate(order)}
-    for k in range(1, steps):
-        home = [(d, order[(place[d // 4] - k) % steps] * 4 + d % 4) for d in range(owners)]
-        result = result + f32(move(total(k).astype(jnp.bfloat16), home))
-    return result.astype(jnp.bfloat16)
+    result = total(0) + f32(move(total(1).astype(jnp.bfloat16), back))
+    passing = total(2)
+    for k in range(3, steps):
+        passing = total(k) + f32(move(passing.astype(jnp.bfloat16), round_ring))
+    return (result + f32(move(passing.astype(jnp.bfloat16), round_ring))).astype(jnp.bfloat16)
 
 
 def shards(

time: 117 us -> 113 us (0.966)
  Pallas kernels: 37.3 us -> 32.7 us
  other arithmetic: 8.8 us -> 10.7 us
  waiting for transfers between devices: 48.7 us -> 47.4 us
    pallas_call x4, Pallas kernels: 37.3 us -> 32.7 us  [run_group(): pl.pallas_call(functools.partial(group_kernel, others=len(earlier), adds=...]
    convert_element_type x5 -> x6, other arithmetic: 7.06 us -> 8.98 us  [the longest x2 2.93 us: by_permutes(): add = lambda a, b: (f32(a) + f32(b)).astype(jnp.bfloat16)]
    ppermute x26, waiting for transfers between devices: 48.7 us -> 47.4 us  [by_permutes(): move = lambda a, pairs: lax.ppermute(a, 'expert', pairs)]
    unnamed x11 -> x13, local copies, waits for them, and re-layouts: 1.55 us -> 2.42 us
  transfers between devices with their start and end apart: 26 -> 26, of which waited for: 12 -> 12; matrix products, arithmetic and copies ran while one was open for 4% -> 6% of each run, Pallas kernels for 32% -> 29%
where the time goes in v9:
time: 113 us
  waiting for transfers between devices  47.4 us (42%)
  Pallas kernels  32.7 us (29%)
  starting transfers between devices  18.7 us (17%)
  other arithmetic  10.7 us (9%)
  local copies, waits for them, and re-layouts  2.42 us (2%)
    ppermute x26, waiting for transfers between devices, by_permutes(): move = lambda a, pairs: lax.ppermute(a, 'expert', pairs)  47.4 us
    pallas_call x4, Pallas kernels, run_group(): pl.pallas_call(functools.partial(group_kernel, others=len(earlier), adds=...  32.7 us
    ppermute x26, starting transfers between devices, by_permutes(): move = lambda a, pairs: lax.ppermute(a, 'expert', pairs)  18.7 us
    convert_element_type x2, other arithmetic, by_permutes(): add = lambda a, b: (f32(a) + f32(b)).astype(jnp.bfloat16)  2.93 us
    unnamed x13, local copies, waits for them, and re-layouts  2.42 us
  transfers between devices with their start and end apart: 26, of which 12 were waited for; matrix products, arithmetic and copies ran while one was open for 6% of the time, Pallas kernels for 29%

profile of v9, /device:TPU:0, one launch (start us, length us, event | category | flops | bytes accessed | tf_op | source)
XLA Modules:
  0.0 112.8 jit_solution(13366918068841229405)
XLA Ops:
  0.0 0.7 fusion.15
  0.7 1.0 fusion.14.refs_0_
  1.8 3.0 %collective-permute-start = (bf16[136,1536]{1,0:T(8,128)(2,1)S(1)}, bf16[136,1536]{1,0:T(8,128)(2,1)S(1)}, u32[]{:S(2)}, u32[]{:S(2)}) collective-permute-start(bf16[136,1536]{1,0:T(8,128)(2,1)S(1)} %fusion.14.refs_0_), channel_id=1, source_target_pairs={{0,2},{1,3},{2,0},{3,1},{4,6},{5,7},{6,4},{7,5},{8,10},{9,11},{10,... | collective-permute-start | bytes 1253384 | tf_op jit(solution)/shard_map/ppermute | solution.py:384
  4.8 1.6 %collective-permute-start.3 = (bf16[136,1536]{1,0:T(8,128)(2,1)S(1)}, bf16[136,1536]{1,0:T(8,128)(2,1)}, u32[]{:S(2)}, u32[]{:S(2)}) collective-permute-start(bf16[136,1536]{1,0:T(8,128)(2,1)S(1)} %fusion.14.refs_0_), channel_id=1, source_target_pairs={{0,4},{1,5},{2,6},{3,7},{4,12},{5,13},{6,14},{7,15},{8,0},{9,1},{1... | collective-permute-start | bytes 1253384 | tf_op jit(solution)/shard_map/ppermute | solution.py:384
  6.4 0.0 collective-permute-start.1
  6.4 8.1 %collective-permute-done.refs_1_ = bf16[136,1536]{1,0:T(8,128)(2,1)S(1)} collective-permute-done((bf16[136,1536]{1,0:T(8,128)(2,1)S(1)}, bf16[136,1536]{1,0:T(8,128)(2,1)S(1)}, u32[]{:S(2)}, u32[]{:S(2)}) %collective-permute-start) | collective-permute-done | bytes 417824 | tf_op jit(solution)/shard_map/ppermute | solution.py:384
  14.4 0.0 collective-permute-start.2
  14.5 2.5 %collective-permute-done.3.refs_0_ = bf16[136,1536]{1,0:T(8,128)(2,1)} collective-permute-done((bf16[136,1536]{1,0:T(8,128)(2,1)S(1)}, bf16[136,1536]{1,0:T(8,128)(2,1)}, u32[]{:S(2)}, u32[]{:S(2)}) %collective-permute-start.3) | collective-permute-done | bytes 417824 | tf_op jit(solution)/shard_map/ppermute | solution.py:384
  16.9 0.7 collective-permute-start.5
  17.6 0.5 collective-permute-start.4
  18.7 0.0 collective-permute-done.1.refs_2_
  18.8 0.0 collective-permute-done.2.refs_3_
  18.8 0.7 copy-done.4
  19.5 0.8 copy-done.5
  20.3 8.1 %group.4 = (bf16[128,1536]{1,0:T(8,128)(2,1)}, bf16[128,1536]{1,0:T(8,128)(2,1)}, bf16[2,128,1536]{2,1,0:T(8,128)(2,1)}) custom-call(s32[1]{0:T(128)S(6)} %copy.27.failed, s32[4,16]{1,0:T(4,128)} %bitcast.43, bf16[136,1536]{1,0:T(8,128)(2,1)} %copy-done.1, bf16[136,1536]{1,0:T(8,128)(2,1)} %copy-done.3, bf16[136,1536]{1,0:T(8,128)(2,1)} %copy-done.4, ...), custom_call_target="tpu_custom_call" | custom-call | flops 3019898880 | bytes 14942208 | tf_op jit(solution)/shard_map/group/pallas_call | solution.py:316
  28.4 0.0 collective-permute-done.5.refs_0_
  28.5 0.1 collective-permute-start.6
  28.5 0.5 collective-permute-start.7
  29.0 0.1 collective-permute-start.8
  29.1 4.5 %collective-permute-start.11 = (bf16[136,1536]{1,0:T(8,128)(2,1)}, bf16[136,1536]{1,0:T(8,128)(2,1)}, u32[]{:S(2)}, u32[]{:S(2)}) collective-permute-start(bf16[136,1536]{1,0:T(8,128)(2,1)} %after.8.refs_2_.refs_0_), channel_id=1, source_target_pairs={{0,4},{1,5},{2,6},{3,7},{4,12},{5,13},{6,14},{7,15},{8,0},{9,1},{1... | collective-permute-start | bytes 1253384 | tf_op jit(solution)/shard_map/ppermute | solution.py:384
  33.7 0.5 collective-permute-start.10
  34.1 0.0 collective-permute-done.7.refs_2_
  34.1 0.0 collective-permute-done.8.refs_3_
  34.1 0.0 collective-permute-done.6.refs_9_
  34.1 8.2 %group.5 = (bf16[128,1536]{1,0:T(8,128)(2,1)}, bf16[128,1536]{1,0:T(8,128)(2,1)}, bf16[2,128,1536]{2,1,0:T(8,128)(2,1)}, bf16[128,1536]{1,0:T(8,128)(2,1)}) custom-call(s32[1]{0:T(128)S(6)} %copy.27.failed, s32[4,16]{1,0:T(4,128)} %bitcast.44, bf16[136,1536]{1,0:T(8,128)(2,1)} %collective-permute-done.3.refs_0_, bf16[136,1536]{1,0:T(8,128)(2,1)} %after.7.refs_1_, ...), custom_call_target="tpu_custom_call" | custom-call | flops 3019898880 | bytes 14942208 | tf_op jit(solution)/shard_map/group/pallas_call | solution.py:316
  42.4 1.1 collective-permute-done.11.refs_0_
  43.5 2.2 %collective-permute-done.10.refs_1_ = bf16[136,1536]{1,0:T(8,128)(2,1)} collective-permute-done((bf16[136,1536]{1,0:T(8,128)(2,1)}, bf16[136,1536]{1,0:T(8,128)(2,1)}, u32[]{:S(2)}, u32[]{:S(2)}) %collective-permute-start.10) | collective-permute-done | bytes 417824 | tf_op jit(solution)/shard_map/ppermute | solution.py:384
  45.7 0.0 collective-permute-start.12
  45.7 0.5 collective-permute-start.13
  46.2 0.0 collective-permute-start.14
  46.2 0.7 collective-permute-start.17
  46.9 0.8 collective-permute-start.9
  47.7 1.2 %collective-permute-done.13.refs_2_ = bf16[136,1536]{1,0:T(8,128)(2,1)} collective-permute-done((bf16[136,1536]{1,0:T(8,128)(2,1)}, bf16[136,1536]{1,0:T(8,128)(2,1)}, u32[]{:S(2)}, u32[]{:S(2)}) %collective-permute-start.13) | collective-permute-done | bytes 417824 | tf_op jit(solution)/shard_map/ppermute | solution.py:384
  48.9 0.6 collective-permute-done.14.refs_3_
  49.5 0.0 collective-permute-done.12.refs_9_
  49.5 8.2 %group.6 = (bf16[128,1536]{1,0:T(8,128)(2,1)}, bf16[128,1536]{1,0:T(8,128)(2,1)}, bf16[2,128,1536]{2,1,0:T(8,128)(2,1)}, bf16[128,1536]{1,0:T(8,128)(2,1)}) custom-call(s32[1]{0:T(128)S(6)} %copy.27.failed, s32[4,16]{1,0:T(4,128)} %bitcast.45, bf16[136,1536]{1,0:T(8,128)(2,1)} %after.8.refs_2_.refs_0_, bf16[136,1536]{1,0:T(8,128)(2,1)} %collective-permute-done.10.refs_1_, ...), custom_call_target="tpu_custom_call" | custom-call | flops 3019898880 | bytes 14942208 | tf_op jit(solution)/shard_map/group/pallas_call | solution.py:316
  57.7 1.7 %collective-permute-done.17.refs_1_ = bf16[136,1536]{1,0:T(8,128)(2,1)} collective-permute-done((bf16[136,1536]{1,0:T(8,128)(2,1)}, bf16[136,1536]{1,0:T(8,128)(2,1)}, u32[]{:S(2)}, u32[]{:S(2)}) %collective-permute-start.17) | collective-permute-done | bytes 417824 | tf_op jit(solution)/shard_map/ppermute | solution.py:384
  59.5 0.0 collective-permute-start.20
  59.5 0.5 collective-permute-start.18
  60.0 0.1 collective-permute-start.19
  60.1 0.5 collective-permute-start.15
  60.5 2.0 %collective-permute-done.20 = bf16[2,128,1536]{2,1,0:T(8,128)(2,1)S(1)} collective-permute-done((bf16[2,128,1536]{2,1,0:T(8,128)(2,1)}, bf16[2,128,1536]{2,1,0:T(8,128)(2,1)S(1)}, u32[]{:S(2)}, u32[]{:S(2)}) %collective-permute-start.20) | collective-permute-done | bytes 786464 | tf_op jit(solution)/shard_map/ppermute | solution.py:384
  62.5 0.9 copy-done.2
  63.4 1.8 %fusion.7.refs_8_ = bf16[128,1536]{1,0:T(8,128)(2,1)} fusion(bf16[128,1536]{1,0:T(8,128)(2,1)} %get-tuple-element.27, bf16[2,128,1536]{2,1,0:T(8,128)(2,1)S(1)} %collective-permute-done.20), kind=kLoop, calls=%fused_computation.12 | loop fusion | flops 786432 | bytes 1179648 | tf_op jit(solution)/shard_map/convert_element_type | solution.py:386
  65.2 0.5 collective-permute-start.23
  65.7 0.0 collective-permute-done.18.refs_2_
  65.7 0.0 collective-permute-done.19.refs_3_
  65.7 8.1 %group.7 = (bf16[128,1536]{1,0:T(8,128)(2,1)}, bf16[128,1536]{1,0:T(8,128)(2,1)}, bf16[2,128,1536]{2,1,0:T(8,128)(2,1)}) custom-call(s32[1]{0:T(128)S(6)} %copy.27.failed, s32[4,16]{1,0:T(4,128)} %bitcast.46, bf16[136,1536]{1,0:T(8,128)(2,1)} %after.10.refs_2_.refs_0_, bf16[136,1536]{1,0:T(8,128)(2,1)} %collective-permute-done.17.refs_1_, ...), custom_call_target="tpu_custom_call" | custom-call | flops 3019898880 | bytes 14942208 | tf_op jit(solution)/shard_map/group/pallas_call | solution.py:316
  73.8 0.0 collective-permute-done.15.refs_1_
  73.8 0.0 copy-start
  73.9 0.1 collective-permute-start.21
  73.9 6.3 %collective-permute-done.23 = bf16[128,1536]{1,0:T(8,128)(2,1)} collective-permute-done((bf16[128,1536]{1,0:T(8,128)(2,1)}, bf16[128,1536]{1,0:T(8,128)(2,1)}, u32[]{:S(2)}, u32[]{:S(2)}) %collective-permute-start.23) | collective-permute-done | bytes 393248 | tf_op jit(solution)/shard_map/ppermute | solution.py:384
  80.3 1.4 %fusion.2 = bf16[128,1536]{1,0:T(8,128)(2,1)S(1)} fusion(bf16[128,1536]{1,0:T(8,128)(2,1)} %collective-permute-done.23, bf16[128,1536]{1,0:T(8,128)(2,1)} %get-tuple-element.32, bf16[2,128,1536]{2,1,0:T(8,128)(2,1)} %copy-done.2), kind=kLoop, calls=%fused_computation.4 | loop fusion | flops 1179648 | bytes 1572864 | tf_op jit(solution)/shard_map/convert_element_type | solution.py:428
  81.6 0.1 collective-permute-start.24
  81.8 1.1 fusion.3
  82.9 1.0 collective-permute-start.22
  83.9 1.4 %fusion.9 = bf16[128,1536]{1,0:T(8,128)(2,1)S(1)} fusion(bf16[128,1536]{1,0:T(8,128)(2,1)} %collective-permute-done.15.refs_1_, bf16[128,1536]{1,0:T(8,128)(2,1)} %get-tuple-element.23.refs_1_, bf16[2,128,1536]{2,1,0:T(8,128)(2,1)} %collective-permute-done.12.refs_9_), kind=kLoop, calls=%fused_computation.15 | loop fusion | flops 1179648 | bytes 1572864 | tf_op jit(solution)/shard_map/convert_element_type | solution.py:425
  85.2 2.4 %collective-permute-start.16 = (bf16[128,1536]{1,0:T(8,128)(2,1)S(1)}, bf16[128,1536]{1,0:T(8,128)(2,1)S(1)}, u32[]{:S(2)}, u32[]{:S(2)}) collective-permute-start(bf16[128,1536]{1,0:T(8,128)(2,1)S(1)} %fusion.9), channel_id=1, source_target_pairs={{4,0},{5,1},{6,2},{7,3},{12,4},{13,5},{14,6},{15,7},{0,8},{1,9},{2... | collective-permute-start | bytes 1179656 | tf_op jit(solution)/shard_map/ppermute | solution.py:384
  87.7 13.1 %collective-permute-done.24 = bf16[128,1536]{1,0:T(8,128)(2,1)S(1)} collective-permute-done((bf16[128,1536]{1,0:T(8,128)(2,1)S(1)}, bf16[128,1536]{1,0:T(8,128)(2,1)S(1)}, u32[]{:S(2)}, u32[]{:S(2)}) %collective-permute-start.24) | collective-permute-done | bytes 393248 | tf_op jit(solution)/shard_map/ppermute | solution.py:384
  100.8 1.2 %fusion.6 = bf16[128,1536]{1,0:T(8,128)(2,1)S(1)} fusion(bf16[128,1536]{1,0:T(8,128)(2,1)S(1)} %collective-permute-done.24, bf16[128,1536]{1,0:T(8,128)(2,1)S(1)} %collective-permute-done.22, bf16[128,1536]{1,0:T(8,128)(2,1)} %get-tuple-element.29, bf16[2,128,1536]{2,1,0:T(8,128)(2,1)S(1)} %collective-permute-done.21), kind=kLoop, calls=%fused_computation.10 | loop fusion | flops 1572864 | bytes 1966080 | tf_op jit(solution)/shard_map/convert_element_type | solution.py:429
  102.0 0.1 collective-permute-start.25
  102.0 0.7 collective-permute-done.16
  102.8 7.9 %collective-permute-done.25 = bf16[128,1536]{1,0:T(8,128)(2,1)S(1)} collective-permute-done((bf16[128,1536]{1,0:T(8,128)(2,1)S(1)}, bf16[128,1536]{1,0:T(8,128)(2,1)S(1)}, u32[]{:S(2)}, u32[]{:S(2)}) %collective-permute-start.25) | collective-permute-done | bytes 393248 | tf_op jit(solution)/shard_map/ppermute | solution.py:384
  110.7 2.1 %fusion.13 = bf16[128,1536]{1,0:T(8,128)(2,1)} fusion(bf16[128,1536]{1,0:T(8,128)(2,1)S(1)} %collective-permute-done.25, bf16[128,1536]{1,0:T(8,128)(2,1)S(1)} %collective-permute-done.16, bf16[128,1536]{1,0:T(8,128)(2,1)} %collective-permute-done.9.refs_3_, bf16[128,1536]{1,0:T(8,128)(2,1)S(1)} %copy-done, ...), kind=kLoop, calls=%fused_computation.20 | loop fusion | flops 1966080 | bytes 2359296 | tf_op jit(solution)/shard_map/convert_element_type | solution.py:429
  (21 shorter events, 0.1 us)
Async XLA Ops:
  1.8 4.6 %copy-start.1 = (bf16[136,1536]{1,0:T(8,128)(2,1)}, bf16[136,1536]{1,0:T(8,128)(2,1)S(1)}, u32[]{:S(2)}) copy-start(bf16[136,1536]{1,0:T(8,128)(2,1)S(1)} %fusion.14.refs_0_) | copy-start | bytes 1253380
  1.8 12.7 %collective-permute-start = (bf16[136,1536]{1,0:T(8,128)(2,1)S(1)}, bf16[136,1536]{1,0:T(8,128)(2,1)S(1)}, u32[]{:S(2)}, u32[]{:S(2)}) collective-permute-start(bf16[136,1536]{1,0:T(8,128)(2,1)S(1)} %fusion.14.refs_0_), channel_id=1, source_target_pairs={{0,2},{1,3},{2,0},{3,1},{4,6},{5,7},{6,4},{7,5},{8,10},{9,11},{10,... | collective-permute-start | bytes 1253384 | tf_op jit(solution)/shard_map/ppermute | solution.py:384
  4.8 12.1 %collective-permute-start.3 = (bf16[136,1536]{1,0:T(8,128)(2,1)S(1)}, bf16[136,1536]{1,0:T(8,128)(2,1)}, u32[]{:S(2)}, u32[]{:S(2)}) collective-permute-start(bf16[136,1536]{1,0:T(8,128)(2,1)S(1)} %fusion.14.refs_0_), channel_id=1, source_target_pairs={{0,4},{1,5},{2,6},{3,7},{4,12},{5,13},{6,14},{7,15},{8,0},{9,1},{1... | collective-permute-start | bytes 1253384 | tf_op jit(solution)/shard_map/ppermute | solution.py:384
  6.4 12.4 %collective-permute-start.1 = (bf16[136,1536]{1,0:T(8,128)(2,1)S(1)}, bf16[136,1536]{1,0:T(8,128)(2,1)S(1)}, u32[]{:S(2)}, u32[]{:S(2)}) collective-permute-start(bf16[136,1536]{1,0:T(8,128)(2,1)S(1)} %fusion.14.refs_0_), channel_id=1, source_target_pairs={{0,1},{1,0},{2,3},{3,2},{4,5},{5,4},{6,7},{7,6},{8,9},{9,8},{10,11... | collective-permute-start | bytes 1253384 | tf_op jit(solution)/shard_map/ppermute | solution.py:384
  14.4 4.3 %copy-start.3 = (bf16[136,1536]{1,0:T(8,128)(2,1)}, bf16[136,1536]{1,0:T(8,128)(2,1)S(1)}, u32[]{:S(2)}) copy-start(bf16[136,1536]{1,0:T(8,128)(2,1)S(1)} %collective-permute-done.refs_1_) | copy-start | bytes 1253380
  14.4 4.3 %collective-permute-start.2 = (bf16[136,1536]{1,0:T(8,128)(2,1)S(1)}, bf16[136,1536]{1,0:T(8,128)(2,1)S(1)}, u32[]{:S(2)}, u32[]{:S(2)}) collective-permute-start(bf16[136,1536]{1,0:T(8,128)(2,1)S(1)} %collective-permute-done.refs_1_), channel_id=1, source_target_pairs={{0,1},{1,0},{2,3},{3,2},{4,5},{5,4},{6,7},{7,6},{8,9},{9,8},{10,11... | collective-permute-start | bytes 1253384 | tf_op jit(solution)/shard_map/ppermute | solution.py:384
  16.9 11.5 %collective-permute-start.5 = (bf16[136,1536]{1,0:T(8,128)(2,1)}, bf16[136,1536]{1,0:T(8,128)(2,1)}, u32[]{:S(2)}, u32[]{:S(2)}) collective-permute-start(bf16[136,1536]{1,0:T(8,128)(2,1)} %collective-permute-done.3.refs_0_), channel_id=1, source_target_pairs={{0,4},{1,5},{2,6},{3,7},{4,12},{5,13},{6,14},{7,15},{8,0},{9,1},{1... | collective-permute-start | bytes 1253384 | tf_op jit(solution)/shard_map/ppermute | solution.py:384
  17.6 10.8 %collective-permute-start.4 = (bf16[136,1536]{1,0:T(8,128)(2,1)}, bf16[136,1536]{1,0:T(8,128)(2,1)}, u32[]{:S(2)}, u32[]{:S(2)}) collective-permute-start(bf16[136,1536]{1,0:T(8,128)(2,1)} %collective-permute-done.3.refs_0_), channel_id=1, source_target_pairs={{0,2},{1,3},{2,0},{3,1},{4,6},{5,7},{6,4},{7,5},{8,10},{9,11},{10,... | collective-permute-start | bytes 1253384 | tf_op jit(solution)/shard_map/ppermute | solution.py:384
  18.8 0.8 copy-start.4
  19.5 0.8 copy-start.5
  28.5 5.7 %collective-permute-start.6 = (bf16[2,128,1536]{2,1,0:T(8,128)(2,1)}, bf16[2,128,1536]{2,1,0:T(8,128)(2,1)}, u32[]{:S(2)}, u32[]{:S(2)}) collective-permute-start(bf16[2,128,1536]{2,1,0:T(8,128)(2,1)} %after.9), channel_id=1, source_target_pairs={{0,1},{1,0},{2,3},{3,2},{4,5},{5,4},{6,7},{7,6},{8,9},{9,8},{10,11... | collective-permute-start | bytes 2359304 | tf_op jit(solution)/shard_map/ppermute | solution.py:384
  28.5 5.6 %collective-permute-start.7 = (bf16[136,1536]{1,0:T(8,128)(2,1)}, bf16[136,1536]{1,0:T(8,128)(2,1)}, u32[]{:S(2)}, u32[]{:S(2)}) collective-permute-start(bf16[136,1536]{1,0:T(8,128)(2,1)} %collective-permute-done.3.refs_0_), channel_id=1, source_target_pairs={{0,1},{1,0},{2,3},{3,2},{4,5},{5,4},{6,7},{7,6},{8,9},{9,8},{10,11... | collective-permute-start | bytes 1253384 | tf_op jit(solution)/shard_map/ppermute | solution.py:384
  29.0 5.1 %collective-permute-start.8 = (bf16[136,1536]{1,0:T(8,128)(2,1)}, bf16[136,1536]{1,0:T(8,128)(2,1)}, u32[]{:S(2)}, u32[]{:S(2)}) collective-permute-start(bf16[136,1536]{1,0:T(8,128)(2,1)} %after.7.refs_1_), channel_id=1, source_target_pairs={{0,1},{1,0},{2,3},{3,2},{4,5},{5,4},{6,7},{7,6},{8,9},{9,8},{10,11... | collective-permute-start | bytes 1253384 | tf_op jit(solution)/shard_map/ppermute | solution.py:384
  29.1 14.4 %collective-permute-start.11 = (bf16[136,1536]{1,0:T(8,128)(2,1)}, bf16[136,1536]{1,0:T(8,128)(2,1)}, u32[]{:S(2)}, u32[]{:S(2)}) collective-permute-start(bf16[136,1536]{1,0:T(8,128)(2,1)} %after.8.refs_2_.refs_0_), channel_id=1, source_target_pairs={{0,4},{1,5},{2,6},{3,7},{4,12},{5,13},{6,14},{7,15},{8,0},{9,1},{1... | collective-permute-start | bytes 1253384 | tf_op jit(solution)/shard_map/ppermute | solution.py:384
  33.7 12.0 %collective-permute-start.10 = (bf16[136,1536]{1,0:T(8,128)(2,1)}, bf16[136,1536]{1,0:T(8,128)(2,1)}, u32[]{:S(2)}, u32[]{:S(2)}) collective-permute-start(bf16[136,1536]{1,0:T(8,128)(2,1)} %after.8.refs_2_.refs_0_), channel_id=1, source_target_pairs={{0,2},{1,3},{2,0},{3,1},{4,6},{5,7},{6,4},{7,5},{8,10},{9,11},{10,... | collective-permute-start | bytes 1253384 | tf_op jit(solution)/shard_map/ppermute | solution.py:384
  45.7 3.8 %collective-permute-start.12 = (bf16[2,128,1536]{2,1,0:T(8,128)(2,1)}, bf16[2,128,1536]{2,1,0:T(8,128)(2,1)}, u32[]{:S(2)}, u32[]{:S(2)}) collective-permute-start(bf16[2,128,1536]{2,1,0:T(8,128)(2,1)} %after.11), channel_id=1, source_target_pairs={{0,1},{1,0},{2,3},{3,2},{4,5},{5,4},{6,7},{7,6},{8,9},{9,8},{10,11... | collective-permute-start | bytes 2359304 | tf_op jit(solution)/shard_map/ppermute | solution.py:384
  45.7 3.2 %collective-permute-start.13 = (bf16[136,1536]{1,0:T(8,128)(2,1)}, bf16[136,1536]{1,0:T(8,128)(2,1)}, u32[]{:S(2)}, u32[]{:S(2)}) collective-permute-start(bf16[136,1536]{1,0:T(8,128)(2,1)} %after.8.refs_2_.refs_0_), channel_id=1, source_target_pairs={{0,1},{1,0},{2,3},{3,2},{4,5},{5,4},{6,7},{7,6},{8,9},{9,8},{10,11... | collective-permute-start | bytes 1253384 | tf_op jit(solution)/shard_map/ppermute | solution.py:384
  46.2 3.3 %collective-permute-start.14 = (bf16[136,1536]{1,0:T(8,128)(2,1)}, bf16[136,1536]{1,0:T(8,128)(2,1)}, u32[]{:S(2)}, u32[]{:S(2)}) collective-permute-start(bf16[136,1536]{1,0:T(8,128)(2,1)} %collective-permute-done.10.refs_1_), channel_id=1, source_target_pairs={{0,1},{1,0},{2,3},{3,2},{4,5},{5,4},{6,7},{7,6},{8,9},{9,8},{10,11... | collective-permute-start | bytes 1253384 | tf_op jit(solution)/shard_map/ppermute | solution.py:384
  46.2 13.3 %collective-permute-start.17 = (bf16[136,1536]{1,0:T(8,128)(2,1)}, bf16[136,1536]{1,0:T(8,128)(2,1)}, u32[]{:S(2)}, u32[]{:S(2)}) collective-permute-start(bf16[136,1536]{1,0:T(8,128)(2,1)} %collective-permute-done.10.refs_1_), channel_id=1, source_target_pairs={{0,4},{1,5},{2,6},{3,7},{4,12},{5,13},{6,14},{7,15},{8,0},{9,1},{1... | collective-permute-start | bytes 1253384 | tf_op jit(solution)/shard_map/ppermute | solution.py:384
  46.9 12.6 %collective-permute-start.9 = (bf16[128,1536]{1,0:T(8,128)(2,1)}, bf16[128,1536]{1,0:T(8,128)(2,1)}, u32[]{:S(2)}, u32[]{:S(2)}) collective-permute-start(bf16[128,1536]{1,0:T(8,128)(2,1)} %get-tuple-element.22), channel_id=1, source_target_pairs={{0,2},{1,3},{2,0},{3,1},{4,6},{5,7},{6,4},{7,5},{8,10},{9,11},{10,... | collective-permute-start | bytes 1179656 | tf_op jit(solution)/shard_map/ppermute | solution.py:384
  59.5 3.0 %collective-permute-start.20 = (bf16[2,128,1536]{2,1,0:T(8,128)(2,1)}, bf16[2,128,1536]{2,1,0:T(8,128)(2,1)S(1)}, u32[]{:S(2)}, u32[]{:S(2)}) collective-permute-start(bf16[2,128,1536]{2,1,0:T(8,128)(2,1)} %after.12), channel_id=1, source_target_pairs={{0,1},{1,0},{2,3},{3,2},{4,5},{5,4},{6,7},{7,6},{8,9},{9,8},{10,11... | collective-permute-start | bytes 2359304 | tf_op jit(solution)/shard_map/ppermute | solution.py:384
  59.5 6.2 %collective-permute-start.18 = (bf16[136,1536]{1,0:T(8,128)(2,1)}, bf16[136,1536]{1,0:T(8,128)(2,1)}, u32[]{:S(2)}, u32[]{:S(2)}) collective-permute-start(bf16[136,1536]{1,0:T(8,128)(2,1)} %after.10.refs_2_.refs_0_), channel_id=1, source_target_pairs={{0,1},{1,0},{2,3},{3,2},{4,5},{5,4},{6,7},{7,6},{8,9},{9,8},{10,11... | collective-permute-start | bytes 1253384 | tf_op jit(solution)/shard_map/ppermute | solution.py:384
  60.0 5.7 %collective-permute-start.19 = (bf16[136,1536]{1,0:T(8,128)(2,1)}, bf16[136,1536]{1,0:T(8,128)(2,1)}, u32[]{:S(2)}, u32[]{:S(2)}) collective-permute-start(bf16[136,1536]{1,0:T(8,128)(2,1)} %collective-permute-done.17.refs_1_), channel_id=1, source_target_pairs={{0,1},{1,0},{2,3},{3,2},{4,5},{5,4},{6,7},{7,6},{8,9},{9,8},{10,11... | collective-permute-start | bytes 1253384 | tf_op jit(solution)/shard_map/ppermute | solution.py:384
  60.1 13.8 %collective-permute-start.15 = (bf16[128,1536]{1,0:T(8,128)(2,1)}, bf16[128,1536]{1,0:T(8,128)(2,1)}, u32[]{:S(2)}, u32[]{:S(2)}) collective-permute-start(bf16[128,1536]{1,0:T(8,128)(2,1)} %get-tuple-element.26), channel_id=1, source_target_pairs={{0,2},{1,3},{2,0},{3,1},{4,6},{5,7},{6,4},{7,5},{8,10},{9,11},{10,... | collective-permute-start | bytes 1179656 | tf_op jit(solution)/shard_map/ppermute | solution.py:384
  62.5 0.9 copy-start.2
  65.2 15.0 %collective-permute-start.23 = (bf16[128,1536]{1,0:T(8,128)(2,1)}, bf16[128,1536]{1,0:T(8,128)(2,1)}, u32[]{:S(2)}, u32[]{:S(2)}) collective-permute-start(bf16[128,1536]{1,0:T(8,128)(2,1)} %fusion.7.refs_8_), channel_id=1, source_target_pairs={{0,2},{1,3},{2,0},{3,1},{4,6},{5,7},{6,4},{7,5},{8,10},{9,11},{10,... | collective-permute-start | bytes 1179656 | tf_op jit(solution)/shard_map/ppermute | solution.py:384
  73.8 36.8 %copy-start = (bf16[128,1536]{1,0:T(8,128)(2,1)S(1)}, bf16[128,1536]{1,0:T(8,128)(2,1)}, u32[]{:S(2)}) copy-start(bf16[128,1536]{1,0:T(8,128)(2,1)} %get-tuple-element.19.refs_1_) | copy-start | bytes 1179652
  73.9 7.9 %collective-permute-start.21 = (bf16[2,128,1536]{2,1,0:T(8,128)(2,1)}, bf16[2,128,1536]{2,1,0:T(8,128)(2,1)S(1)}, u32[]{:S(2)}, u32[]{:S(2)}) collective-permute-start(bf16[2,128,1536]{2,1,0:T(8,128)(2,1)} %after.13), channel_id=1, source_target_pairs={{0,1},{1,0},{2,3},{3,2},{4,5},{5,4},{6,7},{7,6},{8,9},{9,8},{10,11... | collective-permute-start | bytes 2359304 | tf_op jit(solution)/shard_map/ppermute | solution.py:384
  81.6 19.1 %collective-permute-start.24 = (bf16[128,1536]{1,0:T(8,128)(2,1)S(1)}, bf16[128,1536]{1,0:T(8,128)(2,1)S(1)}, u32[]{:S(2)}, u32[]{:S(2)}) collective-permute-start(bf16[128,1536]{1,0:T(8,128)(2,1)S(1)} %fusion.2), channel_id=1, source_target_pairs={{0,4},{1,5},{2,6},{3,7},{4,12},{5,13},{6,14},{7,15},{8,0},{9,1},{1... | collective-permute-start | bytes 1179656 | tf_op jit(solution)/shard_map/ppermute | solution.py:384
  82.9 17.9 %collective-permute-start.22 = (bf16[128,1536]{1,0:T(8,128)(2,1)S(1)}, bf16[128,1536]{1,0:T(8,128)(2,1)S(1)}, u32[]{:S(2)}, u32[]{:S(2)}) collective-permute-start(bf16[128,1536]{1,0:T(8,128)(2,1)S(1)} %fusion.3), channel_id=1, source_target_pairs={{0,2},{1,3},{2,0},{3,1},{4,6},{5,7},{6,4},{7,5},{8,10},{9,11},{10,... | collective-permute-start | bytes 1179656 | tf_op jit(solution)/shard_map/ppermute | solution.py:384
  85.2 17.5 %collective-permute-start.16 = (bf16[128,1536]{1,0:T(8,128)(2,1)S(1)}, bf16[128,1536]{1,0:T(8,128)(2,1)S(1)}, u32[]{:S(2)}, u32[]{:S(2)}) collective-permute-start(bf16[128,1536]{1,0:T(8,128)(2,1)S(1)} %fusion.9), channel_id=1, source_target_pairs={{4,0},{5,1},{6,2},{7,3},{12,4},{13,5},{14,6},{15,7},{0,8},{1,9},{2... | collective-permute-start | bytes 1179656 | tf_op jit(solution)/shard_map/ppermute | solution.py:384
  102.0 8.7 %collective-permute-start.25 = (bf16[128,1536]{1,0:T(8,128)(2,1)S(1)}, bf16[128,1536]{1,0:T(8,128)(2,1)S(1)}, u32[]{:S(2)}, u32[]{:S(2)}) collective-permute-start(bf16[128,1536]{1,0:T(8,128)(2,1)S(1)} %fusion.6), channel_id=1, source_target_pairs={{0,4},{1,5},{2,6},{3,7},{4,12},{5,13},{6,14},{7,15},{8,0},{9,1},{1... | collective-permute-start | bytes 1179656 | tf_op jit(solution)/shard_map/ppermute | solution.py:384

commit v10 on v7

--- a/solution.py
+++ b/solution.py
@@ -354,6 +354,72 @@
     )(*map(in_hbm, (value, *others)))
 
 
+def sum_kernel(*refs, plan):
+    terms = [term for sum_of in plan for term in sum_of]
+    inputs = 1 + max(i for i, _ in terms)
+    sources, outs, (parts, done, fetched, stored) = refs[:inputs], refs[inputs:-4], refs[-4:]
+    half = done.shape[1] // 2
+    halves = (slice(0, half), slice(half, 2 * half))
+    copies = [
+        [
+            pltpu.make_async_copy(
+                (sources[i] if lead is None else sources[i].at[lead]).at[rows],
+                parts.at[t, rows],
+                fetched.at[2 * t + h],
+            )
+            for h, rows in enumerate(halves)
+        ]
+        for t, (i, lead) in enumerate(terms)
+    ]
+    for pair in copies:
+        for copy in pair:
+            copy.start()
+    stores = []
+    at = 0
+    for o, sum_of in enumerate(plan):
+        for h, rows in enumerate(halves):
+            for t in range(at, at + len(sum_of)):
+                copies[t][h].wait()
+            total = parts[at, rows].astype(jnp.float32)
+            for t in range(at + 1, at + len(sum_of)):
+                total = total + parts[t, rows].astype(jnp.float32)
+            done[o, rows] = total.astype(jnp.bfloat16)
+            stores.append(
+                pltpu.make_async_copy(done.at[o, rows], outs[o].at[rows], stored.at[2 * o + h])
+            )
+            stores[-1].start()
+        at += len(sum_of)
+    for copy in stores:
+        copy.wait()
+
+
+def add_up(*sums):
+    arrays = [array for sum_of in sums for array, _ in sum_of]
+    numbers = iter(range(len(arrays)))
+    plan = tuple(tuple((next(numbers), lead) for _, lead in sum_of) for sum_of in sums)
+    tok, width = arrays[0].shape[-2:]
+    hbm = pl.BlockSpec(memory_space=pl.ANY)
+    return pl.pallas_call(
+        functools.partial(sum_kernel, plan=plan),
+        out_shape=(pltpu.HBM((tok, width), jnp.bfloat16),) * len(sums),
+        in_specs=[hbm] * len(arrays),
+        out_specs=(hbm,) * len(sums),
+        scratch_shapes=[
+            pltpu.VMEM((len(arrays), tok, width), jnp.bfloat16),
+            pltpu.VMEM((len(sums), tok, width), jnp.bfloat16),
+            pltpu.SemaphoreType.DMA((2 * len(arrays),)),
+            pltpu.SemaphoreType.DMA((2 * len(sums),)),
+        ],
+        compiler_params=pltpu.CompilerParams(vmem_limit_bytes=VMEM_GRANT),
+        cost_estimate=pl.CostEstimate(
+            flops=len(arrays) * tok * width,
+            bytes_accessed=2 * (len(arrays) + len(sums)) * tok * width,
+            transcendentals=0,
+        ),
+        name="sums",
+    )(*map(in_hbm, arrays))
+
+
 def folded_ring(length):
     return [0] + list(range(1, length, 2)) + list(range(2, length, 2))[::-1]
 
@@ -373,38 +439,50 @@
     meta = meta.astype(jnp.bfloat16).reshape(1, 3 * top * tok)
     meta = jnp.pad(meta, ((0, 7), (0, width - 3 * top * tok)))
     held = [jnp.concatenate([tokens, meta], axis=0)]
-    across, results = [], []
-    for k in range(steps):
-        if k > 0:
-            held.append(move(held[-1], round_ring))
-            if k > 1:
-                held[k] = come_after(held[k], results[k - 2][0])
-        if 1 < k == steps - 1:
-            across.append(move(across[-1], round_ring))
-        else:
-            across.append(move(held[k], over_y))
+    held.append(move(held[0], round_ring))
+    across, kept, got = [], [], []
+    last = steps - 1
+
+    def add_group(k, *earlier):
+        blocks = (held[k], across[k], move(held[k], over_core), move(across[k], over_core))
+        keep0, keep1, send = run_group(failed, holders, blocks, weights, earlier, tok, top, capacity)
+        kept.append((keep0, keep1))
+        return send
+
+    def share(k):
+        return [(kept[k][1], None), (got[k], 1)]
+
+    def total(k, *more):
+        return [(kept[k][0], None), (got[k], 0)] + [(a, None) for a in more]
+
+    across.append(move(held[0], over_y))
+    send = add_group(0)
+    far, from_y, arrived = kept[0][0], None, ()
+    for k in range(1, steps):
+        across.append(move(across[-1], round_ring) if k == last else move(held[k], over_y))
         if k == 1:
-            across[1] = come_after(across[1], results[0][0])
-        blocks = (held[k], across[k], move(held[k], over_core), move(across[k], over_core))
-        earlier = [results[-1][0]] if results else []
-        results.append(run_group(failed, holders, blocks, weights, earlier, tok, top, capacity))
-
-    f32 = lambda a: a.astype(jnp.float32)
-    passing = None
-    for k in list(range(1, steps)) + [0]:
-        keep0, keep1, send = results[k]
-        if k < steps - 1:
-            send = come_after(send, across[k + 1], held[min(k + 2, steps - 1)])
-        got = move(send, over_core)
-        far = (f32(keep1) + f32(got[1])).astype(jnp.bfloat16)
-        if k == 0 and steps > 1:
-            far = come_after(far, from_y)
-        from_y = move(far, over_y)
-        total = f32(keep0) + f32(got[0]) + f32(from_y)
-        if passing is not None:
-            total = total + f32(move(passing, round_ring))
-        passing = total.astype(jnp.bfloat16)
-    return passing
+            across[1] = come_after(across[1], kept[0][0])
+        if k < last:
+            held.append(come_after(move(held[k], round_ring), kept[k - 1][0]))
+        before = () if from_y is None else (from_y,)
+        got.append(move(come_after(send, across[k], held[min(k + 1, last)], *before), over_core))
+        if k == 2:
+            (far,) = add_up(share(1))
+        elif k > 2:
+            far, passing = add_up(share(k - 1), total(k - 2, from_y, *arrived))
+            arrived = (move(passing, round_ring),)
+        if k > 1:
+            from_y = move(far, over_y)
+        send = add_group(k, far)
+    got.append(move(come_after(send, from_y, *arrived), over_core))
+    (passing,) = add_up(total(last - 1, from_y, *arrived))
+    arrived = move(passing, round_ring)
+    (far,) = add_up(share(last))
+    (passing,) = add_up(total(last, move(far, over_y), arrived))
+    arrived = move(passing, round_ring)
+    (far,) = add_up(share(0))
+    from_y = move(come_after(far, passing), over_y)
+    return add_up(total(0, from_y, arrived))[0]
 
 
 def shards(
@@ -427,7 +505,7 @@
     holds = jnp.any(holder_row == my_index).astype(jnp.int32)
     scalars = jnp.stack([my_index, failed_id, holds])
     weights = (w_gate, w_down, spare_gate, spare_down)
-    if owners % 4 == 0 and owners <= 32 and 3 * top_count * tok_count <= tokens.shape[1]:
+    if 12 <= owners <= 32 and owners % 4 == 0 and 3 * top_count * tok_count <= tokens.shape[1]:
         return by_permutes(
             failed_device, replica_holders.T, tokens, expert_ids, gate_levels, weights, owners, capacity
         )

time: 112 us -> 114 us (1.018)
  Pallas kernels: 32.5 us -> 48 us
  other arithmetic: 16.7 us -> 1.74 us
  local copies, waits for them, and re-layouts: 4.09 us -> 1.54 us
  waiting for transfers between devices: 37.1 us -> 39.1 us
  starting transfers between devices: 20.1 us -> 21.9 us
    pallas_call x0 -> x7, Pallas kernels: none -> 15.6 us  [add_up(): pl.pallas_call(functools.partial(sum_kernel, plan=plan), out_shape=(pltpu...]
    convert_element_type x8 -> x0, other arithmetic: 14.9 us -> none  [the longest x4 7.92 us: by_permutes(): passing = total.astype(jnp.bfloat16)]
    unnamed x17 -> x9, local copies, waits for them, and re-layouts: 4.09 us -> 1.54 us
    ppermute x26, waiting for transfers between devices: 37.1 us -> 39.1 us  [by_permutes(): move = lambda a, pairs: lax.ppermute(a, 'expert', pairs)]
    ppermute x26, starting transfers between devices: 20.1 us -> 21.9 us  [by_permutes(): move = lambda a, pairs: lax.ppermute(a, 'expert', pairs)]
  transfers between devices with their start and end apart: 26 -> 26, of which waited for: 12 -> 14; matrix products, arithmetic and copies ran while one was open for 10% -> 0% of each run, Pallas kernels for 29% -> 38%
where the time goes in v10:
time: 114 us; the launch traced here: 113 us
  Pallas kernels  48 us (42%)
  waiting for transfers between devices  39.1 us (34%)
  starting transfers between devices  21.9 us (19%)
  other arithmetic  1.74 us (2%)
  local copies, waits for them, and re-layouts  1.54 us (1%)
    ppermute x26, waiting for transfers between devices, by_permutes(): move = lambda a, pairs: lax.ppermute(a, 'expert', pairs)  39.1 us
    pallas_call x4, Pallas kernels, run_group(): pl.pallas_call(functools.partial(group_kernel, others=len(earlier), tok=t...  32.4 us
    ppermute x26, starting transfers between devices, by_permutes(): move = lambda a, pairs: lax.ppermute(a, 'expert', pairs)  21.9 us
    pallas_call x7, Pallas kernels, add_up(): pl.pallas_call(functools.partial(sum_kernel, plan=plan), out_shape=(pltpu...  15.6 us
  transfers between devices with their start and end apart: 26, of which 14 were waited for; matrix products, arithmetic and copies ran while one was open for 0% of the time, Pallas kernels for 38%

profile of v10, /device:TPU:0, one launch (start us, length us, event | category | flops | bytes accessed | tf_op | source)
XLA Modules:
  0.0 113.2 jit_solution(6273663905124723198)
XLA Ops:
  0.0 0.7 fusion.2
  0.7 1.0 fusion.1.refs_0_
  1.8 3.0 %collective-permute-start = (bf16[136,1536]{1,0:T(8,128)(2,1)S(1)}, bf16[136,1536]{1,0:T(8,128)(2,1)S(1)}, u32[]{:S(2)}, u32[]{:S(2)}) collective-permute-start(bf16[136,1536]{1,0:T(8,128)(2,1)S(1)} %fusion.1.refs_0_), channel_id=1, source_target_pairs={{0,2},{1,3},{2,0},{3,1},{4,6},{5,7},{6,4},{7,5},{8,10},{9,11},{10,... | collective-permute-start | bytes 1253384 | tf_op jit(solution)/shard_map/ppermute | solution.py:436
  4.8 1.6 %collective-permute-start.3 = (bf16[136,1536]{1,0:T(8,128)(2,1)S(1)}, bf16[136,1536]{1,0:T(8,128)(2,1)}, u32[]{:S(2)}, u32[]{:S(2)}) collective-permute-start(bf16[136,1536]{1,0:T(8,128)(2,1)S(1)} %fusion.1.refs_0_), channel_id=1, source_target_pairs={{0,4},{1,5},{2,6},{3,7},{4,12},{5,13},{6,14},{7,15},{8,0},{9,1},{1... | collective-permute-start | bytes 1253384 | tf_op jit(solution)/shard_map/ppermute | solution.py:436
  6.4 0.0 collective-permute-start.1
  6.4 8.1 %collective-permute-done.refs_1_ = bf16[136,1536]{1,0:T(8,128)(2,1)S(1)} collective-permute-done((bf16[136,1536]{1,0:T(8,128)(2,1)S(1)}, bf16[136,1536]{1,0:T(8,128)(2,1)S(1)}, u32[]{:S(2)}, u32[]{:S(2)}) %collective-permute-start) | collective-permute-done | bytes 417824 | tf_op jit(solution)/shard_map/ppermute | solution.py:436
  14.4 0.0 collective-permute-start.2
  14.5 2.5 %collective-permute-done.3.refs_0_ = bf16[136,1536]{1,0:T(8,128)(2,1)} collective-permute-done((bf16[136,1536]{1,0:T(8,128)(2,1)S(1)}, bf16[136,1536]{1,0:T(8,128)(2,1)}, u32[]{:S(2)}, u32[]{:S(2)}) %collective-permute-start.3) | collective-permute-done | bytes 417824 | tf_op jit(solution)/shard_map/ppermute | solution.py:436
  16.9 0.5 collective-permute-start.4
  18.0 0.1 collective-permute-start.8
  18.1 0.8 collective-permute-start.5
  18.9 0.0 collective-permute-done.1.refs_2_
  18.9 0.0 collective-permute-done.2.refs_3_
  18.9 0.8 copy-done.2
  19.7 0.8 copy-done.3
  20.4 8.1 %group.4 = (bf16[128,1536]{1,0:T(8,128)(2,1)}, bf16[128,1536]{1,0:T(8,128)(2,1)}, bf16[2,128,1536]{2,1,0:T(8,128)(2,1)}) custom-call(s32[1]{0:T(128)S(6)} %copy.29.failed, s32[4,16]{1,0:T(4,128)} %bitcast.13, bf16[136,1536]{1,0:T(8,128)(2,1)} %copy-done, bf16[136,1536]{1,0:T(8,128)(2,1)} %copy-done.1, bf16[136,1536]{1,0:T(8,128)(2,1)} %copy-done.2, ...), custom_call_target="tpu_custom_call" | custom-call | flops 3019898880 | bytes 14942208 | tf_op jit(solution)/shard_map/group/pallas_call | solution.py:304
  28.5 0.0 collective-permute-done.4.refs_0_
  28.5 0.2 collective-permute-start.9
  28.7 2.6 %collective-permute-done.5.refs_0_ = bf16[136,1536]{1,0:T(8,128)(2,1)} collective-permute-done((bf16[136,1536]{1,0:T(8,128)(2,1)}, bf16[136,1536]{1,0:T(8,128)(2,1)}, u32[]{:S(2)}, u32[]{:S(2)}) %collective-permute-start.5) | collective-permute-done | bytes 417824 | tf_op jit(solution)/shard_map/ppermute | solution.py:436
  31.4 0.9 collective-permute-start.7
  32.2 2.5 %collective-permute-start.10 = (bf16[136,1536]{1,0:T(8,128)(2,1)}, bf16[136,1536]{1,0:T(8,128)(2,1)}, u32[]{:S(2)}, u32[]{:S(2)}) collective-permute-start(bf16[136,1536]{1,0:T(8,128)(2,1)} %after.9.refs_2_.refs_0_), channel_id=1, source_target_pairs={{0,2},{1,3},{2,0},{3,1},{4,6},{5,7},{6,4},{7,5},{8,10},{9,11},{10,... | collective-permute-start | bytes 1253384 | tf_op jit(solution)/shard_map/ppermute | solution.py:436
  34.7 0.0 collective-permute-done.9.refs_3_
  34.7 8.1 %group.5 = (bf16[128,1536]{1,0:T(8,128)(2,1)}, bf16[128,1536]{1,0:T(8,128)(2,1)}, bf16[2,128,1536]{2,1,0:T(8,128)(2,1)}) custom-call(s32[1]{0:T(128)S(6)} %copy.29.failed, s32[4,16]{1,0:T(4,128)} %bitcast.14, bf16[136,1536]{1,0:T(8,128)(2,1)} %collective-permute-done.3.refs_0_, bf16[136,1536]{1,0:T(8,128)(2,1)} %after.8.refs_1_, ...), custom_call_target="tpu_custom_call" | custom-call | flops 3019898880 | bytes 14942208 | tf_op jit(solution)/shard_map/group/pallas_call | solution.py:304
  42.9 0.9 collective-permute-done.7.refs_0_
  43.8 1.3 %collective-permute-done.10.refs_1_ = bf16[136,1536]{1,0:T(8,128)(2,1)} collective-permute-done((bf16[136,1536]{1,0:T(8,128)(2,1)}, bf16[136,1536]{1,0:T(8,128)(2,1)}, u32[]{:S(2)}, u32[]{:S(2)}) %collective-permute-start.10) | collective-permute-done | bytes 417824 | tf_op jit(solution)/shard_map/ppermute | solution.py:436
  45.1 0.0 collective-permute-start.16
  45.1 0.5 collective-permute-start.14
  45.6 0.0 collective-permute-start.15
  45.6 1.7 %collective-permute-start.11 = (bf16[136,1536]{1,0:T(8,128)(2,1)}, bf16[136,1536]{1,0:T(8,128)(2,1)}, u32[]{:S(2)}, u32[]{:S(2)}) collective-permute-start(bf16[136,1536]{1,0:T(8,128)(2,1)} %collective-permute-done.10.refs_1_), channel_id=1, source_target_pairs={{0,4},{1,5},{2,6},{3,7},{4,12},{5,13},{6,14},{7,15},{8,0},{9,1},{1... | collective-permute-start | bytes 1253384 | tf_op jit(solution)/shard_map/ppermute | solution.py:436
  47.3 0.4 collective-permute-done.16.refs_1_.refs_3_
  47.7 2.0 %sums.8.refs_8_ = bf16[128,1536]{1,0:T(8,128)(2,1)} custom-call(bf16[128,1536]{1,0:T(8,128)(2,1)} %get-tuple-element.23.refs_0_, bf16[2,128,1536]{2,1,0:T(8,128)(2,1)} %collective-permute-done.16.refs_1_.refs_3_), custom_call_target="tpu_custom_call" | custom-call | flops 393216 | bytes 1179648 | tf_op jit(solution)/shard_map/sums/pallas_call | solution.py:402
  49.7 1.8 %collective-permute-start.17 = (bf16[128,1536]{1,0:T(8,128)(2,1)}, bf16[128,1536]{1,0:T(8,128)(2,1)}, u32[]{:S(2)}, u32[]{:S(2)}) collective-permute-start(bf16[128,1536]{1,0:T(8,128)(2,1)} %sums.8.refs_8_), channel_id=1, source_target_pairs={{0,2},{1,3},{2,0},{3,1},{4,6},{5,7},{6,4},{7,5},{8,10},{9,11},{10,... | collective-permute-start | bytes 1179656 | tf_op jit(solution)/shard_map/ppermute | solution.py:436
  51.5 0.0 collective-permute-done.14.refs_2_
  51.5 0.0 collective-permute-done.15.refs_3_
  51.5 8.1 %group.6 = (bf16[128,1536]{1,0:T(8,128)(2,1)}, bf16[128,1536]{1,0:T(8,128)(2,1)}, bf16[2,128,1536]{2,1,0:T(8,128)(2,1)}) custom-call(s32[1]{0:T(128)S(6)} %copy.29.failed, s32[4,16]{1,0:T(4,128)} %bitcast.15, bf16[136,1536]{1,0:T(8,128)(2,1)} %after.9.refs_2_.refs_0_, bf16[136,1536]{1,0:T(8,128)(2,1)} %collective-permute-done.10.refs_1_, ...), custom_call_target="tpu_custom_call" | custom-call | flops 3019898880 | bytes 14942208 | tf_op jit(solution)/shard_map/group/pallas_call | solution.py:304
  59.6 0.0 collective-permute-done.11.refs_1_
  59.6 1.6 %collective-permute-done.17.refs_3_.refs_4_ = bf16[128,1536]{1,0:T(8,128)(2,1)} collective-permute-done((bf16[128,1536]{1,0:T(8,128)(2,1)}, bf16[128,1536]{1,0:T(8,128)(2,1)}, u32[]{:S(2)}, u32[]{:S(2)}) %collective-permute-start.17) | collective-permute-done | bytes 393248 | tf_op jit(solution)/shard_map/ppermute | solution.py:436
  61.2 0.5 collective-permute-start.12
  61.7 0.0 collective-permute-start.13
  61.7 2.1 %collective-permute-done.18.refs_1_ = bf16[2,128,1536]{2,1,0:T(8,128)(2,1)} collective-permute-done((bf16[2,128,1536]{2,1,0:T(8,128)(2,1)}, bf16[2,128,1536]{2,1,0:T(8,128)(2,1)}, u32[]{:S(2)}, u32[]{:S(2)}) %collective-permute-start.18) | collective-permute-done | bytes 786464 | tf_op jit(solution)/shard_map/ppermute | solution.py:436
  63.8 2.5 %sums.9 = (bf16[128,1536]{1,0:T(8,128)(2,1)}, bf16[128,1536]{1,0:T(8,128)(2,1)}) custom-call(bf16[128,1536]{1,0:T(8,128)(2,1)} %get-tuple-element.25.refs_0_, bf16[2,128,1536]{2,1,0:T(8,128)(2,1)} %collective-permute-done.18.refs_1_, bf16[128,1536]{1,0:T(8,128)(2,1)} %get-tuple-element.22.refs_1_.refs_2_, ...), custom_call_target="tpu_custom_call" | custom-call | flops 983040 | bytes 2752512 | tf_op jit(solution)/shard_map/sums/pallas_call | solution.py:402
  66.4 1.8 %collective-permute-start.19 = (bf16[128,1536]{1,0:T(8,128)(2,1)}, bf16[128,1536]{1,0:T(8,128)(2,1)}, u32[]{:S(2)}, u32[]{:S(2)}) collective-permute-start(bf16[128,1536]{1,0:T(8,128)(2,1)} %get-tuple-element.27.refs_8_), channel_id=1, source_target_pairs={{0,2},{1,3},{2,0},{3,1},{4,6},{5,7},{6,4},{7,5},{8,10},{9,11},{10,... | collective-permute-start | bytes 1179656 | tf_op jit(solution)/shard_map/ppermute | solution.py:436
  68.1 1.6 %collective-permute-start.20 = (bf16[128,1536]{1,0:T(8,128)(2,1)}, bf16[128,1536]{1,0:T(8,128)(2,1)}, u32[]{:S(2)}, u32[]{:S(2)}) collective-permute-start(bf16[128,1536]{1,0:T(8,128)(2,1)} %get-tuple-element.30), channel_id=1, source_target_pairs={{0,4},{1,5},{2,6},{3,7},{4,12},{5,13},{6,14},{7,15},{8,0},{9,1},{1... | collective-permute-start | bytes 1179656 | tf_op jit(solution)/shard_map/ppermute | solution.py:436
  69.7 0.0 collective-permute-done.12.refs_2_
  69.7 0.0 collective-permute-done.13.refs_3_
  69.7 8.1 %group.7 = (bf16[128,1536]{1,0:T(8,128)(2,1)}, bf16[128,1536]{1,0:T(8,128)(2,1)}, bf16[2,128,1536]{2,1,0:T(8,128)(2,1)}) custom-call(s32[1]{0:T(128)S(6)} %copy.29.failed, s32[4,16]{1,0:T(4,128)} %bitcast.16, bf16[136,1536]{1,0:T(8,128)(2,1)} %after.11.refs_2_.refs_0_, bf16[136,1536]{1,0:T(8,128)(2,1)} %collective-permute-done.11.refs_1_, ...), custom_call_target="tpu_custom_call" | custom-call | flops 3019898880 | bytes 14942208 | tf_op jit(solution)/shard_map/group/pallas_call | solution.py:304
  77.8 0.1 collective-permute-done.19.refs_1_.refs_2_
  77.9 2.3 %collective-permute-done.20.refs_2_.refs_3_ = bf16[128,1536]{1,0:T(8,128)(2,1)} collective-permute-done((bf16[128,1536]{1,0:T(8,128)(2,1)}, bf16[128,1536]{1,0:T(8,128)(2,1)}, u32[]{:S(2)}, u32[]{:S(2)}) %collective-permute-start.20) | collective-permute-done | bytes 393248 | tf_op jit(solution)/shard_map/ppermute | solution.py:436
  80.2 0.0 collective-permute-start.21
  80.2 0.5 collective-permute-start.6
  80.7 2.4 %sums.11 = bf16[128,1536]{1,0:T(8,128)(2,1)} custom-call(bf16[128,1536]{1,0:T(8,128)(2,1)} %get-tuple-element.32.refs_0_, bf16[2,128,1536]{2,1,0:T(8,128)(2,1)} %collective-permute-done.18.refs_1_, bf16[128,1536]{1,0:T(8,128)(2,1)} %collective-permute-done.19.refs_1_.refs_2_, bf16[128,1536]{1,0:T(8,128)(2,1)} %collective-permute-done.20.refs_2_.refs_3_), custom_call_target="tpu_custom_call" | custom-call | flops 786432 | bytes 1966080 | tf_op jit(solution)/shard_map/sums/pallas_call | solution.py:402
  83.1 0.7 collective-permute-start.23
  83.8 2.0 %sums.10 = bf16[128,1536]{1,0:T(8,128)(2,1)} custom-call(bf16[128,1536]{1,0:T(8,128)(2,1)} %get-tuple-element.31.refs_0_, bf16[2,128,1536]{2,1,0:T(8,128)(2,1)} %collective-permute-done.21.refs_1_), custom_call_target="tpu_custom_call" | custom-call | flops 393216 | bytes 1179648 | tf_op jit(solution)/shard_map/sums/pallas_call | solution.py:402
  85.8 0.6 collective-permute-start.22
  86.4 0.0 collective-permute-done.6.refs_1_
  86.4 2.0 %sums.7.refs_0_ = bf16[128,1536]{1,0:T(8,128)(2,1)} custom-call(bf16[128,1536]{1,0:T(8,128)(2,1)} %get-tuple-element.21.refs_0_, bf16[2,128,1536]{2,1,0:T(8,128)(2,1)} %collective-permute-done.6.refs_1_), custom_call_target="tpu_custom_call" | custom-call | flops 393216 | bytes 1179648 | tf_op jit(solution)/shard_map/sums/pallas_call | solution.py:402
  88.4 7.0 %collective-permute-done.23.refs_3_ = bf16[128,1536]{1,0:T(8,128)(2,1)} collective-permute-done((bf16[128,1536]{1,0:T(8,128)(2,1)}, bf16[128,1536]{1,0:T(8,128)(2,1)}, u32[]{:S(2)}, u32[]{:S(2)}) %collective-permute-start.23) | collective-permute-done | bytes 393248 | tf_op jit(solution)/shard_map/ppermute | solution.py:436
  95.4 1.6 %collective-permute-done.22.refs_2_ = bf16[128,1536]{1,0:T(8,128)(2,1)} collective-permute-done((bf16[128,1536]{1,0:T(8,128)(2,1)}, bf16[128,1536]{1,0:T(8,128)(2,1)}, u32[]{:S(2)}, u32[]{:S(2)}) %collective-permute-start.22) | collective-permute-done | bytes 393248 | tf_op jit(solution)/shard_map/ppermute | solution.py:436
  97.0 2.4 %sums.12.refs_1_ = bf16[128,1536]{1,0:T(8,128)(2,1)} custom-call(bf16[128,1536]{1,0:T(8,128)(2,1)} %get-tuple-element.28.refs_0_, bf16[2,128,1536]{2,1,0:T(8,128)(2,1)} %collective-permute-done.21.refs_1_, bf16[128,1536]{1,0:T(8,128)(2,1)} %collective-permute-done.22.refs_2_, bf16[128,1536]{1,0:T(8,128)(2,1)} %collective-permute-done.23.refs_3_), custom_call_target="tpu_custom_call" | custom-call | flops 786432 | bytes 1966080 | tf_op jit(solution)/shard_map/sums/pallas_call | solution.py:402
  99.3 0.6 collective-permute-start.24
  99.9 2.1 %collective-permute-start.25 = (bf16[128,1536]{1,0:T(8,128)(2,1)}, bf16[128,1536]{1,0:T(8,128)(2,1)}, u32[]{:S(2)}, u32[]{:S(2)}) collective-permute-start(bf16[128,1536]{1,0:T(8,128)(2,1)} %sums.12.refs_1_), channel_id=1, source_target_pairs={{0,4},{1,5},{2,6},{3,7},{4,12},{5,13},{6,14},{7,15},{8,0},{9,1},{1... | collective-permute-start | bytes 1179656 | tf_op jit(solution)/shard_map/ppermute | solution.py:436
  102.0 7.6 %collective-permute-done.24.refs_2_ = bf16[128,1536]{1,0:T(8,128)(2,1)} collective-permute-done((bf16[128,1536]{1,0:T(8,128)(2,1)}, bf16[128,1536]{1,0:T(8,128)(2,1)}, u32[]{:S(2)}, u32[]{:S(2)}) %collective-permute-start.24) | collective-permute-done | bytes 393248 | tf_op jit(solution)/shard_map/ppermute | solution.py:436
  109.6 1.1 collective-permute-done.25.refs_3_
  110.7 2.4 %sums.13 = bf16[128,1536]{1,0:T(8,128)(2,1)} custom-call(bf16[128,1536]{1,0:T(8,128)(2,1)} %get-tuple-element.19.refs_1_.refs_8_.refs_0_, bf16[2,128,1536]{2,1,0:T(8,128)(2,1)} %collective-permute-done.6.refs_1_, bf16[128,1536]{1,0:T(8,128)(2,1)} %collective-permute-done.24.refs_2_, bf16[128,1536]{1,0:T(8,128)(2,1)} %collective-permute-done.25.refs_3_), custom_call_target="tpu_custom_call" | custom-call | flops 786432 | bytes 1966080 | tf_op jit(solution)/shard_map/sums/pallas_call | solution.py:402
  (19 shorter events, 0.0 us)
Async XLA Ops:
  1.8 4.6 %copy-start = (bf16[136,1536]{1,0:T(8,128)(2,1)}, bf16[136,1536]{1,0:T(8,128)(2,1)S(1)}, u32[]{:S(2)}) copy-start(bf16[136,1536]{1,0:T(8,128)(2,1)S(1)} %fusion.1.refs_0_) | copy-start | bytes 1253380
  1.8 12.7 %collective-permute-start = (bf16[136,1536]{1,0:T(8,128)(2,1)S(1)}, bf16[136,1536]{1,0:T(8,128)(2,1)S(1)}, u32[]{:S(2)}, u32[]{:S(2)}) collective-permute-start(bf16[136,1536]{1,0:T(8,128)(2,1)S(1)} %fusion.1.refs_0_), channel_id=1, source_target_pairs={{0,2},{1,3},{2,0},{3,1},{4,6},{5,7},{6,4},{7,5},{8,10},{9,11},{10,... | collective-permute-start | bytes 1253384 | tf_op jit(solution)/shard_map/ppermute | solution.py:436
  4.8 12.1 %collective-permute-start.3 = (bf16[136,1536]{1,0:T(8,128)(2,1)S(1)}, bf16[136,1536]{1,0:T(8,128)(2,1)}, u32[]{:S(2)}, u32[]{:S(2)}) collective-permute-start(bf16[136,1536]{1,0:T(8,128)(2,1)S(1)} %fusion.1.refs_0_), channel_id=1, source_target_pairs={{0,4},{1,5},{2,6},{3,7},{4,12},{5,13},{6,14},{7,15},{8,0},{9,1},{1... | collective-permute-start | bytes 1253384 | tf_op jit(solution)/shard_map/ppermute | solution.py:436
  6.4 12.5 %collective-permute-start.1 = (bf16[136,1536]{1,0:T(8,128)(2,1)S(1)}, bf16[136,1536]{1,0:T(8,128)(2,1)S(1)}, u32[]{:S(2)}, u32[]{:S(2)}) collective-permute-start(bf16[136,1536]{1,0:T(8,128)(2,1)S(1)} %fusion.1.refs_0_), channel_id=1, source_target_pairs={{0,1},{1,0},{2,3},{3,2},{4,5},{5,4},{6,7},{7,6},{8,9},{9,8},{10,11... | collective-permute-start | bytes 1253384 | tf_op jit(solution)/shard_map/ppermute | solution.py:436
  14.4 4.4 %copy-start.1 = (bf16[136,1536]{1,0:T(8,128)(2,1)}, bf16[136,1536]{1,0:T(8,128)(2,1)S(1)}, u32[]{:S(2)}) copy-start(bf16[136,1536]{1,0:T(8,128)(2,1)S(1)} %collective-permute-done.refs_1_) | copy-start | bytes 1253380
  14.4 4.4 %collective-permute-start.2 = (bf16[136,1536]{1,0:T(8,128)(2,1)S(1)}, bf16[136,1536]{1,0:T(8,128)(2,1)S(1)}, u32[]{:S(2)}, u32[]{:S(2)}) collective-permute-start(bf16[136,1536]{1,0:T(8,128)(2,1)S(1)} %collective-permute-done.refs_1_), channel_id=1, source_target_pairs={{0,1},{1,0},{2,3},{3,2},{4,5},{5,4},{6,7},{7,6},{8,9},{9,8},{10,11... | collective-permute-start | bytes 1253384 | tf_op jit(solution)/shard_map/ppermute | solution.py:436
  16.9 11.6 %collective-permute-start.4 = (bf16[136,1536]{1,0:T(8,128)(2,1)}, bf16[136,1536]{1,0:T(8,128)(2,1)}, u32[]{:S(2)}, u32[]{:S(2)}) collective-permute-start(bf16[136,1536]{1,0:T(8,128)(2,1)} %collective-permute-done.3.refs_0_), channel_id=1, source_target_pairs={{0,2},{1,3},{2,0},{3,1},{4,6},{5,7},{6,4},{7,5},{8,10},{9,11},{10,... | collective-permute-start | bytes 1253384 | tf_op jit(solution)/shard_map/ppermute | solution.py:436
  18.0 16.7 %collective-permute-start.8 = (bf16[136,1536]{1,0:T(8,128)(2,1)}, bf16[136,1536]{1,0:T(8,128)(2,1)}, u32[]{:S(2)}, u32[]{:S(2)}) collective-permute-start(bf16[136,1536]{1,0:T(8,128)(2,1)} %collective-permute-done.3.refs_0_), channel_id=1, source_target_pairs={{0,1},{1,0},{2,3},{3,2},{4,5},{5,4},{6,7},{7,6},{8,9},{9,8},{10,11... | collective-permute-start | bytes 1253384 | tf_op jit(solution)/shard_map/ppermute | solution.py:436
  18.1 13.3 %collective-permute-start.5 = (bf16[136,1536]{1,0:T(8,128)(2,1)}, bf16[136,1536]{1,0:T(8,128)(2,1)}, u32[]{:S(2)}, u32[]{:S(2)}) collective-permute-start(bf16[136,1536]{1,0:T(8,128)(2,1)} %collective-permute-done.3.refs_0_), channel_id=1, source_target_pairs={{0,4},{1,5},{2,6},{3,7},{4,12},{5,13},{6,14},{7,15},{8,0},{9,1},{1... | collective-permute-start | bytes 1253384 | tf_op jit(solution)/shard_map/ppermute | solution.py:436
  18.9 0.8 copy-start.2
  19.7 0.8 copy-start.3
  28.5 6.2 %collective-permute-start.9 = (bf16[136,1536]{1,0:T(8,128)(2,1)}, bf16[136,1536]{1,0:T(8,128)(2,1)}, u32[]{:S(2)}, u32[]{:S(2)}) collective-permute-start(bf16[136,1536]{1,0:T(8,128)(2,1)} %after.8.refs_1_), channel_id=1, source_target_pairs={{0,1},{1,0},{2,3},{3,2},{4,5},{5,4},{6,7},{7,6},{8,9},{9,8},{10,11... | collective-permute-start | bytes 1253384 | tf_op jit(solution)/shard_map/ppermute | solution.py:436
  31.4 12.4 %collective-permute-start.7 = (bf16[136,1536]{1,0:T(8,128)(2,1)}, bf16[136,1536]{1,0:T(8,128)(2,1)}, u32[]{:S(2)}, u32[]{:S(2)}) collective-permute-start(bf16[136,1536]{1,0:T(8,128)(2,1)} %after.9.refs_2_.refs_0_), channel_id=1, source_target_pairs={{0,4},{1,5},{2,6},{3,7},{4,12},{5,13},{6,14},{7,15},{8,0},{9,1},{1... | collective-permute-start | bytes 1253384 | tf_op jit(solution)/shard_map/ppermute | solution.py:436
  32.2 12.8 %collective-permute-start.10 = (bf16[136,1536]{1,0:T(8,128)(2,1)}, bf16[136,1536]{1,0:T(8,128)(2,1)}, u32[]{:S(2)}, u32[]{:S(2)}) collective-permute-start(bf16[136,1536]{1,0:T(8,128)(2,1)} %after.9.refs_2_.refs_0_), channel_id=1, source_target_pairs={{0,2},{1,3},{2,0},{3,1},{4,6},{5,7},{6,4},{7,5},{8,10},{9,11},{10,... | collective-permute-start | bytes 1253384 | tf_op jit(solution)/shard_map/ppermute | solution.py:436
  45.1 2.6 %collective-permute-start.16 = (bf16[2,128,1536]{2,1,0:T(8,128)(2,1)}, bf16[2,128,1536]{2,1,0:T(8,128)(2,1)}, u32[]{:S(2)}, u32[]{:S(2)}) collective-permute-start(bf16[2,128,1536]{2,1,0:T(8,128)(2,1)} %after.12), channel_id=1, source_target_pairs={{0,1},{1,0},{2,3},{3,2},{4,5},{5,4},{6,7},{7,6},{8,9},{9,8},{10,11... | collective-permute-start | bytes 2359304 | tf_op jit(solution)/shard_map/ppermute | solution.py:436
  45.1 6.4 %collective-permute-start.14 = (bf16[136,1536]{1,0:T(8,128)(2,1)}, bf16[136,1536]{1,0:T(8,128)(2,1)}, u32[]{:S(2)}, u32[]{:S(2)}) collective-permute-start(bf16[136,1536]{1,0:T(8,128)(2,1)} %after.9.refs_2_.refs_0_), channel_id=1, source_target_pairs={{0,1},{1,0},{2,3},{3,2},{4,5},{5,4},{6,7},{7,6},{8,9},{9,8},{10,11... | collective-permute-start | bytes 1253384 | tf_op jit(solution)/shard_map/ppermute | solution.py:436
  45.6 5.9 %collective-permute-start.15 = (bf16[136,1536]{1,0:T(8,128)(2,1)}, bf16[136,1536]{1,0:T(8,128)(2,1)}, u32[]{:S(2)}, u32[]{:S(2)}) collective-permute-start(bf16[136,1536]{1,0:T(8,128)(2,1)} %collective-permute-done.10.refs_1_), channel_id=1, source_target_pairs={{0,1},{1,0},{2,3},{3,2},{4,5},{5,4},{6,7},{7,6},{8,9},{9,8},{10,11... | collective-permute-start | bytes 1253384 | tf_op jit(solution)/shard_map/ppermute | solution.py:436
  45.6 14.0 %collective-permute-start.11 = (bf16[136,1536]{1,0:T(8,128)(2,1)}, bf16[136,1536]{1,0:T(8,128)(2,1)}, u32[]{:S(2)}, u32[]{:S(2)}) collective-permute-start(bf16[136,1536]{1,0:T(8,128)(2,1)} %collective-permute-done.10.refs_1_), channel_id=1, source_target_pairs={{0,4},{1,5},{2,6},{3,7},{4,12},{5,13},{6,14},{7,15},{8,0},{9,1},{1... | collective-permute-start | bytes 1253384 | tf_op jit(solution)/shard_map/ppermute | solution.py:436
  49.7 11.5 %collective-permute-start.17 = (bf16[128,1536]{1,0:T(8,128)(2,1)}, bf16[128,1536]{1,0:T(8,128)(2,1)}, u32[]{:S(2)}, u32[]{:S(2)}) collective-permute-start(bf16[128,1536]{1,0:T(8,128)(2,1)} %sums.8.refs_8_), channel_id=1, source_target_pairs={{0,2},{1,3},{2,0},{3,1},{4,6},{5,7},{6,4},{7,5},{8,10},{9,11},{10,... | collective-permute-start | bytes 1179656 | tf_op jit(solution)/shard_map/ppermute | solution.py:436
  61.2 2.6 %collective-permute-start.18 = (bf16[2,128,1536]{2,1,0:T(8,128)(2,1)}, bf16[2,128,1536]{2,1,0:T(8,128)(2,1)}, u32[]{:S(2)}, u32[]{:S(2)}) collective-permute-start(bf16[2,128,1536]{2,1,0:T(8,128)(2,1)} %after.13), channel_id=1, source_target_pairs={{0,1},{1,0},{2,3},{3,2},{4,5},{5,4},{6,7},{7,6},{8,9},{9,8},{10,11... | collective-permute-start | bytes 2359304 | tf_op jit(solution)/shard_map/ppermute | solution.py:436
  61.2 8.5 %collective-permute-start.12 = (bf16[136,1536]{1,0:T(8,128)(2,1)}, bf16[136,1536]{1,0:T(8,128)(2,1)}, u32[]{:S(2)}, u32[]{:S(2)}) collective-permute-start(bf16[136,1536]{1,0:T(8,128)(2,1)} %after.11.refs_2_.refs_0_), channel_id=1, source_target_pairs={{0,1},{1,0},{2,3},{3,2},{4,5},{5,4},{6,7},{7,6},{8,9},{9,8},{10,11... | collective-permute-start | bytes 1253384 | tf_op jit(solution)/shard_map/ppermute | solution.py:436
  61.7 8.0 %collective-permute-start.13 = (bf16[136,1536]{1,0:T(8,128)(2,1)}, bf16[136,1536]{1,0:T(8,128)(2,1)}, u32[]{:S(2)}, u32[]{:S(2)}) collective-permute-start(bf16[136,1536]{1,0:T(8,128)(2,1)} %collective-permute-done.11.refs_1_), channel_id=1, source_target_pairs={{0,1},{1,0},{2,3},{3,2},{4,5},{5,4},{6,7},{7,6},{8,9},{9,8},{10,11... | collective-permute-start | bytes 1253384 | tf_op jit(solution)/shard_map/ppermute | solution.py:436
  66.4 11.5 %collective-permute-start.19 = (bf16[128,1536]{1,0:T(8,128)(2,1)}, bf16[128,1536]{1,0:T(8,128)(2,1)}, u32[]{:S(2)}, u32[]{:S(2)}) collective-permute-start(bf16[128,1536]{1,0:T(8,128)(2,1)} %get-tuple-element.27.refs_8_), channel_id=1, source_target_pairs={{0,2},{1,3},{2,0},{3,1},{4,6},{5,7},{6,4},{7,5},{8,10},{9,11},{10,... | collective-permute-start | bytes 1179656 | tf_op jit(solution)/shard_map/ppermute | solution.py:436
  68.1 12.1 %collective-permute-start.20 = (bf16[128,1536]{1,0:T(8,128)(2,1)}, bf16[128,1536]{1,0:T(8,128)(2,1)}, u32[]{:S(2)}, u32[]{:S(2)}) collective-permute-start(bf16[128,1536]{1,0:T(8,128)(2,1)} %get-tuple-element.30), channel_id=1, source_target_pairs={{0,4},{1,5},{2,6},{3,7},{4,12},{5,13},{6,14},{7,15},{8,0},{9,1},{1... | collective-permute-start | bytes 1179656 | tf_op jit(solution)/shard_map/ppermute | solution.py:436
  80.2 3.6 %collective-permute-start.21 = (bf16[2,128,1536]{2,1,0:T(8,128)(2,1)}, bf16[2,128,1536]{2,1,0:T(8,128)(2,1)}, u32[]{:S(2)}, u32[]{:S(2)}) collective-permute-start(bf16[2,128,1536]{2,1,0:T(8,128)(2,1)} %after.14), channel_id=1, source_target_pairs={{0,1},{1,0},{2,3},{3,2},{4,5},{5,4},{6,7},{7,6},{8,9},{9,8},{10,11... | collective-permute-start | bytes 2359304 | tf_op jit(solution)/shard_map/ppermute | solution.py:436
  80.2 6.2 %collective-permute-start.6 = (bf16[2,128,1536]{2,1,0:T(8,128)(2,1)}, bf16[2,128,1536]{2,1,0:T(8,128)(2,1)}, u32[]{:S(2)}, u32[]{:S(2)}) collective-permute-start(bf16[2,128,1536]{2,1,0:T(8,128)(2,1)} %after.10), channel_id=1, source_target_pairs={{0,1},{1,0},{2,3},{3,2},{4,5},{5,4},{6,7},{7,6},{8,9},{9,8},{10,11... | collective-permute-start | bytes 2359304 | tf_op jit(solution)/shard_map/ppermute | solution.py:436
  83.1 12.3 %collective-permute-start.23 = (bf16[128,1536]{1,0:T(8,128)(2,1)}, bf16[128,1536]{1,0:T(8,128)(2,1)}, u32[]{:S(2)}, u32[]{:S(2)}) collective-permute-start(bf16[128,1536]{1,0:T(8,128)(2,1)} %sums.11), channel_id=1, source_target_pairs={{0,4},{1,5},{2,6},{3,7},{4,12},{5,13},{6,14},{7,15},{8,0},{9,1},{1... | collective-permute-start | bytes 1179656 | tf_op jit(solution)/shard_map/ppermute | solution.py:436
  85.8 11.1 %collective-permute-start.22 = (bf16[128,1536]{1,0:T(8,128)(2,1)}, bf16[128,1536]{1,0:T(8,128)(2,1)}, u32[]{:S(2)}, u32[]{:S(2)}) collective-permute-start(bf16[128,1536]{1,0:T(8,128)(2,1)} %sums.10), channel_id=1, source_target_pairs={{0,2},{1,3},{2,0},{3,1},{4,6},{5,7},{6,4},{7,5},{8,10},{9,11},{10,... | collective-permute-start | bytes 1179656 | tf_op jit(solution)/shard_map/ppermute | solution.py:436
  99.3 10.2 %collective-permute-start.24 = (bf16[128,1536]{1,0:T(8,128)(2,1)}, bf16[128,1536]{1,0:T(8,128)(2,1)}, u32[]{:S(2)}, u32[]{:S(2)}) collective-permute-start(bf16[128,1536]{1,0:T(8,128)(2,1)} %after.15), channel_id=1, source_target_pairs={{0,2},{1,3},{2,0},{3,1},{4,6},{5,7},{6,4},{7,5},{8,10},{9,11},{10,... | collective-permute-start | bytes 1179656 | tf_op jit(solution)/shard_map/ppermute | solution.py:436
  99.9 10.8 %collective-permute-start.25 = (bf16[128,1536]{1,0:T(8,128)(2,1)}, bf16[128,1536]{1,0:T(8,128)(2,1)}, u32[]{:S(2)}, u32[]{:S(2)}) collective-permute-start(bf16[128,1536]{1,0:T(8,128)(2,1)} %sums.12.refs_1_), channel_id=1, source_target_pairs={{0,4},{1,5},{2,6},{3,7},{4,12},{5,13},{6,14},{7,15},{8,0},{9,1},{1... | collective-permute-start | bytes 1179656 | tf_op jit(solution)/shard_map/ppermute | solution.py:436

commit v11 on v9

--- a/solution.py
+++ b/solution.py
@@ -378,7 +378,6 @@
     steps = len(order)
     after = {a: order[(i + 1) % steps] for i, a in enumerate(order)}
     round_ring = [(d, after[d // 4] * 4 + d % 4) for d in range(owners)]
-    back = [(b, a) for a, b in round_ring]
     over_y = [(d, d ^ 2) for d in range(owners)]
     over_core = [(d, d ^ 1) for d in range(owners)]
     move = lambda a, pairs: lax.ppermute(a, "expert", pairs)
@@ -390,7 +389,8 @@
     meta = jnp.pad(meta, ((0, 7), (0, width - 3 * top * tok)))
     held = [jnp.concatenate([tokens, meta], axis=0)]
     held.append(move(held[0], round_ring))
-    across, kept, got, from_y = [], [], [], []
+    across, kept, got = [], [], []
+    last = steps - 1
 
     def add_group(k, shares, *earlier):
         blocks = (held[k], across[k], move(held[k], over_core), move(across[k], over_core))
@@ -398,35 +398,47 @@
             failed, holders, blocks, weights, shares, earlier, tok, top, capacity
         )
         kept.append((keep0, keep1))
-        from_y.extend(move(a, over_y) for a in summed)
-        return send
+        return send, *summed
+
+    def total(k, rows, *more):
+        result = f32(kept[k][0][rows]) + f32(got[k][0, rows])
+        for a in more:
+            result = result + f32(a)
+        return result.astype(jnp.bfloat16)
 
     across.append(move(held[0], over_y))
-    send = add_group(0, ())
+    (send,) = add_group(0, ())
+    from_y, arrived, own = None, (), None
+    every = slice(0, tok)
     for k in range(1, steps):
-        last = k == steps - 1
-        across.append(move(across[-1], round_ring) if last else move(held[k], over_y))
+        across.append(move(across[-1], round_ring) if k == last else move(held[k], over_y))
         if k == 1:
             across[1] = come_after(across[1], kept[0][0])
-        if not last:
+        if k < last:
             held.append(come_after(move(held[k], round_ring), kept[k - 1][0]))
-        send = come_after(send, across[k], held[min(k + 1, steps - 1)], *from_y[-2:-1])
-        got.append(move(send, over_core))
-        if last:
-            share = add(kept[-1][1], got[-1][1])
-            from_y.append(move(share, over_y))
-            send = add_group(k, (), share)
+        got.append(move(come_after(send, across[k], held[min(k + 1, last)]), over_core))
+        if k > 2:
+            arrived = (move(total(k - 2, every, from_y, *arrived), round_ring),)
+        if k > 1:
+            from_y = move(add(kept[k - 1][1], got[k - 1][1]), over_y)
+        if k == 2:
+            send, own = add_group(k, (kept[0][1], got[0]), kept[k - 1][0])
+            own = move(own, over_y)
         else:
-            send = add_group(k, (kept[-1][1], got[-1]))
-    got.append(move(come_after(send, *from_y[-2:-1]), over_core))
-    from_y.append(move(add(kept[-1][1], got[-1][1]), over_y))
-
-    total = lambda k: f32(kept[k][0]) + f32(got[k][0]) + f32(from_y[k])
-    result = total(0) + f32(move(total(1).astype(jnp.bfloat16), back))
-    passing = total(2)
-    for k in range(3, steps):
-        passing = total(k) + f32(move(passing.astype(jnp.bfloat16), round_ring))
-    return (result + f32(move(passing.astype(jnp.bfloat16), round_ring))).astype(jnp.bfloat16)
+            (send,) = add_group(k, (), kept[k - 1][0])
+    got.append(move(come_after(send, own), over_core))
+
+    halves = (slice(0, tok // 2), slice(tok // 2, tok))
+    passing = [
+        move(total(last - 1, rows, from_y[rows], *(a[rows] for a in arrived)), round_ring) for rows in halves
+    ]
+    shares = [move(add(kept[last][1][rows], got[last][1, rows]), over_y) for rows in halves]
+    first, second = halves
+    passed = total(last, first, shares[0], passing[0])
+    follows = total(last, second, shares[1], come_after(passing[1], passed))
+    passed = total(0, first, own[first], move(passed, round_ring))
+    follows = come_after(move(follows, round_ring), passed)
+    return jnp.concatenate([passed, total(0, second, own[second], follows)], axis=0)
 
 
 def shards(

time: 113 us -> 110 us (0.973)
  waiting for transfers between devices: 47.4 us -> 28.7 us
  other arithmetic: 10.7 us -> 19.5 us
  starting transfers between devices: 18.7 us -> 23.9 us
  local copies, waits for them, and re-layouts: 2.42 us -> 3.77 us
    ppermute x26 -> x29, waiting for transfers between devices: 47.4 us -> 28.7 us  [by_permutes(): move = lambda a, pairs: lax.ppermute(a, 'expert', pairs)]
    ppermute x26 -> x29, starting transfers between devices: 18.7 us -> 23.9 us  [by_permutes(): move = lambda a, pairs: lax.ppermute(a, 'expert', pairs)]
    convert_element_type x4 -> x6, other arithmetic: 6.05 us -> 10.1 us  [total(): return result.astype(jnp.bfloat16)]
    convert_element_type x2 -> x3, other arithmetic: 2.93 us -> 5.9 us  [by_permutes(): add = lambda a, b: (f32(a) + f32(b)).astype(jnp.bfloat16)]
    concatenate x0 -> x1, other arithmetic: none -> 1.7 us  [by_permutes(): jnp.concatenate([passed, total(0, second, own[second], follows)], axis=0)]
    unnamed x13 -> x17, local copies, waits for them, and re-layouts: 2.42 us -> 3.77 us
  transfers between devices with their start and end apart: 26 -> 29, of which waited for: 12 -> 11; matrix products, arithmetic and copies ran while one was open for 6% -> 13% of each run, Pallas kernels for 29% -> 30%
where the time goes in v11:
time: 110 us
  Pallas kernels  32.9 us (30%)
  waiting for transfers between devices  28.7 us (26%)
  starting transfers between devices  23.9 us (22%)
  other arithmetic  19.5 us (18%)
  local copies, waits for them, and re-layouts  3.77 us (3%)
    pallas_call x4, Pallas kernels, run_group(): pl.pallas_call(functools.partial(group_kernel, others=len(earlier), adds=...  32.8 us
    ppermute x29, waiting for transfers between devices, by_permutes(): move = lambda a, pairs: lax.ppermute(a, 'expert', pairs)  28.7 us
    ppermute x29, starting transfers between devices, by_permutes(): move = lambda a, pairs: lax.ppermute(a, 'expert', pairs)  23.9 us
    convert_element_type x6, other arithmetic, total(): return result.astype(jnp.bfloat16)  10.1 us
    convert_element_type x3, other arithmetic, by_permutes(): add = lambda a, b: (f32(a) + f32(b)).astype(jnp.bfloat16)  5.9 us
    unnamed x17, local copies, waits for them, and re-layouts  3.77 us
  transfers between devices with their start and end apart: 29, of which 11 were waited for; matrix products, arithmetic and copies ran while one was open for 13% of the time, Pallas kernels for 30%

profile of v11, /device:TPU:0, one launch (start us, length us, event | category | flops | bytes accessed | tf_op | source)
XLA Modules:
  0.0 109.5 jit_solution(845958534424336828)
XLA Ops:
  0.0 0.7 fusion.26
  0.7 1.0 fusion.5.refs_0_
  1.8 3.0 %collective-permute-start = (bf16[136,1536]{1,0:T(8,128)(2,1)S(1)}, bf16[136,1536]{1,0:T(8,128)(2,1)S(1)}, u32[]{:S(2)}, u32[]{:S(2)}) collective-permute-start(bf16[136,1536]{1,0:T(8,128)(2,1)S(1)} %fusion.5.refs_0_), channel_id=1, source_target_pairs={{0,2},{1,3},{2,0},{3,1},{4,6},{5,7},{6,4},{7,5},{8,10},{9,11},{10,... | collective-permute-start | bytes 1253384 | tf_op jit(solution)/shard_map/ppermute | solution.py:383
  4.8 1.6 %collective-permute-start.3 = (bf16[136,1536]{1,0:T(8,128)(2,1)S(1)}, bf16[136,1536]{1,0:T(8,128)(2,1)}, u32[]{:S(2)}, u32[]{:S(2)}) collective-permute-start(bf16[136,1536]{1,0:T(8,128)(2,1)S(1)} %fusion.5.refs_0_), channel_id=1, source_target_pairs={{0,4},{1,5},{2,6},{3,7},{4,12},{5,13},{6,14},{7,15},{8,0},{9,1},{1... | collective-permute-start | bytes 1253384 | tf_op jit(solution)/shard_map/ppermute | solution.py:383
  6.4 8.1 %collective-permute-done.refs_1_ = bf16[136,1536]{1,0:T(8,128)(2,1)S(1)} collective-permute-done((bf16[136,1536]{1,0:T(8,128)(2,1)S(1)}, bf16[136,1536]{1,0:T(8,128)(2,1)S(1)}, u32[]{:S(2)}, u32[]{:S(2)}) %collective-permute-start) | collective-permute-done | bytes 417824 | tf_op jit(solution)/shard_map/ppermute | solution.py:383
  14.4 0.0 collective-permute-start.2
  14.5 2.5 %collective-permute-done.3.refs_0_ = bf16[136,1536]{1,0:T(8,128)(2,1)} collective-permute-done((bf16[136,1536]{1,0:T(8,128)(2,1)S(1)}, bf16[136,1536]{1,0:T(8,128)(2,1)}, u32[]{:S(2)}, u32[]{:S(2)}) %collective-permute-start.3) | collective-permute-done | bytes 417824 | tf_op jit(solution)/shard_map/ppermute | solution.py:383
  16.9 0.5 collective-permute-start.4
  18.0 0.1 collective-permute-start.10
  18.1 0.8 collective-permute-start.5
  18.9 0.7 copy-done.6
  19.6 0.8 copy-done.7
  20.4 8.1 %group.4 = (bf16[128,1536]{1,0:T(8,128)(2,1)}, bf16[128,1536]{1,0:T(8,128)(2,1)}, bf16[2,128,1536]{2,1,0:T(8,128)(2,1)}) custom-call(s32[1]{0:T(128)S(6)} %copy.31.failed, s32[4,16]{1,0:T(4,128)} %bitcast.68, bf16[136,1536]{1,0:T(8,128)(2,1)} %copy-done, bf16[136,1536]{1,0:T(8,128)(2,1)} %copy-done.5, bf16[136,1536]{1,0:T(8,128)(2,1)} %copy-done.6, ...), custom_call_target="tpu_custom_call" | custom-call | flops 3019898880 | bytes 14942208 | tf_op jit(solution)/shard_map/group/pallas_call | solution.py:316
  28.5 0.2 collective-permute-start.11
  28.8 2.6 %collective-permute-done.5.refs_0_ = bf16[136,1536]{1,0:T(8,128)(2,1)} collective-permute-done((bf16[136,1536]{1,0:T(8,128)(2,1)}, bf16[136,1536]{1,0:T(8,128)(2,1)}, u32[]{:S(2)}, u32[]{:S(2)}) %collective-permute-start.5) | collective-permute-done | bytes 417824 | tf_op jit(solution)/shard_map/ppermute | solution.py:383
  31.4 1.9 %collective-permute-start.13 = (bf16[136,1536]{1,0:T(8,128)(2,1)}, bf16[136,1536]{1,0:T(8,128)(2,1)}, u32[]{:S(2)}, u32[]{:S(2)}) collective-permute-start(bf16[136,1536]{1,0:T(8,128)(2,1)} %after.10.refs_2_.refs_0_), channel_id=1, source_target_pairs={{0,4},{1,5},{2,6},{3,7},{4,12},{5,13},{6,14},{7,15},{8,0},{9,1},{1... | collective-permute-start | bytes 1253384 | tf_op jit(solution)/shard_map/ppermute | solution.py:383
  33.2 1.6 %collective-permute-start.7 = (bf16[136,1536]{1,0:T(8,128)(2,1)}, bf16[136,1536]{1,0:T(8,128)(2,1)}, u32[]{:S(2)}, u32[]{:S(2)}) collective-permute-start(bf16[136,1536]{1,0:T(8,128)(2,1)} %after.10.refs_2_.refs_0_), channel_id=1, source_target_pairs={{0,2},{1,3},{2,0},{3,1},{4,6},{5,7},{6,4},{7,5},{8,10},{9,11},{10,... | collective-permute-start | bytes 1253384 | tf_op jit(solution)/shard_map/ppermute | solution.py:383
  34.8 0.0 collective-permute-done.11.refs_3_
  34.8 8.2 %group.5 = (bf16[128,1536]{1,0:T(8,128)(2,1)}, bf16[128,1536]{1,0:T(8,128)(2,1)}, bf16[2,128,1536]{2,1,0:T(8,128)(2,1)}) custom-call(s32[1]{0:T(128)S(6)} %copy.31.failed, s32[4,16]{1,0:T(4,128)} %bitcast.69, bf16[136,1536]{1,0:T(8,128)(2,1)} %collective-permute-done.3.refs_0_, bf16[136,1536]{1,0:T(8,128)(2,1)} %after.9.refs_1_, ...), custom_call_target="tpu_custom_call" | custom-call | flops 3019898880 | bytes 14942208 | tf_op jit(solution)/shard_map/group/pallas_call | solution.py:316
  43.1 0.7 collective-permute-done.13.refs_0_
  43.8 1.5 %collective-permute-done.7.refs_1_ = bf16[136,1536]{1,0:T(8,128)(2,1)} collective-permute-done((bf16[136,1536]{1,0:T(8,128)(2,1)}, bf16[136,1536]{1,0:T(8,128)(2,1)}, u32[]{:S(2)}, u32[]{:S(2)}) %collective-permute-start.7) | collective-permute-done | bytes 417824 | tf_op jit(solution)/shard_map/ppermute | solution.py:383
  45.3 0.5 collective-permute-start.6
  45.8 0.0 collective-permute-start.8
  45.8 0.5 collective-permute-start.9
  46.3 1.6 %collective-permute-start.14 = (bf16[136,1536]{1,0:T(8,128)(2,1)}, bf16[136,1536]{1,0:T(8,128)(2,1)}, u32[]{:S(2)}, u32[]{:S(2)}) collective-permute-start(bf16[136,1536]{1,0:T(8,128)(2,1)} %collective-permute-done.7.refs_1_), channel_id=1, source_target_pairs={{0,4},{1,5},{2,6},{3,7},{4,12},{5,13},{6,14},{7,15},{8,0},{9,1},{1... | collective-permute-start | bytes 1253384 | tf_op jit(solution)/shard_map/ppermute | solution.py:383
  47.8 0.1 collective-permute-done.21
  47.9 2.0 %fusion.1 = bf16[128,1536]{1,0:T(8,128)(2,1)} fusion(bf16[128,1536]{1,0:T(8,128)(2,1)} %get-tuple-element.30, bf16[2,128,1536]{2,1,0:T(8,128)(2,1)} %collective-permute-done.21), kind=kLoop, calls=%fused_computation.3 | loop fusion | flops 786432 | bytes 1179648 | tf_op jit(solution)/shard_map/convert_element_type | solution.py:385
  49.8 1.5 %collective-permute-start.22 = (bf16[128,1536]{1,0:T(8,128)(2,1)}, bf16[128,1536]{1,0:T(8,128)(2,1)}, u32[]{:S(2)}, u32[]{:S(2)}) collective-permute-start(bf16[128,1536]{1,0:T(8,128)(2,1)} %fusion.1), channel_id=1, source_target_pairs={{0,2},{1,3},{2,0},{3,1},{4,6},{5,7},{6,4},{7,5},{8,10},{9,11},{10,... | collective-permute-start | bytes 1179656 | tf_op jit(solution)/shard_map/ppermute | solution.py:383
  51.4 8.3 %group.6 = (bf16[128,1536]{1,0:T(8,128)(2,1)}, bf16[128,1536]{1,0:T(8,128)(2,1)}, bf16[2,128,1536]{2,1,0:T(8,128)(2,1)}, bf16[128,1536]{1,0:T(8,128)(2,1)}) custom-call(s32[1]{0:T(128)S(6)} %copy.31.failed, s32[4,16]{1,0:T(4,128)} %bitcast.70, bf16[136,1536]{1,0:T(8,128)(2,1)} %after.10.refs_2_.refs_0_, bf16[136,1536]{1,0:T(8,128)(2,1)} %collective-permute-done.7.refs_1_, ...), custom_call_target="tpu_custom_call" | custom-call | flops 3019898880 | bytes 14942208 | tf_op jit(solution)/shard_map/group/pallas_call | solution.py:316
  59.7 0.1 collective-permute-start.19
  59.8 0.5 collective-permute-start.15
  60.3 0.8 collective-permute-start.12
  61.1 0.0 collective-permute-start.16
  61.1 0.3 collective-permute-done.22
  61.3 2.1 %fusion.3 = bf16[128,1536]{1,0:T(8,128)(2,1)} fusion(bf16[128,1536]{1,0:T(8,128)(2,1)} %collective-permute-done.22, bf16[128,1536]{1,0:T(8,128)(2,1)} %get-tuple-element.21.refs_10_.refs_1_, bf16[2,128,1536]{2,1,0:T(8,128)(2,1)} %collective-permute-done.21), kind=kLoop, calls=%fused_computation.6 | loop fusion | flops 1179648 | bytes 1572864 | tf_op jit(solution)/shard_map/convert_element_type | solution.py:407
  63.4 2.1 %collective-permute-start.23 = (bf16[128,1536]{1,0:T(8,128)(2,1)}, bf16[128,1536]{1,0:T(8,128)(2,1)}, u32[]{:S(2)}, u32[]{:S(2)}) collective-permute-start(bf16[128,1536]{1,0:T(8,128)(2,1)} %fusion.3), channel_id=1, source_target_pairs={{0,4},{1,5},{2,6},{3,7},{4,12},{5,13},{6,14},{7,15},{8,0},{9,1},{1... | collective-permute-start | bytes 1179656 | tf_op jit(solution)/shard_map/ppermute | solution.py:383
  65.6 0.9 copy-done.1
  66.5 1.8 %fusion.4 = bf16[128,1536]{1,0:T(8,128)(2,1)} fusion(bf16[128,1536]{1,0:T(8,128)(2,1)} %get-tuple-element.28, bf16[2,128,1536]{2,1,0:T(8,128)(2,1)S(1)} %collective-permute-done.19), kind=kLoop, calls=%fused_computation.8 | loop fusion | flops 786432 | bytes 1179648 | tf_op jit(solution)/shard_map/convert_element_type | solution.py:385
  68.3 1.5 %collective-permute-start.20 = (bf16[128,1536]{1,0:T(8,128)(2,1)}, bf16[128,1536]{1,0:T(8,128)(2,1)}, u32[]{:S(2)}, u32[]{:S(2)}) collective-permute-start(bf16[128,1536]{1,0:T(8,128)(2,1)} %fusion.4), channel_id=1, source_target_pairs={{0,2},{1,3},{2,0},{3,1},{4,6},{5,7},{6,4},{7,5},{8,10},{9,11},{10,... | collective-permute-start | bytes 1179656 | tf_op jit(solution)/shard_map/ppermute | solution.py:383
  69.8 0.0 collective-permute-done.15.refs_2_
  69.8 0.0 collective-permute-done.16.refs_3_
  69.8 8.2 %group.7 = (bf16[128,1536]{1,0:T(8,128)(2,1)}, bf16[128,1536]{1,0:T(8,128)(2,1)}, bf16[2,128,1536]{2,1,0:T(8,128)(2,1)}) custom-call(s32[1]{0:T(128)S(6)} %copy.31.failed, s32[4,16]{1,0:T(4,128)} %bitcast.71, bf16[136,1536]{1,0:T(8,128)(2,1)} %after.12.refs_0_.refs_2_, bf16[136,1536]{1,0:T(8,128)(2,1)} %collective-permute-done.14.refs_1_, ...), custom_call_target="tpu_custom_call" | custom-call | flops 3019898880 | bytes 14942208 | tf_op jit(solution)/shard_map/group/pallas_call | solution.py:316
  78.0 0.1 collective-permute-start.17
  78.1 0.0 collective-permute-done.23
  78.1 2.0 %collective-permute-done.20 = bf16[128,1536]{1,0:T(8,128)(2,1)} collective-permute-done((bf16[128,1536]{1,0:T(8,128)(2,1)}, bf16[128,1536]{1,0:T(8,128)(2,1)}, u32[]{:S(2)}, u32[]{:S(2)}) %collective-permute-start.20) | collective-permute-done | bytes 393248 | tf_op jit(solution)/shard_map/ppermute | solution.py:383
  80.1 1.6 %fusion.18 = (bf16[64,1536]{1,0:T(8,128)(2,1)S(1)}, bf16[64,1536]{1,0:T(8,128)(2,1)S(1)}) fusion(bf16[128,1536]{1,0:T(8,128)(2,1)} %collective-permute-done.23, bf16[128,1536]{1,0:T(8,128)(2,1)} %collective-permute-done.20, bf16[2,128,1536]{2,1,0:T(8,128)(2,1)} %copy-done.1, bf16[128,1536]{1,0:T(8,128)(2,1)} %get-tuple-element.23.refs_8_), kind=kLoop, calls=%fused_computation.31 | loop fusion | flops 1572864 | bytes 1966080 | tf_op jit(solution)/shard_map/convert_element_type | solution.py:407
  81.8 2.7 %collective-permute-start.24 = (bf16[64,1536]{1,0:T(8,128)(2,1)S(1)}, bf16[64,1536]{1,0:T(8,128)(2,1)S(1)}, u32[]{:S(2)}, u32[]{:S(2)}) collective-permute-start(bf16[64,1536]{1,0:T(8,128)(2,1)S(1)} %get-tuple-element.31), channel_id=1, source_target_pairs={{0,4},{1,5},{2,6},{3,7},{4,12},{5,13},{6,14},{7,15},{8,0},{9,1},{1... | collective-permute-start | bytes 589832 | tf_op jit(solution)/shard_map/ppermute | solution.py:383
  84.5 2.1 %fusion.9 = (bf16[64,1536]{1,0:T(8,128)(2,1)}, bf16[64,1536]{1,0:T(8,128)(2,1)S(1)}) fusion(bf16[2,128,1536]{2,1,0:T(8,128)(2,1)S(1)} %collective-permute-done.17, bf16[128,1536]{1,0:T(8,128)(2,1)} %get-tuple-element.26), kind=kLoop, calls=%fused_computation.19 | loop fusion | flops 786432 | bytes 1179648 | tf_op jit(solution)/shard_map/convert_element_type | solution.py:385
  86.5 0.5 collective-permute-start.18
  87.1 0.4 collective-permute-start.27
  87.4 1.3 %collective-permute-start.26 = (bf16[64,1536]{1,0:T(8,128)(2,1)}, bf16[64,1536]{1,0:T(8,128)(2,1)}, u32[]{:S(2)}, u32[]{:S(2)}) collective-permute-start(bf16[64,1536]{1,0:T(8,128)(2,1)} %get-tuple-element.33), channel_id=1, source_target_pairs={{0,2},{1,3},{2,0},{3,1},{4,6},{5,7},{6,4},{7,5},{8,10},{9,11},{10,... | collective-permute-start | bytes 589832 | tf_op jit(solution)/shard_map/ppermute | solution.py:383
  88.7 1.1 %collective-permute-done.24 = bf16[64,1536]{1,0:T(8,128)(2,1)S(1)} collective-permute-done((bf16[64,1536]{1,0:T(8,128)(2,1)S(1)}, bf16[64,1536]{1,0:T(8,128)(2,1)S(1)}, u32[]{:S(2)}, u32[]{:S(2)}) %collective-permute-start.24) | collective-permute-done | bytes 196640 | tf_op jit(solution)/shard_map/ppermute | solution.py:383
  89.8 4.6 %collective-permute-done.18 = bf16[64,1536]{1,0:T(8,128)(2,1)S(1)} collective-permute-done((bf16[64,1536]{1,0:T(8,128)(2,1)S(1)}, bf16[64,1536]{1,0:T(8,128)(2,1)S(1)}, u32[]{:S(2)}, u32[]{:S(2)}) %collective-permute-start.18) | collective-permute-done | bytes 196640 | tf_op jit(solution)/shard_map/ppermute | solution.py:383
  94.4 1.7 %fusion.22.refs_1_ = bf16[64,1536]{1,0:T(8,128)(2,1)} fusion(bf16[64,1536]{1,0:T(8,128)(2,1)S(1)} %collective-permute-done.24, bf16[64,1536]{1,0:T(8,128)(2,1)S(1)} %collective-permute-done.18, bf16[2,128,1536]{2,1,0:T(8,128)(2,1)S(1)} %collective-permute-done.17, bf16[128,1536]{1,0:T(8,128)(2,1)} %get-tuple-element.24), kind=kLoop, calls=%fused_computation.37 | loop fusion | flops 786432 | bytes 983040 | tf_op jit(solution)/shard_map/convert_element_type | solution.py:407
  96.1 0.1 collective-permute-start.25
  96.2 0.7 copy-done.3
  96.9 1.3 %fusion.12 = bf16[64,1536]{1,0:T(8,128)(2,1)S(1)} fusion(bf16[64,1536]{1,0:T(8,128)(2,1)} %after.16, bf16[64,1536]{1,0:T(8,128)(2,1)} %collective-permute-done.26, bf16[2,128,1536]{2,1,0:T(8,128)(2,1)} %copy-done.2, bf16[128,1536]{1,0:T(8,128)(2,1)} %get-tuple-element.24), kind=kLoop, calls=%fused_computation.23 | loop fusion | flops 786432 | bytes 983040 | tf_op jit(solution)/shard_map/convert_element_type | solution.py:407
  98.2 0.2 collective-permute-start.28
  98.4 5.4 %collective-permute-done.25 = bf16[64,1536]{1,0:T(8,128)(2,1)} collective-permute-done((bf16[64,1536]{1,0:T(8,128)(2,1)}, bf16[64,1536]{1,0:T(8,128)(2,1)}, u32[]{:S(2)}, u32[]{:S(2)}) %collective-permute-start.25) | collective-permute-done | bytes 196640 | tf_op jit(solution)/shard_map/ppermute | solution.py:383
  103.8 2.0 %fusion.25.refs_1_ = bf16[64,1536]{1,0:T(8,128)(2,1)} fusion(bf16[64,1536]{1,0:T(8,128)(2,1)} %collective-permute-done.25, bf16[128,1536]{1,0:T(8,128)(2,1)} %collective-permute-done.12.refs_1_, bf16[2,128,1536]{2,1,0:T(8,128)(2,1)} %collective-permute-done.6.refs_9_, bf16[128,1536]{1,0:T(8,128)(2,1)} %get-tuple-element.18.refs_1_.refs_8_), kind=kLoop, calls=%fused_computation.41 | loop fusion | flops 786432 | bytes 983040 | tf_op jit(solution)/shard_map/convert_element_type | solution.py:407
  105.8 0.0 collective-permute-done.28.refs_0_
  105.9 0.7 copy-done.4
  106.5 1.3 %fusion.15 = bf16[64,1536]{1,0:T(8,128)(2,1)S(1)} fusion(bf16[64,1536]{1,0:T(8,128)(2,1)} %after.17, bf16[128,1536]{1,0:T(8,128)(2,1)} %collective-permute-done.12.refs_1_, bf16[2,128,1536]{2,1,0:T(8,128)(2,1)} %collective-permute-done.6.refs_9_, bf16[128,1536]{1,0:T(8,128)(2,1)} %get-tuple-element.18.refs_1_.refs_8_), kind=kLoop, calls=%fused_computation.27 | loop fusion | flops 786432 | bytes 983040 | tf_op jit(solution)/shard_map/convert_element_type | solution.py:407
  107.8 1.7 %pad_maximum_fusion = bf16[128,1536]{1,0:T(8,128)(2,1)} fusion(bf16[64,1536]{1,0:T(8,128)(2,1)S(1)} %fusion.15, bf16[64,1536]{1,0:T(8,128)(2,1)} %fusion.25.refs_1_), kind=kLoop, calls=%fused_computation.13 | loop fusion | flops 786432 | bytes 786432 | tf_op jit(solution)/shard_map/concatenate | solution.py:441
  (37 shorter events, 0.1 us)
Async XLA Ops:
  1.8 4.6 %copy-start = (bf16[136,1536]{1,0:T(8,128)(2,1)}, bf16[136,1536]{1,0:T(8,128)(2,1)S(1)}, u32[]{:S(2)}) copy-start(bf16[136,1536]{1,0:T(8,128)(2,1)S(1)} %fusion.5.refs_0_) | copy-start | bytes 1253380
  1.8 12.7 %collective-permute-start = (bf16[136,1536]{1,0:T(8,128)(2,1)S(1)}, bf16[136,1536]{1,0:T(8,128)(2,1)S(1)}, u32[]{:S(2)}, u32[]{:S(2)}) collective-permute-start(bf16[136,1536]{1,0:T(8,128)(2,1)S(1)} %fusion.5.refs_0_), channel_id=1, source_target_pairs={{0,2},{1,3},{2,0},{3,1},{4,6},{5,7},{6,4},{7,5},{8,10},{9,11},{10,... | collective-permute-start | bytes 1253384 | tf_op jit(solution)/shard_map/ppermute | solution.py:383
  4.8 12.1 %collective-permute-start.3 = (bf16[136,1536]{1,0:T(8,128)(2,1)S(1)}, bf16[136,1536]{1,0:T(8,128)(2,1)}, u32[]{:S(2)}, u32[]{:S(2)}) collective-permute-start(bf16[136,1536]{1,0:T(8,128)(2,1)S(1)} %fusion.5.refs_0_), channel_id=1, source_target_pairs={{0,4},{1,5},{2,6},{3,7},{4,12},{5,13},{6,14},{7,15},{8,0},{9,1},{1... | collective-permute-start | bytes 1253384 | tf_op jit(solution)/shard_map/ppermute | solution.py:383
  6.4 12.5 %collective-permute-start.1 = (bf16[136,1536]{1,0:T(8,128)(2,1)S(1)}, bf16[136,1536]{1,0:T(8,128)(2,1)S(1)}, u32[]{:S(2)}, u32[]{:S(2)}) collective-permute-start(bf16[136,1536]{1,0:T(8,128)(2,1)S(1)} %fusion.5.refs_0_), channel_id=1, source_target_pairs={{0,1},{1,0},{2,3},{3,2},{4,5},{5,4},{6,7},{7,6},{8,9},{9,8},{10,11... | collective-permute-start | bytes 1253384 | tf_op jit(solution)/shard_map/ppermute | solution.py:383
  14.4 4.4 %copy-start.5 = (bf16[136,1536]{1,0:T(8,128)(2,1)}, bf16[136,1536]{1,0:T(8,128)(2,1)S(1)}, u32[]{:S(2)}) copy-start(bf16[136,1536]{1,0:T(8,128)(2,1)S(1)} %collective-permute-done.refs_1_) | copy-start | bytes 1253380
  14.4 4.4 %collective-permute-start.2 = (bf16[136,1536]{1,0:T(8,128)(2,1)S(1)}, bf16[136,1536]{1,0:T(8,128)(2,1)S(1)}, u32[]{:S(2)}, u32[]{:S(2)}) collective-permute-start(bf16[136,1536]{1,0:T(8,128)(2,1)S(1)} %collective-permute-done.refs_1_), channel_id=1, source_target_pairs={{0,1},{1,0},{2,3},{3,2},{4,5},{5,4},{6,7},{7,6},{8,9},{9,8},{10,11... | collective-permute-start | bytes 1253384 | tf_op jit(solution)/shard_map/ppermute | solution.py:383
  16.9 11.6 %collective-permute-start.4 = (bf16[136,1536]{1,0:T(8,128)(2,1)}, bf16[136,1536]{1,0:T(8,128)(2,1)}, u32[]{:S(2)}, u32[]{:S(2)}) collective-permute-start(bf16[136,1536]{1,0:T(8,128)(2,1)} %collective-permute-done.3.refs_0_), channel_id=1, source_target_pairs={{0,2},{1,3},{2,0},{3,1},{4,6},{5,7},{6,4},{7,5},{8,10},{9,11},{10,... | collective-permute-start | bytes 1253384 | tf_op jit(solution)/shard_map/ppermute | solution.py:383
  18.0 16.8 %collective-permute-start.10 = (bf16[136,1536]{1,0:T(8,128)(2,1)}, bf16[136,1536]{1,0:T(8,128)(2,1)}, u32[]{:S(2)}, u32[]{:S(2)}) collective-permute-start(bf16[136,1536]{1,0:T(8,128)(2,1)} %collective-permute-done.3.refs_0_), channel_id=1, source_target_pairs={{0,1},{1,0},{2,3},{3,2},{4,5},{5,4},{6,7},{7,6},{8,9},{9,8},{10,11... | collective-permute-start | bytes 1253384 | tf_op jit(solution)/shard_map/ppermute | solution.py:383
  18.1 13.3 %collective-permute-start.5 = (bf16[136,1536]{1,0:T(8,128)(2,1)}, bf16[136,1536]{1,0:T(8,128)(2,1)}, u32[]{:S(2)}, u32[]{:S(2)}) collective-permute-start(bf16[136,1536]{1,0:T(8,128)(2,1)} %collective-permute-done.3.refs_0_), channel_id=1, source_target_pairs={{0,4},{1,5},{2,6},{3,7},{4,12},{5,13},{6,14},{7,15},{8,0},{9,1},{1... | collective-permute-start | bytes 1253384 | tf_op jit(solution)/shard_map/ppermute | solution.py:383
  18.9 0.8 copy-start.6
  19.6 0.8 copy-start.7
  28.5 6.3 %collective-permute-start.11 = (bf16[136,1536]{1,0:T(8,128)(2,1)}, bf16[136,1536]{1,0:T(8,128)(2,1)}, u32[]{:S(2)}, u32[]{:S(2)}) collective-permute-start(bf16[136,1536]{1,0:T(8,128)(2,1)} %after.9.refs_1_), channel_id=1, source_target_pairs={{0,1},{1,0},{2,3},{3,2},{4,5},{5,4},{6,7},{7,6},{8,9},{9,8},{10,11... | collective-permute-start | bytes 1253384 | tf_op jit(solution)/shard_map/ppermute | solution.py:383
  31.4 12.4 %collective-permute-start.13 = (bf16[136,1536]{1,0:T(8,128)(2,1)}, bf16[136,1536]{1,0:T(8,128)(2,1)}, u32[]{:S(2)}, u32[]{:S(2)}) collective-permute-start(bf16[136,1536]{1,0:T(8,128)(2,1)} %after.10.refs_2_.refs_0_), channel_id=1, source_target_pairs={{0,4},{1,5},{2,6},{3,7},{4,12},{5,13},{6,14},{7,15},{8,0},{9,1},{1... | collective-permute-start | bytes 1253384 | tf_op jit(solution)/shard_map/ppermute | solution.py:383
  33.2 12.0 %collective-permute-start.7 = (bf16[136,1536]{1,0:T(8,128)(2,1)}, bf16[136,1536]{1,0:T(8,128)(2,1)}, u32[]{:S(2)}, u32[]{:S(2)}) collective-permute-start(bf16[136,1536]{1,0:T(8,128)(2,1)} %after.10.refs_2_.refs_0_), channel_id=1, source_target_pairs={{0,2},{1,3},{2,0},{3,1},{4,6},{5,7},{6,4},{7,5},{8,10},{9,11},{10,... | collective-permute-start | bytes 1253384 | tf_op jit(solution)/shard_map/ppermute | solution.py:383
  45.3 2.6 %collective-permute-start.21 = (bf16[2,128,1536]{2,1,0:T(8,128)(2,1)}, bf16[2,128,1536]{2,1,0:T(8,128)(2,1)}, u32[]{:S(2)}, u32[]{:S(2)}) collective-permute-start(bf16[2,128,1536]{2,1,0:T(8,128)(2,1)} %after.15), channel_id=1, source_target_pairs={{0,1},{1,0},{2,3},{3,2},{4,5},{5,4},{6,7},{7,6},{8,9},{9,8},{10,11... | collective-permute-start | bytes 2359304 | tf_op jit(solution)/shard_map/ppermute | solution.py:383
  45.3 6.1 %collective-permute-start.6 = (bf16[2,128,1536]{2,1,0:T(8,128)(2,1)}, bf16[2,128,1536]{2,1,0:T(8,128)(2,1)}, u32[]{:S(2)}, u32[]{:S(2)}) collective-permute-start(bf16[2,128,1536]{2,1,0:T(8,128)(2,1)} %after.11), channel_id=1, source_target_pairs={{0,1},{1,0},{2,3},{3,2},{4,5},{5,4},{6,7},{7,6},{8,9},{9,8},{10,11... | collective-permute-start | bytes 2359304 | tf_op jit(solution)/shard_map/ppermute | solution.py:383
  45.8 5.6 %collective-permute-start.8 = (bf16[136,1536]{1,0:T(8,128)(2,1)}, bf16[136,1536]{1,0:T(8,128)(2,1)}, u32[]{:S(2)}, u32[]{:S(2)}) collective-permute-start(bf16[136,1536]{1,0:T(8,128)(2,1)} %after.10.refs_2_.refs_0_), channel_id=1, source_target_pairs={{0,1},{1,0},{2,3},{3,2},{4,5},{5,4},{6,7},{7,6},{8,9},{9,8},{10,11... | collective-permute-start | bytes 1253384 | tf_op jit(solution)/shard_map/ppermute | solution.py:383
  45.8 5.6 %collective-permute-start.9 = (bf16[136,1536]{1,0:T(8,128)(2,1)}, bf16[136,1536]{1,0:T(8,128)(2,1)}, u32[]{:S(2)}, u32[]{:S(2)}) collective-permute-start(bf16[136,1536]{1,0:T(8,128)(2,1)} %collective-permute-done.7.refs_1_), channel_id=1, source_target_pairs={{0,1},{1,0},{2,3},{3,2},{4,5},{5,4},{6,7},{7,6},{8,9},{9,8},{10,11... | collective-permute-start | bytes 1253384 | tf_op jit(solution)/shard_map/ppermute | solution.py:383
  46.3 13.4 %collective-permute-start.14 = (bf16[136,1536]{1,0:T(8,128)(2,1)}, bf16[136,1536]{1,0:T(8,128)(2,1)}, u32[]{:S(2)}, u32[]{:S(2)}) collective-permute-start(bf16[136,1536]{1,0:T(8,128)(2,1)} %collective-permute-done.7.refs_1_), channel_id=1, source_target_pairs={{0,4},{1,5},{2,6},{3,7},{4,12},{5,13},{6,14},{7,15},{8,0},{9,1},{1... | collective-permute-start | bytes 1253384 | tf_op jit(solution)/shard_map/ppermute | solution.py:383
  49.8 11.5 %collective-permute-start.22 = (bf16[128,1536]{1,0:T(8,128)(2,1)}, bf16[128,1536]{1,0:T(8,128)(2,1)}, u32[]{:S(2)}, u32[]{:S(2)}) collective-permute-start(bf16[128,1536]{1,0:T(8,128)(2,1)} %fusion.1), channel_id=1, source_target_pairs={{0,2},{1,3},{2,0},{3,1},{4,6},{5,7},{6,4},{7,5},{8,10},{9,11},{10,... | collective-permute-start | bytes 1179656 | tf_op jit(solution)/shard_map/ppermute | solution.py:383
  59.7 5.9 %collective-permute-start.19 = (bf16[2,128,1536]{2,1,0:T(8,128)(2,1)}, bf16[2,128,1536]{2,1,0:T(8,128)(2,1)S(1)}, u32[]{:S(2)}, u32[]{:S(2)}) collective-permute-start(bf16[2,128,1536]{2,1,0:T(8,128)(2,1)} %after.14), channel_id=1, source_target_pairs={{0,1},{1,0},{2,3},{3,2},{4,5},{5,4},{6,7},{7,6},{8,9},{9,8},{10,11... | collective-permute-start | bytes 2359304 | tf_op jit(solution)/shard_map/ppermute | solution.py:383
  59.8 10.0 %collective-permute-start.15 = (bf16[136,1536]{1,0:T(8,128)(2,1)}, bf16[136,1536]{1,0:T(8,128)(2,1)}, u32[]{:S(2)}, u32[]{:S(2)}) collective-permute-start(bf16[136,1536]{1,0:T(8,128)(2,1)} %after.12.refs_0_.refs_2_), channel_id=1, source_target_pairs={{0,1},{1,0},{2,3},{3,2},{4,5},{5,4},{6,7},{7,6},{8,9},{9,8},{10,11... | collective-permute-start | bytes 1253384 | tf_op jit(solution)/shard_map/ppermute | solution.py:383
  60.3 17.7 %collective-permute-start.12 = (bf16[128,1536]{1,0:T(8,128)(2,1)}, bf16[128,1536]{1,0:T(8,128)(2,1)}, u32[]{:S(2)}, u32[]{:S(2)}) collective-permute-start(bf16[128,1536]{1,0:T(8,128)(2,1)} %get-tuple-element.22), channel_id=1, source_target_pairs={{0,2},{1,3},{2,0},{3,1},{4,6},{5,7},{6,4},{7,5},{8,10},{9,11},{10,... | collective-permute-start | bytes 1179656 | tf_op jit(solution)/shard_map/ppermute | solution.py:383
  61.1 8.8 %collective-permute-start.16 = (bf16[136,1536]{1,0:T(8,128)(2,1)}, bf16[136,1536]{1,0:T(8,128)(2,1)}, u32[]{:S(2)}, u32[]{:S(2)}) collective-permute-start(bf16[136,1536]{1,0:T(8,128)(2,1)} %collective-permute-done.14.refs_1_), channel_id=1, source_target_pairs={{0,1},{1,0},{2,3},{3,2},{4,5},{5,4},{6,7},{7,6},{8,9},{9,8},{10,11... | collective-permute-start | bytes 1253384 | tf_op jit(solution)/shard_map/ppermute | solution.py:383
  63.4 14.7 %collective-permute-start.23 = (bf16[128,1536]{1,0:T(8,128)(2,1)}, bf16[128,1536]{1,0:T(8,128)(2,1)}, u32[]{:S(2)}, u32[]{:S(2)}) collective-permute-start(bf16[128,1536]{1,0:T(8,128)(2,1)} %fusion.3), channel_id=1, source_target_pairs={{0,4},{1,5},{2,6},{3,7},{4,12},{5,13},{6,14},{7,15},{8,0},{9,1},{1... | collective-permute-start | bytes 1179656 | tf_op jit(solution)/shard_map/ppermute | solution.py:383
  65.6 0.9 copy-start.1
  68.3 11.8 %collective-permute-start.20 = (bf16[128,1536]{1,0:T(8,128)(2,1)}, bf16[128,1536]{1,0:T(8,128)(2,1)}, u32[]{:S(2)}, u32[]{:S(2)}) collective-permute-start(bf16[128,1536]{1,0:T(8,128)(2,1)} %fusion.4), channel_id=1, source_target_pairs={{0,2},{1,3},{2,0},{3,1},{4,6},{5,7},{6,4},{7,5},{8,10},{9,11},{10,... | collective-permute-start | bytes 1179656 | tf_op jit(solution)/shard_map/ppermute | solution.py:383
  78.0 6.4 %collective-permute-start.17 = (bf16[2,128,1536]{2,1,0:T(8,128)(2,1)}, bf16[2,128,1536]{2,1,0:T(8,128)(2,1)S(1)}, u32[]{:S(2)}, u32[]{:S(2)}) collective-permute-start(bf16[2,128,1536]{2,1,0:T(8,128)(2,1)} %after.13), channel_id=1, source_target_pairs={{0,1},{1,0},{2,3},{3,2},{4,5},{5,4},{6,7},{7,6},{8,9},{9,8},{10,11... | collective-permute-start | bytes 2359304 | tf_op jit(solution)/shard_map/ppermute | solution.py:383
  81.8 8.0 %collective-permute-start.24 = (bf16[64,1536]{1,0:T(8,128)(2,1)S(1)}, bf16[64,1536]{1,0:T(8,128)(2,1)S(1)}, u32[]{:S(2)}, u32[]{:S(2)}) collective-permute-start(bf16[64,1536]{1,0:T(8,128)(2,1)S(1)} %get-tuple-element.31), channel_id=1, source_target_pairs={{0,4},{1,5},{2,6},{3,7},{4,12},{5,13},{6,14},{7,15},{8,0},{9,1},{1... | collective-permute-start | bytes 589832 | tf_op jit(solution)/shard_map/ppermute | solution.py:383
  84.5 9.9 %copy-start.2 = (bf16[2,128,1536]{2,1,0:T(8,128)(2,1)}, bf16[2,128,1536]{2,1,0:T(8,128)(2,1)S(1)}, u32[]{:S(2)}) copy-start(bf16[2,128,1536]{2,1,0:T(8,128)(2,1)S(1)} %collective-permute-done.17) | copy-start | bytes 2359300
  86.5 7.8 %collective-permute-start.18 = (bf16[64,1536]{1,0:T(8,128)(2,1)S(1)}, bf16[64,1536]{1,0:T(8,128)(2,1)S(1)}, u32[]{:S(2)}, u32[]{:S(2)}) collective-permute-start(bf16[64,1536]{1,0:T(8,128)(2,1)S(1)} %get-tuple-element.34), channel_id=1, source_target_pairs={{0,2},{1,3},{2,0},{3,1},{4,6},{5,7},{6,4},{7,5},{8,10},{9,11},{10,... | collective-permute-start | bytes 589832 | tf_op jit(solution)/shard_map/ppermute | solution.py:383
  87.1 9.2 %collective-permute-start.27 = (bf16[64,1536]{1,0:T(8,128)(2,1)S(1)}, bf16[64,1536]{1,0:T(8,128)(2,1)S(1)}, u32[]{:S(2)}, u32[]{:S(2)}) collective-permute-start(bf16[64,1536]{1,0:T(8,128)(2,1)S(1)} %get-tuple-element.32), channel_id=1, source_target_pairs={{0,4},{1,5},{2,6},{3,7},{4,12},{5,13},{6,14},{7,15},{8,0},{9,1},{1... | collective-permute-start | bytes 589832 | tf_op jit(solution)/shard_map/ppermute | solution.py:383
  87.4 9.5 %collective-permute-start.26 = (bf16[64,1536]{1,0:T(8,128)(2,1)}, bf16[64,1536]{1,0:T(8,128)(2,1)}, u32[]{:S(2)}, u32[]{:S(2)}) collective-permute-start(bf16[64,1536]{1,0:T(8,128)(2,1)} %get-tuple-element.33), channel_id=1, source_target_pairs={{0,2},{1,3},{2,0},{3,1},{4,6},{5,7},{6,4},{7,5},{8,10},{9,11},{10,... | collective-permute-start | bytes 589832 | tf_op jit(solution)/shard_map/ppermute | solution.py:383
  96.1 7.7 %collective-permute-start.25 = (bf16[64,1536]{1,0:T(8,128)(2,1)}, bf16[64,1536]{1,0:T(8,128)(2,1)}, u32[]{:S(2)}, u32[]{:S(2)}) collective-permute-start(bf16[64,1536]{1,0:T(8,128)(2,1)} %fusion.22.refs_1_), channel_id=1, source_target_pairs={{0,4},{1,5},{2,6},{3,7},{4,12},{5,13},{6,14},{7,15},{8,0},{9,1},{1... | collective-permute-start | bytes 589832 | tf_op jit(solution)/shard_map/ppermute | solution.py:383
  96.2 0.7 copy-start.3
  98.2 7.6 %collective-permute-start.28 = (bf16[64,1536]{1,0:T(8,128)(2,1)S(1)}, bf16[64,1536]{1,0:T(8,128)(2,1)S(1)}, u32[]{:S(2)}, u32[]{:S(2)}) collective-permute-start(bf16[64,1536]{1,0:T(8,128)(2,1)S(1)} %fusion.12), channel_id=1, source_target_pairs={{0,4},{1,5},{2,6},{3,7},{4,12},{5,13},{6,14},{7,15},{8,0},{9,1},{1... | collective-permute-start | bytes 589832 | tf_op jit(solution)/shard_map/ppermute | solution.py:383
  105.8 0.7 copy-start.4

commit v12 on v11

--- a/solution.py
+++ b/solution.py
@@ -354,7 +354,7 @@
     pass
 
 
-def come_after(value, *others):
+def come_after(value, *others, flops=0):
     return pl.pallas_call(
         nothing,
         out_shape=pltpu.HBM(value.shape, value.dtype),
@@ -362,7 +362,7 @@
         out_specs=pl.BlockSpec(memory_space=pl.ANY),
         input_output_aliases={0: 0},
         compiler_params=pltpu.CompilerParams(vmem_limit_bytes=VMEM_GRANT),
-        cost_estimate=pl.CostEstimate(flops=0, bytes_accessed=0, transcendentals=0),
+        cost_estimate=pl.CostEstimate(flops=flops, bytes_accessed=0, transcendentals=0),
         name="after",
     )(*map(in_hbm, (value, *others)))
 
@@ -423,10 +423,9 @@
             from_y = move(add(kept[k - 1][1], got[k - 1][1]), over_y)
         if k == 2:
             send, own = add_group(k, (kept[0][1], got[0]), kept[k - 1][0])
-            own = move(own, over_y)
         else:
             (send,) = add_group(k, (), kept[k - 1][0])
-    got.append(move(come_after(send, own), over_core))
+    got.append(move(send, over_core))
 
     halves = (slice(0, tok // 2), slice(tok // 2, tok))
     passing = [
@@ -436,9 +435,9 @@
     first, second = halves
     passed = total(last, first, shares[0], passing[0])
     follows = total(last, second, shares[1], come_after(passing[1], passed))
-    passed = total(0, first, own[first], move(passed, round_ring))
-    follows = come_after(move(follows, round_ring), passed)
-    return jnp.concatenate([passed, total(0, second, own[second], follows)], axis=0)
+    own = move(come_after(own, passed), over_y)
+    passed = come_after(move(passed, round_ring), flops=4 * 10**9)
+    return total(0, every, own, jnp.concatenate([passed, move(follows, round_ring)], axis=0))
 
 
 def shards(

time: 110 us -> 106 us (0.964)
  other arithmetic: 19.5 us -> 17.4 us
  starting transfers between devices: 23.9 us -> 22.1 us
  local copies, waits for them, and re-layouts: 3.77 us -> 2.46 us
    ppermute x29, starting transfers between devices: 23.9 us -> 22.1 us  [by_permutes(): move = lambda a, pairs: lax.ppermute(a, 'expert', pairs)]
    concatenate x1 -> x0, other arithmetic: 1.7 us -> none  [by_permutes(): jnp.concatenate([passed, total(0, second, own[second], follows)], axis=0)]
    unnamed x17 -> x15, local copies, waits for them, and re-layouts: 3.77 us -> 2.46 us
    convert_element_type x6 -> x5, other arithmetic: 10.1 us -> 9.76 us  [total(): return result.astype(jnp.bfloat16)]
  transfers between devices with their start and end apart: 29 -> 29, of which waited for: 11 -> 14; matrix products, arithmetic and copies ran while one was open for 13% -> 13% of each run, Pallas kernels for 30% -> 31%
where the time goes in v12:
time: 106 us; the launch traced here: 105 us
  Pallas kernels  32.6 us (31%)
  waiting for transfers between devices  29.7 us (28%)
  starting transfers between devices  22.1 us (21%)
  other arithmetic  17.4 us (16%)
  local copies, waits for them, and re-layouts  2.46 us (2%)
    pallas_call x4, Pallas kernels, run_group(): pl.pallas_call(functools.partial(group_kernel, others=len(earlier), adds=...  32.6 us
    ppermute x29, waiting for transfers between devices, by_permutes(): move = lambda a, pairs: lax.ppermute(a, 'expert', pairs)  29.7 us
    ppermute x29, starting transfers between devices, by_permutes(): move = lambda a, pairs: lax.ppermute(a, 'expert', pairs)  22.1 us
    convert_element_type x5, other arithmetic, total(): return result.astype(jnp.bfloat16)  9.76 us
    convert_element_type x3, other arithmetic, by_permutes(): add = lambda a, b: (f32(a) + f32(b)).astype(jnp.bfloat16)  5.86 us
    unnamed x15, local copies, waits for them, and re-layouts  2.46 us
  transfers between devices with their start and end apart: 29, of which 14 were waited for; matrix products, arithmetic and copies ran while one was open for 13% of the time, Pallas kernels for 31%

profile of v12, /device:TPU:0, one launch (start us, length us, event | category | flops | bytes accessed | tf_op | source)
XLA Modules:
  0.0 105.1 jit_solution(12430788987246662092)
XLA Ops:
  0.0 0.7 fusion.23
  0.7 1.0 fusion.8.refs_0_
  1.8 3.0 %collective-permute-start = (bf16[136,1536]{1,0:T(8,128)(2,1)S(1)}, bf16[136,1536]{1,0:T(8,128)(2,1)S(1)}, u32[]{:S(2)}, u32[]{:S(2)}) collective-permute-start(bf16[136,1536]{1,0:T(8,128)(2,1)S(1)} %fusion.8.refs_0_), channel_id=1, source_target_pairs={{0,2},{1,3},{2,0},{3,1},{4,6},{5,7},{6,4},{7,5},{8,10},{9,11},{10,... | collective-permute-start | bytes 1253384 | tf_op jit(solution)/shard_map/ppermute | solution.py:383
  4.8 1.6 %collective-permute-start.3 = (bf16[136,1536]{1,0:T(8,128)(2,1)S(1)}, bf16[136,1536]{1,0:T(8,128)(2,1)}, u32[]{:S(2)}, u32[]{:S(2)}) collective-permute-start(bf16[136,1536]{1,0:T(8,128)(2,1)S(1)} %fusion.8.refs_0_), channel_id=1, source_target_pairs={{0,4},{1,5},{2,6},{3,7},{4,12},{5,13},{6,14},{7,15},{8,0},{9,1},{1... | collective-permute-start | bytes 1253384 | tf_op jit(solution)/shard_map/ppermute | solution.py:383
  6.4 8.1 %collective-permute-done.refs_1_ = bf16[136,1536]{1,0:T(8,128)(2,1)S(1)} collective-permute-done((bf16[136,1536]{1,0:T(8,128)(2,1)S(1)}, bf16[136,1536]{1,0:T(8,128)(2,1)S(1)}, u32[]{:S(2)}, u32[]{:S(2)}) %collective-permute-start) | collective-permute-done | bytes 417824 | tf_op jit(solution)/shard_map/ppermute | solution.py:383
  14.4 0.0 collective-permute-start.2
  14.5 2.5 %collective-permute-done.3.refs_0_ = bf16[136,1536]{1,0:T(8,128)(2,1)} collective-permute-done((bf16[136,1536]{1,0:T(8,128)(2,1)S(1)}, bf16[136,1536]{1,0:T(8,128)(2,1)}, u32[]{:S(2)}, u32[]{:S(2)}) %collective-permute-start.3) | collective-permute-done | bytes 417824 | tf_op jit(solution)/shard_map/ppermute | solution.py:383
  16.9 0.5 collective-permute-start.4
  18.0 0.8 collective-permute-start.5
  18.8 0.7 copy-done.5
  19.6 0.8 copy-done.6
  20.4 8.1 %group.4 = (bf16[128,1536]{1,0:T(8,128)(2,1)}, bf16[128,1536]{1,0:T(8,128)(2,1)}, bf16[2,128,1536]{2,1,0:T(8,128)(2,1)}) custom-call(s32[1]{0:T(128)S(6)} %copy.31.failed, s32[4,16]{1,0:T(4,128)} %bitcast.63, bf16[136,1536]{1,0:T(8,128)(2,1)} %copy-done.1, bf16[136,1536]{1,0:T(8,128)(2,1)} %copy-done.4, bf16[136,1536]{1,0:T(8,128)(2,1)} %copy-done.5, ...), custom_call_target="tpu_custom_call" | custom-call | flops 3019898880 | bytes 14942208 | tf_op jit(solution)/shard_map/group/pallas_call | solution.py:316
  28.5 0.0 collective-permute-done.4.refs_0_
  28.5 0.6 collective-permute-start.11
  29.0 0.8 collective-permute-done.5.refs_0_
  29.9 3.7 %collective-permute-start.12 = (bf16[136,1536]{1,0:T(8,128)(2,1)}, bf16[136,1536]{1,0:T(8,128)(2,1)}, u32[]{:S(2)}, u32[]{:S(2)}) collective-permute-start(bf16[136,1536]{1,0:T(8,128)(2,1)} %after.10.refs_2_.refs_0_), channel_id=1, source_target_pairs={{0,4},{1,5},{2,6},{3,7},{4,12},{5,13},{6,14},{7,15},{8,0},{9,1},{1... | collective-permute-start | bytes 1253384 | tf_op jit(solution)/shard_map/ppermute | solution.py:383
  33.6 0.5 collective-permute-start.7
  34.1 0.0 collective-permute-done.10.refs_2_
  34.1 8.1 %group.5 = (bf16[128,1536]{1,0:T(8,128)(2,1)}, bf16[128,1536]{1,0:T(8,128)(2,1)}, bf16[2,128,1536]{2,1,0:T(8,128)(2,1)}) custom-call(s32[1]{0:T(128)S(6)} %copy.31.failed, s32[4,16]{1,0:T(4,128)} %bitcast.64, bf16[136,1536]{1,0:T(8,128)(2,1)} %collective-permute-done.3.refs_0_, bf16[136,1536]{1,0:T(8,128)(2,1)} %after.9.refs_1_, ...), custom_call_target="tpu_custom_call" | custom-call | flops 3019898880 | bytes 14942208 | tf_op jit(solution)/shard_map/group/pallas_call | solution.py:316
  42.2 0.8 collective-permute-done.12.refs_0_
  43.1 2.2 %collective-permute-done.7.refs_1_ = bf16[136,1536]{1,0:T(8,128)(2,1)} collective-permute-done((bf16[136,1536]{1,0:T(8,128)(2,1)}, bf16[136,1536]{1,0:T(8,128)(2,1)}, u32[]{:S(2)}, u32[]{:S(2)}) %collective-permute-start.7) | collective-permute-done | bytes 417824 | tf_op jit(solution)/shard_map/ppermute | solution.py:383
  45.3 0.5 collective-permute-start.6
  45.8 0.0 collective-permute-start.8
  45.8 0.5 collective-permute-start.9
  46.3 0.4 collective-permute-start.13
  46.6 1.2 %collective-permute-done.20 = bf16[2,128,1536]{2,1,0:T(8,128)(2,1)} collective-permute-done((bf16[2,128,1536]{2,1,0:T(8,128)(2,1)}, bf16[2,128,1536]{2,1,0:T(8,128)(2,1)}, u32[]{:S(2)}, u32[]{:S(2)}) %collective-permute-start.20) | collective-permute-done | bytes 786464 | tf_op jit(solution)/shard_map/ppermute | solution.py:383
  47.9 2.0 %fusion.1 = bf16[128,1536]{1,0:T(8,128)(2,1)} fusion(bf16[128,1536]{1,0:T(8,128)(2,1)} %get-tuple-element.30, bf16[2,128,1536]{2,1,0:T(8,128)(2,1)} %collective-permute-done.20), kind=kLoop, calls=%fused_computation.3 | loop fusion | flops 786432 | bytes 1179648 | tf_op jit(solution)/shard_map/convert_element_type | solution.py:385
  49.9 0.5 collective-permute-start.21
  50.3 0.0 collective-permute-done.8.refs_2_
  50.3 0.0 collective-permute-done.6.refs_9_
  50.3 0.0 collective-permute-done.9.refs_3_
  50.3 8.2 %group.6 = (bf16[128,1536]{1,0:T(8,128)(2,1)}, bf16[128,1536]{1,0:T(8,128)(2,1)}, bf16[2,128,1536]{2,1,0:T(8,128)(2,1)}, bf16[128,1536]{1,0:T(8,128)(2,1)}) custom-call(s32[1]{0:T(128)S(6)} %copy.31.failed, s32[4,16]{1,0:T(4,128)} %bitcast.65, bf16[136,1536]{1,0:T(8,128)(2,1)} %after.10.refs_2_.refs_0_, bf16[136,1536]{1,0:T(8,128)(2,1)} %collective-permute-done.7.refs_1_, ...), custom_call_target="tpu_custom_call" | custom-call | flops 3019898880 | bytes 14942208 | tf_op jit(solution)/shard_map/group/pallas_call | solution.py:316
  58.6 0.5 collective-permute-done.13.refs_1_
  59.1 0.5 collective-permute-start.14
  59.6 0.0 collective-permute-start.15
  59.6 1.8 %collective-permute-done.21 = bf16[128,1536]{1,0:T(8,128)(2,1)} collective-permute-done((bf16[128,1536]{1,0:T(8,128)(2,1)}, bf16[128,1536]{1,0:T(8,128)(2,1)}, u32[]{:S(2)}, u32[]{:S(2)}) %collective-permute-start.21) | collective-permute-done | bytes 393248 | tf_op jit(solution)/shard_map/ppermute | solution.py:383
  61.3 2.1 %fusion.3 = bf16[128,1536]{1,0:T(8,128)(2,1)} fusion(bf16[128,1536]{1,0:T(8,128)(2,1)} %collective-permute-done.21, bf16[128,1536]{1,0:T(8,128)(2,1)} %get-tuple-element.21.refs_10_.refs_1_, bf16[2,128,1536]{2,1,0:T(8,128)(2,1)} %collective-permute-done.20), kind=kLoop, calls=%fused_computation.6 | loop fusion | flops 1179648 | bytes 1572864 | tf_op jit(solution)/shard_map/convert_element_type | solution.py:407
  63.5 0.4 collective-permute-start.22
  63.8 0.9 copy-done.3
  64.7 1.8 %fusion.4 = bf16[128,1536]{1,0:T(8,128)(2,1)} fusion(bf16[128,1536]{1,0:T(8,128)(2,1)} %get-tuple-element.28, bf16[2,128,1536]{2,1,0:T(8,128)(2,1)S(1)} %collective-permute-done.18), kind=kLoop, calls=%fused_computation.8 | loop fusion | flops 786432 | bytes 1179648 | tf_op jit(solution)/shard_map/convert_element_type | solution.py:385
  66.6 0.5 collective-permute-start.19
  67.0 0.0 collective-permute-done.14.refs_2_
  67.0 8.1 %group.7 = (bf16[128,1536]{1,0:T(8,128)(2,1)}, bf16[128,1536]{1,0:T(8,128)(2,1)}, bf16[2,128,1536]{2,1,0:T(8,128)(2,1)}) custom-call(s32[1]{0:T(128)S(6)} %copy.31.failed, s32[4,16]{1,0:T(4,128)} %bitcast.66, bf16[136,1536]{1,0:T(8,128)(2,1)} %after.12.refs_0_.refs_2_, bf16[136,1536]{1,0:T(8,128)(2,1)} %collective-permute-done.13.refs_1_, ...), custom_call_target="tpu_custom_call" | custom-call | flops 3019898880 | bytes 14942208 | tf_op jit(solution)/shard_map/group/pallas_call | solution.py:316
  75.2 0.1 collective-permute-start.16
  75.3 0.0 collective-permute-done.22
  75.3 1.8 %collective-permute-done.19 = bf16[128,1536]{1,0:T(8,128)(2,1)} collective-permute-done((bf16[128,1536]{1,0:T(8,128)(2,1)}, bf16[128,1536]{1,0:T(8,128)(2,1)}, u32[]{:S(2)}, u32[]{:S(2)}) %collective-permute-start.19) | collective-permute-done | bytes 393248 | tf_op jit(solution)/shard_map/ppermute | solution.py:383
  77.0 2.3 %fusion.11 = (bf16[64,1536]{1,0:T(8,128)(2,1)}, bf16[64,1536]{1,0:T(8,128)(2,1)S(1)}) fusion(bf16[128,1536]{1,0:T(8,128)(2,1)} %collective-permute-done.22, bf16[128,1536]{1,0:T(8,128)(2,1)} %collective-permute-done.19, bf16[2,128,1536]{2,1,0:T(8,128)(2,1)} %copy-done.3, bf16[128,1536]{1,0:T(8,128)(2,1)} %get-tuple-element.23.refs_8_), kind=kLoop, calls=%fused_computation.21 | loop fusion | flops 1572864 | bytes 1966080 | tf_op jit(solution)/shard_map/convert_element_type | solution.py:407
  79.4 1.0 collective-permute-start.23
  80.4 0.0 collective-permute-done.16
  80.4 2.1 %fusion.12 = (bf16[64,1536]{1,0:T(8,128)(2,1)}, bf16[64,1536]{1,0:T(8,128)(2,1)S(1)}) fusion(bf16[2,128,1536]{2,1,0:T(8,128)(2,1)S(1)} %collective-permute-done.16, bf16[128,1536]{1,0:T(8,128)(2,1)} %get-tuple-element.26), kind=kLoop, calls=%fused_computation.23 | loop fusion | flops 786432 | bytes 1179648 | tf_op jit(solution)/shard_map/convert_element_type | solution.py:385
  82.4 0.8 collective-permute-start.17
  83.3 1.7 %collective-permute-start.27 = (bf16[64,1536]{1,0:T(8,128)(2,1)}, bf16[64,1536]{1,0:T(8,128)(2,1)}, u32[]{:S(2)}, u32[]{:S(2)}) collective-permute-start(bf16[64,1536]{1,0:T(8,128)(2,1)} %get-tuple-element.31), channel_id=1, source_target_pairs={{0,4},{1,5},{2,6},{3,7},{4,12},{5,13},{6,14},{7,15},{8,0},{9,1},{1... | collective-permute-start | bytes 589832 | tf_op jit(solution)/shard_map/ppermute | solution.py:383
  85.0 1.4 %collective-permute-start.26 = (bf16[64,1536]{1,0:T(8,128)(2,1)}, bf16[64,1536]{1,0:T(8,128)(2,1)}, u32[]{:S(2)}, u32[]{:S(2)}) collective-permute-start(bf16[64,1536]{1,0:T(8,128)(2,1)} %get-tuple-element.33), channel_id=1, source_target_pairs={{0,2},{1,3},{2,0},{3,1},{4,6},{5,7},{6,4},{7,5},{8,10},{9,11},{10,... | collective-permute-start | bytes 589832 | tf_op jit(solution)/shard_map/ppermute | solution.py:383
  86.5 0.9 collective-permute-done.23
  87.3 2.9 %collective-permute-done.17 = bf16[64,1536]{1,0:T(8,128)(2,1)S(1)} collective-permute-done((bf16[64,1536]{1,0:T(8,128)(2,1)S(1)}, bf16[64,1536]{1,0:T(8,128)(2,1)S(1)}, u32[]{:S(2)}, u32[]{:S(2)}) %collective-permute-start.17) | collective-permute-done | bytes 196640 | tf_op jit(solution)/shard_map/ppermute | solution.py:383
  90.2 1.0 fusion.22.refs_1_
  91.2 1.7 %collective-permute-start.25 = (bf16[64,1536]{1,0:T(8,128)(2,1)S(1)}, bf16[64,1536]{1,0:T(8,128)(2,1)}, u32[]{:S(2)}, u32[]{:S(2)}) collective-permute-start(bf16[64,1536]{1,0:T(8,128)(2,1)S(1)} %fusion.22.refs_1_), channel_id=1, source_target_pairs={{0,4},{1,5},{2,6},{3,7},{4,12},{5,13},{6,14},{7,15},{8,0},{9,1},{1... | collective-permute-start | bytes 589832 | tf_op jit(solution)/shard_map/ppermute | solution.py:383
  93.0 0.0 collective-permute-start.24
  93.0 0.9 collective-permute-done.26
  93.9 2.0 %fusion.15 = bf16[64,1536]{1,0:T(8,128)(2,1)} fusion(bf16[64,1536]{1,0:T(8,128)(2,1)} %after.17, bf16[64,1536]{1,0:T(8,128)(2,1)} %collective-permute-done.26, bf16[2,128,1536]{2,1,0:T(8,128)(2,1)} %copy-done.2, bf16[128,1536]{1,0:T(8,128)(2,1)} %get-tuple-element.24), kind=kLoop, calls=%fused_computation.27 | loop fusion | flops 786432 | bytes 983040 | tf_op jit(solution)/shard_map/convert_element_type | solution.py:407
  95.9 1.5 %collective-permute-start.28 = (bf16[64,1536]{1,0:T(8,128)(2,1)}, bf16[64,1536]{1,0:T(8,128)(2,1)}, u32[]{:S(2)}, u32[]{:S(2)}) collective-permute-start(bf16[64,1536]{1,0:T(8,128)(2,1)} %fusion.15), channel_id=1, source_target_pairs={{0,4},{1,5},{2,6},{3,7},{4,12},{5,13},{6,14},{7,15},{8,0},{9,1},{1... | collective-permute-start | bytes 589832 | tf_op jit(solution)/shard_map/ppermute | solution.py:383
  97.5 0.5 collective-permute-done.25.refs_0_
  98.0 4.8 %collective-permute-done.28 = bf16[64,1536]{1,0:T(8,128)(2,1)} collective-permute-done((bf16[64,1536]{1,0:T(8,128)(2,1)}, bf16[64,1536]{1,0:T(8,128)(2,1)}, u32[]{:S(2)}, u32[]{:S(2)}) %collective-permute-start.28) | collective-permute-done | bytes 196640 | tf_op jit(solution)/shard_map/ppermute | solution.py:383
  102.8 2.3 %fusion.7 = bf16[128,1536]{1,0:T(8,128)(2,1)} fusion(bf16[128,1536]{1,0:T(8,128)(2,1)} %collective-permute-done.24, bf16[128,1536]{1,0:T(8,128)(2,1)} %get-tuple-element.18.refs_1_.refs_8_, bf16[2,128,1536]{2,1,0:T(8,128)(2,1)} %collective-permute-done.6.refs_9_, bf16[64,1536]{1,0:T(8,128)(2,1)} %collective-permute-done.28, bf16[64,1536]{1,0:T(8,128)(2,1)} %after.16), kind=kLoop, calls=%fused_computation.12 | loop fusion | flops 2162688 | bytes 1966080 | tf_op jit(solution)/shard_map/convert_element_type | solution.py:407
  (33 shorter events, 0.1 us)
Async XLA Ops:
  1.8 4.6 %copy-start.1 = (bf16[136,1536]{1,0:T(8,128)(2,1)}, bf16[136,1536]{1,0:T(8,128)(2,1)S(1)}, u32[]{:S(2)}) copy-start(bf16[136,1536]{1,0:T(8,128)(2,1)S(1)} %fusion.8.refs_0_) | copy-start | bytes 1253380
  1.8 12.7 %collective-permute-start = (bf16[136,1536]{1,0:T(8,128)(2,1)S(1)}, bf16[136,1536]{1,0:T(8,128)(2,1)S(1)}, u32[]{:S(2)}, u32[]{:S(2)}) collective-permute-start(bf16[136,1536]{1,0:T(8,128)(2,1)S(1)} %fusion.8.refs_0_), channel_id=1, source_target_pairs={{0,2},{1,3},{2,0},{3,1},{4,6},{5,7},{6,4},{7,5},{8,10},{9,11},{10,... | collective-permute-start | bytes 1253384 | tf_op jit(solution)/shard_map/ppermute | solution.py:383
  4.8 12.1 %collective-permute-start.3 = (bf16[136,1536]{1,0:T(8,128)(2,1)S(1)}, bf16[136,1536]{1,0:T(8,128)(2,1)}, u32[]{:S(2)}, u32[]{:S(2)}) collective-permute-start(bf16[136,1536]{1,0:T(8,128)(2,1)S(1)} %fusion.8.refs_0_), channel_id=1, source_target_pairs={{0,4},{1,5},{2,6},{3,7},{4,12},{5,13},{6,14},{7,15},{8,0},{9,1},{1... | collective-permute-start | bytes 1253384 | tf_op jit(solution)/shard_map/ppermute | solution.py:383
  6.4 12.4 %collective-permute-start.1 = (bf16[136,1536]{1,0:T(8,128)(2,1)S(1)}, bf16[136,1536]{1,0:T(8,128)(2,1)S(1)}, u32[]{:S(2)}, u32[]{:S(2)}) collective-permute-start(bf16[136,1536]{1,0:T(8,128)(2,1)S(1)} %fusion.8.refs_0_), channel_id=1, source_target_pairs={{0,1},{1,0},{2,3},{3,2},{4,5},{5,4},{6,7},{7,6},{8,9},{9,8},{10,11... | collective-permute-start | bytes 1253384 | tf_op jit(solution)/shard_map/ppermute | solution.py:383
  14.4 4.4 %copy-start.4 = (bf16[136,1536]{1,0:T(8,128)(2,1)}, bf16[136,1536]{1,0:T(8,128)(2,1)S(1)}, u32[]{:S(2)}) copy-start(bf16[136,1536]{1,0:T(8,128)(2,1)S(1)} %collective-permute-done.refs_1_) | copy-start | bytes 1253380
  14.4 4.4 %collective-permute-start.2 = (bf16[136,1536]{1,0:T(8,128)(2,1)S(1)}, bf16[136,1536]{1,0:T(8,128)(2,1)S(1)}, u32[]{:S(2)}, u32[]{:S(2)}) collective-permute-start(bf16[136,1536]{1,0:T(8,128)(2,1)S(1)} %collective-permute-done.refs_1_), channel_id=1, source_target_pairs={{0,1},{1,0},{2,3},{3,2},{4,5},{5,4},{6,7},{7,6},{8,9},{9,8},{10,11... | collective-permute-start | bytes 1253384 | tf_op jit(solution)/shard_map/ppermute | solution.py:383
  16.9 11.5 %collective-permute-start.4 = (bf16[136,1536]{1,0:T(8,128)(2,1)}, bf16[136,1536]{1,0:T(8,128)(2,1)}, u32[]{:S(2)}, u32[]{:S(2)}) collective-permute-start(bf16[136,1536]{1,0:T(8,128)(2,1)} %collective-permute-done.3.refs_0_), channel_id=1, source_target_pairs={{0,2},{1,3},{2,0},{3,1},{4,6},{5,7},{6,4},{7,5},{8,10},{9,11},{10,... | collective-permute-start | bytes 1253384 | tf_op jit(solution)/shard_map/ppermute | solution.py:383
  18.0 11.9 %collective-permute-start.5 = (bf16[136,1536]{1,0:T(8,128)(2,1)}, bf16[136,1536]{1,0:T(8,128)(2,1)}, u32[]{:S(2)}, u32[]{:S(2)}) collective-permute-start(bf16[136,1536]{1,0:T(8,128)(2,1)} %collective-permute-done.3.refs_0_), channel_id=1, source_target_pairs={{0,4},{1,5},{2,6},{3,7},{4,12},{5,13},{6,14},{7,15},{8,0},{9,1},{1... | collective-permute-start | bytes 1253384 | tf_op jit(solution)/shard_map/ppermute | solution.py:383
  18.8 15.3 %collective-permute-start.10 = (bf16[136,1536]{1,0:T(8,128)(2,1)}, bf16[136,1536]{1,0:T(8,128)(2,1)}, u32[]{:S(2)}, u32[]{:S(2)}) collective-permute-start(bf16[136,1536]{1,0:T(8,128)(2,1)} %collective-permute-done.3.refs_0_), channel_id=1, source_target_pairs={{0,1},{1,0},{2,3},{3,2},{4,5},{5,4},{6,7},{7,6},{8,9},{9,8},{10,11... | collective-permute-start | bytes 1253384 | tf_op jit(solution)/shard_map/ppermute | solution.py:383
  18.8 0.8 copy-start.5
  19.6 0.8 copy-start.6
  28.5 5.6 %collective-permute-start.11 = (bf16[136,1536]{1,0:T(8,128)(2,1)}, bf16[136,1536]{1,0:T(8,128)(2,1)}, u32[]{:S(2)}, u32[]{:S(2)}) collective-permute-start(bf16[136,1536]{1,0:T(8,128)(2,1)} %after.9.refs_1_), channel_id=1, source_target_pairs={{0,1},{1,0},{2,3},{3,2},{4,5},{5,4},{6,7},{7,6},{8,9},{9,8},{10,11... | collective-permute-start | bytes 1253384 | tf_op jit(solution)/shard_map/ppermute | solution.py:383
  29.9 13.2 %collective-permute-start.12 = (bf16[136,1536]{1,0:T(8,128)(2,1)}, bf16[136,1536]{1,0:T(8,128)(2,1)}, u32[]{:S(2)}, u32[]{:S(2)}) collective-permute-start(bf16[136,1536]{1,0:T(8,128)(2,1)} %after.10.refs_2_.refs_0_), channel_id=1, source_target_pairs={{0,4},{1,5},{2,6},{3,7},{4,12},{5,13},{6,14},{7,15},{8,0},{9,1},{1... | collective-permute-start | bytes 1253384 | tf_op jit(solution)/shard_map/ppermute | solution.py:383
  33.6 11.7 %collective-permute-start.7 = (bf16[136,1536]{1,0:T(8,128)(2,1)}, bf16[136,1536]{1,0:T(8,128)(2,1)}, u32[]{:S(2)}, u32[]{:S(2)}) collective-permute-start(bf16[136,1536]{1,0:T(8,128)(2,1)} %after.10.refs_2_.refs_0_), channel_id=1, source_target_pairs={{0,2},{1,3},{2,0},{3,1},{4,6},{5,7},{6,4},{7,5},{8,10},{9,11},{10,... | collective-permute-start | bytes 1253384 | tf_op jit(solution)/shard_map/ppermute | solution.py:383
  45.3 2.6 %collective-permute-start.20 = (bf16[2,128,1536]{2,1,0:T(8,128)(2,1)}, bf16[2,128,1536]{2,1,0:T(8,128)(2,1)}, u32[]{:S(2)}, u32[]{:S(2)}) collective-permute-start(bf16[2,128,1536]{2,1,0:T(8,128)(2,1)} %after.14), channel_id=1, source_target_pairs={{0,1},{1,0},{2,3},{3,2},{4,5},{5,4},{6,7},{7,6},{8,9},{9,8},{10,11... | collective-permute-start | bytes 2359304 | tf_op jit(solution)/shard_map/ppermute | solution.py:383
  45.3 5.1 %collective-permute-start.6 = (bf16[2,128,1536]{2,1,0:T(8,128)(2,1)}, bf16[2,128,1536]{2,1,0:T(8,128)(2,1)}, u32[]{:S(2)}, u32[]{:S(2)}) collective-permute-start(bf16[2,128,1536]{2,1,0:T(8,128)(2,1)} %after.11), channel_id=1, source_target_pairs={{0,1},{1,0},{2,3},{3,2},{4,5},{5,4},{6,7},{7,6},{8,9},{9,8},{10,11... | collective-permute-start | bytes 2359304 | tf_op jit(solution)/shard_map/ppermute | solution.py:383
  45.8 4.5 %collective-permute-start.8 = (bf16[136,1536]{1,0:T(8,128)(2,1)}, bf16[136,1536]{1,0:T(8,128)(2,1)}, u32[]{:S(2)}, u32[]{:S(2)}) collective-permute-start(bf16[136,1536]{1,0:T(8,128)(2,1)} %after.10.refs_2_.refs_0_), channel_id=1, source_target_pairs={{0,1},{1,0},{2,3},{3,2},{4,5},{5,4},{6,7},{7,6},{8,9},{9,8},{10,11... | collective-permute-start | bytes 1253384 | tf_op jit(solution)/shard_map/ppermute | solution.py:383
  45.8 4.5 %collective-permute-start.9 = (bf16[136,1536]{1,0:T(8,128)(2,1)}, bf16[136,1536]{1,0:T(8,128)(2,1)}, u32[]{:S(2)}, u32[]{:S(2)}) collective-permute-start(bf16[136,1536]{1,0:T(8,128)(2,1)} %collective-permute-done.7.refs_1_), channel_id=1, source_target_pairs={{0,1},{1,0},{2,3},{3,2},{4,5},{5,4},{6,7},{7,6},{8,9},{9,8},{10,11... | collective-permute-start | bytes 1253384 | tf_op jit(solution)/shard_map/ppermute | solution.py:383
  46.3 12.8 %collective-permute-start.13 = (bf16[136,1536]{1,0:T(8,128)(2,1)}, bf16[136,1536]{1,0:T(8,128)(2,1)}, u32[]{:S(2)}, u32[]{:S(2)}) collective-permute-start(bf16[136,1536]{1,0:T(8,128)(2,1)} %collective-permute-done.7.refs_1_), channel_id=1, source_target_pairs={{0,4},{1,5},{2,6},{3,7},{4,12},{5,13},{6,14},{7,15},{8,0},{9,1},{1... | collective-permute-start | bytes 1253384 | tf_op jit(solution)/shard_map/ppermute | solution.py:383
  49.9 11.5 %collective-permute-start.21 = (bf16[128,1536]{1,0:T(8,128)(2,1)}, bf16[128,1536]{1,0:T(8,128)(2,1)}, u32[]{:S(2)}, u32[]{:S(2)}) collective-permute-start(bf16[128,1536]{1,0:T(8,128)(2,1)} %fusion.1), channel_id=1, source_target_pairs={{0,2},{1,3},{2,0},{3,1},{4,6},{5,7},{6,4},{7,5},{8,10},{9,11},{10,... | collective-permute-start | bytes 1179656 | tf_op jit(solution)/shard_map/ppermute | solution.py:383
  59.1 4.8 %collective-permute-start.18 = (bf16[2,128,1536]{2,1,0:T(8,128)(2,1)}, bf16[2,128,1536]{2,1,0:T(8,128)(2,1)S(1)}, u32[]{:S(2)}, u32[]{:S(2)}) collective-permute-start(bf16[2,128,1536]{2,1,0:T(8,128)(2,1)} %after.13), channel_id=1, source_target_pairs={{0,1},{1,0},{2,3},{3,2},{4,5},{5,4},{6,7},{7,6},{8,9},{9,8},{10,11... | collective-permute-start | bytes 2359304 | tf_op jit(solution)/shard_map/ppermute | solution.py:383
  59.1 8.0 %collective-permute-start.14 = (bf16[136,1536]{1,0:T(8,128)(2,1)}, bf16[136,1536]{1,0:T(8,128)(2,1)}, u32[]{:S(2)}, u32[]{:S(2)}) collective-permute-start(bf16[136,1536]{1,0:T(8,128)(2,1)} %after.12.refs_0_.refs_2_), channel_id=1, source_target_pairs={{0,1},{1,0},{2,3},{3,2},{4,5},{5,4},{6,7},{7,6},{8,9},{9,8},{10,11... | collective-permute-start | bytes 1253384 | tf_op jit(solution)/shard_map/ppermute | solution.py:383
  59.6 7.5 %collective-permute-start.15 = (bf16[136,1536]{1,0:T(8,128)(2,1)}, bf16[136,1536]{1,0:T(8,128)(2,1)}, u32[]{:S(2)}, u32[]{:S(2)}) collective-permute-start(bf16[136,1536]{1,0:T(8,128)(2,1)} %collective-permute-done.13.refs_1_), channel_id=1, source_target_pairs={{0,1},{1,0},{2,3},{3,2},{4,5},{5,4},{6,7},{7,6},{8,9},{9,8},{10,11... | collective-permute-start | bytes 1253384 | tf_op jit(solution)/shard_map/ppermute | solution.py:383
  63.5 11.8 %collective-permute-start.22 = (bf16[128,1536]{1,0:T(8,128)(2,1)}, bf16[128,1536]{1,0:T(8,128)(2,1)}, u32[]{:S(2)}, u32[]{:S(2)}) collective-permute-start(bf16[128,1536]{1,0:T(8,128)(2,1)} %fusion.3), channel_id=1, source_target_pairs={{0,4},{1,5},{2,6},{3,7},{4,12},{5,13},{6,14},{7,15},{8,0},{9,1},{1... | collective-permute-start | bytes 1179656 | tf_op jit(solution)/shard_map/ppermute | solution.py:383
  63.8 0.9 copy-start.3
  66.6 10.5 %collective-permute-start.19 = (bf16[128,1536]{1,0:T(8,128)(2,1)}, bf16[128,1536]{1,0:T(8,128)(2,1)}, u32[]{:S(2)}, u32[]{:S(2)}) collective-permute-start(bf16[128,1536]{1,0:T(8,128)(2,1)} %fusion.4), channel_id=1, source_target_pairs={{0,2},{1,3},{2,0},{3,1},{4,6},{5,7},{6,4},{7,5},{8,10},{9,11},{10,... | collective-permute-start | bytes 1179656 | tf_op jit(solution)/shard_map/ppermute | solution.py:383
  75.2 5.2 %collective-permute-start.16 = (bf16[2,128,1536]{2,1,0:T(8,128)(2,1)}, bf16[2,128,1536]{2,1,0:T(8,128)(2,1)S(1)}, u32[]{:S(2)}, u32[]{:S(2)}) collective-permute-start(bf16[2,128,1536]{2,1,0:T(8,128)(2,1)} %get-tuple-element.25), channel_id=1, source_target_pairs={{0,1},{1,0},{2,3},{3,2},{4,5},{5,4},{6,7},{7,6},{8,9},{9,8},{10,11... | collective-permute-start | bytes 2359304 | tf_op jit(solution)/shard_map/ppermute | solution.py:383
  79.4 8.0 %collective-permute-start.23 = (bf16[64,1536]{1,0:T(8,128)(2,1)S(1)}, bf16[64,1536]{1,0:T(8,128)(2,1)S(1)}, u32[]{:S(2)}, u32[]{:S(2)}) collective-permute-start(bf16[64,1536]{1,0:T(8,128)(2,1)S(1)} %get-tuple-element.32), channel_id=1, source_target_pairs={{0,4},{1,5},{2,6},{3,7},{4,12},{5,13},{6,14},{7,15},{8,0},{9,1},{1... | collective-permute-start | bytes 589832 | tf_op jit(solution)/shard_map/ppermute | solution.py:383
  80.4 9.8 %copy-start.2 = (bf16[2,128,1536]{2,1,0:T(8,128)(2,1)}, bf16[2,128,1536]{2,1,0:T(8,128)(2,1)S(1)}, u32[]{:S(2)}) copy-start(bf16[2,128,1536]{2,1,0:T(8,128)(2,1)S(1)} %collective-permute-done.16) | copy-start | bytes 2359300
  82.4 7.8 %collective-permute-start.17 = (bf16[64,1536]{1,0:T(8,128)(2,1)S(1)}, bf16[64,1536]{1,0:T(8,128)(2,1)S(1)}, u32[]{:S(2)}, u32[]{:S(2)}) collective-permute-start(bf16[64,1536]{1,0:T(8,128)(2,1)S(1)} %get-tuple-element.34), channel_id=1, source_target_pairs={{0,2},{1,3},{2,0},{3,1},{4,6},{5,7},{6,4},{7,5},{8,10},{9,11},{10,... | collective-permute-start | bytes 589832 | tf_op jit(solution)/shard_map/ppermute | solution.py:383
  83.3 9.7 %collective-permute-start.27 = (bf16[64,1536]{1,0:T(8,128)(2,1)}, bf16[64,1536]{1,0:T(8,128)(2,1)}, u32[]{:S(2)}, u32[]{:S(2)}) collective-permute-start(bf16[64,1536]{1,0:T(8,128)(2,1)} %get-tuple-element.31), channel_id=1, source_target_pairs={{0,4},{1,5},{2,6},{3,7},{4,12},{5,13},{6,14},{7,15},{8,0},{9,1},{1... | collective-permute-start | bytes 589832 | tf_op jit(solution)/shard_map/ppermute | solution.py:383
  85.0 8.9 %collective-permute-start.26 = (bf16[64,1536]{1,0:T(8,128)(2,1)}, bf16[64,1536]{1,0:T(8,128)(2,1)}, u32[]{:S(2)}, u32[]{:S(2)}) collective-permute-start(bf16[64,1536]{1,0:T(8,128)(2,1)} %get-tuple-element.33), channel_id=1, source_target_pairs={{0,2},{1,3},{2,0},{3,1},{4,6},{5,7},{6,4},{7,5},{8,10},{9,11},{10,... | collective-permute-start | bytes 589832 | tf_op jit(solution)/shard_map/ppermute | solution.py:383
  91.2 1.8 %copy-start = (bf16[64,1536]{1,0:T(8,128)(2,1)}, bf16[64,1536]{1,0:T(8,128)(2,1)S(1)}, u32[]{:S(2)}) copy-start(bf16[64,1536]{1,0:T(8,128)(2,1)S(1)} %fusion.22.refs_1_) | copy-start | bytes 589828
  91.2 6.7 %collective-permute-start.25 = (bf16[64,1536]{1,0:T(8,128)(2,1)S(1)}, bf16[64,1536]{1,0:T(8,128)(2,1)}, u32[]{:S(2)}, u32[]{:S(2)}) collective-permute-start(bf16[64,1536]{1,0:T(8,128)(2,1)S(1)} %fusion.22.refs_1_), channel_id=1, source_target_pairs={{0,4},{1,5},{2,6},{3,7},{4,12},{5,13},{6,14},{7,15},{8,0},{9,1},{1... | collective-permute-start | bytes 589832 | tf_op jit(solution)/shard_map/ppermute | solution.py:383
  93.0 9.8 %collective-permute-start.24 = (bf16[128,1536]{1,0:T(8,128)(2,1)}, bf16[128,1536]{1,0:T(8,128)(2,1)}, u32[]{:S(2)}, u32[]{:S(2)}) collective-permute-start(bf16[128,1536]{1,0:T(8,128)(2,1)} %after.15), channel_id=1, source_target_pairs={{0,2},{1,3},{2,0},{3,1},{4,6},{5,7},{6,4},{7,5},{8,10},{9,11},{10,... | collective-permute-start | bytes 1179656 | tf_op jit(solution)/shard_map/ppermute | solution.py:383
  95.9 6.9 %collective-permute-start.28 = (bf16[64,1536]{1,0:T(8,128)(2,1)}, bf16[64,1536]{1,0:T(8,128)(2,1)}, u32[]{:S(2)}, u32[]{:S(2)}) collective-permute-start(bf16[64,1536]{1,0:T(8,128)(2,1)} %fusion.15), channel_id=1, source_target_pairs={{0,4},{1,5},{2,6},{3,7},{4,12},{5,13},{6,14},{7,15},{8,0},{9,1},{1... | collective-permute-start | bytes 589832 | tf_op jit(solution)/shard_map/ppermute | solution.py:383

commit v13 on v12

--- a/solution.py
+++ b/solution.py
@@ -163,7 +163,7 @@
     held, w_gate, w_down, spare_gate, spare_down = refs[:5]
     rows_in, spare_in, hidden, spare_hidden, rows_out, dense, summed, fetched, stored = refs[5:]
     width, inner = w_gate.shape
-    tile = 512
+    tile = 768
     my_id, failed_id = lax.axis_index("expert"), failed[0]
     holds = holders[0, failed_id] == my_id
     for j in range(1, holders.shape[0]):
@@ -287,7 +287,6 @@
     for i, n in enumerate(range(0, width, tile)):
         down_copies[i].wait()
         result = jnp.dot(hidden[...], w_down[:, n : n + tile], preferred_element_type=jnp.float32)
-        result = result.astype(jnp.bfloat16).astype(jnp.float32)
         for s in range(count):
             rows_out[s, :capacity, n : n + tile] = (
                 result[s * capacity : (s + 1) * capacity] * weights[s][:capacity]

time: 106 us -> 107 us (level)
  waiting for transfers between devices: 29.7 us -> 25.5 us
  starting transfers between devices: 22.1 us -> 25.3 us
  Pallas kernels: 32.6 us -> 34.6 us
    ppermute x29, waiting for transfers between devices: 29.7 us -> 25.5 us  [by_permutes(): move = lambda a, pairs: lax.ppermute(a, 'expert', pairs)]
    ppermute x29, starting transfers between devices: 22.1 us -> 25.3 us  [by_permutes(): move = lambda a, pairs: lax.ppermute(a, 'expert', pairs)]
    pallas_call x4, Pallas kernels: 32.6 us -> 34.6 us  [run_group(): pl.pallas_call(functools.partial(group_kernel, others=len(earlier), adds=...]
  transfers between devices with their start and end apart: 29 -> 29, of which waited for: 14 -> 11; matrix products, arithmetic and copies ran while one was open for 13% -> 13% of each run, Pallas kernels for 31% -> 33%
where the time goes in v13:
time: 107 us; the launch traced here: 106 us
  Pallas kernels  34.6 us (32%)
  waiting for transfers between devices  25.5 us (24%)
  starting transfers between devices  25.3 us (24%)
  other arithmetic  17.4 us (16%)
  local copies, waits for them, and re-layouts  2.87 us (3%)
    pallas_call x4, Pallas kernels, run_group(): pl.pallas_call(functools.partial(group_kernel, others=len(earlier), adds=...  34.6 us
    ppermute x29, waiting for transfers between devices, by_permutes(): move = lambda a, pairs: lax.ppermute(a, 'expert', pairs)  25.5 us
    ppermute x29, starting transfers between devices, by_permutes(): move = lambda a, pairs: lax.ppermute(a, 'expert', pairs)  25.3 us
    convert_element_type x5, other arithmetic, total(): return result.astype(jnp.bfloat16)  9.76 us
    convert_element_type x3, other arithmetic, by_permutes(): add = lambda a, b: (f32(a) + f32(b)).astype(jnp.bfloat16)  5.86 us
    unnamed x15, local copies, waits for them, and re-layouts  2.87 us
  transfers between devices with their start and end apart: 29, of which 11 were waited for; matrix products, arithmetic and copies ran while one was open for 13% of the time, Pallas kernels for 33%

profile of v13, /device:TPU:0, one launch (start us, length us, event | category | flops | bytes accessed | tf_op | source)
XLA Modules:
  0.0 106.5 jit_solution(9187731026146819437)
XLA Ops:
  0.0 0.7 fusion.23
  0.7 1.0 fusion.8.refs_0_
  1.8 3.0 %collective-permute-start = (bf16[136,1536]{1,0:T(8,128)(2,1)S(1)}, bf16[136,1536]{1,0:T(8,128)(2,1)S(1)}, u32[]{:S(2)}, u32[]{:S(2)}) collective-permute-start(bf16[136,1536]{1,0:T(8,128)(2,1)S(1)} %fusion.8.refs_0_), channel_id=1, source_target_pairs={{0,2},{1,3},{2,0},{3,1},{4,6},{5,7},{6,4},{7,5},{8,10},{9,11},{10,... | collective-permute-start | bytes 1253384 | tf_op jit(solution)/shard_map/ppermute | solution.py:382
  4.8 1.6 %collective-permute-start.3 = (bf16[136,1536]{1,0:T(8,128)(2,1)S(1)}, bf16[136,1536]{1,0:T(8,128)(2,1)}, u32[]{:S(2)}, u32[]{:S(2)}) collective-permute-start(bf16[136,1536]{1,0:T(8,128)(2,1)S(1)} %fusion.8.refs_0_), channel_id=1, source_target_pairs={{0,4},{1,5},{2,6},{3,7},{4,12},{5,13},{6,14},{7,15},{8,0},{9,1},{1... | collective-permute-start | bytes 1253384 | tf_op jit(solution)/shard_map/ppermute | solution.py:382
  6.4 0.0 collective-permute-start.1
  6.4 8.1 %collective-permute-done.refs_1_ = bf16[136,1536]{1,0:T(8,128)(2,1)S(1)} collective-permute-done((bf16[136,1536]{1,0:T(8,128)(2,1)S(1)}, bf16[136,1536]{1,0:T(8,128)(2,1)S(1)}, u32[]{:S(2)}, u32[]{:S(2)}) %collective-permute-start) | collective-permute-done | bytes 417824 | tf_op jit(solution)/shard_map/ppermute | solution.py:382
  14.4 0.0 collective-permute-start.2
  14.5 2.5 %collective-permute-done.3.refs_0_ = bf16[136,1536]{1,0:T(8,128)(2,1)} collective-permute-done((bf16[136,1536]{1,0:T(8,128)(2,1)S(1)}, bf16[136,1536]{1,0:T(8,128)(2,1)}, u32[]{:S(2)}, u32[]{:S(2)}) %collective-permute-start.3) | collective-permute-done | bytes 417824 | tf_op jit(solution)/shard_map/ppermute | solution.py:382
  16.9 0.5 collective-permute-start.4
  18.0 0.8 collective-permute-start.5
  18.8 0.7 copy-done.5
  19.6 0.8 copy-done.6
  20.4 8.6 %group.4 = (bf16[128,1536]{1,0:T(8,128)(2,1)}, bf16[128,1536]{1,0:T(8,128)(2,1)}, bf16[2,128,1536]{2,1,0:T(8,128)(2,1)}) custom-call(s32[1]{0:T(128)S(6)} %copy.31.failed, s32[4,16]{1,0:T(4,128)} %bitcast.63, bf16[136,1536]{1,0:T(8,128)(2,1)} %copy-done.1, bf16[136,1536]{1,0:T(8,128)(2,1)} %copy-done.4, bf16[136,1536]{1,0:T(8,128)(2,1)} %copy-done.5, ...), custom_call_target="tpu_custom_call" | custom-call | flops 3019898880 | bytes 14942208 | tf_op jit(solution)/shard_map/group/pallas_call | solution.py:315
  29.0 1.6 %collective-permute-start.11 = (bf16[136,1536]{1,0:T(8,128)(2,1)}, bf16[136,1536]{1,0:T(8,128)(2,1)}, u32[]{:S(2)}, u32[]{:S(2)}) collective-permute-start(bf16[136,1536]{1,0:T(8,128)(2,1)} %after.9.refs_1_), channel_id=1, source_target_pairs={{0,1},{1,0},{2,3},{3,2},{4,5},{5,4},{6,7},{7,6},{8,9},{9,8},{10,11... | collective-permute-start | bytes 1253384 | tf_op jit(solution)/shard_map/ppermute | solution.py:382
  30.6 0.0 collective-permute-done.5.refs_0_
  30.6 2.4 %collective-permute-start.12 = (bf16[136,1536]{1,0:T(8,128)(2,1)}, bf16[136,1536]{1,0:T(8,128)(2,1)}, u32[]{:S(2)}, u32[]{:S(2)}) collective-permute-start(bf16[136,1536]{1,0:T(8,128)(2,1)} %after.10.refs_2_.refs_0_), channel_id=1, source_target_pairs={{0,4},{1,5},{2,6},{3,7},{4,12},{5,13},{6,14},{7,15},{8,0},{9,1},{1... | collective-permute-start | bytes 1253384 | tf_op jit(solution)/shard_map/ppermute | solution.py:382
  33.1 1.5 %collective-permute-start.7 = (bf16[136,1536]{1,0:T(8,128)(2,1)}, bf16[136,1536]{1,0:T(8,128)(2,1)}, u32[]{:S(2)}, u32[]{:S(2)}) collective-permute-start(bf16[136,1536]{1,0:T(8,128)(2,1)} %after.10.refs_2_.refs_0_), channel_id=1, source_target_pairs={{0,2},{1,3},{2,0},{3,1},{4,6},{5,7},{6,4},{7,5},{8,10},{9,11},{10,... | collective-permute-start | bytes 1253384 | tf_op jit(solution)/shard_map/ppermute | solution.py:382
  34.6 8.6 %group.5 = (bf16[128,1536]{1,0:T(8,128)(2,1)}, bf16[128,1536]{1,0:T(8,128)(2,1)}, bf16[2,128,1536]{2,1,0:T(8,128)(2,1)}) custom-call(s32[1]{0:T(128)S(6)} %copy.31.failed, s32[4,16]{1,0:T(4,128)} %bitcast.64, bf16[136,1536]{1,0:T(8,128)(2,1)} %collective-permute-done.3.refs_0_, bf16[136,1536]{1,0:T(8,128)(2,1)} %after.9.refs_1_, ...), custom_call_target="tpu_custom_call" | custom-call | flops 3019898880 | bytes 14942208 | tf_op jit(solution)/shard_map/group/pallas_call | solution.py:315
  43.2 0.2 collective-permute-done.12.refs_0_
  43.5 1.3 %collective-permute-done.7.refs_1_ = bf16[136,1536]{1,0:T(8,128)(2,1)} collective-permute-done((bf16[136,1536]{1,0:T(8,128)(2,1)}, bf16[136,1536]{1,0:T(8,128)(2,1)}, u32[]{:S(2)}, u32[]{:S(2)}) %collective-permute-start.7) | collective-permute-done | bytes 417824 | tf_op jit(solution)/shard_map/ppermute | solution.py:382
  44.7 0.0 collective-permute-start.20
  44.7 0.5 collective-permute-start.6
  45.3 0.0 collective-permute-start.8
  45.3 0.5 collective-permute-start.9
  45.8 1.1 collective-permute-start.13
  46.8 0.5 collective-permute-done.20
  47.4 2.0 %fusion.1 = bf16[128,1536]{1,0:T(8,128)(2,1)} fusion(bf16[128,1536]{1,0:T(8,128)(2,1)} %get-tuple-element.30, bf16[2,128,1536]{2,1,0:T(8,128)(2,1)} %collective-permute-done.20), kind=kLoop, calls=%fused_computation.3 | loop fusion | flops 786432 | bytes 1179648 | tf_op jit(solution)/shard_map/convert_element_type | solution.py:384
  49.3 1.5 %collective-permute-start.21 = (bf16[128,1536]{1,0:T(8,128)(2,1)}, bf16[128,1536]{1,0:T(8,128)(2,1)}, u32[]{:S(2)}, u32[]{:S(2)}) collective-permute-start(bf16[128,1536]{1,0:T(8,128)(2,1)} %fusion.1), channel_id=1, source_target_pairs={{0,2},{1,3},{2,0},{3,1},{4,6},{5,7},{6,4},{7,5},{8,10},{9,11},{10,... | collective-permute-start | bytes 1179656 | tf_op jit(solution)/shard_map/ppermute | solution.py:382
  50.9 0.0 collective-permute-done.8.refs_2_
  50.9 0.0 collective-permute-done.6.refs_9_
  50.9 0.0 collective-permute-done.9.refs_3_
  50.9 8.7 %group.6 = (bf16[128,1536]{1,0:T(8,128)(2,1)}, bf16[128,1536]{1,0:T(8,128)(2,1)}, bf16[2,128,1536]{2,1,0:T(8,128)(2,1)}, bf16[128,1536]{1,0:T(8,128)(2,1)}) custom-call(s32[1]{0:T(128)S(6)} %copy.31.failed, s32[4,16]{1,0:T(4,128)} %bitcast.65, bf16[136,1536]{1,0:T(8,128)(2,1)} %after.10.refs_2_.refs_0_, bf16[136,1536]{1,0:T(8,128)(2,1)} %collective-permute-done.7.refs_1_, ...), custom_call_target="tpu_custom_call" | custom-call | flops 3019898880 | bytes 14942208 | tf_op jit(solution)/shard_map/group/pallas_call | solution.py:315
  59.6 0.0 collective-permute-done.13.refs_1_
  59.6 1.0 collective-permute-start.18
  60.6 0.1 collective-permute-start.14
  60.7 0.4 collective-permute-start.15
  61.1 2.1 %fusion.3 = bf16[128,1536]{1,0:T(8,128)(2,1)} fusion(bf16[128,1536]{1,0:T(8,128)(2,1)} %collective-permute-done.21, bf16[128,1536]{1,0:T(8,128)(2,1)} %get-tuple-element.21.refs_10_.refs_1_, bf16[2,128,1536]{2,1,0:T(8,128)(2,1)} %collective-permute-done.20), kind=kLoop, calls=%fused_computation.6 | loop fusion | flops 1179648 | bytes 1572864 | tf_op jit(solution)/shard_map/convert_element_type | solution.py:406
  63.3 0.8 collective-permute-start.22
  64.0 0.0 collective-permute-done.18
  64.0 0.9 copy-done.3
  64.9 1.8 %fusion.4 = bf16[128,1536]{1,0:T(8,128)(2,1)} fusion(bf16[128,1536]{1,0:T(8,128)(2,1)} %get-tuple-element.28, bf16[2,128,1536]{2,1,0:T(8,128)(2,1)S(1)} %collective-permute-done.18), kind=kLoop, calls=%fused_computation.8 | loop fusion | flops 786432 | bytes 1179648 | tf_op jit(solution)/shard_map/convert_element_type | solution.py:384
  66.7 1.5 %collective-permute-start.19 = (bf16[128,1536]{1,0:T(8,128)(2,1)}, bf16[128,1536]{1,0:T(8,128)(2,1)}, u32[]{:S(2)}, u32[]{:S(2)}) collective-permute-start(bf16[128,1536]{1,0:T(8,128)(2,1)} %fusion.4), channel_id=1, source_target_pairs={{0,2},{1,3},{2,0},{3,1},{4,6},{5,7},{6,4},{7,5},{8,10},{9,11},{10,... | collective-permute-start | bytes 1179656 | tf_op jit(solution)/shard_map/ppermute | solution.py:382
  68.3 0.0 collective-permute-done.15.refs_3_
  68.3 8.6 %group.7 = (bf16[128,1536]{1,0:T(8,128)(2,1)}, bf16[128,1536]{1,0:T(8,128)(2,1)}, bf16[2,128,1536]{2,1,0:T(8,128)(2,1)}) custom-call(s32[1]{0:T(128)S(6)} %copy.31.failed, s32[4,16]{1,0:T(4,128)} %bitcast.66, bf16[136,1536]{1,0:T(8,128)(2,1)} %after.12.refs_0_.refs_2_, bf16[136,1536]{1,0:T(8,128)(2,1)} %collective-permute-done.13.refs_1_, ...), custom_call_target="tpu_custom_call" | custom-call | flops 3019898880 | bytes 14942208 | tf_op jit(solution)/shard_map/group/pallas_call | solution.py:315
  76.9 0.1 collective-permute-start.16
  77.0 0.7 collective-permute-done.19
  77.7 2.3 %fusion.11 = (bf16[64,1536]{1,0:T(8,128)(2,1)}, bf16[64,1536]{1,0:T(8,128)(2,1)S(1)}) fusion(bf16[128,1536]{1,0:T(8,128)(2,1)} %collective-permute-done.22, bf16[128,1536]{1,0:T(8,128)(2,1)} %collective-permute-done.19, bf16[2,128,1536]{2,1,0:T(8,128)(2,1)} %copy-done.3, bf16[128,1536]{1,0:T(8,128)(2,1)} %get-tuple-element.23.refs_8_), kind=kLoop, calls=%fused_computation.21 | loop fusion | flops 1572864 | bytes 1966080 | tf_op jit(solution)/shard_map/convert_element_type | solution.py:406
  80.0 2.2 %collective-permute-start.23 = (bf16[64,1536]{1,0:T(8,128)(2,1)S(1)}, bf16[64,1536]{1,0:T(8,128)(2,1)S(1)}, u32[]{:S(2)}, u32[]{:S(2)}) collective-permute-start(bf16[64,1536]{1,0:T(8,128)(2,1)S(1)} %get-tuple-element.32), channel_id=1, source_target_pairs={{0,4},{1,5},{2,6},{3,7},{4,12},{5,13},{6,14},{7,15},{8,0},{9,1},{1... | collective-permute-start | bytes 589832 | tf_op jit(solution)/shard_map/ppermute | solution.py:382
  82.3 2.1 %fusion.12 = (bf16[64,1536]{1,0:T(8,128)(2,1)}, bf16[64,1536]{1,0:T(8,128)(2,1)S(1)}) fusion(bf16[2,128,1536]{2,1,0:T(8,128)(2,1)S(1)} %collective-permute-done.16, bf16[128,1536]{1,0:T(8,128)(2,1)} %get-tuple-element.26), kind=kLoop, calls=%fused_computation.23 | loop fusion | flops 786432 | bytes 1179648 | tf_op jit(solution)/shard_map/convert_element_type | solution.py:384
  84.4 0.5 collective-permute-start.17
  84.8 0.3 collective-permute-start.27
  85.1 1.5 %collective-permute-start.26 = (bf16[64,1536]{1,0:T(8,128)(2,1)}, bf16[64,1536]{1,0:T(8,128)(2,1)}, u32[]{:S(2)}, u32[]{:S(2)}) collective-permute-start(bf16[64,1536]{1,0:T(8,128)(2,1)} %get-tuple-element.33), channel_id=1, source_target_pairs={{0,2},{1,3},{2,0},{3,1},{4,6},{5,7},{6,4},{7,5},{8,10},{9,11},{10,... | collective-permute-start | bytes 589832 | tf_op jit(solution)/shard_map/ppermute | solution.py:382
  86.7 1.1 %collective-permute-done.23 = bf16[64,1536]{1,0:T(8,128)(2,1)S(1)} collective-permute-done((bf16[64,1536]{1,0:T(8,128)(2,1)S(1)}, bf16[64,1536]{1,0:T(8,128)(2,1)S(1)}, u32[]{:S(2)}, u32[]{:S(2)}) %collective-permute-start.23) | collective-permute-done | bytes 196640 | tf_op jit(solution)/shard_map/ppermute | solution.py:382
  87.7 4.5 %collective-permute-done.17 = bf16[64,1536]{1,0:T(8,128)(2,1)S(1)} collective-permute-done((bf16[64,1536]{1,0:T(8,128)(2,1)S(1)}, bf16[64,1536]{1,0:T(8,128)(2,1)S(1)}, u32[]{:S(2)}, u32[]{:S(2)}) %collective-permute-start.17) | collective-permute-done | bytes 196640 | tf_op jit(solution)/shard_map/ppermute | solution.py:382
  92.2 1.0 fusion.22.refs_1_
  93.2 0.3 collective-permute-start.25
  93.5 0.4 copy-done
  93.9 0.3 collective-permute-start.24
  94.2 0.6 collective-permute-done.26
  94.8 2.0 %fusion.15 = bf16[64,1536]{1,0:T(8,128)(2,1)} fusion(bf16[64,1536]{1,0:T(8,128)(2,1)} %after.17, bf16[64,1536]{1,0:T(8,128)(2,1)} %collective-permute-done.26, bf16[2,128,1536]{2,1,0:T(8,128)(2,1)} %copy-done.2, bf16[128,1536]{1,0:T(8,128)(2,1)} %get-tuple-element.24), kind=kLoop, calls=%fused_computation.27 | loop fusion | flops 786432 | bytes 983040 | tf_op jit(solution)/shard_map/convert_element_type | solution.py:406
  96.8 1.3 %collective-permute-start.28 = (bf16[64,1536]{1,0:T(8,128)(2,1)}, bf16[64,1536]{1,0:T(8,128)(2,1)}, u32[]{:S(2)}, u32[]{:S(2)}) collective-permute-start(bf16[64,1536]{1,0:T(8,128)(2,1)} %fusion.15), channel_id=1, source_target_pairs={{0,4},{1,5},{2,6},{3,7},{4,12},{5,13},{6,14},{7,15},{8,0},{9,1},{1... | collective-permute-start | bytes 589832 | tf_op jit(solution)/shard_map/ppermute | solution.py:382
  98.1 3.4 %collective-permute-done.25.refs_0_ = bf16[64,1536]{1,0:T(8,128)(2,1)} collective-permute-done((bf16[64,1536]{1,0:T(8,128)(2,1)S(1)}, bf16[64,1536]{1,0:T(8,128)(2,1)}, u32[]{:S(2)}, u32[]{:S(2)}) %collective-permute-start.25) | collective-permute-done | bytes 196640 | tf_op jit(solution)/shard_map/ppermute | solution.py:382
  101.5 2.7 %collective-permute-done.28 = bf16[64,1536]{1,0:T(8,128)(2,1)} collective-permute-done((bf16[64,1536]{1,0:T(8,128)(2,1)}, bf16[64,1536]{1,0:T(8,128)(2,1)}, u32[]{:S(2)}, u32[]{:S(2)}) %collective-permute-start.28) | collective-permute-done | bytes 196640 | tf_op jit(solution)/shard_map/ppermute | solution.py:382
  104.2 2.3 %fusion.7 = bf16[128,1536]{1,0:T(8,128)(2,1)} fusion(bf16[128,1536]{1,0:T(8,128)(2,1)} %collective-permute-done.24, bf16[128,1536]{1,0:T(8,128)(2,1)} %get-tuple-element.18.refs_1_.refs_8_, bf16[2,128,1536]{2,1,0:T(8,128)(2,1)} %collective-permute-done.6.refs_9_, bf16[64,1536]{1,0:T(8,128)(2,1)} %collective-permute-done.28, bf16[64,1536]{1,0:T(8,128)(2,1)} %after.16), kind=kLoop, calls=%fused_computation.12 | loop fusion | flops 2162688 | bytes 1966080 | tf_op jit(solution)/shard_map/convert_element_type | solution.py:406
  (33 shorter events, 0.1 us)
Async XLA Ops:
  1.8 4.6 %copy-start.1 = (bf16[136,1536]{1,0:T(8,128)(2,1)}, bf16[136,1536]{1,0:T(8,128)(2,1)S(1)}, u32[]{:S(2)}) copy-start(bf16[136,1536]{1,0:T(8,128)(2,1)S(1)} %fusion.8.refs_0_) | copy-start | bytes 1253380
  1.8 12.7 %collective-permute-start = (bf16[136,1536]{1,0:T(8,128)(2,1)S(1)}, bf16[136,1536]{1,0:T(8,128)(2,1)S(1)}, u32[]{:S(2)}, u32[]{:S(2)}) collective-permute-start(bf16[136,1536]{1,0:T(8,128)(2,1)S(1)} %fusion.8.refs_0_), channel_id=1, source_target_pairs={{0,2},{1,3},{2,0},{3,1},{4,6},{5,7},{6,4},{7,5},{8,10},{9,11},{10,... | collective-permute-start | bytes 1253384 | tf_op jit(solution)/shard_map/ppermute | solution.py:382
  4.8 12.1 %collective-permute-start.3 = (bf16[136,1536]{1,0:T(8,128)(2,1)S(1)}, bf16[136,1536]{1,0:T(8,128)(2,1)}, u32[]{:S(2)}, u32[]{:S(2)}) collective-permute-start(bf16[136,1536]{1,0:T(8,128)(2,1)S(1)} %fusion.8.refs_0_), channel_id=1, source_target_pairs={{0,4},{1,5},{2,6},{3,7},{4,12},{5,13},{6,14},{7,15},{8,0},{9,1},{1... | collective-permute-start | bytes 1253384 | tf_op jit(solution)/shard_map/ppermute | solution.py:382
  6.4 12.4 %collective-permute-start.1 = (bf16[136,1536]{1,0:T(8,128)(2,1)S(1)}, bf16[136,1536]{1,0:T(8,128)(2,1)S(1)}, u32[]{:S(2)}, u32[]{:S(2)}) collective-permute-start(bf16[136,1536]{1,0:T(8,128)(2,1)S(1)} %fusion.8.refs_0_), channel_id=1, source_target_pairs={{0,1},{1,0},{2,3},{3,2},{4,5},{5,4},{6,7},{7,6},{8,9},{9,8},{10,11... | collective-permute-start | bytes 1253384 | tf_op jit(solution)/shard_map/ppermute | solution.py:382
  14.4 4.4 %copy-start.4 = (bf16[136,1536]{1,0:T(8,128)(2,1)}, bf16[136,1536]{1,0:T(8,128)(2,1)S(1)}, u32[]{:S(2)}) copy-start(bf16[136,1536]{1,0:T(8,128)(2,1)S(1)} %collective-permute-done.refs_1_) | copy-start | bytes 1253380
  14.4 4.4 %collective-permute-start.2 = (bf16[136,1536]{1,0:T(8,128)(2,1)S(1)}, bf16[136,1536]{1,0:T(8,128)(2,1)S(1)}, u32[]{:S(2)}, u32[]{:S(2)}) collective-permute-start(bf16[136,1536]{1,0:T(8,128)(2,1)S(1)} %collective-permute-done.refs_1_), channel_id=1, source_target_pairs={{0,1},{1,0},{2,3},{3,2},{4,5},{5,4},{6,7},{7,6},{8,9},{9,8},{10,11... | collective-permute-start | bytes 1253384 | tf_op jit(solution)/shard_map/ppermute | solution.py:382
  16.9 12.1 %collective-permute-start.4 = (bf16[136,1536]{1,0:T(8,128)(2,1)}, bf16[136,1536]{1,0:T(8,128)(2,1)}, u32[]{:S(2)}, u32[]{:S(2)}) collective-permute-start(bf16[136,1536]{1,0:T(8,128)(2,1)} %collective-permute-done.3.refs_0_), channel_id=1, source_target_pairs={{0,2},{1,3},{2,0},{3,1},{4,6},{5,7},{6,4},{7,5},{8,10},{9,11},{10,... | collective-permute-start | bytes 1253384 | tf_op jit(solution)/shard_map/ppermute | solution.py:382
  18.0 12.6 %collective-permute-start.5 = (bf16[136,1536]{1,0:T(8,128)(2,1)}, bf16[136,1536]{1,0:T(8,128)(2,1)}, u32[]{:S(2)}, u32[]{:S(2)}) collective-permute-start(bf16[136,1536]{1,0:T(8,128)(2,1)} %collective-permute-done.3.refs_0_), channel_id=1, source_target_pairs={{0,4},{1,5},{2,6},{3,7},{4,12},{5,13},{6,14},{7,15},{8,0},{9,1},{1... | collective-permute-start | bytes 1253384 | tf_op jit(solution)/shard_map/ppermute | solution.py:382
  18.8 15.8 %collective-permute-start.10 = (bf16[136,1536]{1,0:T(8,128)(2,1)}, bf16[136,1536]{1,0:T(8,128)(2,1)}, u32[]{:S(2)}, u32[]{:S(2)}) collective-permute-start(bf16[136,1536]{1,0:T(8,128)(2,1)} %collective-permute-done.3.refs_0_), channel_id=1, source_target_pairs={{0,1},{1,0},{2,3},{3,2},{4,5},{5,4},{6,7},{7,6},{8,9},{9,8},{10,11... | collective-permute-start | bytes 1253384 | tf_op jit(solution)/shard_map/ppermute | solution.py:382
  18.8 0.8 copy-start.5
  19.6 0.8 copy-start.6
  29.0 5.6 %collective-permute-start.11 = (bf16[136,1536]{1,0:T(8,128)(2,1)}, bf16[136,1536]{1,0:T(8,128)(2,1)}, u32[]{:S(2)}, u32[]{:S(2)}) collective-permute-start(bf16[136,1536]{1,0:T(8,128)(2,1)} %after.9.refs_1_), channel_id=1, source_target_pairs={{0,1},{1,0},{2,3},{3,2},{4,5},{5,4},{6,7},{7,6},{8,9},{9,8},{10,11... | collective-permute-start | bytes 1253384 | tf_op jit(solution)/shard_map/ppermute | solution.py:382
  30.6 12.8 %collective-permute-start.12 = (bf16[136,1536]{1,0:T(8,128)(2,1)}, bf16[136,1536]{1,0:T(8,128)(2,1)}, u32[]{:S(2)}, u32[]{:S(2)}) collective-permute-start(bf16[136,1536]{1,0:T(8,128)(2,1)} %after.10.refs_2_.refs_0_), channel_id=1, source_target_pairs={{0,4},{1,5},{2,6},{3,7},{4,12},{5,13},{6,14},{7,15},{8,0},{9,1},{1... | collective-permute-start | bytes 1253384 | tf_op jit(solution)/shard_map/ppermute | solution.py:382
  33.1 11.7 %collective-permute-start.7 = (bf16[136,1536]{1,0:T(8,128)(2,1)}, bf16[136,1536]{1,0:T(8,128)(2,1)}, u32[]{:S(2)}, u32[]{:S(2)}) collective-permute-start(bf16[136,1536]{1,0:T(8,128)(2,1)} %after.10.refs_2_.refs_0_), channel_id=1, source_target_pairs={{0,2},{1,3},{2,0},{3,1},{4,6},{5,7},{6,4},{7,5},{8,10},{9,11},{10,... | collective-permute-start | bytes 1253384 | tf_op jit(solution)/shard_map/ppermute | solution.py:382
  44.7 2.6 %collective-permute-start.20 = (bf16[2,128,1536]{2,1,0:T(8,128)(2,1)}, bf16[2,128,1536]{2,1,0:T(8,128)(2,1)}, u32[]{:S(2)}, u32[]{:S(2)}) collective-permute-start(bf16[2,128,1536]{2,1,0:T(8,128)(2,1)} %after.14), channel_id=1, source_target_pairs={{0,1},{1,0},{2,3},{3,2},{4,5},{5,4},{6,7},{7,6},{8,9},{9,8},{10,11... | collective-permute-start | bytes 2359304 | tf_op jit(solution)/shard_map/ppermute | solution.py:382
  44.7 6.1 %collective-permute-start.6 = (bf16[2,128,1536]{2,1,0:T(8,128)(2,1)}, bf16[2,128,1536]{2,1,0:T(8,128)(2,1)}, u32[]{:S(2)}, u32[]{:S(2)}) collective-permute-start(bf16[2,128,1536]{2,1,0:T(8,128)(2,1)} %after.11), channel_id=1, source_target_pairs={{0,1},{1,0},{2,3},{3,2},{4,5},{5,4},{6,7},{7,6},{8,9},{9,8},{10,11... | collective-permute-start | bytes 2359304 | tf_op jit(solution)/shard_map/ppermute | solution.py:382
  45.3 5.6 %collective-permute-start.8 = (bf16[136,1536]{1,0:T(8,128)(2,1)}, bf16[136,1536]{1,0:T(8,128)(2,1)}, u32[]{:S(2)}, u32[]{:S(2)}) collective-permute-start(bf16[136,1536]{1,0:T(8,128)(2,1)} %after.10.refs_2_.refs_0_), channel_id=1, source_target_pairs={{0,1},{1,0},{2,3},{3,2},{4,5},{5,4},{6,7},{7,6},{8,9},{9,8},{10,11... | collective-permute-start | bytes 1253384 | tf_op jit(solution)/shard_map/ppermute | solution.py:382
  45.3 5.6 %collective-permute-start.9 = (bf16[136,1536]{1,0:T(8,128)(2,1)}, bf16[136,1536]{1,0:T(8,128)(2,1)}, u32[]{:S(2)}, u32[]{:S(2)}) collective-permute-start(bf16[136,1536]{1,0:T(8,128)(2,1)} %collective-permute-done.7.refs_1_), channel_id=1, source_target_pairs={{0,1},{1,0},{2,3},{3,2},{4,5},{5,4},{6,7},{7,6},{8,9},{9,8},{10,11... | collective-permute-start | bytes 1253384 | tf_op jit(solution)/shard_map/ppermute | solution.py:382
  45.8 13.8 %collective-permute-start.13 = (bf16[136,1536]{1,0:T(8,128)(2,1)}, bf16[136,1536]{1,0:T(8,128)(2,1)}, u32[]{:S(2)}, u32[]{:S(2)}) collective-permute-start(bf16[136,1536]{1,0:T(8,128)(2,1)} %collective-permute-done.7.refs_1_), channel_id=1, source_target_pairs={{0,4},{1,5},{2,6},{3,7},{4,12},{5,13},{6,14},{7,15},{8,0},{9,1},{1... | collective-permute-start | bytes 1253384 | tf_op jit(solution)/shard_map/ppermute | solution.py:382
  49.3 11.8 %collective-permute-start.21 = (bf16[128,1536]{1,0:T(8,128)(2,1)}, bf16[128,1536]{1,0:T(8,128)(2,1)}, u32[]{:S(2)}, u32[]{:S(2)}) collective-permute-start(bf16[128,1536]{1,0:T(8,128)(2,1)} %fusion.1), channel_id=1, source_target_pairs={{0,2},{1,3},{2,0},{3,1},{4,6},{5,7},{6,4},{7,5},{8,10},{9,11},{10,... | collective-permute-start | bytes 1179656 | tf_op jit(solution)/shard_map/ppermute | solution.py:382
  59.6 4.4 %collective-permute-start.18 = (bf16[2,128,1536]{2,1,0:T(8,128)(2,1)}, bf16[2,128,1536]{2,1,0:T(8,128)(2,1)S(1)}, u32[]{:S(2)}, u32[]{:S(2)}) collective-permute-start(bf16[2,128,1536]{2,1,0:T(8,128)(2,1)} %after.13), channel_id=1, source_target_pairs={{0,1},{1,0},{2,3},{3,2},{4,5},{5,4},{6,7},{7,6},{8,9},{9,8},{10,11... | collective-permute-start | bytes 2359304 | tf_op jit(solution)/shard_map/ppermute | solution.py:382
  60.6 7.7 %collective-permute-start.14 = (bf16[136,1536]{1,0:T(8,128)(2,1)}, bf16[136,1536]{1,0:T(8,128)(2,1)}, u32[]{:S(2)}, u32[]{:S(2)}) collective-permute-start(bf16[136,1536]{1,0:T(8,128)(2,1)} %after.12.refs_0_.refs_2_), channel_id=1, source_target_pairs={{0,1},{1,0},{2,3},{3,2},{4,5},{5,4},{6,7},{7,6},{8,9},{9,8},{10,11... | collective-permute-start | bytes 1253384 | tf_op jit(solution)/shard_map/ppermute | solution.py:382
  60.7 7.6 %collective-permute-start.15 = (bf16[136,1536]{1,0:T(8,128)(2,1)}, bf16[136,1536]{1,0:T(8,128)(2,1)}, u32[]{:S(2)}, u32[]{:S(2)}) collective-permute-start(bf16[136,1536]{1,0:T(8,128)(2,1)} %collective-permute-done.13.refs_1_), channel_id=1, source_target_pairs={{0,1},{1,0},{2,3},{3,2},{4,5},{5,4},{6,7},{7,6},{8,9},{9,8},{10,11... | collective-permute-start | bytes 1253384 | tf_op jit(solution)/shard_map/ppermute | solution.py:382
  63.3 13.8 %collective-permute-start.22 = (bf16[128,1536]{1,0:T(8,128)(2,1)}, bf16[128,1536]{1,0:T(8,128)(2,1)}, u32[]{:S(2)}, u32[]{:S(2)}) collective-permute-start(bf16[128,1536]{1,0:T(8,128)(2,1)} %fusion.3), channel_id=1, source_target_pairs={{0,4},{1,5},{2,6},{3,7},{4,12},{5,13},{6,14},{7,15},{8,0},{9,1},{1... | collective-permute-start | bytes 1179656 | tf_op jit(solution)/shard_map/ppermute | solution.py:382
  64.0 0.9 copy-start.3
  66.7 11.0 %collective-permute-start.19 = (bf16[128,1536]{1,0:T(8,128)(2,1)}, bf16[128,1536]{1,0:T(8,128)(2,1)}, u32[]{:S(2)}, u32[]{:S(2)}) collective-permute-start(bf16[128,1536]{1,0:T(8,128)(2,1)} %fusion.4), channel_id=1, source_target_pairs={{0,2},{1,3},{2,0},{3,1},{4,6},{5,7},{6,4},{7,5},{8,10},{9,11},{10,... | collective-permute-start | bytes 1179656 | tf_op jit(solution)/shard_map/ppermute | solution.py:382
  76.9 5.4 %collective-permute-start.16 = (bf16[2,128,1536]{2,1,0:T(8,128)(2,1)}, bf16[2,128,1536]{2,1,0:T(8,128)(2,1)S(1)}, u32[]{:S(2)}, u32[]{:S(2)}) collective-permute-start(bf16[2,128,1536]{2,1,0:T(8,128)(2,1)} %get-tuple-element.25), channel_id=1, source_target_pairs={{0,1},{1,0},{2,3},{3,2},{4,5},{5,4},{6,7},{7,6},{8,9},{9,8},{10,11... | collective-permute-start | bytes 2359304 | tf_op jit(solution)/shard_map/ppermute | solution.py:382
  80.0 7.7 %collective-permute-start.23 = (bf16[64,1536]{1,0:T(8,128)(2,1)S(1)}, bf16[64,1536]{1,0:T(8,128)(2,1)S(1)}, u32[]{:S(2)}, u32[]{:S(2)}) collective-permute-start(bf16[64,1536]{1,0:T(8,128)(2,1)S(1)} %get-tuple-element.32), channel_id=1, source_target_pairs={{0,4},{1,5},{2,6},{3,7},{4,12},{5,13},{6,14},{7,15},{8,0},{9,1},{1... | collective-permute-start | bytes 589832 | tf_op jit(solution)/shard_map/ppermute | solution.py:382
  82.3 9.9 %copy-start.2 = (bf16[2,128,1536]{2,1,0:T(8,128)(2,1)}, bf16[2,128,1536]{2,1,0:T(8,128)(2,1)S(1)}, u32[]{:S(2)}) copy-start(bf16[2,128,1536]{2,1,0:T(8,128)(2,1)S(1)} %collective-permute-done.16) | copy-start | bytes 2359300
  84.4 7.8 %collective-permute-start.17 = (bf16[64,1536]{1,0:T(8,128)(2,1)S(1)}, bf16[64,1536]{1,0:T(8,128)(2,1)S(1)}, u32[]{:S(2)}, u32[]{:S(2)}) collective-permute-start(bf16[64,1536]{1,0:T(8,128)(2,1)S(1)} %get-tuple-element.34), channel_id=1, source_target_pairs={{0,2},{1,3},{2,0},{3,1},{4,6},{5,7},{6,4},{7,5},{8,10},{9,11},{10,... | collective-permute-start | bytes 589832 | tf_op jit(solution)/shard_map/ppermute | solution.py:382
  84.8 9.3 %collective-permute-start.27 = (bf16[64,1536]{1,0:T(8,128)(2,1)}, bf16[64,1536]{1,0:T(8,128)(2,1)}, u32[]{:S(2)}, u32[]{:S(2)}) collective-permute-start(bf16[64,1536]{1,0:T(8,128)(2,1)} %get-tuple-element.31), channel_id=1, source_target_pairs={{0,4},{1,5},{2,6},{3,7},{4,12},{5,13},{6,14},{7,15},{8,0},{9,1},{1... | collective-permute-start | bytes 589832 | tf_op jit(solution)/shard_map/ppermute | solution.py:382
  85.1 9.7 %collective-permute-start.26 = (bf16[64,1536]{1,0:T(8,128)(2,1)}, bf16[64,1536]{1,0:T(8,128)(2,1)}, u32[]{:S(2)}, u32[]{:S(2)}) collective-permute-start(bf16[64,1536]{1,0:T(8,128)(2,1)} %get-tuple-element.33), channel_id=1, source_target_pairs={{0,2},{1,3},{2,0},{3,1},{4,6},{5,7},{6,4},{7,5},{8,10},{9,11},{10,... | collective-permute-start | bytes 589832 | tf_op jit(solution)/shard_map/ppermute | solution.py:382
  93.2 0.7 copy-start
  93.2 8.3 %collective-permute-start.25 = (bf16[64,1536]{1,0:T(8,128)(2,1)S(1)}, bf16[64,1536]{1,0:T(8,128)(2,1)}, u32[]{:S(2)}, u32[]{:S(2)}) collective-permute-start(bf16[64,1536]{1,0:T(8,128)(2,1)S(1)} %fusion.22.refs_1_), channel_id=1, source_target_pairs={{0,4},{1,5},{2,6},{3,7},{4,12},{5,13},{6,14},{7,15},{8,0},{9,1},{1... | collective-permute-start | bytes 589832 | tf_op jit(solution)/shard_map/ppermute | solution.py:382
  93.9 10.3 %collective-permute-start.24 = (bf16[128,1536]{1,0:T(8,128)(2,1)}, bf16[128,1536]{1,0:T(8,128)(2,1)}, u32[]{:S(2)}, u32[]{:S(2)}) collective-permute-start(bf16[128,1536]{1,0:T(8,128)(2,1)} %after.15), channel_id=1, source_target_pairs={{0,2},{1,3},{2,0},{3,1},{4,6},{5,7},{6,4},{7,5},{8,10},{9,11},{10,... | collective-permute-start | bytes 1179656 | tf_op jit(solution)/shard_map/ppermute | solution.py:382
  96.8 7.4 %collective-permute-start.28 = (bf16[64,1536]{1,0:T(8,128)(2,1)}, bf16[64,1536]{1,0:T(8,128)(2,1)}, u32[]{:S(2)}, u32[]{:S(2)}) collective-permute-start(bf16[64,1536]{1,0:T(8,128)(2,1)} %fusion.15), channel_id=1, source_target_pairs={{0,4},{1,5},{2,6},{3,7},{4,12},{5,13},{6,14},{7,15},{8,0},{9,1},{1... | collective-permute-start | bytes 589832 | tf_op jit(solution)/shard_map/ppermute | solution.py:382

commit v14 on v12

--- a/solution.py
+++ b/solution.py
@@ -8,6 +8,7 @@
 
 LEVELS = 1024
 VMEM_GRANT = 65200 * 1024
+TILE = 256
 
 
 def gated_unit(values):
@@ -163,7 +164,7 @@
     held, w_gate, w_down, spare_gate, spare_down = refs[:5]
     rows_in, spare_in, hidden, spare_hidden, rows_out, dense, summed, fetched, stored = refs[5:]
     width, inner = w_gate.shape
-    tile = 512
+    tile = TILE
     my_id, failed_id = lax.axis_index("expert"), failed[0]
     holds = holders[0, failed_id] == my_id
     for j in range(1, holders.shape[0]):
@@ -333,8 +334,8 @@
             pltpu.VMEM((count, 2 * capacity, width), jnp.bfloat16),
             pltpu.VMEM((count, tok, width), jnp.bfloat16),
             pltpu.VMEM((2, tok, width), jnp.bfloat16),
-            pltpu.SemaphoreType.DMA((count + inner // 512 + width // 512 + 4,)),
-            pltpu.SemaphoreType.DMA((1 + count * (width // 512),)),
+            pltpu.SemaphoreType.DMA((count + inner // TILE + width // TILE + 4,)),
+            pltpu.SemaphoreType.DMA((1 + count * (width // TILE),)),
         ],
         compiler_params=pltpu.CompilerParams(vmem_limit_bytes=VMEM_GRANT),
         cost_estimate=pl.CostEstimate(

time: 106 us -> 118 us (1.11); the launches traced: 105 us -> 119 us
  Pallas kernels: 32.6 us -> 48.1 us
  waiting for transfers between devices: 29.7 us -> 23.3 us
  starting transfers between devices: 22.1 us -> 26.4 us
    pallas_call x4, Pallas kernels: 32.6 us -> 48.1 us  [run_group(): pl.pallas_call(functools.partial(group_kernel, others=len(earlier), adds=...]
    ppermute x29, waiting for transfers between devices: 29.7 us -> 23.3 us  [by_permutes(): move = lambda a, pairs: lax.ppermute(a, 'expert', pairs)]
    ppermute x29, starting transfers between devices: 22.1 us -> 26.4 us  [by_permutes(): move = lambda a, pairs: lax.ppermute(a, 'expert', pairs)]
  transfers between devices with their start and end apart: 29 -> 29, of which waited for: 14 -> 8; matrix products, arithmetic and copies ran while one was open for 13% -> 11% of each run, Pallas kernels for 31% -> 41%
where the time goes in v14:
time: 118 us; the launch traced here: 119 us
  Pallas kernels  48.1 us (41%)
  starting transfers between devices  26.4 us (22%)
  waiting for transfers between devices  23.3 us (20%)
  other arithmetic  17.4 us (15%)
  local copies, waits for them, and re-layouts  2.46 us (2%)
    pallas_call x4, Pallas kernels, run_group(): pl.pallas_call(functools.partial(group_kernel, others=len(earlier), adds=...  48.1 us
    ppermute x29, starting transfers between devices, by_permutes(): move = lambda a, pairs: lax.ppermute(a, 'expert', pairs)  26.4 us
    ppermute x29, waiting for transfers between devices, by_permutes(): move = lambda a, pairs: lax.ppermute(a, 'expert', pairs)  23.3 us
    convert_element_type x5, other arithmetic, total(): return result.astype(jnp.bfloat16)  9.77 us
    convert_element_type x3, other arithmetic, by_permutes(): add = lambda a, b: (f32(a) + f32(b)).astype(jnp.bfloat16)  5.86 us
    unnamed x15, local copies, waits for them, and re-layouts  2.46 us
  transfers between devices with their start and end apart: 29, of which 8 were waited for; matrix products, arithmetic and copies ran while one was open for 11% of the time, Pallas kernels for 41%

profile of v14, /device:TPU:0, one launch (start us, length us, event | category | flops | bytes accessed | tf_op | source)
XLA Modules:
  0.0 118.6 jit_solution(8152318912595236554)
XLA Ops:
  0.0 0.7 fusion.23
  0.7 1.0 fusion.8.refs_0_
  1.8 3.0 %collective-permute-start = (bf16[136,1536]{1,0:T(8,128)(2,1)S(1)}, bf16[136,1536]{1,0:T(8,128)(2,1)S(1)}, u32[]{:S(2)}, u32[]{:S(2)}) collective-permute-start(bf16[136,1536]{1,0:T(8,128)(2,1)S(1)} %fusion.8.refs_0_), channel_id=1, source_target_pairs={{0,2},{1,3},{2,0},{3,1},{4,6},{5,7},{6,4},{7,5},{8,10},{9,11},{10,... | collective-permute-start | bytes 1253384 | tf_op jit(solution)/shard_map/ppermute | solution.py:384
  4.8 1.6 %collective-permute-start.3 = (bf16[136,1536]{1,0:T(8,128)(2,1)S(1)}, bf16[136,1536]{1,0:T(8,128)(2,1)}, u32[]{:S(2)}, u32[]{:S(2)}) collective-permute-start(bf16[136,1536]{1,0:T(8,128)(2,1)S(1)} %fusion.8.refs_0_), channel_id=1, source_target_pairs={{0,4},{1,5},{2,6},{3,7},{4,12},{5,13},{6,14},{7,15},{8,0},{9,1},{1... | collective-permute-start | bytes 1253384 | tf_op jit(solution)/shard_map/ppermute | solution.py:384
  6.4 0.0 collective-permute-start.1
  6.4 8.1 %collective-permute-done.refs_1_ = bf16[136,1536]{1,0:T(8,128)(2,1)S(1)} collective-permute-done((bf16[136,1536]{1,0:T(8,128)(2,1)S(1)}, bf16[136,1536]{1,0:T(8,128)(2,1)S(1)}, u32[]{:S(2)}, u32[]{:S(2)}) %collective-permute-start) | collective-permute-done | bytes 417824 | tf_op jit(solution)/shard_map/ppermute | solution.py:384
  14.4 0.0 collective-permute-start.2
  14.5 2.5 %collective-permute-done.3.refs_0_ = bf16[136,1536]{1,0:T(8,128)(2,1)} collective-permute-done((bf16[136,1536]{1,0:T(8,128)(2,1)S(1)}, bf16[136,1536]{1,0:T(8,128)(2,1)}, u32[]{:S(2)}, u32[]{:S(2)}) %collective-permute-start.3) | collective-permute-done | bytes 417824 | tf_op jit(solution)/shard_map/ppermute | solution.py:384
  16.9 0.5 collective-permute-start.4
  18.0 0.8 collective-permute-start.5
  18.8 0.0 collective-permute-start.10
  18.8 0.0 collective-permute-done.1.refs_2_
  18.8 0.7 copy-done.5
  19.6 0.8 copy-done.6
  20.4 12.0 %group.4 = (bf16[128,1536]{1,0:T(8,128)(2,1)}, bf16[128,1536]{1,0:T(8,128)(2,1)}, bf16[2,128,1536]{2,1,0:T(8,128)(2,1)}) custom-call(s32[1]{0:T(128)S(6)} %copy.31.failed, s32[4,16]{1,0:T(4,128)} %bitcast.63, bf16[136,1536]{1,0:T(8,128)(2,1)} %copy-done.1, bf16[136,1536]{1,0:T(8,128)(2,1)} %copy-done.4, bf16[136,1536]{1,0:T(8,128)(2,1)} %copy-done.5, ...), custom_call_target="tpu_custom_call" | custom-call | flops 3019898880 | bytes 14942208 | tf_op jit(solution)/shard_map/group/pallas_call | solution.py:317
  32.3 0.0 collective-permute-done.4.refs_0_
  32.3 0.6 collective-permute-start.11
  32.9 0.0 collective-permute-done.5.refs_0_
  32.9 3.5 %collective-permute-start.12 = (bf16[136,1536]{1,0:T(8,128)(2,1)}, bf16[136,1536]{1,0:T(8,128)(2,1)}, u32[]{:S(2)}, u32[]{:S(2)}) collective-permute-start(bf16[136,1536]{1,0:T(8,128)(2,1)} %after.10.refs_2_.refs_0_), channel_id=1, source_target_pairs={{0,4},{1,5},{2,6},{3,7},{4,12},{5,13},{6,14},{7,15},{8,0},{9,1},{1... | collective-permute-start | bytes 1253384 | tf_op jit(solution)/shard_map/ppermute | solution.py:384
  36.4 2.2 %collective-permute-start.7 = (bf16[136,1536]{1,0:T(8,128)(2,1)}, bf16[136,1536]{1,0:T(8,128)(2,1)}, u32[]{:S(2)}, u32[]{:S(2)}) collective-permute-start(bf16[136,1536]{1,0:T(8,128)(2,1)} %after.10.refs_2_.refs_0_), channel_id=1, source_target_pairs={{0,2},{1,3},{2,0},{3,1},{4,6},{5,7},{6,4},{7,5},{8,10},{9,11},{10,... | collective-permute-start | bytes 1253384 | tf_op jit(solution)/shard_map/ppermute | solution.py:384
  38.6 12.1 %group.5 = (bf16[128,1536]{1,0:T(8,128)(2,1)}, bf16[128,1536]{1,0:T(8,128)(2,1)}, bf16[2,128,1536]{2,1,0:T(8,128)(2,1)}) custom-call(s32[1]{0:T(128)S(6)} %copy.31.failed, s32[4,16]{1,0:T(4,128)} %bitcast.64, bf16[136,1536]{1,0:T(8,128)(2,1)} %collective-permute-done.3.refs_0_, bf16[136,1536]{1,0:T(8,128)(2,1)} %after.9.refs_1_, ...), custom_call_target="tpu_custom_call" | custom-call | flops 3019898880 | bytes 14942208 | tf_op jit(solution)/shard_map/group/pallas_call | solution.py:317
  50.7 0.0 collective-permute-done.12.refs_0_
  50.8 0.1 collective-permute-start.20
  50.8 0.5 collective-permute-start.6
  51.3 0.1 collective-permute-start.8
  51.4 0.4 collective-permute-start.9
  51.8 0.5 collective-permute-start.13
  52.3 1.1 collective-permute-done.20
  53.4 2.0 %fusion.1 = bf16[128,1536]{1,0:T(8,128)(2,1)} fusion(bf16[128,1536]{1,0:T(8,128)(2,1)} %get-tuple-element.30, bf16[2,128,1536]{2,1,0:T(8,128)(2,1)} %collective-permute-done.20), kind=kLoop, calls=%fused_computation.3 | loop fusion | flops 786432 | bytes 1179648 | tf_op jit(solution)/shard_map/convert_element_type | solution.py:386
  55.4 1.5 %collective-permute-start.21 = (bf16[128,1536]{1,0:T(8,128)(2,1)}, bf16[128,1536]{1,0:T(8,128)(2,1)}, u32[]{:S(2)}, u32[]{:S(2)}) collective-permute-start(bf16[128,1536]{1,0:T(8,128)(2,1)} %fusion.1), channel_id=1, source_target_pairs={{0,2},{1,3},{2,0},{3,1},{4,6},{5,7},{6,4},{7,5},{8,10},{9,11},{10,... | collective-permute-start | bytes 1179656 | tf_op jit(solution)/shard_map/ppermute | solution.py:384
  56.9 12.1 %group.6 = (bf16[128,1536]{1,0:T(8,128)(2,1)}, bf16[128,1536]{1,0:T(8,128)(2,1)}, bf16[2,128,1536]{2,1,0:T(8,128)(2,1)}, bf16[128,1536]{1,0:T(8,128)(2,1)}) custom-call(s32[1]{0:T(128)S(6)} %copy.31.failed, s32[4,16]{1,0:T(4,128)} %bitcast.65, bf16[136,1536]{1,0:T(8,128)(2,1)} %after.10.refs_2_.refs_0_, bf16[136,1536]{1,0:T(8,128)(2,1)} %collective-permute-done.7.refs_1_, ...), custom_call_target="tpu_custom_call" | custom-call | flops 3019898880 | bytes 14942208 | tf_op jit(solution)/shard_map/group/pallas_call | solution.py:317
  69.0 0.1 collective-permute-start.18
  69.1 0.5 collective-permute-start.14
  69.6 0.1 collective-permute-start.15
  69.6 2.1 %fusion.3 = bf16[128,1536]{1,0:T(8,128)(2,1)} fusion(bf16[128,1536]{1,0:T(8,128)(2,1)} %collective-permute-done.21, bf16[128,1536]{1,0:T(8,128)(2,1)} %get-tuple-element.21.refs_10_.refs_1_, bf16[2,128,1536]{2,1,0:T(8,128)(2,1)} %collective-permute-done.20), kind=kLoop, calls=%fused_computation.6 | loop fusion | flops 1179648 | bytes 1572864 | tf_op jit(solution)/shard_map/convert_element_type | solution.py:408
  71.8 1.6 %collective-permute-start.22 = (bf16[128,1536]{1,0:T(8,128)(2,1)}, bf16[128,1536]{1,0:T(8,128)(2,1)}, u32[]{:S(2)}, u32[]{:S(2)}) collective-permute-start(bf16[128,1536]{1,0:T(8,128)(2,1)} %fusion.3), channel_id=1, source_target_pairs={{0,4},{1,5},{2,6},{3,7},{4,12},{5,13},{6,14},{7,15},{8,0},{9,1},{1... | collective-permute-start | bytes 1179656 | tf_op jit(solution)/shard_map/ppermute | solution.py:384
  73.4 0.0 collective-permute-done.18
  73.4 0.9 copy-done.3
  74.3 1.8 %fusion.4 = bf16[128,1536]{1,0:T(8,128)(2,1)} fusion(bf16[128,1536]{1,0:T(8,128)(2,1)} %get-tuple-element.28, bf16[2,128,1536]{2,1,0:T(8,128)(2,1)S(1)} %collective-permute-done.18), kind=kLoop, calls=%fused_computation.8 | loop fusion | flops 786432 | bytes 1179648 | tf_op jit(solution)/shard_map/convert_element_type | solution.py:386
  76.1 1.4 %collective-permute-start.19 = (bf16[128,1536]{1,0:T(8,128)(2,1)}, bf16[128,1536]{1,0:T(8,128)(2,1)}, u32[]{:S(2)}, u32[]{:S(2)}) collective-permute-start(bf16[128,1536]{1,0:T(8,128)(2,1)} %fusion.4), channel_id=1, source_target_pairs={{0,2},{1,3},{2,0},{3,1},{4,6},{5,7},{6,4},{7,5},{8,10},{9,11},{10,... | collective-permute-start | bytes 1179656 | tf_op jit(solution)/shard_map/ppermute | solution.py:384
  77.5 0.0 collective-permute-done.14.refs_2_
  77.5 0.0 collective-permute-done.15.refs_3_
  77.5 12.0 %group.7 = (bf16[128,1536]{1,0:T(8,128)(2,1)}, bf16[128,1536]{1,0:T(8,128)(2,1)}, bf16[2,128,1536]{2,1,0:T(8,128)(2,1)}) custom-call(s32[1]{0:T(128)S(6)} %copy.31.failed, s32[4,16]{1,0:T(4,128)} %bitcast.66, bf16[136,1536]{1,0:T(8,128)(2,1)} %after.12.refs_0_.refs_2_, bf16[136,1536]{1,0:T(8,128)(2,1)} %collective-permute-done.13.refs_1_, ...), custom_call_target="tpu_custom_call" | custom-call | flops 3019898880 | bytes 14942208 | tf_op jit(solution)/shard_map/group/pallas_call | solution.py:317
  89.5 0.1 collective-permute-start.16
  89.6 0.0 collective-permute-done.22
  89.6 2.3 %fusion.11 = (bf16[64,1536]{1,0:T(8,128)(2,1)}, bf16[64,1536]{1,0:T(8,128)(2,1)S(1)}) fusion(bf16[128,1536]{1,0:T(8,128)(2,1)} %collective-permute-done.22, bf16[128,1536]{1,0:T(8,128)(2,1)} %collective-permute-done.19, bf16[2,128,1536]{2,1,0:T(8,128)(2,1)} %copy-done.3, bf16[128,1536]{1,0:T(8,128)(2,1)} %get-tuple-element.23.refs_8_), kind=kLoop, calls=%fused_computation.21 | loop fusion | flops 1572864 | bytes 1966080 | tf_op jit(solution)/shard_map/convert_element_type | solution.py:408
  91.9 0.5 collective-permute-start.23
  92.4 0.0 collective-permute-done.16
  92.4 2.1 %fusion.12 = (bf16[64,1536]{1,0:T(8,128)(2,1)}, bf16[64,1536]{1,0:T(8,128)(2,1)S(1)}) fusion(bf16[2,128,1536]{2,1,0:T(8,128)(2,1)S(1)} %collective-permute-done.16, bf16[128,1536]{1,0:T(8,128)(2,1)} %get-tuple-element.26), kind=kLoop, calls=%fused_computation.23 | loop fusion | flops 786432 | bytes 1179648 | tf_op jit(solution)/shard_map/convert_element_type | solution.py:386
  94.5 2.5 %collective-permute-start.17 = (bf16[64,1536]{1,0:T(8,128)(2,1)S(1)}, bf16[64,1536]{1,0:T(8,128)(2,1)S(1)}, u32[]{:S(2)}, u32[]{:S(2)}) collective-permute-start(bf16[64,1536]{1,0:T(8,128)(2,1)S(1)} %get-tuple-element.34), channel_id=1, source_target_pairs={{0,2},{1,3},{2,0},{3,1},{4,6},{5,7},{6,4},{7,5},{8,10},{9,11},{10,... | collective-permute-start | bytes 589832 | tf_op jit(solution)/shard_map/ppermute | solution.py:384
  97.0 0.1 collective-permute-start.27
  97.1 0.9 collective-permute-start.26
  98.0 2.1 %collective-permute-done.23 = bf16[64,1536]{1,0:T(8,128)(2,1)S(1)} collective-permute-done((bf16[64,1536]{1,0:T(8,128)(2,1)S(1)}, bf16[64,1536]{1,0:T(8,128)(2,1)S(1)}, u32[]{:S(2)}, u32[]{:S(2)}) %collective-permute-start.23) | collective-permute-done | bytes 196640 | tf_op jit(solution)/shard_map/ppermute | solution.py:384
  100.1 2.6 %collective-permute-done.17 = bf16[64,1536]{1,0:T(8,128)(2,1)S(1)} collective-permute-done((bf16[64,1536]{1,0:T(8,128)(2,1)S(1)}, bf16[64,1536]{1,0:T(8,128)(2,1)S(1)}, u32[]{:S(2)}, u32[]{:S(2)}) %collective-permute-start.17) | collective-permute-done | bytes 196640 | tf_op jit(solution)/shard_map/ppermute | solution.py:384
  102.7 1.0 fusion.22.refs_1_
  103.7 1.1 collective-permute-start.25
  104.8 1.6 %collective-permute-start.24 = (bf16[128,1536]{1,0:T(8,128)(2,1)}, bf16[128,1536]{1,0:T(8,128)(2,1)}, u32[]{:S(2)}, u32[]{:S(2)}) collective-permute-start(bf16[128,1536]{1,0:T(8,128)(2,1)} %after.15), channel_id=1, source_target_pairs={{0,2},{1,3},{2,0},{3,1},{4,6},{5,7},{6,4},{7,5},{8,10},{9,11},{10,... | collective-permute-start | bytes 1179656 | tf_op jit(solution)/shard_map/ppermute | solution.py:384
  106.4 0.1 collective-permute-done.26
  106.6 2.0 %fusion.15 = bf16[64,1536]{1,0:T(8,128)(2,1)} fusion(bf16[64,1536]{1,0:T(8,128)(2,1)} %after.17, bf16[64,1536]{1,0:T(8,128)(2,1)} %collective-permute-done.26, bf16[2,128,1536]{2,1,0:T(8,128)(2,1)} %copy-done.2, bf16[128,1536]{1,0:T(8,128)(2,1)} %get-tuple-element.24), kind=kLoop, calls=%fused_computation.27 | loop fusion | flops 786432 | bytes 983040 | tf_op jit(solution)/shard_map/convert_element_type | solution.py:408
  108.6 0.9 collective-permute-start.28
  109.4 1.5 %collective-permute-done.25.refs_0_ = bf16[64,1536]{1,0:T(8,128)(2,1)} collective-permute-done((bf16[64,1536]{1,0:T(8,128)(2,1)S(1)}, bf16[64,1536]{1,0:T(8,128)(2,1)}, u32[]{:S(2)}, u32[]{:S(2)}) %collective-permute-start.25) | collective-permute-done | bytes 196640 | tf_op jit(solution)/shard_map/ppermute | solution.py:384
  111.0 5.3 %collective-permute-done.28 = bf16[64,1536]{1,0:T(8,128)(2,1)} collective-permute-done((bf16[64,1536]{1,0:T(8,128)(2,1)}, bf16[64,1536]{1,0:T(8,128)(2,1)}, u32[]{:S(2)}, u32[]{:S(2)}) %collective-permute-start.28) | collective-permute-done | bytes 196640 | tf_op jit(solution)/shard_map/ppermute | solution.py:384
  116.3 0.0 collective-permute-done.24
  116.3 2.3 %fusion.7 = bf16[128,1536]{1,0:T(8,128)(2,1)} fusion(bf16[128,1536]{1,0:T(8,128)(2,1)} %collective-permute-done.24, bf16[128,1536]{1,0:T(8,128)(2,1)} %get-tuple-element.18.refs_1_.refs_8_, bf16[2,128,1536]{2,1,0:T(8,128)(2,1)} %collective-permute-done.6.refs_9_, bf16[64,1536]{1,0:T(8,128)(2,1)} %collective-permute-done.28, bf16[64,1536]{1,0:T(8,128)(2,1)} %after.16), kind=kLoop, calls=%fused_computation.12 | loop fusion | flops 2162688 | bytes 1966080 | tf_op jit(solution)/shard_map/convert_element_type | solution.py:408
  (33 shorter events, 0.1 us)
Async XLA Ops:
  1.8 4.6 %copy-start.1 = (bf16[136,1536]{1,0:T(8,128)(2,1)}, bf16[136,1536]{1,0:T(8,128)(2,1)S(1)}, u32[]{:S(2)}) copy-start(bf16[136,1536]{1,0:T(8,128)(2,1)S(1)} %fusion.8.refs_0_) | copy-start | bytes 1253380
  1.8 12.7 %collective-permute-start = (bf16[136,1536]{1,0:T(8,128)(2,1)S(1)}, bf16[136,1536]{1,0:T(8,128)(2,1)S(1)}, u32[]{:S(2)}, u32[]{:S(2)}) collective-permute-start(bf16[136,1536]{1,0:T(8,128)(2,1)S(1)} %fusion.8.refs_0_), channel_id=1, source_target_pairs={{0,2},{1,3},{2,0},{3,1},{4,6},{5,7},{6,4},{7,5},{8,10},{9,11},{10,... | collective-permute-start | bytes 1253384 | tf_op jit(solution)/shard_map/ppermute | solution.py:384
  4.8 12.1 %collective-permute-start.3 = (bf16[136,1536]{1,0:T(8,128)(2,1)S(1)}, bf16[136,1536]{1,0:T(8,128)(2,1)}, u32[]{:S(2)}, u32[]{:S(2)}) collective-permute-start(bf16[136,1536]{1,0:T(8,128)(2,1)S(1)} %fusion.8.refs_0_), channel_id=1, source_target_pairs={{0,4},{1,5},{2,6},{3,7},{4,12},{5,13},{6,14},{7,15},{8,0},{9,1},{1... | collective-permute-start | bytes 1253384 | tf_op jit(solution)/shard_map/ppermute | solution.py:384
  6.4 12.4 %collective-permute-start.1 = (bf16[136,1536]{1,0:T(8,128)(2,1)S(1)}, bf16[136,1536]{1,0:T(8,128)(2,1)S(1)}, u32[]{:S(2)}, u32[]{:S(2)}) collective-permute-start(bf16[136,1536]{1,0:T(8,128)(2,1)S(1)} %fusion.8.refs_0_), channel_id=1, source_target_pairs={{0,1},{1,0},{2,3},{3,2},{4,5},{5,4},{6,7},{7,6},{8,9},{9,8},{10,11... | collective-permute-start | bytes 1253384 | tf_op jit(solution)/shard_map/ppermute | solution.py:384
  14.4 4.4 %copy-start.4 = (bf16[136,1536]{1,0:T(8,128)(2,1)}, bf16[136,1536]{1,0:T(8,128)(2,1)S(1)}, u32[]{:S(2)}) copy-start(bf16[136,1536]{1,0:T(8,128)(2,1)S(1)} %collective-permute-done.refs_1_) | copy-start | bytes 1253380
  14.4 4.4 %collective-permute-start.2 = (bf16[136,1536]{1,0:T(8,128)(2,1)S(1)}, bf16[136,1536]{1,0:T(8,128)(2,1)S(1)}, u32[]{:S(2)}, u32[]{:S(2)}) collective-permute-start(bf16[136,1536]{1,0:T(8,128)(2,1)S(1)} %collective-permute-done.refs_1_), channel_id=1, source_target_pairs={{0,1},{1,0},{2,3},{3,2},{4,5},{5,4},{6,7},{7,6},{8,9},{9,8},{10,11... | collective-permute-start | bytes 1253384 | tf_op jit(solution)/shard_map/ppermute | solution.py:384
  16.9 15.4 %collective-permute-start.4 = (bf16[136,1536]{1,0:T(8,128)(2,1)}, bf16[136,1536]{1,0:T(8,128)(2,1)}, u32[]{:S(2)}, u32[]{:S(2)}) collective-permute-start(bf16[136,1536]{1,0:T(8,128)(2,1)} %collective-permute-done.3.refs_0_), channel_id=1, source_target_pairs={{0,2},{1,3},{2,0},{3,1},{4,6},{5,7},{6,4},{7,5},{8,10},{9,11},{10,... | collective-permute-start | bytes 1253384 | tf_op jit(solution)/shard_map/ppermute | solution.py:384
  18.0 14.9 %collective-permute-start.5 = (bf16[136,1536]{1,0:T(8,128)(2,1)}, bf16[136,1536]{1,0:T(8,128)(2,1)}, u32[]{:S(2)}, u32[]{:S(2)}) collective-permute-start(bf16[136,1536]{1,0:T(8,128)(2,1)} %collective-permute-done.3.refs_0_), channel_id=1, source_target_pairs={{0,4},{1,5},{2,6},{3,7},{4,12},{5,13},{6,14},{7,15},{8,0},{9,1},{1... | collective-permute-start | bytes 1253384 | tf_op jit(solution)/shard_map/ppermute | solution.py:384
  18.8 19.8 %collective-permute-start.10 = (bf16[136,1536]{1,0:T(8,128)(2,1)}, bf16[136,1536]{1,0:T(8,128)(2,1)}, u32[]{:S(2)}, u32[]{:S(2)}) collective-permute-start(bf16[136,1536]{1,0:T(8,128)(2,1)} %collective-permute-done.3.refs_0_), channel_id=1, source_target_pairs={{0,1},{1,0},{2,3},{3,2},{4,5},{5,4},{6,7},{7,6},{8,9},{9,8},{10,11... | collective-permute-start | bytes 1253384 | tf_op jit(solution)/shard_map/ppermute | solution.py:384
  18.8 0.8 copy-start.5
  19.6 0.8 copy-start.6
  32.3 6.2 %collective-permute-start.11 = (bf16[136,1536]{1,0:T(8,128)(2,1)}, bf16[136,1536]{1,0:T(8,128)(2,1)}, u32[]{:S(2)}, u32[]{:S(2)}) collective-permute-start(bf16[136,1536]{1,0:T(8,128)(2,1)} %after.9.refs_1_), channel_id=1, source_target_pairs={{0,1},{1,0},{2,3},{3,2},{4,5},{5,4},{6,7},{7,6},{8,9},{9,8},{10,11... | collective-permute-start | bytes 1253384 | tf_op jit(solution)/shard_map/ppermute | solution.py:384
  32.9 17.8 %collective-permute-start.12 = (bf16[136,1536]{1,0:T(8,128)(2,1)}, bf16[136,1536]{1,0:T(8,128)(2,1)}, u32[]{:S(2)}, u32[]{:S(2)}) collective-permute-start(bf16[136,1536]{1,0:T(8,128)(2,1)} %after.10.refs_2_.refs_0_), channel_id=1, source_target_pairs={{0,4},{1,5},{2,6},{3,7},{4,12},{5,13},{6,14},{7,15},{8,0},{9,1},{1... | collective-permute-start | bytes 1253384 | tf_op jit(solution)/shard_map/ppermute | solution.py:384
  36.4 14.3 %collective-permute-start.7 = (bf16[136,1536]{1,0:T(8,128)(2,1)}, bf16[136,1536]{1,0:T(8,128)(2,1)}, u32[]{:S(2)}, u32[]{:S(2)}) collective-permute-start(bf16[136,1536]{1,0:T(8,128)(2,1)} %after.10.refs_2_.refs_0_), channel_id=1, source_target_pairs={{0,2},{1,3},{2,0},{3,1},{4,6},{5,7},{6,4},{7,5},{8,10},{9,11},{10,... | collective-permute-start | bytes 1253384 | tf_op jit(solution)/shard_map/ppermute | solution.py:384
  50.8 2.7 %collective-permute-start.20 = (bf16[2,128,1536]{2,1,0:T(8,128)(2,1)}, bf16[2,128,1536]{2,1,0:T(8,128)(2,1)}, u32[]{:S(2)}, u32[]{:S(2)}) collective-permute-start(bf16[2,128,1536]{2,1,0:T(8,128)(2,1)} %after.14), channel_id=1, source_target_pairs={{0,1},{1,0},{2,3},{3,2},{4,5},{5,4},{6,7},{7,6},{8,9},{9,8},{10,11... | collective-permute-start | bytes 2359304 | tf_op jit(solution)/shard_map/ppermute | solution.py:384
  50.8 6.0 %collective-permute-start.6 = (bf16[2,128,1536]{2,1,0:T(8,128)(2,1)}, bf16[2,128,1536]{2,1,0:T(8,128)(2,1)}, u32[]{:S(2)}, u32[]{:S(2)}) collective-permute-start(bf16[2,128,1536]{2,1,0:T(8,128)(2,1)} %after.11), channel_id=1, source_target_pairs={{0,1},{1,0},{2,3},{3,2},{4,5},{5,4},{6,7},{7,6},{8,9},{9,8},{10,11... | collective-permute-start | bytes 2359304 | tf_op jit(solution)/shard_map/ppermute | solution.py:384
  51.3 5.6 %collective-permute-start.8 = (bf16[136,1536]{1,0:T(8,128)(2,1)}, bf16[136,1536]{1,0:T(8,128)(2,1)}, u32[]{:S(2)}, u32[]{:S(2)}) collective-permute-start(bf16[136,1536]{1,0:T(8,128)(2,1)} %after.10.refs_2_.refs_0_), channel_id=1, source_target_pairs={{0,1},{1,0},{2,3},{3,2},{4,5},{5,4},{6,7},{7,6},{8,9},{9,8},{10,11... | collective-permute-start | bytes 1253384 | tf_op jit(solution)/shard_map/ppermute | solution.py:384
  51.4 5.5 %collective-permute-start.9 = (bf16[136,1536]{1,0:T(8,128)(2,1)}, bf16[136,1536]{1,0:T(8,128)(2,1)}, u32[]{:S(2)}, u32[]{:S(2)}) collective-permute-start(bf16[136,1536]{1,0:T(8,128)(2,1)} %collective-permute-done.7.refs_1_), channel_id=1, source_target_pairs={{0,1},{1,0},{2,3},{3,2},{4,5},{5,4},{6,7},{7,6},{8,9},{9,8},{10,11... | collective-permute-start | bytes 1253384 | tf_op jit(solution)/shard_map/ppermute | solution.py:384
  51.8 17.1 %collective-permute-start.13 = (bf16[136,1536]{1,0:T(8,128)(2,1)}, bf16[136,1536]{1,0:T(8,128)(2,1)}, u32[]{:S(2)}, u32[]{:S(2)}) collective-permute-start(bf16[136,1536]{1,0:T(8,128)(2,1)} %collective-permute-done.7.refs_1_), channel_id=1, source_target_pairs={{0,4},{1,5},{2,6},{3,7},{4,12},{5,13},{6,14},{7,15},{8,0},{9,1},{1... | collective-permute-start | bytes 1253384 | tf_op jit(solution)/shard_map/ppermute | solution.py:384
  55.4 14.2 %collective-permute-start.21 = (bf16[128,1536]{1,0:T(8,128)(2,1)}, bf16[128,1536]{1,0:T(8,128)(2,1)}, u32[]{:S(2)}, u32[]{:S(2)}) collective-permute-start(bf16[128,1536]{1,0:T(8,128)(2,1)} %fusion.1), channel_id=1, source_target_pairs={{0,2},{1,3},{2,0},{3,1},{4,6},{5,7},{6,4},{7,5},{8,10},{9,11},{10,... | collective-permute-start | bytes 1179656 | tf_op jit(solution)/shard_map/ppermute | solution.py:384
  69.0 4.4 %collective-permute-start.18 = (bf16[2,128,1536]{2,1,0:T(8,128)(2,1)}, bf16[2,128,1536]{2,1,0:T(8,128)(2,1)S(1)}, u32[]{:S(2)}, u32[]{:S(2)}) collective-permute-start(bf16[2,128,1536]{2,1,0:T(8,128)(2,1)} %after.13), channel_id=1, source_target_pairs={{0,1},{1,0},{2,3},{3,2},{4,5},{5,4},{6,7},{7,6},{8,9},{9,8},{10,11... | collective-permute-start | bytes 2359304 | tf_op jit(solution)/shard_map/ppermute | solution.py:384
  69.1 8.5 %collective-permute-start.14 = (bf16[136,1536]{1,0:T(8,128)(2,1)}, bf16[136,1536]{1,0:T(8,128)(2,1)}, u32[]{:S(2)}, u32[]{:S(2)}) collective-permute-start(bf16[136,1536]{1,0:T(8,128)(2,1)} %after.12.refs_0_.refs_2_), channel_id=1, source_target_pairs={{0,1},{1,0},{2,3},{3,2},{4,5},{5,4},{6,7},{7,6},{8,9},{9,8},{10,11... | collective-permute-start | bytes 1253384 | tf_op jit(solution)/shard_map/ppermute | solution.py:384
  69.6 8.0 %collective-permute-start.15 = (bf16[136,1536]{1,0:T(8,128)(2,1)}, bf16[136,1536]{1,0:T(8,128)(2,1)}, u32[]{:S(2)}, u32[]{:S(2)}) collective-permute-start(bf16[136,1536]{1,0:T(8,128)(2,1)} %collective-permute-done.13.refs_1_), channel_id=1, source_target_pairs={{0,1},{1,0},{2,3},{3,2},{4,5},{5,4},{6,7},{7,6},{8,9},{9,8},{10,11... | collective-permute-start | bytes 1253384 | tf_op jit(solution)/shard_map/ppermute | solution.py:384
  71.8 17.8 %collective-permute-start.22 = (bf16[128,1536]{1,0:T(8,128)(2,1)}, bf16[128,1536]{1,0:T(8,128)(2,1)}, u32[]{:S(2)}, u32[]{:S(2)}) collective-permute-start(bf16[128,1536]{1,0:T(8,128)(2,1)} %fusion.3), channel_id=1, source_target_pairs={{0,4},{1,5},{2,6},{3,7},{4,12},{5,13},{6,14},{7,15},{8,0},{9,1},{1... | collective-permute-start | bytes 1179656 | tf_op jit(solution)/shard_map/ppermute | solution.py:384
  73.4 0.9 copy-start.3
  76.1 13.5 %collective-permute-start.19 = (bf16[128,1536]{1,0:T(8,128)(2,1)}, bf16[128,1536]{1,0:T(8,128)(2,1)}, u32[]{:S(2)}, u32[]{:S(2)}) collective-permute-start(bf16[128,1536]{1,0:T(8,128)(2,1)} %fusion.4), channel_id=1, source_target_pairs={{0,2},{1,3},{2,0},{3,1},{4,6},{5,7},{6,4},{7,5},{8,10},{9,11},{10,... | collective-permute-start | bytes 1179656 | tf_op jit(solution)/shard_map/ppermute | solution.py:384
  89.5 2.9 %collective-permute-start.16 = (bf16[2,128,1536]{2,1,0:T(8,128)(2,1)}, bf16[2,128,1536]{2,1,0:T(8,128)(2,1)S(1)}, u32[]{:S(2)}, u32[]{:S(2)}) collective-permute-start(bf16[2,128,1536]{2,1,0:T(8,128)(2,1)} %get-tuple-element.25), channel_id=1, source_target_pairs={{0,1},{1,0},{2,3},{3,2},{4,5},{5,4},{6,7},{7,6},{8,9},{9,8},{10,11... | collective-permute-start | bytes 2359304 | tf_op jit(solution)/shard_map/ppermute | solution.py:384
  91.9 8.2 %collective-permute-start.23 = (bf16[64,1536]{1,0:T(8,128)(2,1)S(1)}, bf16[64,1536]{1,0:T(8,128)(2,1)S(1)}, u32[]{:S(2)}, u32[]{:S(2)}) collective-permute-start(bf16[64,1536]{1,0:T(8,128)(2,1)S(1)} %get-tuple-element.32), channel_id=1, source_target_pairs={{0,4},{1,5},{2,6},{3,7},{4,12},{5,13},{6,14},{7,15},{8,0},{9,1},{1... | collective-permute-start | bytes 589832 | tf_op jit(solution)/shard_map/ppermute | solution.py:384
  92.4 10.3 %copy-start.2 = (bf16[2,128,1536]{2,1,0:T(8,128)(2,1)}, bf16[2,128,1536]{2,1,0:T(8,128)(2,1)S(1)}, u32[]{:S(2)}) copy-start(bf16[2,128,1536]{2,1,0:T(8,128)(2,1)S(1)} %collective-permute-done.16) | copy-start | bytes 2359300
  94.5 8.2 %collective-permute-start.17 = (bf16[64,1536]{1,0:T(8,128)(2,1)S(1)}, bf16[64,1536]{1,0:T(8,128)(2,1)S(1)}, u32[]{:S(2)}, u32[]{:S(2)}) collective-permute-start(bf16[64,1536]{1,0:T(8,128)(2,1)S(1)} %get-tuple-element.34), channel_id=1, source_target_pairs={{0,2},{1,3},{2,0},{3,1},{4,6},{5,7},{6,4},{7,5},{8,10},{9,11},{10,... | collective-permute-start | bytes 589832 | tf_op jit(solution)/shard_map/ppermute | solution.py:384
  97.0 9.5 %collective-permute-start.27 = (bf16[64,1536]{1,0:T(8,128)(2,1)}, bf16[64,1536]{1,0:T(8,128)(2,1)}, u32[]{:S(2)}, u32[]{:S(2)}) collective-permute-start(bf16[64,1536]{1,0:T(8,128)(2,1)} %get-tuple-element.31), channel_id=1, source_target_pairs={{0,4},{1,5},{2,6},{3,7},{4,12},{5,13},{6,14},{7,15},{8,0},{9,1},{1... | collective-permute-start | bytes 589832 | tf_op jit(solution)/shard_map/ppermute | solution.py:384
  97.1 9.4 %collective-permute-start.26 = (bf16[64,1536]{1,0:T(8,128)(2,1)}, bf16[64,1536]{1,0:T(8,128)(2,1)}, u32[]{:S(2)}, u32[]{:S(2)}) collective-permute-start(bf16[64,1536]{1,0:T(8,128)(2,1)} %get-tuple-element.33), channel_id=1, source_target_pairs={{0,2},{1,3},{2,0},{3,1},{4,6},{5,7},{6,4},{7,5},{8,10},{9,11},{10,... | collective-permute-start | bytes 589832 | tf_op jit(solution)/shard_map/ppermute | solution.py:384
  103.7 1.1 copy-start
  103.7 7.2 %collective-permute-start.25 = (bf16[64,1536]{1,0:T(8,128)(2,1)S(1)}, bf16[64,1536]{1,0:T(8,128)(2,1)}, u32[]{:S(2)}, u32[]{:S(2)}) collective-permute-start(bf16[64,1536]{1,0:T(8,128)(2,1)S(1)} %fusion.22.refs_1_), channel_id=1, source_target_pairs={{0,4},{1,5},{2,6},{3,7},{4,12},{5,13},{6,14},{7,15},{8,0},{9,1},{1... | collective-permute-start | bytes 589832 | tf_op jit(solution)/shard_map/ppermute | solution.py:384
  104.8 11.5 %collective-permute-start.24 = (bf16[128,1536]{1,0:T(8,128)(2,1)}, bf16[128,1536]{1,0:T(8,128)(2,1)}, u32[]{:S(2)}, u32[]{:S(2)}) collective-permute-start(bf16[128,1536]{1,0:T(8,128)(2,1)} %after.15), channel_id=1, source_target_pairs={{0,2},{1,3},{2,0},{3,1},{4,6},{5,7},{6,4},{7,5},{8,10},{9,11},{10,... | collective-permute-start | bytes 1179656 | tf_op jit(solution)/shard_map/ppermute | solution.py:384
  108.6 7.7 %collective-permute-start.28 = (bf16[64,1536]{1,0:T(8,128)(2,1)}, bf16[64,1536]{1,0:T(8,128)(2,1)}, u32[]{:S(2)}, u32[]{:S(2)}) collective-permute-start(bf16[64,1536]{1,0:T(8,128)(2,1)} %fusion.15), channel_id=1, source_target_pairs={{0,4},{1,5},{2,6},{3,7},{4,12},{5,13},{6,14},{7,15},{8,0},{9,1},{1... | collective-permute-start | bytes 589832 | tf_op jit(solution)/shard_map/ppermute | solution.py:384

commit v15 on v12

--- a/solution.py
+++ b/solution.py
@@ -180,7 +180,7 @@
     gate_hbm, down_hbm, spare_gate_hbm, spare_down_hbm = weights_hbm
     block_copies = [fetch(block, held.at[s]) for s, block in enumerate(blocks)]
     gate_copies = [
-        fetch(gate_hbm.at[0, :, n : n + tile], w_gate.at[:, n : n + tile]) for n in range(0, inner, tile)
+        fetch(gate_hbm.at[0, n : n + tile], w_gate.at[n : n + tile]) for n in range(0, width, tile)
     ]
     share_copies = []
     if adds:
@@ -196,7 +196,7 @@
             copy.start()
 
     down_copies = [
-        fetch(down_hbm.at[0, :, n : n + tile], w_down.at[:, n : n + tile]) for n in range(0, width, tile)
+        fetch(down_hbm.at[0, n : n + tile], w_down.at[n : n + tile]) for n in range(0, inner, tile)
     ]
 
     count = len(blocks)
@@ -250,8 +250,9 @@
             rows_in[s * capacity : (s + 1) * capacity, n : n + tile] = got[:capacity]
             spare_in[s * capacity : (s + 1) * capacity, n : n + tile] = got[capacity:]
 
-    for i, n in enumerate(range(0, inner, tile)):
-        gate_copies[i].wait()
+    for copy in gate_copies:
+        copy.wait()
+    for n in range(0, inner, tile):
         hidden[:, n : n + tile] = gated_unit(
             jnp.dot(rows_in[...], w_gate[:, n : n + tile], preferred_element_type=jnp.float32)
         ).astype(jnp.bfloat16)
@@ -284,8 +285,9 @@
     def _():
         rows_out[:, capacity:, :] = jnp.zeros((count, capacity, width), jnp.bfloat16)
 
-    for i, n in enumerate(range(0, width, tile)):
-        down_copies[i].wait()
+    for copy in down_copies:
+        copy.wait()
+    for n in range(0, width, tile):
         result = jnp.dot(hidden[...], w_down[:, n : n + tile], preferred_element_type=jnp.float32)
         result = result.astype(jnp.bfloat16).astype(jnp.float32)
         for s in range(count):

time: 106 us -> 106 us (level)
  waiting for transfers between devices: 29.7 us -> 27.7 us
  starting transfers between devices: 22.1 us -> 23.6 us
    ppermute x29, waiting for transfers between devices: 29.7 us -> 27.7 us  [by_permutes(): move = lambda a, pairs: lax.ppermute(a, 'expert', pairs)]
    ppermute x29, starting transfers between devices: 22.1 us -> 23.6 us  [by_permutes(): move = lambda a, pairs: lax.ppermute(a, 'expert', pairs)]
  transfers between devices with their start and end apart: 29 -> 29, of which waited for: 14 -> 13; matrix products, arithmetic and copies ran while one was open for 13% -> 13% of each run, Pallas kernels for 31% -> 31%
where the time goes in v15:
time: 106 us; the launch traced here: 105 us
  Pallas kernels  32.5 us (31%)
  waiting for transfers between devices  27.7 us (26%)
  starting transfers between devices  23.6 us (22%)
  other arithmetic  17.4 us (16%)
  local copies, waits for them, and re-layouts  2.46 us (2%)
    pallas_call x4, Pallas kernels, run_group(): pl.pallas_call(functools.partial(group_kernel, others=len(earlier), adds=...  32.5 us
    ppermute x29, waiting for transfers between devices, by_permutes(): move = lambda a, pairs: lax.ppermute(a, 'expert', pairs)  27.7 us
    ppermute x29, starting transfers between devices, by_permutes(): move = lambda a, pairs: lax.ppermute(a, 'expert', pairs)  23.6 us
    convert_element_type x5, other arithmetic, total(): return result.astype(jnp.bfloat16)  9.77 us
    convert_element_type x3, other arithmetic, by_permutes(): add = lambda a, b: (f32(a) + f32(b)).astype(jnp.bfloat16)  5.86 us
    unnamed x15, local copies, waits for them, and re-layouts  2.46 us
  transfers between devices with their start and end apart: 29, of which 13 were waited for; matrix products, arithmetic and copies ran while one was open for 13% of the time, Pallas kernels for 31%

profile of v15, /device:TPU:0, one launch (start us, length us, event | category | flops | bytes accessed | tf_op | source)
XLA Modules:
  0.0 104.5 jit_solution(171077987432639347)
XLA Ops:
  0.0 0.7 fusion.23
  0.7 1.0 fusion.8.refs_0_
  1.8 3.0 %collective-permute-start = (bf16[136,1536]{1,0:T(8,128)(2,1)S(1)}, bf16[136,1536]{1,0:T(8,128)(2,1)S(1)}, u32[]{:S(2)}, u32[]{:S(2)}) collective-permute-start(bf16[136,1536]{1,0:T(8,128)(2,1)S(1)} %fusion.8.refs_0_), channel_id=1, source_target_pairs={{0,2},{1,3},{2,0},{3,1},{4,6},{5,7},{6,4},{7,5},{8,10},{9,11},{10,... | collective-permute-start | bytes 1253384 | tf_op jit(solution)/shard_map/ppermute | solution.py:385
  4.8 1.6 %collective-permute-start.3 = (bf16[136,1536]{1,0:T(8,128)(2,1)S(1)}, bf16[136,1536]{1,0:T(8,128)(2,1)}, u32[]{:S(2)}, u32[]{:S(2)}) collective-permute-start(bf16[136,1536]{1,0:T(8,128)(2,1)S(1)} %fusion.8.refs_0_), channel_id=1, source_target_pairs={{0,4},{1,5},{2,6},{3,7},{4,12},{5,13},{6,14},{7,15},{8,0},{9,1},{1... | collective-permute-start | bytes 1253384 | tf_op jit(solution)/shard_map/ppermute | solution.py:385
  6.4 0.0 collective-permute-start.1
  6.4 8.1 %collective-permute-done.refs_1_ = bf16[136,1536]{1,0:T(8,128)(2,1)S(1)} collective-permute-done((bf16[136,1536]{1,0:T(8,128)(2,1)S(1)}, bf16[136,1536]{1,0:T(8,128)(2,1)S(1)}, u32[]{:S(2)}, u32[]{:S(2)}) %collective-permute-start) | collective-permute-done | bytes 417824 | tf_op jit(solution)/shard_map/ppermute | solution.py:385
  14.4 0.0 collective-permute-start.2
  14.5 2.5 %collective-permute-done.3.refs_0_ = bf16[136,1536]{1,0:T(8,128)(2,1)} collective-permute-done((bf16[136,1536]{1,0:T(8,128)(2,1)S(1)}, bf16[136,1536]{1,0:T(8,128)(2,1)}, u32[]{:S(2)}, u32[]{:S(2)}) %collective-permute-start.3) | collective-permute-done | bytes 417824 | tf_op jit(solution)/shard_map/ppermute | solution.py:385
  16.9 0.5 collective-permute-start.4
  18.0 0.8 collective-permute-start.5
  18.8 0.0 collective-permute-done.1.refs_2_
  18.8 0.0 collective-permute-done.2.refs_3_
  18.8 0.7 copy-done.5
  19.6 0.8 copy-done.6
  20.4 8.1 %group.4 = (bf16[128,1536]{1,0:T(8,128)(2,1)}, bf16[128,1536]{1,0:T(8,128)(2,1)}, bf16[2,128,1536]{2,1,0:T(8,128)(2,1)}) custom-call(s32[1]{0:T(128)S(6)} %copy.31.failed, s32[4,16]{1,0:T(4,128)} %bitcast.63, bf16[136,1536]{1,0:T(8,128)(2,1)} %copy-done.1, bf16[136,1536]{1,0:T(8,128)(2,1)} %copy-done.4, bf16[136,1536]{1,0:T(8,128)(2,1)} %copy-done.5, ...), custom_call_target="tpu_custom_call" | custom-call | flops 3019898880 | bytes 14942208 | tf_op jit(solution)/shard_map/group/pallas_call | solution.py:318
  28.4 0.0 collective-permute-done.4.refs_0_
  28.4 0.6 collective-permute-start.11
  29.0 0.9 collective-permute-done.5.refs_0_
  29.9 3.7 %collective-permute-start.12 = (bf16[136,1536]{1,0:T(8,128)(2,1)}, bf16[136,1536]{1,0:T(8,128)(2,1)}, u32[]{:S(2)}, u32[]{:S(2)}) collective-permute-start(bf16[136,1536]{1,0:T(8,128)(2,1)} %after.10.refs_2_.refs_0_), channel_id=1, source_target_pairs={{0,4},{1,5},{2,6},{3,7},{4,12},{5,13},{6,14},{7,15},{8,0},{9,1},{1... | collective-permute-start | bytes 1253384 | tf_op jit(solution)/shard_map/ppermute | solution.py:385
  33.6 0.5 collective-permute-start.7
  34.0 0.0 collective-permute-done.10.refs_2_
  34.0 0.0 collective-permute-done.11.refs_3_
  34.0 8.1 %group.5 = (bf16[128,1536]{1,0:T(8,128)(2,1)}, bf16[128,1536]{1,0:T(8,128)(2,1)}, bf16[2,128,1536]{2,1,0:T(8,128)(2,1)}) custom-call(s32[1]{0:T(128)S(6)} %copy.31.failed, s32[4,16]{1,0:T(4,128)} %bitcast.64, bf16[136,1536]{1,0:T(8,128)(2,1)} %collective-permute-done.3.refs_0_, bf16[136,1536]{1,0:T(8,128)(2,1)} %after.9.refs_1_, ...), custom_call_target="tpu_custom_call" | custom-call | flops 3019898880 | bytes 14942208 | tf_op jit(solution)/shard_map/group/pallas_call | solution.py:318
  42.2 0.9 collective-permute-done.12.refs_0_
  43.0 2.2 %collective-permute-done.7.refs_1_ = bf16[136,1536]{1,0:T(8,128)(2,1)} collective-permute-done((bf16[136,1536]{1,0:T(8,128)(2,1)}, bf16[136,1536]{1,0:T(8,128)(2,1)}, u32[]{:S(2)}, u32[]{:S(2)}) %collective-permute-start.7) | collective-permute-done | bytes 417824 | tf_op jit(solution)/shard_map/ppermute | solution.py:385
  45.2 0.0 collective-permute-start.20
  45.2 0.5 collective-permute-start.6
  45.7 0.0 collective-permute-start.8
  45.7 0.5 collective-permute-start.9
  46.3 0.4 collective-permute-start.13
  46.6 1.2 %collective-permute-done.20 = bf16[2,128,1536]{2,1,0:T(8,128)(2,1)} collective-permute-done((bf16[2,128,1536]{2,1,0:T(8,128)(2,1)}, bf16[2,128,1536]{2,1,0:T(8,128)(2,1)}, u32[]{:S(2)}, u32[]{:S(2)}) %collective-permute-start.20) | collective-permute-done | bytes 786464 | tf_op jit(solution)/shard_map/ppermute | solution.py:385
  47.9 2.0 %fusion.1 = bf16[128,1536]{1,0:T(8,128)(2,1)} fusion(bf16[128,1536]{1,0:T(8,128)(2,1)} %get-tuple-element.30, bf16[2,128,1536]{2,1,0:T(8,128)(2,1)} %collective-permute-done.20), kind=kLoop, calls=%fused_computation.3 | loop fusion | flops 786432 | bytes 1179648 | tf_op jit(solution)/shard_map/convert_element_type | solution.py:387
  49.8 0.5 collective-permute-start.21
  50.3 0.0 collective-permute-done.8.refs_2_
  50.3 0.0 collective-permute-done.6.refs_9_
  50.3 0.0 collective-permute-done.9.refs_3_
  50.3 8.2 %group.6 = (bf16[128,1536]{1,0:T(8,128)(2,1)}, bf16[128,1536]{1,0:T(8,128)(2,1)}, bf16[2,128,1536]{2,1,0:T(8,128)(2,1)}, bf16[128,1536]{1,0:T(8,128)(2,1)}) custom-call(s32[1]{0:T(128)S(6)} %copy.31.failed, s32[4,16]{1,0:T(4,128)} %bitcast.65, bf16[136,1536]{1,0:T(8,128)(2,1)} %after.10.refs_2_.refs_0_, bf16[136,1536]{1,0:T(8,128)(2,1)} %collective-permute-done.7.refs_1_, ...), custom_call_target="tpu_custom_call" | custom-call | flops 3019898880 | bytes 14942208 | tf_op jit(solution)/shard_map/group/pallas_call | solution.py:318
  58.5 0.5 collective-permute-done.13.refs_1_
  59.0 0.5 collective-permute-start.14
  59.5 0.0 collective-permute-start.15
  59.5 1.8 %collective-permute-done.21 = bf16[128,1536]{1,0:T(8,128)(2,1)} collective-permute-done((bf16[128,1536]{1,0:T(8,128)(2,1)}, bf16[128,1536]{1,0:T(8,128)(2,1)}, u32[]{:S(2)}, u32[]{:S(2)}) %collective-permute-start.21) | collective-permute-done | bytes 393248 | tf_op jit(solution)/shard_map/ppermute | solution.py:385
  61.3 2.1 %fusion.3 = bf16[128,1536]{1,0:T(8,128)(2,1)} fusion(bf16[128,1536]{1,0:T(8,128)(2,1)} %collective-permute-done.21, bf16[128,1536]{1,0:T(8,128)(2,1)} %get-tuple-element.21.refs_10_.refs_1_, bf16[2,128,1536]{2,1,0:T(8,128)(2,1)} %collective-permute-done.20), kind=kLoop, calls=%fused_computation.6 | loop fusion | flops 1179648 | bytes 1572864 | tf_op jit(solution)/shard_map/convert_element_type | solution.py:409
  63.4 0.4 collective-permute-start.22
  63.8 0.9 copy-done.3
  64.7 1.8 %fusion.4 = bf16[128,1536]{1,0:T(8,128)(2,1)} fusion(bf16[128,1536]{1,0:T(8,128)(2,1)} %get-tuple-element.28, bf16[2,128,1536]{2,1,0:T(8,128)(2,1)S(1)} %collective-permute-done.18), kind=kLoop, calls=%fused_computation.8 | loop fusion | flops 786432 | bytes 1179648 | tf_op jit(solution)/shard_map/convert_element_type | solution.py:387
  66.5 0.5 collective-permute-start.19
  67.0 8.1 %group.7 = (bf16[128,1536]{1,0:T(8,128)(2,1)}, bf16[128,1536]{1,0:T(8,128)(2,1)}, bf16[2,128,1536]{2,1,0:T(8,128)(2,1)}) custom-call(s32[1]{0:T(128)S(6)} %copy.31.failed, s32[4,16]{1,0:T(4,128)} %bitcast.66, bf16[136,1536]{1,0:T(8,128)(2,1)} %after.12.refs_0_.refs_2_, bf16[136,1536]{1,0:T(8,128)(2,1)} %collective-permute-done.13.refs_1_, ...), custom_call_target="tpu_custom_call" | custom-call | flops 3019898880 | bytes 14942208 | tf_op jit(solution)/shard_map/group/pallas_call | solution.py:318
  75.1 0.1 collective-permute-start.16
  75.2 1.7 %collective-permute-done.19 = bf16[128,1536]{1,0:T(8,128)(2,1)} collective-permute-done((bf16[128,1536]{1,0:T(8,128)(2,1)}, bf16[128,1536]{1,0:T(8,128)(2,1)}, u32[]{:S(2)}, u32[]{:S(2)}) %collective-permute-start.19) | collective-permute-done | bytes 393248 | tf_op jit(solution)/shard_map/ppermute | solution.py:385
  76.9 2.3 %fusion.11 = (bf16[64,1536]{1,0:T(8,128)(2,1)}, bf16[64,1536]{1,0:T(8,128)(2,1)S(1)}) fusion(bf16[128,1536]{1,0:T(8,128)(2,1)} %collective-permute-done.22, bf16[128,1536]{1,0:T(8,128)(2,1)} %collective-permute-done.19, bf16[2,128,1536]{2,1,0:T(8,128)(2,1)} %copy-done.3, bf16[128,1536]{1,0:T(8,128)(2,1)} %get-tuple-element.23.refs_8_), kind=kLoop, calls=%fused_computation.21 | loop fusion | flops 1572864 | bytes 1966080 | tf_op jit(solution)/shard_map/convert_element_type | solution.py:409
  79.2 1.2 %collective-permute-start.23 = (bf16[64,1536]{1,0:T(8,128)(2,1)S(1)}, bf16[64,1536]{1,0:T(8,128)(2,1)S(1)}, u32[]{:S(2)}, u32[]{:S(2)}) collective-permute-start(bf16[64,1536]{1,0:T(8,128)(2,1)S(1)} %get-tuple-element.32), channel_id=1, source_target_pairs={{0,4},{1,5},{2,6},{3,7},{4,12},{5,13},{6,14},{7,15},{8,0},{9,1},{1... | collective-permute-start | bytes 589832 | tf_op jit(solution)/shard_map/ppermute | solution.py:385
  80.4 2.1 %fusion.12 = (bf16[64,1536]{1,0:T(8,128)(2,1)}, bf16[64,1536]{1,0:T(8,128)(2,1)S(1)}) fusion(bf16[2,128,1536]{2,1,0:T(8,128)(2,1)S(1)} %collective-permute-done.16, bf16[128,1536]{1,0:T(8,128)(2,1)} %get-tuple-element.26), kind=kLoop, calls=%fused_computation.23 | loop fusion | flops 786432 | bytes 1179648 | tf_op jit(solution)/shard_map/convert_element_type | solution.py:387
  82.5 0.5 collective-permute-start.17
  83.0 1.9 %collective-permute-start.27 = (bf16[64,1536]{1,0:T(8,128)(2,1)}, bf16[64,1536]{1,0:T(8,128)(2,1)}, u32[]{:S(2)}, u32[]{:S(2)}) collective-permute-start(bf16[64,1536]{1,0:T(8,128)(2,1)} %get-tuple-element.31), channel_id=1, source_target_pairs={{0,4},{1,5},{2,6},{3,7},{4,12},{5,13},{6,14},{7,15},{8,0},{9,1},{1... | collective-permute-start | bytes 589832 | tf_op jit(solution)/shard_map/ppermute | solution.py:385
  84.9 1.5 %collective-permute-start.26 = (bf16[64,1536]{1,0:T(8,128)(2,1)}, bf16[64,1536]{1,0:T(8,128)(2,1)}, u32[]{:S(2)}, u32[]{:S(2)}) collective-permute-start(bf16[64,1536]{1,0:T(8,128)(2,1)} %get-tuple-element.33), channel_id=1, source_target_pairs={{0,2},{1,3},{2,0},{3,1},{4,6},{5,7},{6,4},{7,5},{8,10},{9,11},{10,... | collective-permute-start | bytes 589832 | tf_op jit(solution)/shard_map/ppermute | solution.py:385
  86.4 1.0 collective-permute-done.23
  87.4 2.7 %collective-permute-done.17 = bf16[64,1536]{1,0:T(8,128)(2,1)S(1)} collective-permute-done((bf16[64,1536]{1,0:T(8,128)(2,1)S(1)}, bf16[64,1536]{1,0:T(8,128)(2,1)S(1)}, u32[]{:S(2)}, u32[]{:S(2)}) %collective-permute-start.17) | collective-permute-done | bytes 196640 | tf_op jit(solution)/shard_map/ppermute | solution.py:385
  90.1 1.0 fusion.22.refs_1_
  91.1 2.2 %collective-permute-start.25 = (bf16[64,1536]{1,0:T(8,128)(2,1)S(1)}, bf16[64,1536]{1,0:T(8,128)(2,1)}, u32[]{:S(2)}, u32[]{:S(2)}) collective-permute-start(bf16[64,1536]{1,0:T(8,128)(2,1)S(1)} %fusion.22.refs_1_), channel_id=1, source_target_pairs={{0,4},{1,5},{2,6},{3,7},{4,12},{5,13},{6,14},{7,15},{8,0},{9,1},{1... | collective-permute-start | bytes 589832 | tf_op jit(solution)/shard_map/ppermute | solution.py:385
  93.3 2.0 %fusion.15 = bf16[64,1536]{1,0:T(8,128)(2,1)} fusion(bf16[64,1536]{1,0:T(8,128)(2,1)} %after.17, bf16[64,1536]{1,0:T(8,128)(2,1)} %collective-permute-done.26, bf16[2,128,1536]{2,1,0:T(8,128)(2,1)} %copy-done.2, bf16[128,1536]{1,0:T(8,128)(2,1)} %get-tuple-element.24), kind=kLoop, calls=%fused_computation.27 | loop fusion | flops 786432 | bytes 983040 | tf_op jit(solution)/shard_map/convert_element_type | solution.py:409
  95.3 2.6 %collective-permute-start.28 = (bf16[64,1536]{1,0:T(8,128)(2,1)}, bf16[64,1536]{1,0:T(8,128)(2,1)}, u32[]{:S(2)}, u32[]{:S(2)}) collective-permute-start(bf16[64,1536]{1,0:T(8,128)(2,1)} %fusion.15), channel_id=1, source_target_pairs={{0,4},{1,5},{2,6},{3,7},{4,12},{5,13},{6,14},{7,15},{8,0},{9,1},{1... | collective-permute-start | bytes 589832 | tf_op jit(solution)/shard_map/ppermute | solution.py:385
  97.9 1.2 %collective-permute-done.25.refs_0_ = bf16[64,1536]{1,0:T(8,128)(2,1)} collective-permute-done((bf16[64,1536]{1,0:T(8,128)(2,1)S(1)}, bf16[64,1536]{1,0:T(8,128)(2,1)}, u32[]{:S(2)}, u32[]{:S(2)}) %collective-permute-start.25) | collective-permute-done | bytes 196640 | tf_op jit(solution)/shard_map/ppermute | solution.py:385
  99.1 3.1 %collective-permute-done.28 = bf16[64,1536]{1,0:T(8,128)(2,1)} collective-permute-done((bf16[64,1536]{1,0:T(8,128)(2,1)}, bf16[64,1536]{1,0:T(8,128)(2,1)}, u32[]{:S(2)}, u32[]{:S(2)}) %collective-permute-start.28) | collective-permute-done | bytes 196640 | tf_op jit(solution)/shard_map/ppermute | solution.py:385
  102.2 2.3 %fusion.7 = bf16[128,1536]{1,0:T(8,128)(2,1)} fusion(bf16[128,1536]{1,0:T(8,128)(2,1)} %collective-permute-done.24, bf16[128,1536]{1,0:T(8,128)(2,1)} %get-tuple-element.18.refs_1_.refs_8_, bf16[2,128,1536]{2,1,0:T(8,128)(2,1)} %collective-permute-done.6.refs_9_, bf16[64,1536]{1,0:T(8,128)(2,1)} %collective-permute-done.28, bf16[64,1536]{1,0:T(8,128)(2,1)} %after.16), kind=kLoop, calls=%fused_computation.12 | loop fusion | flops 2162688 | bytes 1966080 | tf_op jit(solution)/shard_map/convert_element_type | solution.py:409
  (33 shorter events, 0.1 us)
Async XLA Ops:
  1.8 4.6 %copy-start.1 = (bf16[136,1536]{1,0:T(8,128)(2,1)}, bf16[136,1536]{1,0:T(8,128)(2,1)S(1)}, u32[]{:S(2)}) copy-start(bf16[136,1536]{1,0:T(8,128)(2,1)S(1)} %fusion.8.refs_0_) | copy-start | bytes 1253380
  1.8 12.7 %collective-permute-start = (bf16[136,1536]{1,0:T(8,128)(2,1)S(1)}, bf16[136,1536]{1,0:T(8,128)(2,1)S(1)}, u32[]{:S(2)}, u32[]{:S(2)}) collective-permute-start(bf16[136,1536]{1,0:T(8,128)(2,1)S(1)} %fusion.8.refs_0_), channel_id=1, source_target_pairs={{0,2},{1,3},{2,0},{3,1},{4,6},{5,7},{6,4},{7,5},{8,10},{9,11},{10,... | collective-permute-start | bytes 1253384 | tf_op jit(solution)/shard_map/ppermute | solution.py:385
  4.8 12.1 %collective-permute-start.3 = (bf16[136,1536]{1,0:T(8,128)(2,1)S(1)}, bf16[136,1536]{1,0:T(8,128)(2,1)}, u32[]{:S(2)}, u32[]{:S(2)}) collective-permute-start(bf16[136,1536]{1,0:T(8,128)(2,1)S(1)} %fusion.8.refs_0_), channel_id=1, source_target_pairs={{0,4},{1,5},{2,6},{3,7},{4,12},{5,13},{6,14},{7,15},{8,0},{9,1},{1... | collective-permute-start | bytes 1253384 | tf_op jit(solution)/shard_map/ppermute | solution.py:385
  6.4 12.4 %collective-permute-start.1 = (bf16[136,1536]{1,0:T(8,128)(2,1)S(1)}, bf16[136,1536]{1,0:T(8,128)(2,1)S(1)}, u32[]{:S(2)}, u32[]{:S(2)}) collective-permute-start(bf16[136,1536]{1,0:T(8,128)(2,1)S(1)} %fusion.8.refs_0_), channel_id=1, source_target_pairs={{0,1},{1,0},{2,3},{3,2},{4,5},{5,4},{6,7},{7,6},{8,9},{9,8},{10,11... | collective-permute-start | bytes 1253384 | tf_op jit(solution)/shard_map/ppermute | solution.py:385
  14.4 4.4 %copy-start.4 = (bf16[136,1536]{1,0:T(8,128)(2,1)}, bf16[136,1536]{1,0:T(8,128)(2,1)S(1)}, u32[]{:S(2)}) copy-start(bf16[136,1536]{1,0:T(8,128)(2,1)S(1)} %collective-permute-done.refs_1_) | copy-start | bytes 1253380
  14.4 4.4 %collective-permute-start.2 = (bf16[136,1536]{1,0:T(8,128)(2,1)S(1)}, bf16[136,1536]{1,0:T(8,128)(2,1)S(1)}, u32[]{:S(2)}, u32[]{:S(2)}) collective-permute-start(bf16[136,1536]{1,0:T(8,128)(2,1)S(1)} %collective-permute-done.refs_1_), channel_id=1, source_target_pairs={{0,1},{1,0},{2,3},{3,2},{4,5},{5,4},{6,7},{7,6},{8,9},{9,8},{10,11... | collective-permute-start | bytes 1253384 | tf_op jit(solution)/shard_map/ppermute | solution.py:385
  16.9 11.5 %collective-permute-start.4 = (bf16[136,1536]{1,0:T(8,128)(2,1)}, bf16[136,1536]{1,0:T(8,128)(2,1)}, u32[]{:S(2)}, u32[]{:S(2)}) collective-permute-start(bf16[136,1536]{1,0:T(8,128)(2,1)} %collective-permute-done.3.refs_0_), channel_id=1, source_target_pairs={{0,2},{1,3},{2,0},{3,1},{4,6},{5,7},{6,4},{7,5},{8,10},{9,11},{10,... | collective-permute-start | bytes 1253384 | tf_op jit(solution)/shard_map/ppermute | solution.py:385
  18.0 11.9 %collective-permute-start.5 = (bf16[136,1536]{1,0:T(8,128)(2,1)}, bf16[136,1536]{1,0:T(8,128)(2,1)}, u32[]{:S(2)}, u32[]{:S(2)}) collective-permute-start(bf16[136,1536]{1,0:T(8,128)(2,1)} %collective-permute-done.3.refs_0_), channel_id=1, source_target_pairs={{0,4},{1,5},{2,6},{3,7},{4,12},{5,13},{6,14},{7,15},{8,0},{9,1},{1... | collective-permute-start | bytes 1253384 | tf_op jit(solution)/shard_map/ppermute | solution.py:385
  18.8 15.2 %collective-permute-start.10 = (bf16[136,1536]{1,0:T(8,128)(2,1)}, bf16[136,1536]{1,0:T(8,128)(2,1)}, u32[]{:S(2)}, u32[]{:S(2)}) collective-permute-start(bf16[136,1536]{1,0:T(8,128)(2,1)} %collective-permute-done.3.refs_0_), channel_id=1, source_target_pairs={{0,1},{1,0},{2,3},{3,2},{4,5},{5,4},{6,7},{7,6},{8,9},{9,8},{10,11... | collective-permute-start | bytes 1253384 | tf_op jit(solution)/shard_map/ppermute | solution.py:385
  18.8 0.8 copy-start.5
  19.6 0.8 copy-start.6
  28.4 5.6 %collective-permute-start.11 = (bf16[136,1536]{1,0:T(8,128)(2,1)}, bf16[136,1536]{1,0:T(8,128)(2,1)}, u32[]{:S(2)}, u32[]{:S(2)}) collective-permute-start(bf16[136,1536]{1,0:T(8,128)(2,1)} %after.9.refs_1_), channel_id=1, source_target_pairs={{0,1},{1,0},{2,3},{3,2},{4,5},{5,4},{6,7},{7,6},{8,9},{9,8},{10,11... | collective-permute-start | bytes 1253384 | tf_op jit(solution)/shard_map/ppermute | solution.py:385
  29.9 13.1 %collective-permute-start.12 = (bf16[136,1536]{1,0:T(8,128)(2,1)}, bf16[136,1536]{1,0:T(8,128)(2,1)}, u32[]{:S(2)}, u32[]{:S(2)}) collective-permute-start(bf16[136,1536]{1,0:T(8,128)(2,1)} %after.10.refs_2_.refs_0_), channel_id=1, source_target_pairs={{0,4},{1,5},{2,6},{3,7},{4,12},{5,13},{6,14},{7,15},{8,0},{9,1},{1... | collective-permute-start | bytes 1253384 | tf_op jit(solution)/shard_map/ppermute | solution.py:385
  33.6 11.7 %collective-permute-start.7 = (bf16[136,1536]{1,0:T(8,128)(2,1)}, bf16[136,1536]{1,0:T(8,128)(2,1)}, u32[]{:S(2)}, u32[]{:S(2)}) collective-permute-start(bf16[136,1536]{1,0:T(8,128)(2,1)} %after.10.refs_2_.refs_0_), channel_id=1, source_target_pairs={{0,2},{1,3},{2,0},{3,1},{4,6},{5,7},{6,4},{7,5},{8,10},{9,11},{10,... | collective-permute-start | bytes 1253384 | tf_op jit(solution)/shard_map/ppermute | solution.py:385
  45.2 2.6 %collective-permute-start.20 = (bf16[2,128,1536]{2,1,0:T(8,128)(2,1)}, bf16[2,128,1536]{2,1,0:T(8,128)(2,1)}, u32[]{:S(2)}, u32[]{:S(2)}) collective-permute-start(bf16[2,128,1536]{2,1,0:T(8,128)(2,1)} %after.14), channel_id=1, source_target_pairs={{0,1},{1,0},{2,3},{3,2},{4,5},{5,4},{6,7},{7,6},{8,9},{9,8},{10,11... | collective-permute-start | bytes 2359304 | tf_op jit(solution)/shard_map/ppermute | solution.py:385
  45.2 5.1 %collective-permute-start.6 = (bf16[2,128,1536]{2,1,0:T(8,128)(2,1)}, bf16[2,128,1536]{2,1,0:T(8,128)(2,1)}, u32[]{:S(2)}, u32[]{:S(2)}) collective-permute-start(bf16[2,128,1536]{2,1,0:T(8,128)(2,1)} %after.11), channel_id=1, source_target_pairs={{0,1},{1,0},{2,3},{3,2},{4,5},{5,4},{6,7},{7,6},{8,9},{9,8},{10,11... | collective-permute-start | bytes 2359304 | tf_op jit(solution)/shard_map/ppermute | solution.py:385
  45.7 4.5 %collective-permute-start.8 = (bf16[136,1536]{1,0:T(8,128)(2,1)}, bf16[136,1536]{1,0:T(8,128)(2,1)}, u32[]{:S(2)}, u32[]{:S(2)}) collective-permute-start(bf16[136,1536]{1,0:T(8,128)(2,1)} %after.10.refs_2_.refs_0_), channel_id=1, source_target_pairs={{0,1},{1,0},{2,3},{3,2},{4,5},{5,4},{6,7},{7,6},{8,9},{9,8},{10,11... | collective-permute-start | bytes 1253384 | tf_op jit(solution)/shard_map/ppermute | solution.py:385
  45.7 4.5 %collective-permute-start.9 = (bf16[136,1536]{1,0:T(8,128)(2,1)}, bf16[136,1536]{1,0:T(8,128)(2,1)}, u32[]{:S(2)}, u32[]{:S(2)}) collective-permute-start(bf16[136,1536]{1,0:T(8,128)(2,1)} %collective-permute-done.7.refs_1_), channel_id=1, source_target_pairs={{0,1},{1,0},{2,3},{3,2},{4,5},{5,4},{6,7},{7,6},{8,9},{9,8},{10,11... | collective-permute-start | bytes 1253384 | tf_op jit(solution)/shard_map/ppermute | solution.py:385
  46.3 12.8 %collective-permute-start.13 = (bf16[136,1536]{1,0:T(8,128)(2,1)}, bf16[136,1536]{1,0:T(8,128)(2,1)}, u32[]{:S(2)}, u32[]{:S(2)}) collective-permute-start(bf16[136,1536]{1,0:T(8,128)(2,1)} %collective-permute-done.7.refs_1_), channel_id=1, source_target_pairs={{0,4},{1,5},{2,6},{3,7},{4,12},{5,13},{6,14},{7,15},{8,0},{9,1},{1... | collective-permute-start | bytes 1253384 | tf_op jit(solution)/shard_map/ppermute | solution.py:385
  49.8 11.5 %collective-permute-start.21 = (bf16[128,1536]{1,0:T(8,128)(2,1)}, bf16[128,1536]{1,0:T(8,128)(2,1)}, u32[]{:S(2)}, u32[]{:S(2)}) collective-permute-start(bf16[128,1536]{1,0:T(8,128)(2,1)} %fusion.1), channel_id=1, source_target_pairs={{0,2},{1,3},{2,0},{3,1},{4,6},{5,7},{6,4},{7,5},{8,10},{9,11},{10,... | collective-permute-start | bytes 1179656 | tf_op jit(solution)/shard_map/ppermute | solution.py:385
  59.0 4.8 %collective-permute-start.18 = (bf16[2,128,1536]{2,1,0:T(8,128)(2,1)}, bf16[2,128,1536]{2,1,0:T(8,128)(2,1)S(1)}, u32[]{:S(2)}, u32[]{:S(2)}) collective-permute-start(bf16[2,128,1536]{2,1,0:T(8,128)(2,1)} %after.13), channel_id=1, source_target_pairs={{0,1},{1,0},{2,3},{3,2},{4,5},{5,4},{6,7},{7,6},{8,9},{9,8},{10,11... | collective-permute-start | bytes 2359304 | tf_op jit(solution)/shard_map/ppermute | solution.py:385
  59.0 8.0 %collective-permute-start.14 = (bf16[136,1536]{1,0:T(8,128)(2,1)}, bf16[136,1536]{1,0:T(8,128)(2,1)}, u32[]{:S(2)}, u32[]{:S(2)}) collective-permute-start(bf16[136,1536]{1,0:T(8,128)(2,1)} %after.12.refs_0_.refs_2_), channel_id=1, source_target_pairs={{0,1},{1,0},{2,3},{3,2},{4,5},{5,4},{6,7},{7,6},{8,9},{9,8},{10,11... | collective-permute-start | bytes 1253384 | tf_op jit(solution)/shard_map/ppermute | solution.py:385
  59.5 7.5 %collective-permute-start.15 = (bf16[136,1536]{1,0:T(8,128)(2,1)}, bf16[136,1536]{1,0:T(8,128)(2,1)}, u32[]{:S(2)}, u32[]{:S(2)}) collective-permute-start(bf16[136,1536]{1,0:T(8,128)(2,1)} %collective-permute-done.13.refs_1_), channel_id=1, source_target_pairs={{0,1},{1,0},{2,3},{3,2},{4,5},{5,4},{6,7},{7,6},{8,9},{9,8},{10,11... | collective-permute-start | bytes 1253384 | tf_op jit(solution)/shard_map/ppermute | solution.py:385
  63.4 11.8 %collective-permute-start.22 = (bf16[128,1536]{1,0:T(8,128)(2,1)}, bf16[128,1536]{1,0:T(8,128)(2,1)}, u32[]{:S(2)}, u32[]{:S(2)}) collective-permute-start(bf16[128,1536]{1,0:T(8,128)(2,1)} %fusion.3), channel_id=1, source_target_pairs={{0,4},{1,5},{2,6},{3,7},{4,12},{5,13},{6,14},{7,15},{8,0},{9,1},{1... | collective-permute-start | bytes 1179656 | tf_op jit(solution)/shard_map/ppermute | solution.py:385
  63.8 0.9 copy-start.3
  66.5 10.4 %collective-permute-start.19 = (bf16[128,1536]{1,0:T(8,128)(2,1)}, bf16[128,1536]{1,0:T(8,128)(2,1)}, u32[]{:S(2)}, u32[]{:S(2)}) collective-permute-start(bf16[128,1536]{1,0:T(8,128)(2,1)} %fusion.4), channel_id=1, source_target_pairs={{0,2},{1,3},{2,0},{3,1},{4,6},{5,7},{6,4},{7,5},{8,10},{9,11},{10,... | collective-permute-start | bytes 1179656 | tf_op jit(solution)/shard_map/ppermute | solution.py:385
  75.1 5.3 %collective-permute-start.16 = (bf16[2,128,1536]{2,1,0:T(8,128)(2,1)}, bf16[2,128,1536]{2,1,0:T(8,128)(2,1)S(1)}, u32[]{:S(2)}, u32[]{:S(2)}) collective-permute-start(bf16[2,128,1536]{2,1,0:T(8,128)(2,1)} %get-tuple-element.25), channel_id=1, source_target_pairs={{0,1},{1,0},{2,3},{3,2},{4,5},{5,4},{6,7},{7,6},{8,9},{9,8},{10,11... | collective-permute-start | bytes 2359304 | tf_op jit(solution)/shard_map/ppermute | solution.py:385
  79.2 8.2 %collective-permute-start.23 = (bf16[64,1536]{1,0:T(8,128)(2,1)S(1)}, bf16[64,1536]{1,0:T(8,128)(2,1)S(1)}, u32[]{:S(2)}, u32[]{:S(2)}) collective-permute-start(bf16[64,1536]{1,0:T(8,128)(2,1)S(1)} %get-tuple-element.32), channel_id=1, source_target_pairs={{0,4},{1,5},{2,6},{3,7},{4,12},{5,13},{6,14},{7,15},{8,0},{9,1},{1... | collective-permute-start | bytes 589832 | tf_op jit(solution)/shard_map/ppermute | solution.py:385
  80.4 9.7 %copy-start.2 = (bf16[2,128,1536]{2,1,0:T(8,128)(2,1)}, bf16[2,128,1536]{2,1,0:T(8,128)(2,1)S(1)}, u32[]{:S(2)}) copy-start(bf16[2,128,1536]{2,1,0:T(8,128)(2,1)S(1)} %collective-permute-done.16) | copy-start | bytes 2359300
  82.5 7.6 %collective-permute-start.17 = (bf16[64,1536]{1,0:T(8,128)(2,1)S(1)}, bf16[64,1536]{1,0:T(8,128)(2,1)S(1)}, u32[]{:S(2)}, u32[]{:S(2)}) collective-permute-start(bf16[64,1536]{1,0:T(8,128)(2,1)S(1)} %get-tuple-element.34), channel_id=1, source_target_pairs={{0,2},{1,3},{2,0},{3,1},{4,6},{5,7},{6,4},{7,5},{8,10},{9,11},{10,... | collective-permute-start | bytes 589832 | tf_op jit(solution)/shard_map/ppermute | solution.py:385
  83.0 10.3 %collective-permute-start.27 = (bf16[64,1536]{1,0:T(8,128)(2,1)}, bf16[64,1536]{1,0:T(8,128)(2,1)}, u32[]{:S(2)}, u32[]{:S(2)}) collective-permute-start(bf16[64,1536]{1,0:T(8,128)(2,1)} %get-tuple-element.31), channel_id=1, source_target_pairs={{0,4},{1,5},{2,6},{3,7},{4,12},{5,13},{6,14},{7,15},{8,0},{9,1},{1... | collective-permute-start | bytes 589832 | tf_op jit(solution)/shard_map/ppermute | solution.py:385
  84.9 8.5 %collective-permute-start.26 = (bf16[64,1536]{1,0:T(8,128)(2,1)}, bf16[64,1536]{1,0:T(8,128)(2,1)}, u32[]{:S(2)}, u32[]{:S(2)}) collective-permute-start(bf16[64,1536]{1,0:T(8,128)(2,1)} %get-tuple-element.33), channel_id=1, source_target_pairs={{0,2},{1,3},{2,0},{3,1},{4,6},{5,7},{6,4},{7,5},{8,10},{9,11},{10,... | collective-permute-start | bytes 589832 | tf_op jit(solution)/shard_map/ppermute | solution.py:385
  91.1 2.2 %copy-start = (bf16[64,1536]{1,0:T(8,128)(2,1)}, bf16[64,1536]{1,0:T(8,128)(2,1)S(1)}, u32[]{:S(2)}) copy-start(bf16[64,1536]{1,0:T(8,128)(2,1)S(1)} %fusion.22.refs_1_) | copy-start | bytes 589828
  91.1 8.0 %collective-permute-start.25 = (bf16[64,1536]{1,0:T(8,128)(2,1)S(1)}, bf16[64,1536]{1,0:T(8,128)(2,1)}, u32[]{:S(2)}, u32[]{:S(2)}) collective-permute-start(bf16[64,1536]{1,0:T(8,128)(2,1)S(1)} %fusion.22.refs_1_), channel_id=1, source_target_pairs={{0,4},{1,5},{2,6},{3,7},{4,12},{5,13},{6,14},{7,15},{8,0},{9,1},{1... | collective-permute-start | bytes 589832 | tf_op jit(solution)/shard_map/ppermute | solution.py:385
  93.3 8.9 %collective-permute-start.24 = (bf16[128,1536]{1,0:T(8,128)(2,1)}, bf16[128,1536]{1,0:T(8,128)(2,1)}, u32[]{:S(2)}, u32[]{:S(2)}) collective-permute-start(bf16[128,1536]{1,0:T(8,128)(2,1)} %after.15), channel_id=1, source_target_pairs={{0,2},{1,3},{2,0},{3,1},{4,6},{5,7},{6,4},{7,5},{8,10},{9,11},{10,... | collective-permute-start | bytes 1179656 | tf_op jit(solution)/shard_map/ppermute | solution.py:385
  95.3 6.9 %collective-permute-start.28 = (bf16[64,1536]{1,0:T(8,128)(2,1)}, bf16[64,1536]{1,0:T(8,128)(2,1)}, u32[]{:S(2)}, u32[]{:S(2)}) collective-permute-start(bf16[64,1536]{1,0:T(8,128)(2,1)} %fusion.15), channel_id=1, source_target_pairs={{0,4},{1,5},{2,6},{3,7},{4,12},{5,13},{6,14},{7,15},{8,0},{9,1},{1... | collective-permute-start | bytes 589832 | tf_op jit(solution)/shard_map/ppermute | solution.py:385

commit v16 on v15

--- a/solution.py
+++ b/solution.py
@@ -163,7 +163,7 @@
     held, w_gate, w_down, spare_gate, spare_down = refs[:5]
     rows_in, spare_in, hidden, spare_hidden, rows_out, dense, summed, fetched, stored = refs[5:]
     width, inner = w_gate.shape
-    tile = 512
+    tile = 768
     my_id, failed_id = lax.axis_index("expert"), failed[0]
     holds = holders[0, failed_id] == my_id
     for j in range(1, holders.shape[0]):

time: 106 us -> 106 us (level)
  waiting for transfers between devices: 27.7 us -> 22.3 us
  Pallas kernels: 32.5 us -> 37.3 us
  starting transfers between devices: 23.6 us -> 25.1 us
    ppermute x29, waiting for transfers between devices: 27.7 us -> 22.3 us  [by_permutes(): move = lambda a, pairs: lax.ppermute(a, 'expert', pairs)]
    pallas_call x4, Pallas kernels: 32.5 us -> 37.3 us  [run_group(): pl.pallas_call(functools.partial(group_kernel, others=len(earlier), adds=...]
    ppermute x29, starting transfers between devices: 23.6 us -> 25.1 us  [by_permutes(): move = lambda a, pairs: lax.ppermute(a, 'expert', pairs)]
  transfers between devices with their start and end apart: 29 -> 29, of which waited for: 13 -> 10; matrix products, arithmetic and copies ran while one was open for 13% -> 13% of each run, Pallas kernels for 31% -> 35%
where the time goes in v16:
time: 106 us; the launch traced here: 105 us
  Pallas kernels  37.3 us (35%)
  starting transfers between devices  25.1 us (24%)
  waiting for transfers between devices  22.3 us (21%)
  other arithmetic  17.4 us (16%)
  local copies, waits for them, and re-layouts  2.46 us (2%)
    pallas_call x4, Pallas kernels, run_group(): pl.pallas_call(functools.partial(group_kernel, others=len(earlier), adds=...  37.3 us
    ppermute x29, starting transfers between devices, by_permutes(): move = lambda a, pairs: lax.ppermute(a, 'expert', pairs)  25.1 us
    ppermute x29, waiting for transfers between devices, by_permutes(): move = lambda a, pairs: lax.ppermute(a, 'expert', pairs)  22.3 us
    convert_element_type x5, other arithmetic, total(): return result.astype(jnp.bfloat16)  9.76 us
    convert_element_type x3, other arithmetic, by_permutes(): add = lambda a, b: (f32(a) + f32(b)).astype(jnp.bfloat16)  5.86 us
    unnamed x15, local copies, waits for them, and re-layouts  2.46 us
  transfers between devices with their start and end apart: 29, of which 10 were waited for; matrix products, arithmetic and copies ran while one was open for 13% of the time, Pallas kernels for 35%

profile of v16, /device:TPU:0, one launch (start us, length us, event | category | flops | bytes accessed | tf_op | source)
XLA Modules:
  0.0 105.5 jit_solution(745272843506842815)
XLA Ops:
  0.0 0.7 fusion.23
  0.7 1.0 fusion.8.refs_0_
  1.8 3.0 %collective-permute-start = (bf16[136,1536]{1,0:T(8,128)(2,1)S(1)}, bf16[136,1536]{1,0:T(8,128)(2,1)S(1)}, u32[]{:S(2)}, u32[]{:S(2)}) collective-permute-start(bf16[136,1536]{1,0:T(8,128)(2,1)S(1)} %fusion.8.refs_0_), channel_id=1, source_target_pairs={{0,2},{1,3},{2,0},{3,1},{4,6},{5,7},{6,4},{7,5},{8,10},{9,11},{10,... | collective-permute-start | bytes 1253384 | tf_op jit(solution)/shard_map/ppermute | solution.py:385
  4.8 1.6 %collective-permute-start.3 = (bf16[136,1536]{1,0:T(8,128)(2,1)S(1)}, bf16[136,1536]{1,0:T(8,128)(2,1)}, u32[]{:S(2)}, u32[]{:S(2)}) collective-permute-start(bf16[136,1536]{1,0:T(8,128)(2,1)S(1)} %fusion.8.refs_0_), channel_id=1, source_target_pairs={{0,4},{1,5},{2,6},{3,7},{4,12},{5,13},{6,14},{7,15},{8,0},{9,1},{1... | collective-permute-start | bytes 1253384 | tf_op jit(solution)/shard_map/ppermute | solution.py:385
  6.4 0.0 collective-permute-start.1
  6.4 8.1 %collective-permute-done.refs_1_ = bf16[136,1536]{1,0:T(8,128)(2,1)S(1)} collective-permute-done((bf16[136,1536]{1,0:T(8,128)(2,1)S(1)}, bf16[136,1536]{1,0:T(8,128)(2,1)S(1)}, u32[]{:S(2)}, u32[]{:S(2)}) %collective-permute-start) | collective-permute-done | bytes 417824 | tf_op jit(solution)/shard_map/ppermute | solution.py:385
  14.4 0.0 collective-permute-start.2
  14.5 2.5 %collective-permute-done.3.refs_0_ = bf16[136,1536]{1,0:T(8,128)(2,1)} collective-permute-done((bf16[136,1536]{1,0:T(8,128)(2,1)S(1)}, bf16[136,1536]{1,0:T(8,128)(2,1)}, u32[]{:S(2)}, u32[]{:S(2)}) %collective-permute-start.3) | collective-permute-done | bytes 417824 | tf_op jit(solution)/shard_map/ppermute | solution.py:385
  16.9 0.5 collective-permute-start.4
  18.0 0.8 collective-permute-start.5
  18.8 0.0 collective-permute-start.10
  18.8 0.0 collective-permute-done.1.refs_2_
  18.8 0.0 collective-permute-done.2.refs_3_
  18.8 0.7 copy-done.5
  19.6 0.8 copy-done.6
  20.4 9.3 %group.4 = (bf16[128,1536]{1,0:T(8,128)(2,1)}, bf16[128,1536]{1,0:T(8,128)(2,1)}, bf16[2,128,1536]{2,1,0:T(8,128)(2,1)}) custom-call(s32[1]{0:T(128)S(6)} %copy.31.failed, s32[4,16]{1,0:T(4,128)} %bitcast.63, bf16[136,1536]{1,0:T(8,128)(2,1)} %copy-done.1, bf16[136,1536]{1,0:T(8,128)(2,1)} %copy-done.4, bf16[136,1536]{1,0:T(8,128)(2,1)} %copy-done.5, ...), custom_call_target="tpu_custom_call" | custom-call | flops 3019898880 | bytes 14942208 | tf_op jit(solution)/shard_map/group/pallas_call | solution.py:318
  29.7 0.0 collective-permute-done.4.refs_0_
  29.7 0.1 collective-permute-start.11
  29.8 0.1 collective-permute-done.5.refs_0_
  29.9 2.8 %collective-permute-start.12 = (bf16[136,1536]{1,0:T(8,128)(2,1)}, bf16[136,1536]{1,0:T(8,128)(2,1)}, u32[]{:S(2)}, u32[]{:S(2)}) collective-permute-start(bf16[136,1536]{1,0:T(8,128)(2,1)} %after.10.refs_2_.refs_0_), channel_id=1, source_target_pairs={{0,4},{1,5},{2,6},{3,7},{4,12},{5,13},{6,14},{7,15},{8,0},{9,1},{1... | collective-permute-start | bytes 1253384 | tf_op jit(solution)/shard_map/ppermute | solution.py:385
  32.7 2.1 %collective-permute-start.7 = (bf16[136,1536]{1,0:T(8,128)(2,1)}, bf16[136,1536]{1,0:T(8,128)(2,1)}, u32[]{:S(2)}, u32[]{:S(2)}) collective-permute-start(bf16[136,1536]{1,0:T(8,128)(2,1)} %after.10.refs_2_.refs_0_), channel_id=1, source_target_pairs={{0,2},{1,3},{2,0},{3,1},{4,6},{5,7},{6,4},{7,5},{8,10},{9,11},{10,... | collective-permute-start | bytes 1253384 | tf_op jit(solution)/shard_map/ppermute | solution.py:385
  34.8 0.0 collective-permute-done.10.refs_2_
  34.9 9.3 %group.5 = (bf16[128,1536]{1,0:T(8,128)(2,1)}, bf16[128,1536]{1,0:T(8,128)(2,1)}, bf16[2,128,1536]{2,1,0:T(8,128)(2,1)}) custom-call(s32[1]{0:T(128)S(6)} %copy.31.failed, s32[4,16]{1,0:T(4,128)} %bitcast.64, bf16[136,1536]{1,0:T(8,128)(2,1)} %collective-permute-done.3.refs_0_, bf16[136,1536]{1,0:T(8,128)(2,1)} %after.9.refs_1_, ...), custom_call_target="tpu_custom_call" | custom-call | flops 3019898880 | bytes 14942208 | tf_op jit(solution)/shard_map/group/pallas_call | solution.py:318
  44.2 1.0 collective-permute-done.7.refs_1_
  45.2 0.5 collective-permute-start.6
  45.7 0.0 collective-permute-start.8
  45.7 0.5 collective-permute-start.9
  46.2 0.3 collective-permute-start.13
  46.5 1.3 %collective-permute-done.20 = bf16[2,128,1536]{2,1,0:T(8,128)(2,1)} collective-permute-done((bf16[2,128,1536]{2,1,0:T(8,128)(2,1)}, bf16[2,128,1536]{2,1,0:T(8,128)(2,1)}, u32[]{:S(2)}, u32[]{:S(2)}) %collective-permute-start.20) | collective-permute-done | bytes 786464 | tf_op jit(solution)/shard_map/ppermute | solution.py:385
  47.8 2.0 %fusion.1 = bf16[128,1536]{1,0:T(8,128)(2,1)} fusion(bf16[128,1536]{1,0:T(8,128)(2,1)} %get-tuple-element.30, bf16[2,128,1536]{2,1,0:T(8,128)(2,1)} %collective-permute-done.20), kind=kLoop, calls=%fused_computation.3 | loop fusion | flops 786432 | bytes 1179648 | tf_op jit(solution)/shard_map/convert_element_type | solution.py:387
  49.8 1.7 %collective-permute-start.21 = (bf16[128,1536]{1,0:T(8,128)(2,1)}, bf16[128,1536]{1,0:T(8,128)(2,1)}, u32[]{:S(2)}, u32[]{:S(2)}) collective-permute-start(bf16[128,1536]{1,0:T(8,128)(2,1)} %fusion.1), channel_id=1, source_target_pairs={{0,2},{1,3},{2,0},{3,1},{4,6},{5,7},{6,4},{7,5},{8,10},{9,11},{10,... | collective-permute-start | bytes 1179656 | tf_op jit(solution)/shard_map/ppermute | solution.py:385
  51.5 9.4 %group.6 = (bf16[128,1536]{1,0:T(8,128)(2,1)}, bf16[128,1536]{1,0:T(8,128)(2,1)}, bf16[2,128,1536]{2,1,0:T(8,128)(2,1)}, bf16[128,1536]{1,0:T(8,128)(2,1)}) custom-call(s32[1]{0:T(128)S(6)} %copy.31.failed, s32[4,16]{1,0:T(4,128)} %bitcast.65, bf16[136,1536]{1,0:T(8,128)(2,1)} %after.10.refs_2_.refs_0_, bf16[136,1536]{1,0:T(8,128)(2,1)} %collective-permute-done.7.refs_1_, ...), custom_call_target="tpu_custom_call" | custom-call | flops 3019898880 | bytes 14942208 | tf_op jit(solution)/shard_map/group/pallas_call | solution.py:318
  60.9 0.1 collective-permute-start.18
  61.0 0.5 collective-permute-start.14
  61.5 0.1 collective-permute-start.15
  61.6 2.1 %fusion.3 = bf16[128,1536]{1,0:T(8,128)(2,1)} fusion(bf16[128,1536]{1,0:T(8,128)(2,1)} %collective-permute-done.21, bf16[128,1536]{1,0:T(8,128)(2,1)} %get-tuple-element.21.refs_10_.refs_1_, bf16[2,128,1536]{2,1,0:T(8,128)(2,1)} %collective-permute-done.20), kind=kLoop, calls=%fused_computation.6 | loop fusion | flops 1179648 | bytes 1572864 | tf_op jit(solution)/shard_map/convert_element_type | solution.py:409
  63.7 0.0 collective-permute-start.22
  63.7 0.1 collective-permute-done.18
  63.8 0.9 copy-done.3
  64.7 1.8 %fusion.4 = bf16[128,1536]{1,0:T(8,128)(2,1)} fusion(bf16[128,1536]{1,0:T(8,128)(2,1)} %get-tuple-element.28, bf16[2,128,1536]{2,1,0:T(8,128)(2,1)S(1)} %collective-permute-done.18), kind=kLoop, calls=%fused_computation.8 | loop fusion | flops 786432 | bytes 1179648 | tf_op jit(solution)/shard_map/convert_element_type | solution.py:387
  66.5 1.6 %collective-permute-start.19 = (bf16[128,1536]{1,0:T(8,128)(2,1)}, bf16[128,1536]{1,0:T(8,128)(2,1)}, u32[]{:S(2)}, u32[]{:S(2)}) collective-permute-start(bf16[128,1536]{1,0:T(8,128)(2,1)} %fusion.4), channel_id=1, source_target_pairs={{0,2},{1,3},{2,0},{3,1},{4,6},{5,7},{6,4},{7,5},{8,10},{9,11},{10,... | collective-permute-start | bytes 1179656 | tf_op jit(solution)/shard_map/ppermute | solution.py:385
  68.1 0.0 collective-permute-done.14.refs_2_
  68.1 0.0 collective-permute-done.15.refs_3_
  68.1 9.3 %group.7 = (bf16[128,1536]{1,0:T(8,128)(2,1)}, bf16[128,1536]{1,0:T(8,128)(2,1)}, bf16[2,128,1536]{2,1,0:T(8,128)(2,1)}) custom-call(s32[1]{0:T(128)S(6)} %copy.31.failed, s32[4,16]{1,0:T(4,128)} %bitcast.66, bf16[136,1536]{1,0:T(8,128)(2,1)} %after.12.refs_0_.refs_2_, bf16[136,1536]{1,0:T(8,128)(2,1)} %collective-permute-done.13.refs_1_, ...), custom_call_target="tpu_custom_call" | custom-call | flops 3019898880 | bytes 14942208 | tf_op jit(solution)/shard_map/group/pallas_call | solution.py:318
  77.4 0.1 collective-permute-start.16
  77.5 0.7 collective-permute-done.19
  78.2 2.3 %fusion.11 = (bf16[64,1536]{1,0:T(8,128)(2,1)}, bf16[64,1536]{1,0:T(8,128)(2,1)S(1)}) fusion(bf16[128,1536]{1,0:T(8,128)(2,1)} %collective-permute-done.22, bf16[128,1536]{1,0:T(8,128)(2,1)} %collective-permute-done.19, bf16[2,128,1536]{2,1,0:T(8,128)(2,1)} %copy-done.3, bf16[128,1536]{1,0:T(8,128)(2,1)} %get-tuple-element.23.refs_8_), kind=kLoop, calls=%fused_computation.21 | loop fusion | flops 1572864 | bytes 1966080 | tf_op jit(solution)/shard_map/convert_element_type | solution.py:409
  80.5 0.1 collective-permute-start.23
  80.7 2.1 %fusion.12 = (bf16[64,1536]{1,0:T(8,128)(2,1)}, bf16[64,1536]{1,0:T(8,128)(2,1)S(1)}) fusion(bf16[2,128,1536]{2,1,0:T(8,128)(2,1)S(1)} %collective-permute-done.16, bf16[128,1536]{1,0:T(8,128)(2,1)} %get-tuple-element.26), kind=kLoop, calls=%fused_computation.23 | loop fusion | flops 786432 | bytes 1179648 | tf_op jit(solution)/shard_map/convert_element_type | solution.py:387
  82.8 1.4 %collective-permute-start.17 = (bf16[64,1536]{1,0:T(8,128)(2,1)S(1)}, bf16[64,1536]{1,0:T(8,128)(2,1)S(1)}, u32[]{:S(2)}, u32[]{:S(2)}) collective-permute-start(bf16[64,1536]{1,0:T(8,128)(2,1)S(1)} %get-tuple-element.34), channel_id=1, source_target_pairs={{0,2},{1,3},{2,0},{3,1},{4,6},{5,7},{6,4},{7,5},{8,10},{9,11},{10,... | collective-permute-start | bytes 589832 | tf_op jit(solution)/shard_map/ppermute | solution.py:385
  84.1 0.9 collective-permute-start.27
  85.0 1.6 %collective-permute-start.26 = (bf16[64,1536]{1,0:T(8,128)(2,1)}, bf16[64,1536]{1,0:T(8,128)(2,1)}, u32[]{:S(2)}, u32[]{:S(2)}) collective-permute-start(bf16[64,1536]{1,0:T(8,128)(2,1)} %get-tuple-element.33), channel_id=1, source_target_pairs={{0,2},{1,3},{2,0},{3,1},{4,6},{5,7},{6,4},{7,5},{8,10},{9,11},{10,... | collective-permute-start | bytes 589832 | tf_op jit(solution)/shard_map/ppermute | solution.py:385
  86.7 2.3 %collective-permute-done.23 = bf16[64,1536]{1,0:T(8,128)(2,1)S(1)} collective-permute-done((bf16[64,1536]{1,0:T(8,128)(2,1)S(1)}, bf16[64,1536]{1,0:T(8,128)(2,1)S(1)}, u32[]{:S(2)}, u32[]{:S(2)}) %collective-permute-start.23) | collective-permute-done | bytes 196640 | tf_op jit(solution)/shard_map/ppermute | solution.py:385
  89.0 1.6 %collective-permute-done.17 = bf16[64,1536]{1,0:T(8,128)(2,1)S(1)} collective-permute-done((bf16[64,1536]{1,0:T(8,128)(2,1)S(1)}, bf16[64,1536]{1,0:T(8,128)(2,1)S(1)}, u32[]{:S(2)}, u32[]{:S(2)}) %collective-permute-start.17) | collective-permute-done | bytes 196640 | tf_op jit(solution)/shard_map/ppermute | solution.py:385
  90.6 1.0 fusion.22.refs_1_
  91.6 1.5 %collective-permute-start.25 = (bf16[64,1536]{1,0:T(8,128)(2,1)S(1)}, bf16[64,1536]{1,0:T(8,128)(2,1)}, u32[]{:S(2)}, u32[]{:S(2)}) collective-permute-start(bf16[64,1536]{1,0:T(8,128)(2,1)S(1)} %fusion.22.refs_1_), channel_id=1, source_target_pairs={{0,4},{1,5},{2,6},{3,7},{4,12},{5,13},{6,14},{7,15},{8,0},{9,1},{1... | collective-permute-start | bytes 589832 | tf_op jit(solution)/shard_map/ppermute | solution.py:385
  93.1 0.8 collective-permute-start.24
  93.9 0.0 collective-permute-done.27.refs_0_
  93.9 2.0 %fusion.15 = bf16[64,1536]{1,0:T(8,128)(2,1)} fusion(bf16[64,1536]{1,0:T(8,128)(2,1)} %after.17, bf16[64,1536]{1,0:T(8,128)(2,1)} %collective-permute-done.26, bf16[2,128,1536]{2,1,0:T(8,128)(2,1)} %copy-done.2, bf16[128,1536]{1,0:T(8,128)(2,1)} %get-tuple-element.24), kind=kLoop, calls=%fused_computation.27 | loop fusion | flops 786432 | bytes 983040 | tf_op jit(solution)/shard_map/convert_element_type | solution.py:409
  95.9 2.6 %collective-permute-start.28 = (bf16[64,1536]{1,0:T(8,128)(2,1)}, bf16[64,1536]{1,0:T(8,128)(2,1)}, u32[]{:S(2)}, u32[]{:S(2)}) collective-permute-start(bf16[64,1536]{1,0:T(8,128)(2,1)} %fusion.15), channel_id=1, source_target_pairs={{0,4},{1,5},{2,6},{3,7},{4,12},{5,13},{6,14},{7,15},{8,0},{9,1},{1... | collective-permute-start | bytes 589832 | tf_op jit(solution)/shard_map/ppermute | solution.py:385
  98.5 0.0 collective-permute-done.25.refs_0_
  98.5 4.6 %collective-permute-done.28 = bf16[64,1536]{1,0:T(8,128)(2,1)} collective-permute-done((bf16[64,1536]{1,0:T(8,128)(2,1)}, bf16[64,1536]{1,0:T(8,128)(2,1)}, u32[]{:S(2)}, u32[]{:S(2)}) %collective-permute-start.28) | collective-permute-done | bytes 196640 | tf_op jit(solution)/shard_map/ppermute | solution.py:385
  103.2 0.0 collective-permute-done.24
  103.2 2.3 %fusion.7 = bf16[128,1536]{1,0:T(8,128)(2,1)} fusion(bf16[128,1536]{1,0:T(8,128)(2,1)} %collective-permute-done.24, bf16[128,1536]{1,0:T(8,128)(2,1)} %get-tuple-element.18.refs_1_.refs_8_, bf16[2,128,1536]{2,1,0:T(8,128)(2,1)} %collective-permute-done.6.refs_9_, bf16[64,1536]{1,0:T(8,128)(2,1)} %collective-permute-done.28, bf16[64,1536]{1,0:T(8,128)(2,1)} %after.16), kind=kLoop, calls=%fused_computation.12 | loop fusion | flops 2162688 | bytes 1966080 | tf_op jit(solution)/shard_map/convert_element_type | solution.py:409
  (33 shorter events, 0.1 us)
Async XLA Ops:
  1.8 4.6 %copy-start.1 = (bf16[136,1536]{1,0:T(8,128)(2,1)}, bf16[136,1536]{1,0:T(8,128)(2,1)S(1)}, u32[]{:S(2)}) copy-start(bf16[136,1536]{1,0:T(8,128)(2,1)S(1)} %fusion.8.refs_0_) | copy-start | bytes 1253380
  1.8 12.7 %collective-permute-start = (bf16[136,1536]{1,0:T(8,128)(2,1)S(1)}, bf16[136,1536]{1,0:T(8,128)(2,1)S(1)}, u32[]{:S(2)}, u32[]{:S(2)}) collective-permute-start(bf16[136,1536]{1,0:T(8,128)(2,1)S(1)} %fusion.8.refs_0_), channel_id=1, source_target_pairs={{0,2},{1,3},{2,0},{3,1},{4,6},{5,7},{6,4},{7,5},{8,10},{9,11},{10,... | collective-permute-start | bytes 1253384 | tf_op jit(solution)/shard_map/ppermute | solution.py:385
  4.8 12.1 %collective-permute-start.3 = (bf16[136,1536]{1,0:T(8,128)(2,1)S(1)}, bf16[136,1536]{1,0:T(8,128)(2,1)}, u32[]{:S(2)}, u32[]{:S(2)}) collective-permute-start(bf16[136,1536]{1,0:T(8,128)(2,1)S(1)} %fusion.8.refs_0_), channel_id=1, source_target_pairs={{0,4},{1,5},{2,6},{3,7},{4,12},{5,13},{6,14},{7,15},{8,0},{9,1},{1... | collective-permute-start | bytes 1253384 | tf_op jit(solution)/shard_map/ppermute | solution.py:385
  6.4 12.4 %collective-permute-start.1 = (bf16[136,1536]{1,0:T(8,128)(2,1)S(1)}, bf16[136,1536]{1,0:T(8,128)(2,1)S(1)}, u32[]{:S(2)}, u32[]{:S(2)}) collective-permute-start(bf16[136,1536]{1,0:T(8,128)(2,1)S(1)} %fusion.8.refs_0_), channel_id=1, source_target_pairs={{0,1},{1,0},{2,3},{3,2},{4,5},{5,4},{6,7},{7,6},{8,9},{9,8},{10,11... | collective-permute-start | bytes 1253384 | tf_op jit(solution)/shard_map/ppermute | solution.py:385
  14.4 4.4 %copy-start.4 = (bf16[136,1536]{1,0:T(8,128)(2,1)}, bf16[136,1536]{1,0:T(8,128)(2,1)S(1)}, u32[]{:S(2)}) copy-start(bf16[136,1536]{1,0:T(8,128)(2,1)S(1)} %collective-permute-done.refs_1_) | copy-start | bytes 1253380
  14.4 4.4 %collective-permute-start.2 = (bf16[136,1536]{1,0:T(8,128)(2,1)S(1)}, bf16[136,1536]{1,0:T(8,128)(2,1)S(1)}, u32[]{:S(2)}, u32[]{:S(2)}) collective-permute-start(bf16[136,1536]{1,0:T(8,128)(2,1)S(1)} %collective-permute-done.refs_1_), channel_id=1, source_target_pairs={{0,1},{1,0},{2,3},{3,2},{4,5},{5,4},{6,7},{7,6},{8,9},{9,8},{10,11... | collective-permute-start | bytes 1253384 | tf_op jit(solution)/shard_map/ppermute | solution.py:385
  16.9 12.8 %collective-permute-start.4 = (bf16[136,1536]{1,0:T(8,128)(2,1)}, bf16[136,1536]{1,0:T(8,128)(2,1)}, u32[]{:S(2)}, u32[]{:S(2)}) collective-permute-start(bf16[136,1536]{1,0:T(8,128)(2,1)} %collective-permute-done.3.refs_0_), channel_id=1, source_target_pairs={{0,2},{1,3},{2,0},{3,1},{4,6},{5,7},{6,4},{7,5},{8,10},{9,11},{10,... | collective-permute-start | bytes 1253384 | tf_op jit(solution)/shard_map/ppermute | solution.py:385
  18.0 11.9 %collective-permute-start.5 = (bf16[136,1536]{1,0:T(8,128)(2,1)}, bf16[136,1536]{1,0:T(8,128)(2,1)}, u32[]{:S(2)}, u32[]{:S(2)}) collective-permute-start(bf16[136,1536]{1,0:T(8,128)(2,1)} %collective-permute-done.3.refs_0_), channel_id=1, source_target_pairs={{0,4},{1,5},{2,6},{3,7},{4,12},{5,13},{6,14},{7,15},{8,0},{9,1},{1... | collective-permute-start | bytes 1253384 | tf_op jit(solution)/shard_map/ppermute | solution.py:385
  18.8 16.0 %collective-permute-start.10 = (bf16[136,1536]{1,0:T(8,128)(2,1)}, bf16[136,1536]{1,0:T(8,128)(2,1)}, u32[]{:S(2)}, u32[]{:S(2)}) collective-permute-start(bf16[136,1536]{1,0:T(8,128)(2,1)} %collective-permute-done.3.refs_0_), channel_id=1, source_target_pairs={{0,1},{1,0},{2,3},{3,2},{4,5},{5,4},{6,7},{7,6},{8,9},{9,8},{10,11... | collective-permute-start | bytes 1253384 | tf_op jit(solution)/shard_map/ppermute | solution.py:385
  18.8 0.8 copy-start.5
  19.6 0.8 copy-start.6
  29.7 5.2 %collective-permute-start.11 = (bf16[136,1536]{1,0:T(8,128)(2,1)}, bf16[136,1536]{1,0:T(8,128)(2,1)}, u32[]{:S(2)}, u32[]{:S(2)}) collective-permute-start(bf16[136,1536]{1,0:T(8,128)(2,1)} %after.9.refs_1_), channel_id=1, source_target_pairs={{0,1},{1,0},{2,3},{3,2},{4,5},{5,4},{6,7},{7,6},{8,9},{9,8},{10,11... | collective-permute-start | bytes 1253384 | tf_op jit(solution)/shard_map/ppermute | solution.py:385
  29.9 14.3 %collective-permute-start.12 = (bf16[136,1536]{1,0:T(8,128)(2,1)}, bf16[136,1536]{1,0:T(8,128)(2,1)}, u32[]{:S(2)}, u32[]{:S(2)}) collective-permute-start(bf16[136,1536]{1,0:T(8,128)(2,1)} %after.10.refs_2_.refs_0_), channel_id=1, source_target_pairs={{0,4},{1,5},{2,6},{3,7},{4,12},{5,13},{6,14},{7,15},{8,0},{9,1},{1... | collective-permute-start | bytes 1253384 | tf_op jit(solution)/shard_map/ppermute | solution.py:385
  32.7 12.4 %collective-permute-start.7 = (bf16[136,1536]{1,0:T(8,128)(2,1)}, bf16[136,1536]{1,0:T(8,128)(2,1)}, u32[]{:S(2)}, u32[]{:S(2)}) collective-permute-start(bf16[136,1536]{1,0:T(8,128)(2,1)} %after.10.refs_2_.refs_0_), channel_id=1, source_target_pairs={{0,2},{1,3},{2,0},{3,1},{4,6},{5,7},{6,4},{7,5},{8,10},{9,11},{10,... | collective-permute-start | bytes 1253384 | tf_op jit(solution)/shard_map/ppermute | solution.py:385
  45.2 2.6 %collective-permute-start.20 = (bf16[2,128,1536]{2,1,0:T(8,128)(2,1)}, bf16[2,128,1536]{2,1,0:T(8,128)(2,1)}, u32[]{:S(2)}, u32[]{:S(2)}) collective-permute-start(bf16[2,128,1536]{2,1,0:T(8,128)(2,1)} %after.14), channel_id=1, source_target_pairs={{0,1},{1,0},{2,3},{3,2},{4,5},{5,4},{6,7},{7,6},{8,9},{9,8},{10,11... | collective-permute-start | bytes 2359304 | tf_op jit(solution)/shard_map/ppermute | solution.py:385
  45.2 6.3 %collective-permute-start.6 = (bf16[2,128,1536]{2,1,0:T(8,128)(2,1)}, bf16[2,128,1536]{2,1,0:T(8,128)(2,1)}, u32[]{:S(2)}, u32[]{:S(2)}) collective-permute-start(bf16[2,128,1536]{2,1,0:T(8,128)(2,1)} %after.11), channel_id=1, source_target_pairs={{0,1},{1,0},{2,3},{3,2},{4,5},{5,4},{6,7},{7,6},{8,9},{9,8},{10,11... | collective-permute-start | bytes 2359304 | tf_op jit(solution)/shard_map/ppermute | solution.py:385
  45.7 5.8 %collective-permute-start.8 = (bf16[136,1536]{1,0:T(8,128)(2,1)}, bf16[136,1536]{1,0:T(8,128)(2,1)}, u32[]{:S(2)}, u32[]{:S(2)}) collective-permute-start(bf16[136,1536]{1,0:T(8,128)(2,1)} %after.10.refs_2_.refs_0_), channel_id=1, source_target_pairs={{0,1},{1,0},{2,3},{3,2},{4,5},{5,4},{6,7},{7,6},{8,9},{9,8},{10,11... | collective-permute-start | bytes 1253384 | tf_op jit(solution)/shard_map/ppermute | solution.py:385
  45.7 5.8 %collective-permute-start.9 = (bf16[136,1536]{1,0:T(8,128)(2,1)}, bf16[136,1536]{1,0:T(8,128)(2,1)}, u32[]{:S(2)}, u32[]{:S(2)}) collective-permute-start(bf16[136,1536]{1,0:T(8,128)(2,1)} %collective-permute-done.7.refs_1_), channel_id=1, source_target_pairs={{0,1},{1,0},{2,3},{3,2},{4,5},{5,4},{6,7},{7,6},{8,9},{9,8},{10,11... | collective-permute-start | bytes 1253384 | tf_op jit(solution)/shard_map/ppermute | solution.py:385
  46.2 14.7 %collective-permute-start.13 = (bf16[136,1536]{1,0:T(8,128)(2,1)}, bf16[136,1536]{1,0:T(8,128)(2,1)}, u32[]{:S(2)}, u32[]{:S(2)}) collective-permute-start(bf16[136,1536]{1,0:T(8,128)(2,1)} %collective-permute-done.7.refs_1_), channel_id=1, source_target_pairs={{0,4},{1,5},{2,6},{3,7},{4,12},{5,13},{6,14},{7,15},{8,0},{9,1},{1... | collective-permute-start | bytes 1253384 | tf_op jit(solution)/shard_map/ppermute | solution.py:385
  49.8 11.8 %collective-permute-start.21 = (bf16[128,1536]{1,0:T(8,128)(2,1)}, bf16[128,1536]{1,0:T(8,128)(2,1)}, u32[]{:S(2)}, u32[]{:S(2)}) collective-permute-start(bf16[128,1536]{1,0:T(8,128)(2,1)} %fusion.1), channel_id=1, source_target_pairs={{0,2},{1,3},{2,0},{3,1},{4,6},{5,7},{6,4},{7,5},{8,10},{9,11},{10,... | collective-permute-start | bytes 1179656 | tf_op jit(solution)/shard_map/ppermute | solution.py:385
  60.9 2.9 %collective-permute-start.18 = (bf16[2,128,1536]{2,1,0:T(8,128)(2,1)}, bf16[2,128,1536]{2,1,0:T(8,128)(2,1)S(1)}, u32[]{:S(2)}, u32[]{:S(2)}) collective-permute-start(bf16[2,128,1536]{2,1,0:T(8,128)(2,1)} %after.13), channel_id=1, source_target_pairs={{0,1},{1,0},{2,3},{3,2},{4,5},{5,4},{6,7},{7,6},{8,9},{9,8},{10,11... | collective-permute-start | bytes 2359304 | tf_op jit(solution)/shard_map/ppermute | solution.py:385
  61.0 7.1 %collective-permute-start.14 = (bf16[136,1536]{1,0:T(8,128)(2,1)}, bf16[136,1536]{1,0:T(8,128)(2,1)}, u32[]{:S(2)}, u32[]{:S(2)}) collective-permute-start(bf16[136,1536]{1,0:T(8,128)(2,1)} %after.12.refs_0_.refs_2_), channel_id=1, source_target_pairs={{0,1},{1,0},{2,3},{3,2},{4,5},{5,4},{6,7},{7,6},{8,9},{9,8},{10,11... | collective-permute-start | bytes 1253384 | tf_op jit(solution)/shard_map/ppermute | solution.py:385
  61.5 6.6 %collective-permute-start.15 = (bf16[136,1536]{1,0:T(8,128)(2,1)}, bf16[136,1536]{1,0:T(8,128)(2,1)}, u32[]{:S(2)}, u32[]{:S(2)}) collective-permute-start(bf16[136,1536]{1,0:T(8,128)(2,1)} %collective-permute-done.13.refs_1_), channel_id=1, source_target_pairs={{0,1},{1,0},{2,3},{3,2},{4,5},{5,4},{6,7},{7,6},{8,9},{9,8},{10,11... | collective-permute-start | bytes 1253384 | tf_op jit(solution)/shard_map/ppermute | solution.py:385
  63.7 13.8 %collective-permute-start.22 = (bf16[128,1536]{1,0:T(8,128)(2,1)}, bf16[128,1536]{1,0:T(8,128)(2,1)}, u32[]{:S(2)}, u32[]{:S(2)}) collective-permute-start(bf16[128,1536]{1,0:T(8,128)(2,1)} %fusion.3), channel_id=1, source_target_pairs={{0,4},{1,5},{2,6},{3,7},{4,12},{5,13},{6,14},{7,15},{8,0},{9,1},{1... | collective-permute-start | bytes 1179656 | tf_op jit(solution)/shard_map/ppermute | solution.py:385
  63.8 0.9 copy-start.3
  66.5 11.7 %collective-permute-start.19 = (bf16[128,1536]{1,0:T(8,128)(2,1)}, bf16[128,1536]{1,0:T(8,128)(2,1)}, u32[]{:S(2)}, u32[]{:S(2)}) collective-permute-start(bf16[128,1536]{1,0:T(8,128)(2,1)} %fusion.4), channel_id=1, source_target_pairs={{0,2},{1,3},{2,0},{3,1},{4,6},{5,7},{6,4},{7,5},{8,10},{9,11},{10,... | collective-permute-start | bytes 1179656 | tf_op jit(solution)/shard_map/ppermute | solution.py:385
  77.4 3.2 %collective-permute-start.16 = (bf16[2,128,1536]{2,1,0:T(8,128)(2,1)}, bf16[2,128,1536]{2,1,0:T(8,128)(2,1)S(1)}, u32[]{:S(2)}, u32[]{:S(2)}) collective-permute-start(bf16[2,128,1536]{2,1,0:T(8,128)(2,1)} %get-tuple-element.25), channel_id=1, source_target_pairs={{0,1},{1,0},{2,3},{3,2},{4,5},{5,4},{6,7},{7,6},{8,9},{9,8},{10,11... | collective-permute-start | bytes 2359304 | tf_op jit(solution)/shard_map/ppermute | solution.py:385
  80.5 8.5 %collective-permute-start.23 = (bf16[64,1536]{1,0:T(8,128)(2,1)S(1)}, bf16[64,1536]{1,0:T(8,128)(2,1)S(1)}, u32[]{:S(2)}, u32[]{:S(2)}) collective-permute-start(bf16[64,1536]{1,0:T(8,128)(2,1)S(1)} %get-tuple-element.32), channel_id=1, source_target_pairs={{0,4},{1,5},{2,6},{3,7},{4,12},{5,13},{6,14},{7,15},{8,0},{9,1},{1... | collective-permute-start | bytes 589832 | tf_op jit(solution)/shard_map/ppermute | solution.py:385
  80.7 9.9 %copy-start.2 = (bf16[2,128,1536]{2,1,0:T(8,128)(2,1)}, bf16[2,128,1536]{2,1,0:T(8,128)(2,1)S(1)}, u32[]{:S(2)}) copy-start(bf16[2,128,1536]{2,1,0:T(8,128)(2,1)S(1)} %collective-permute-done.16) | copy-start | bytes 2359300
  82.8 7.8 %collective-permute-start.17 = (bf16[64,1536]{1,0:T(8,128)(2,1)S(1)}, bf16[64,1536]{1,0:T(8,128)(2,1)S(1)}, u32[]{:S(2)}, u32[]{:S(2)}) collective-permute-start(bf16[64,1536]{1,0:T(8,128)(2,1)S(1)} %get-tuple-element.34), channel_id=1, source_target_pairs={{0,2},{1,3},{2,0},{3,1},{4,6},{5,7},{6,4},{7,5},{8,10},{9,11},{10,... | collective-permute-start | bytes 589832 | tf_op jit(solution)/shard_map/ppermute | solution.py:385
  84.1 9.8 %collective-permute-start.27 = (bf16[64,1536]{1,0:T(8,128)(2,1)}, bf16[64,1536]{1,0:T(8,128)(2,1)}, u32[]{:S(2)}, u32[]{:S(2)}) collective-permute-start(bf16[64,1536]{1,0:T(8,128)(2,1)} %get-tuple-element.31), channel_id=1, source_target_pairs={{0,4},{1,5},{2,6},{3,7},{4,12},{5,13},{6,14},{7,15},{8,0},{9,1},{1... | collective-permute-start | bytes 589832 | tf_op jit(solution)/shard_map/ppermute | solution.py:385
  85.0 8.9 %collective-permute-start.26 = (bf16[64,1536]{1,0:T(8,128)(2,1)}, bf16[64,1536]{1,0:T(8,128)(2,1)}, u32[]{:S(2)}, u32[]{:S(2)}) collective-permute-start(bf16[64,1536]{1,0:T(8,128)(2,1)} %get-tuple-element.33), channel_id=1, source_target_pairs={{0,2},{1,3},{2,0},{3,1},{4,6},{5,7},{6,4},{7,5},{8,10},{9,11},{10,... | collective-permute-start | bytes 589832 | tf_op jit(solution)/shard_map/ppermute | solution.py:385
  91.6 1.5 %copy-start = (bf16[64,1536]{1,0:T(8,128)(2,1)}, bf16[64,1536]{1,0:T(8,128)(2,1)S(1)}, u32[]{:S(2)}) copy-start(bf16[64,1536]{1,0:T(8,128)(2,1)S(1)} %fusion.22.refs_1_) | copy-start | bytes 589828
  91.6 6.9 %collective-permute-start.25 = (bf16[64,1536]{1,0:T(8,128)(2,1)S(1)}, bf16[64,1536]{1,0:T(8,128)(2,1)}, u32[]{:S(2)}, u32[]{:S(2)}) collective-permute-start(bf16[64,1536]{1,0:T(8,128)(2,1)S(1)} %fusion.22.refs_1_), channel_id=1, source_target_pairs={{0,4},{1,5},{2,6},{3,7},{4,12},{5,13},{6,14},{7,15},{8,0},{9,1},{1... | collective-permute-start | bytes 589832 | tf_op jit(solution)/shard_map/ppermute | solution.py:385
  93.1 10.1 %collective-permute-start.24 = (bf16[128,1536]{1,0:T(8,128)(2,1)}, bf16[128,1536]{1,0:T(8,128)(2,1)}, u32[]{:S(2)}, u32[]{:S(2)}) collective-permute-start(bf16[128,1536]{1,0:T(8,128)(2,1)} %after.15), channel_id=1, source_target_pairs={{0,2},{1,3},{2,0},{3,1},{4,6},{5,7},{6,4},{7,5},{8,10},{9,11},{10,... | collective-permute-start | bytes 1179656 | tf_op jit(solution)/shard_map/ppermute | solution.py:385
  95.9 7.3 %collective-permute-start.28 = (bf16[64,1536]{1,0:T(8,128)(2,1)}, bf16[64,1536]{1,0:T(8,128)(2,1)}, u32[]{:S(2)}, u32[]{:S(2)}) collective-permute-start(bf16[64,1536]{1,0:T(8,128)(2,1)} %fusion.15), channel_id=1, source_target_pairs={{0,4},{1,5},{2,6},{3,7},{4,12},{5,13},{6,14},{7,15},{8,0},{9,1},{1... | collective-permute-start | bytes 589832 | tf_op jit(solution)/shard_map/ppermute | solution.py:385
